TPU v7x, 256 devices: a whole 4x4x8 slice. The times are simulated.
256 devices in a mesh: grp: 8 (over z_lo, core), seq: 32 (over z_hi, y, x).
Axes of the slice: x: 4, y: 4, z: 8 (z_hi: 2, z_lo: 4; z = z_hi * 4 + z_lo), core: 2. Of those that a mesh axis runs over, the one named last changes fastest.
Arguments:
- resp_len: int32 [128], P('grp'), parts along dimension 0, may hold values from 1 to 384, 4096 in all
- prompt_keys: bfloat16 [16384, 512], P(('grp', 'seq')), parts along dimension 0, may hold values from -6 to 6
- prompt_values: bfloat16 [16384, 512], P(('grp', 'seq')), parts along dimension 0, may hold values from -6 to 6
- resp_q: bfloat16 [32768, 2560], P(('grp', 'seq')), parts along dimension 0, may hold values from -16 to 16
- resp_k: bfloat16 [32768, 512], P(('grp', 'seq')), parts along dimension 0, may hold values from -6 to 6
- resp_v: bfloat16 [32768, 512], P(('grp', 'seq')), parts along dimension 0, may hold values from -6 to 6
- out_grad: bfloat16 [32768, 2560], P(('grp', 'seq')), parts along dimension 0, may hold values from -6 to 6
Outputs:
- attn_out: bfloat16 [32768, 2560], P(('grp', 'seq')), parts along dimension 0
- q_grad: bfloat16 [32768, 2560], P(('grp', 'seq')), parts along dimension 0
- resp_k_grad: bfloat16 [32768, 512], P(('grp', 'seq')), parts along dimension 0
- resp_v_grad: bfloat16 [32768, 512], P(('grp', 'seq')), parts along dimension 0
- prompt_k_grad: bfloat16 [16384, 512], P(('grp', 'seq')), parts along dimension 0
- prompt_v_grad: bfloat16 [16384, 512], P(('grp', 'seq')), parts along dimension 0
There are 8 independent parts, one for each index of `grp`. A program takes and returns all parts, laid end to end along the dimension named above; each array names one. Nothing has to cross between parts.
Inputs may be any that keep to these rules, and one draw needn't show every extreme that they name: `resp_len`: the 16 responses lie one after another in the response tokens, in this order, and their lengths sum to 4096.
All inputs are finite; a program needn't handle non-finite values.
Results may differ from a plain program's by a relative error of at most 0.04.
Values may be sent and summed in bfloat16 or wider, within the bound.
No kernel may reach another device: no remote copies, remote signals or barrier semaphores. Data moves between devices by JAX's collectives and lax.ppermute only.
A program may use at most 128 MiB of HBM per device.

v0:
```python
import jax
import jax.numpy as jnp
from jax import lax
from jax.sharding import PartitionSpec as P

HEADS = 20
KV_HEADS = 4
HEAD_DIM = 128
REACH = 3


negative_big = -1e30


def passed_along(value, axis, steps):
    count = lax.axis_size(axis)
    initial, last = (max(0, -steps), min(count, count - steps))
    return lax.ppermute(value, axis, [(source, source + steps) for source in range(initial, last)])


def segments_of(positions, resp_ends):
    return jnp.sum((positions[:, None] >= resp_ends[None, :]).astype(jnp.int32), axis=1)


def local(resp_len, prompt_keys, prompt_values, resp_q, resp_k, resp_v, out_grad):
    row_count = resp_q.shape[0]
    per_group = HEADS // KV_HEADS
    factor = HEAD_DIM ** (-0.5)
    kv_width = KV_HEADS * HEAD_DIM
    slot_count = REACH + 1
    my_index = lax.axis_index("seq")
    queries = resp_q.reshape(row_count, KV_HEADS, per_group, HEAD_DIM)
    upstream = out_grad.reshape(row_count, KV_HEADS, per_group, HEAD_DIM)
    cached_keys, cached_values = (
        lax.all_gather(prompt_keys, "seq", axis=0, tiled=True),
        lax.all_gather(prompt_values, "seq", axis=0, tiled=True),
    )
    prompt_rows = cached_keys.shape[0]
    key_block = min(512, prompt_rows)
    block_count = prompt_rows // key_block
    key_tiles = cached_keys.reshape(block_count, key_block, KV_HEADS, HEAD_DIM)
    value_tiles = cached_values.reshape(block_count, key_block, KV_HEADS, HEAD_DIM)
    key_parts = [resp_k]
    value_parts = [resp_v]
    for distance in range(1, slot_count):
        far_keys, far_values = passed_along((resp_k, resp_v), "seq", distance)
        key_parts = [far_keys] + key_parts
        value_parts = [far_values] + value_parts
    window_keys = jnp.concatenate(key_parts, 0)
    window_values = jnp.concatenate(value_parts, 0)
    window_keys = window_keys.reshape(slot_count * row_count, KV_HEADS, HEAD_DIM)
    window_values = window_values.reshape(slot_count * row_count, KV_HEADS, HEAD_DIM)
    resp_ends = jnp.cumsum(resp_len)
    query_pos = my_index * row_count + jnp.arange(row_count, dtype=jnp.int32)
    key_pos = (my_index - REACH) * row_count + jnp.arange(slot_count * row_count, dtype=jnp.int32)
    same_seg = (
        segments_of(key_pos, resp_ends)[None, :] == segments_of(query_pos, resp_ends)[:, None]
    )
    visible = (key_pos[None, :] >= 0) & (key_pos[None, :] <= query_pos[:, None]) & same_seg

    def logits(key_tile):
        return (
            jnp.einsum("qhgd,nhd->qhgn", queries, key_tile, preferred_element_type=jnp.float32)
            * factor
        )

    window_scores = jnp.where(visible[:, None, None, :], logits(window_keys), negative_big)

    def merge_stats(carry, scores):
        running_max, running_sum = carry
        new_max = jnp.maximum(running_max, jnp.max(scores, -1))
        running_sum = running_sum * jnp.exp(running_max - new_max) + jnp.sum(
            jnp.exp(scores - new_max[..., None]), -1
        )
        return (new_max, running_sum)

    def stat_step(carry, key_tile):
        return (merge_stats(carry, logits(key_tile)), None)

    stat_shape = (row_count, KV_HEADS, per_group)
    start_stats = (
        jnp.full(stat_shape, negative_big, jnp.float32),
        jnp.zeros(stat_shape, jnp.float32),
    )
    stats, unused = lax.scan(stat_step, start_stats, key_tiles)
    running_max, running_sum = merge_stats(stats, window_scores)
    log_total = (running_max + jnp.log(running_sum))[..., None]

    def weigh(scores, value_tile):
        rounded = jnp.exp(scores - log_total).astype(jnp.bfloat16)
        return jnp.einsum("qhgn,nhd->qhgd", rounded, value_tile, preferred_element_type=jnp.float32)

    def out_step(output_sum, tile_pair):
        return (output_sum + weigh(logits(tile_pair[0]), tile_pair[1]), None)

    query_shape = (row_count, KV_HEADS, per_group, HEAD_DIM)
    output_sum, unused = lax.scan(
        out_step, jnp.zeros(query_shape, jnp.float32), (key_tiles, value_tiles)
    )
    attention = (output_sum + weigh(window_scores, window_values)).astype(jnp.bfloat16)
    row_dot = jnp.sum(
        upstream.astype(jnp.float32) * attention.astype(jnp.float32), -1, keepdims=True
    )

    def score_parts(scores, value_tile):
        weights = jnp.exp(scores - log_total)
        weight_grad = jnp.einsum(
            "qhgd,nhd->qhgn", upstream, value_tile, preferred_element_type=jnp.float32
        )
        score_grad = (weights * (weight_grad - row_dot)).astype(jnp.bfloat16)
        return (weights.astype(jnp.bfloat16), score_grad)

    def key_terms(scores, value_tile):
        rounded, score_grad = score_parts(scores, value_tile)
        key_grad = (
            jnp.einsum("qhgn,qhgd->nhd", score_grad, queries, preferred_element_type=jnp.float32)
            * factor
        )
        value_grad = jnp.einsum(
            "qhgn,qhgd->nhd", rounded, upstream, preferred_element_type=jnp.float32
        )
        return (score_grad, key_grad, value_grad)

    def query_term(score_grad, key_tile):
        return jnp.einsum(
            "qhgn,nhd->qhgd", score_grad, key_tile, preferred_element_type=jnp.float32
        )

    def back_step(query_grad, tile_pair):
        key_tile, value_tile = tile_pair
        score_grad, key_grad, value_grad = key_terms(logits(key_tile), value_tile)
        stacked = jnp.concatenate(
            [key_grad.reshape(key_block, kv_width), value_grad.reshape(key_block, kv_width)], 1
        )
        return (query_grad + query_term(score_grad, key_tile), stacked)

    query_grad, row_terms = lax.scan(
        back_step, jnp.zeros(query_shape, jnp.float32), (key_tiles, value_tiles)
    )
    summed = lax.psum_scatter(
        row_terms.reshape(prompt_rows, 2 * kv_width), "seq", scatter_dimension=0, tiled=True
    )
    window_grad, window_key_grad, window_value_grad = key_terms(window_scores, window_values)
    query_grad = query_grad + query_term(window_grad, window_keys)
    part_keys = window_key_grad.reshape(slot_count * row_count, kv_width)
    part_values = window_value_grad.reshape(slot_count * row_count, kv_width)
    own_keys = part_keys[REACH * row_count :]
    own_values = part_values[REACH * row_count :]
    for distance in range(1, slot_count):
        slot_start = (REACH - distance) * row_count
        back_keys, back_values = passed_along(
            (
                part_keys[slot_start : slot_start + row_count],
                part_values[slot_start : slot_start + row_count],
            ),
            "seq",
            -distance,
        )
        own_keys = own_keys + back_keys
        own_values = own_values + back_values
    attn_out = attention.reshape(row_count, HEADS * HEAD_DIM)
    q_grad = (query_grad * factor).astype(jnp.bfloat16).reshape(row_count, HEADS * HEAD_DIM)
    return (
        attn_out,
        q_grad,
        own_keys.astype(jnp.bfloat16),
        own_values.astype(jnp.bfloat16),
        summed[:, :kv_width].astype(jnp.bfloat16),
        summed[:, kv_width:].astype(jnp.bfloat16),
    )


def solution(mesh):
    placed = (
        P("grp"),
        P(("grp", "seq"), None),
        P(("grp", "seq"), None),
        P(("grp", "seq"), None),
        P(("grp", "seq"), None),
        P(("grp", "seq"), None),
        P(("grp", "seq"), None),
    )
    return jax.shard_map(
        local,
        mesh=mesh,
        in_specs=placed,
        out_specs=(
            P(("grp", "seq"), None),
            P(("grp", "seq"), None),
            P(("grp", "seq"), None),
            P(("grp", "seq"), None),
            P(("grp", "seq"), None),
            P(("grp", "seq"), None),
        ),
        check_vma=False,
    )
```

profile of v0, /device:TPU:192, one launch (start us, length us, event | category | flops | bytes accessed | tf_op | source)
XLA Modules:
  0.0 599.0 jit_solution(18133879287538395304)
XLA Ops:
  12.4 4.6 collective-permute-start.1
  17.0 4.4 collective-permute-start
  24.8 4.7 collective-permute-start.3
  30.7 16.0 %collective-permute-done.4 = bf16[128,512]{1,0:T(8,128)(2,1)S(1)} collective-permute-done((bf16[128,512]{1,0:T(8,128)(2,1)}, bf16[128,512]{1,0:T(8,128)(2,1)S(1)}, u32[]{:S(2)}, u32[]{:S(2)}) %collective-permute-start.4) | collective-permute-done | bytes 131104 | tf_op jit(solution)/shard_map/ppermute | solution.py:18
  46.7 5.4 collective-permute-start.5
  55.7 8.6 %collective-permute-done.5 = bf16[128,512]{1,0:T(8,128)(2,1)} collective-permute-done((bf16[128,512]{1,0:T(8,128)(2,1)}, bf16[128,512]{1,0:T(8,128)(2,1)}, u32[]{:S(2)}, u32[]{:S(2)}) %collective-permute-start.5) | collective-permute-done | bytes 131104 | tf_op jit(solution)/shard_map/ppermute | solution.py:18
  70.5 34.9 %all-gather.5.cloned.1.call-done = bf16[2048,512]{1,0:T(8,128)(2,1)} async-done(((bf16[64,512]{1,0:T(8,128)(2,1)}), bf16[2048,512]{1,0:T(8,128)(2,1)}) %all-gather.5.cloned.1.call-update) | async-done | bytes 2097168 | tf_op jit(solution)/shard_map/all_gather | solution.py:35
  112.7 11.4 %while.37 = (s32[]{:T(128)}, f32[128,4,5]{0,2,1:T(8,128)S(1)}, f32[128,4,5]{0,2,1:T(8,128)S(1)}, bf16[4,512,4,128]{3,1,2,0:T(8,128)(2,1)}, bf16[128,4,5,128]{3,0,2,1:T(8,128)(2,1)S(1)}, /*index=5*/s32[]{:T(128)}, s32[]{:T(128)}) while((s32[]{:T(128)}, f32[128,4,5]{0,2,1:T(8,128)S(1)}, f32[128,4,5]{0,2,1:T(8,128)S(1)}, ...), condition=%wide.region_3.4_spmd.clone, body=%wide.region_0.3_spmd.clone.sunk | while | flops 342110720 | bytes 11798628 | solution.py:85
  127.7 66.9 %all-gather.3.cloned.1.call-done = bf16[2048,512]{1,0:T(8,128)(2,1)} async-done(((bf16[64,512]{1,0:T(8,128)(2,1)}), bf16[2048,512]{1,0:T(8,128)(2,1)}) %all-gather.3.cloned.1.call-update) | async-done | bytes 2097168 | tf_op jit(solution)/shard_map/all_gather | solution.py:36
  198.6 22.2 %while.38 = (s32[]{:T(128)}, f32[128,4,5,128]{0,3,2,1:T(8,128)}, bf16[4,512,4,128]{3,2,1,0:T(4,128)(2,1)}, bf16[4,512,4,128]{3,1,2,0:T(8,128)(2,1)}, bf16[128,4,...) while((s32[]{:T(128)}, f32[128,4,5,128]{0,3,2,1:T(8,128)}, ...), condition=%wide.region_10.11_spmd.clone, body=%wide.region_9.10_spmd.clone.sunk | while | flops 675676160 | bytes 6432879 | solution.py:97
  205.3 4.1 fusion.114
  211.0 4.1 fusion.114
  220.8 5.4 multiply_reduce_fusion
  226.2 58.4 %while.39 = (s32[]{:T(128)}, f32[128,4,5,128]{0,3,2,1:T(8,128)}, f32[4,512,1024]{2,1,0:T(8,128)}, bf16[4,512,4,128]{3,1,2,0:T(8,128)(2,1)}, bf16[128,4,5,128]{0,...) while((s32[]{:T(128)}, f32[128,4,5,128]{0,3,2,1:T(8,128)}, ...), condition=%wide.region_13.14_spmd.clone, body=%wide.region_12.13_spmd.clone.sunk | while | flops 1689649152 | bytes 46168204 | solution.py:137
  290.4 8.2 %collective-permute-start.10 = (f32[128,512]{1,0:T(8,128)}, f32[128,512]{1,0:T(8,128)}, u32[]{:S(2)}, u32[]{:S(2)}) collective-permute-start(f32[128,512]{1,0:T(8,128)} %copy.121), channel_id=1, source_target_pairs={{2,0},{3,1},{4,2},{5,3},{6,4},{7,5},{8,6},{9,7},{10,8},{11,9},{12,... | collective-permute-start | bytes 786440 | tf_op jit(solution)/shard_map/ppermute | solution.py:18
  304.9 4.4 fusion.48
  317.2 12.8 %collective-permute-done.10 = f32[128,512]{1,0:T(8,128)} collective-permute-done((f32[128,512]{1,0:T(8,128)}, f32[128,512]{1,0:T(8,128)}, u32[]{:S(2)}, u32[]{:S(2)}) %collective-permute-start.10) | collective-permute-done | bytes 262176 | tf_op jit(solution)/shard_map/ppermute | solution.py:18
  330.0 10.8 %collective-permute-start.6 = (f32[128,512]{1,0:T(8,128)S(1)}, f32[128,512]{1,0:T(8,128)}, u32[]{:S(2)}, u32[]{:S(2)}) collective-permute-start(f32[128,512]{1,0:T(8,128)S(1)} %copy.114), channel_id=1, source_target_pairs={{1,0},{2,1},{3,2},{4,3},{5,4},{6,5},{7,6},{8,7},{9,8},{10,9},{11,1... | collective-permute-start | bytes 786440 | tf_op jit(solution)/shard_map/ppermute | solution.py:18
  346.0 12.2 %collective-permute-done.11 = f32[128,512]{1,0:T(8,128)} collective-permute-done((f32[128,512]{1,0:T(8,128)S(1)}, f32[128,512]{1,0:T(8,128)}, u32[]{:S(2)}, u32[]{:S(2)}) %collective-permute-start.11) | collective-permute-done | bytes 262176 | tf_op jit(solution)/shard_map/ppermute | solution.py:18
  358.3 30.5 %collective-permute-done.9 = f32[128,512]{1,0:T(8,128)} collective-permute-done((f32[128,512]{1,0:T(8,128)}, f32[128,512]{1,0:T(8,128)}, u32[]{:S(2)}, u32[]{:S(2)}) %collective-permute-start.9) | collective-permute-done | bytes 262176 | tf_op jit(solution)/shard_map/ppermute | solution.py:18
  390.6 24.3 %collective-permute-done.7 = f32[128,512]{1,0:T(8,128)} collective-permute-done((f32[128,512]{1,0:T(8,128)S(1)}, f32[128,512]{1,0:T(8,128)}, u32[]{:S(2)}, u32[]{:S(2)}) %collective-permute-start.7) | collective-permute-done | bytes 262176 | tf_op jit(solution)/shard_map/ppermute | solution.py:18
  414.9 16.7 %collective-permute-done.8 = f32[128,512]{1,0:T(8,128)} collective-permute-done((f32[128,512]{1,0:T(8,128)S(1)}, f32[128,512]{1,0:T(8,128)}, u32[]{:S(2)}, u32[]{:S(2)}) %collective-permute-start.8) | collective-permute-done | bytes 262176 | tf_op jit(solution)/shard_map/ppermute | solution.py:18
  431.6 15.8 %collective-permute-done.6 = f32[128,512]{1,0:T(8,128)} collective-permute-done((f32[128,512]{1,0:T(8,128)S(1)}, f32[128,512]{1,0:T(8,128)}, u32[]{:S(2)}, u32[]{:S(2)}) %collective-permute-start.6) | collective-permute-done | bytes 262176 | tf_op jit(solution)/shard_map/ppermute | solution.py:18
  449.3 141.5 %reduce-scatter.2.cloned.1.call-done = f32[64,1024]{1,0:T(8,128)} async-done(((f32[2048,1024]{1,0:T(8,128)}), f32[64,1024]{1,0:T(8,128)}) %reduce-scatter.2.cloned.1.call-update) | async-done | bytes 262160 | tf_op jit(solution)/shard_map/reduce_scatter | solution.py:140
  (137 shorter events, 147.9 us)
Async XLA Ops:
  7.2 98.3 %all-gather.5.cloned.1.call-start = ((), (), s32[]{:S(2)}) async-start(), calls=%async_computation.2 | async-start | bytes 2162688 | tf_op jit(solution)/shard_map/all_gather | solution.py:35
  7.9 186.7 %all-gather.3.cloned.1.call-start = ((), (), s32[]{:S(2)}) async-start(), calls=%async_computation.1 | async-start | bytes 2162688 | tf_op jit(solution)/shard_map/all_gather | solution.py:36
  9.0 57.4 %collective-permute-start.2 = (bf16[128,512]{0,1:T(8,128)(2,1)S(1)}, bf16[128,512]{0,1:T(8,128)(2,1)S(1)}, u32[]{:S(2)}, u32[]{:S(2)}) collective-permute-start(bf16[128,512]{0,1:T(8,128)(2,1)S(1)} %copy.96), channel_id=1, source_target_pairs={{0,1},{1,2},{2,3},{3,4},{4,5},{5,6},{6,7},{7,8},{8,9},{9,10},{10,1... | collective-permute-start | bytes 393224 | tf_op jit(solution)/shard_map/ppermute | solution.py:18
  12.4 53.9 %collective-permute-start.1 = (bf16[128,512]{0,1:T(8,128)(2,1)S(1)}, bf16[128,512]{0,1:T(8,128)(2,1)S(1)}, u32[]{:S(2)}, u32[]{:S(2)}) collective-permute-start(bf16[128,512]{0,1:T(8,128)(2,1)S(1)} %copy.96), channel_id=1, source_target_pairs={{0,2},{1,3},{2,4},{3,5},{4,6},{5,7},{6,8},{7,9},{8,10},{9,11},{10,... | collective-permute-start | bytes 393224 | tf_op jit(solution)/shard_map/ppermute | solution.py:18
  17.0 49.3 %collective-permute-start = (bf16[128,512]{0,1:T(8,128)(2,1)S(1)}, bf16[128,512]{0,1:T(8,128)(2,1)S(1)}, u32[]{:S(2)}, u32[]{:S(2)}) collective-permute-start(bf16[128,512]{0,1:T(8,128)(2,1)S(1)} %copy.96), channel_id=1, source_target_pairs={{0,3},{1,4},{2,5},{3,6},{4,7},{5,8},{6,9},{7,10},{8,11},{9,12},{10... | collective-permute-start | bytes 393224 | tf_op jit(solution)/shard_map/ppermute | solution.py:18
  21.4 25.3 %collective-permute-start.4 = (bf16[128,512]{1,0:T(8,128)(2,1)}, bf16[128,512]{1,0:T(8,128)(2,1)S(1)}, u32[]{:S(2)}, u32[]{:S(2)}) collective-permute-start(bf16[128,512]{1,0:T(8,128)(2,1)} %param.18), channel_id=1, source_target_pairs={{0,2},{1,3},{2,4},{3,5},{4,6},{5,7},{6,8},{7,9},{8,10},{9,11},{10,... | collective-permute-start | bytes 393224 | tf_op jit(solution)/shard_map/ppermute | solution.py:18
  24.8 30.8 %collective-permute-start.3 = (bf16[128,512]{1,0:T(8,128)(2,1)}, bf16[128,512]{1,0:T(8,128)(2,1)S(1)}, u32[]{:S(2)}, u32[]{:S(2)}) collective-permute-start(bf16[128,512]{1,0:T(8,128)(2,1)} %param.18), channel_id=1, source_target_pairs={{0,3},{1,4},{2,5},{3,6},{4,7},{5,8},{6,9},{7,10},{8,11},{9,12},{10... | collective-permute-start | bytes 393224 | tf_op jit(solution)/shard_map/ppermute | solution.py:18
  29.5 561.3 %reduce-scatter.2.cloned.1.call-start = ((), (), s32[]{:S(2)}) async-start(), calls=%async_computation.3 | async-start | bytes 8650752 | tf_op jit(solution)/shard_map/reduce_scatter | solution.py:140
  46.7 17.6 %collective-permute-start.5 = (bf16[128,512]{1,0:T(8,128)(2,1)}, bf16[128,512]{1,0:T(8,128)(2,1)}, u32[]{:S(2)}, u32[]{:S(2)}) collective-permute-start(bf16[128,512]{1,0:T(8,128)(2,1)} %param.18), channel_id=1, source_target_pairs={{0,1},{1,2},{2,3},{3,4},{4,5},{5,6},{6,7},{7,8},{8,9},{9,10},{10,1... | collective-permute-start | bytes 393224 | tf_op jit(solution)/shard_map/ppermute | solution.py:18
  66.4 0.8 copy-start.1
  290.4 39.6 %collective-permute-start.10 = (f32[128,512]{1,0:T(8,128)}, f32[128,512]{1,0:T(8,128)}, u32[]{:S(2)}, u32[]{:S(2)}) collective-permute-start(f32[128,512]{1,0:T(8,128)} %copy.121), channel_id=1, source_target_pairs={{2,0},{3,1},{4,2},{5,3},{6,4},{7,5},{8,6},{9,7},{10,8},{11,9},{12,... | collective-permute-start | bytes 786440 | tf_op jit(solution)/shard_map/ppermute | solution.py:18
  298.6 59.7 %collective-permute-start.11 = (f32[128,512]{1,0:T(8,128)S(1)}, f32[128,512]{1,0:T(8,128)}, u32[]{:S(2)}, u32[]{:S(2)}) collective-permute-start(f32[128,512]{1,0:T(8,128)S(1)} %copy.122), channel_id=1, source_target_pairs={{3,0},{4,1},{5,2},{6,3},{7,4},{8,5},{9,6},{10,7},{11,8},{12,9},{13... | collective-permute-start | bytes 786440 | tf_op jit(solution)/shard_map/ppermute | solution.py:18
  301.2 87.5 %collective-permute-start.9 = (f32[128,512]{1,0:T(8,128)}, f32[128,512]{1,0:T(8,128)}, u32[]{:S(2)}, u32[]{:S(2)}) collective-permute-start(f32[128,512]{1,0:T(8,128)} %copy.119), channel_id=1, source_target_pairs={{1,0},{2,1},{3,2},{4,3},{5,4},{6,5},{7,6},{8,7},{9,8},{10,9},{11,1... | collective-permute-start | bytes 786440 | tf_op jit(solution)/shard_map/ppermute | solution.py:18
  309.4 1.6 copy-start
  309.4 31.4 %copy-start.2 = (bf16[512,512]{0,1:T(8,128)(2,1)S(1)}, bf16[512,512]{0,1:T(8,128)(2,1)}, u32[]{:S(2)}) copy-start(bf16[512,512]{0,1:T(8,128)(2,1)} %copy-done.1) | copy-start | bytes 1572868
  311.0 32.6 %copy-start.3 = (bf16[128,4,5,128]{0,3,2,1:T(8,128)(2,1)S(1)}, bf16[128,4,5,128]{0,3,2,1:T(8,128)(2,1)}, u32[]{:S(2)}) copy-start(bf16[128,4,5,128]{0,3,2,1:T(8,128)(2,1)} %get-tuple-element.312) | copy-start | bytes 1966084
  311.5 103.4 %collective-permute-start.7 = (f32[128,512]{1,0:T(8,128)S(1)}, f32[128,512]{1,0:T(8,128)}, u32[]{:S(2)}, u32[]{:S(2)}) collective-permute-start(f32[128,512]{1,0:T(8,128)S(1)} %copy.116), channel_id=1, source_target_pairs={{2,0},{3,1},{4,2},{5,3},{6,4},{7,5},{8,6},{9,7},{10,8},{11,9},{12,... | collective-permute-start | bytes 786440 | tf_op jit(solution)/shard_map/ppermute | solution.py:18
  314.2 117.4 %collective-permute-start.8 = (f32[128,512]{1,0:T(8,128)S(1)}, f32[128,512]{1,0:T(8,128)}, u32[]{:S(2)}, u32[]{:S(2)}) collective-permute-start(f32[128,512]{1,0:T(8,128)S(1)} %copy.117), channel_id=1, source_target_pairs={{3,0},{4,1},{5,2},{6,3},{7,4},{8,5},{9,6},{10,7},{11,8},{12,9},{13... | collective-permute-start | bytes 786440 | tf_op jit(solution)/shard_map/ppermute | solution.py:18
  330.0 117.4 %collective-permute-start.6 = (f32[128,512]{1,0:T(8,128)S(1)}, f32[128,512]{1,0:T(8,128)}, u32[]{:S(2)}, u32[]{:S(2)}) collective-permute-start(f32[128,512]{1,0:T(8,128)S(1)} %copy.114), channel_id=1, source_target_pairs={{1,0},{2,1},{3,2},{4,3},{5,4},{6,5},{7,6},{8,7},{9,8},{10,9},{11,1... | collective-permute-start | bytes 786440 | tf_op jit(solution)/shard_map/ppermute | solution.py:18
Sparse Core Ops, SparseCore 0:
  11.5 93.8 all-gather.4
  109.0 85.6 all-gather.2
  284.7 306.0 reduce-scatter.1
where the time goes:
time: 601 us; the launch traced here: 599 us
  waiting for transfers between devices  381 us (63%)
  matrix products  78.1 us (13%)
  starting transfers between devices  57 us (9%)
  local copies, waits for them, and re-layouts  48.7 us (8%)
  other arithmetic  19.5 us (3%)
  between operations  14.1 us (2%)
    reduce_scatter x1, waiting for transfers between devices, local(): lax.psum_scatter(row_terms.reshape(prompt_rows, 2 * kv_width), 'seq', sca...  142 us
    ppermute x12, waiting for transfers between devices, passed_along(): lax.ppermute(value, axis, [(source, source + steps) for source in range(i...  137 us
    all_gather x1, waiting for transfers between devices, local(): lax.all_gather(prompt_values, 'seq', axis=0, tiled=True)  66.9 us
    ppermute x12, starting transfers between devices, passed_along(): lax.ppermute(value, axis, [(source, source + steps) for source in range(i...  56.9 us
    all_gather x1, waiting for transfers between devices, local(): lax.all_gather(prompt_keys, 'seq', axis=0, tiled=True)  34.9 us
    dot_general x5, matrix products, weigh(): jnp.einsum('qhgn,nhd->qhgd', rounded, value_tile, preferred_element_type=...  21.4 us
    dot_general x9, matrix products, logits(): jnp.einsum('qhgd,nhd->qhgn', queries, key_tile, preferred_element_type=jn...  18.4 us
    dot_general x5, matrix products, query_term(): jnp.einsum('qhgn,nhd->qhgd', score_grad, key_tile, preferred_element_type...  15.2 us
  transfers between devices with their start and end apart: 15, of which 11 were waited for; matrix products, arithmetic and copies ran while one was open for 9% of the time, Pallas kernels for 0%

commit v1 on v0

v1 whole, which is shorter than its diff:
```python
import jax
import jax.numpy as jnp
from jax import lax
from jax.experimental import pallas as pl
from jax.experimental.pallas import tpu as pltpu
from jax.sharding import PartitionSpec as P

HEADS = 20
KV_HEADS = 4
HEAD_DIM = 128
PER_GROUP = HEADS // KV_HEADS
BACK = 384
NEGATIVE = -1e30
LOG2E = 1.4426950408889634
FACTOR = HEAD_DIM ** (-0.5)

ROWS = 256
KEYS = 512
SPAN = 640
PROMPT_ROWS = 2048
OWN_ROWS = 512
WIDE = PER_GROUP * HEAD_DIM


def nt(a, b):
    return lax.dot_general(a, b, (((1,), (1,)), ((), ())), preferred_element_type=jnp.float32)


def nn(a, b):
    return lax.dot_general(a, b, (((1,), (0,)), ((), ())), preferred_element_type=jnp.float32)


def block_at(x, distance):
    return pl.ds(pl.multiple_of(lax.rem(x + 4 - distance, 4) * 128, 128), 128)


def attention_kernel(
    len_ref, where_ref, q0, q1, q2, q3, s0, s1, s2, s3, before_ref, p0, p1, p2a, p2b, p3,
    o0, o1, o2, o3, stay_ref, minus_ref, plus_ref, minus2_ref, plus2_ref, back_grad_ref, own_grad_ref,
    key2, value1, key_t, value_t, q_all, o_all, s_ref, p_ref, key_sum, value_sum,
):
    base, x = where_ref[0], where_ref[1]
    window = PROMPT_ROWS
    total_rows = PROMPT_ROWS + BACK + OWN_ROWS

    def place(at, source):
        key2[at, :128] = source[:, :128]
        key2[at, 128:] = source[:, :128]
        value1[at, :128] = source[:, 128:]

    value1[:, 128:] = jnp.ones((total_rows, 128), jnp.bfloat16)
    for at, source in ((0, p0), (512, p1), (1024, p2a), (1280, p2b), (1536, p3), (window, before_ref)):
        place(pl.ds(at, source.shape[0]), source)
    for d, source in enumerate((s0, s1, s2, s3)):
        first = window + BACK + lax.rem(x + 4 - d, 4) * 128
        place(pl.ds(pl.multiple_of(first, 128), 128), source.at[128:256, :])
    value_t[128:, :] = jnp.ones((16, total_rows), jnp.bfloat16)
    for c in range(0, total_rows, 128):
        at = slice(c, c + 128)
        key_t[:, at] = key2[at, :128].astype(jnp.float32).T.astype(jnp.bfloat16)
        value_t[:128, at] = value1[at, :128].astype(jnp.float32).T.astype(jnp.bfloat16)
    for d, source in enumerate((q0, q1, q2, q3)):
        q_all[block_at(x, d), :] = source[...]
    key_sum[...] = jnp.zeros_like(key_sum)
    value_sum[...] = jnp.zeros_like(value_sum)

    def step(i, carry):
        block, head = i // PER_GROUP, lax.rem(i, PER_GROUP)
        mine = pl.ds(pl.multiple_of(block * ROWS, ROWS), ROWS)
        q_cols = pl.ds(pl.multiple_of(head * 128, 128), 128)
        g_cols = pl.ds(pl.multiple_of(WIDE + head * 128, 128), 128)
        q = q_all[mine, q_cols]
        scaled = q.astype(jnp.float32).T * (FACTOR * LOG2E)
        grad_t = q_all[mine, g_cols].astype(jnp.float32).T
        high = scaled.astype(jnp.bfloat16)
        low = (scaled - high.astype(jnp.float32)).astype(jnp.bfloat16)
        q2t = jnp.concatenate([high, low], 0)

        own = base + block * ROWS
        row_pos = own + lax.broadcasted_iota(jnp.int32, (1, ROWS), 1)
        seg_start = jnp.zeros((1, ROWS), jnp.int32)
        end = jnp.int32(0)
        for j in range(16):
            end = end + len_ref[j]
            seg_start = jnp.maximum(seg_start, jnp.where(row_pos >= end, end, 0))
        key_pos = own - BACK + lax.broadcasted_iota(jnp.int32, (SPAN, ROWS), 0)
        seen = (key_pos <= row_pos) & (key_pos >= seg_start)
        span_first = window + block * ROWS
        span = pl.ds(pl.multiple_of(span_first, 128), SPAN)
        tiles = [(slice(c, c + KEYS), slice(c, c + KEYS)) for c in range(0, PROMPT_ROWS, KEYS)]
        tiles.append((span, slice(PROMPT_ROWS, PROMPT_ROWS + SPAN)))

        top = None
        for keys, at in tiles:
            s = nn(key2[keys, :], q2t)
            if keys is span:
                s = jnp.where(seen, s, NEGATIVE)
            s_ref[at, :] = s
            tile_top = jnp.max(s, axis=0, keepdims=True)
            top = tile_top if top is None else jnp.maximum(top, tile_top)

        total = jnp.zeros((144, ROWS), jnp.float32)
        for keys, at in tiles:
            p = jnp.exp2(s_ref[at, :] - top).astype(jnp.bfloat16)
            p_ref[at, :] = p
            total = total + nn(value_t[:, keys], p)

        inverse = 1.0 / total[128:129, :]
        out = (total[:128, :] * inverse).astype(jnp.bfloat16).astype(jnp.float32)
        o_all[mine, q_cols] = out.T.astype(jnp.bfloat16)
        grad_n = (grad_t * inverse).astype(jnp.bfloat16)
        row_dot = -jnp.sum(grad_n.astype(jnp.float32) * out, axis=0, keepdims=True)
        dot_high = row_dot.astype(jnp.bfloat16).astype(jnp.float32)
        line = lax.broadcasted_iota(jnp.int32, (128, ROWS), 0)
        extra = jnp.where(line == 0, dot_high, jnp.where(line == 1, row_dot - dot_high, 0.0))
        grad2 = jnp.concatenate([grad_n, extra.astype(jnp.bfloat16)], 0)

        dq = jnp.zeros((HEAD_DIM, ROWS), jnp.float32)
        for keys, at in tiles:
            p = p_ref[at, :]
            ds = (p.astype(jnp.float32) * nn(value1[keys, :], grad2)).astype(jnp.bfloat16)
            dq = dq + nn(key_t[:, keys], ds)
            key_sum[keys, :] += nn(ds, q)
            value_sum[keys, :] += nt(p, grad_n)
        o_all[mine, g_cols] = (dq * FACTOR).T.astype(jnp.bfloat16)
        return carry

    lax.fori_loop(0, OWN_ROWS // ROWS * PER_GROUP, step, 0)

    for d, target in enumerate((o0, o1, o2, o3)):
        target[...] = o_all[block_at(x, d), :]
    places = (
        (0, 512, stay_ref, 0), (1024, 1280, minus_ref, 0), (768, 1024, minus_ref, 256),
        (1280, 1536, plus_ref, 0), (1536, 1792, plus_ref, 256),
        (512, 768, minus2_ref, 0), (1792, 2048, plus2_ref, 0),
        (window, window + BACK, back_grad_ref, 0), (window + BACK, total_rows, own_grad_ref, 0),
    )
    for first, last, target, at in places:
        target[at : at + last - first, :128] = key_sum[first:last, :] * FACTOR
        target[at : at + last - first, 128:] = value_sum[first:last, :]


def call(body, scalars, operands, outs, name, scratch=(), limit=24, after=(), cost=None):
    vmem, smem = pl.BlockSpec(memory_space=pltpu.VMEM), pl.BlockSpec(memory_space=pltpu.SMEM)
    count = len(scalars) + len(operands)

    def kernel(*refs):
        body(*refs[:count], *refs[count + len(after) :])

    return pl.pallas_call(
        kernel,
        in_specs=[smem] * len(scalars) + [vmem] * len(operands) + [pl.BlockSpec(memory_space=pl.ANY)] * len(after),
        out_specs=[vmem] * len(outs),
        out_shape=[jax.ShapeDtypeStruct(shape, dtype) for shape, dtype in outs],
        scratch_shapes=list(scratch),
        compiler_params=pltpu.CompilerParams(vmem_limit_bytes=limit * 1024 * 1024),
        cost_estimate=cost,
        name=name,
    )(*scalars, *operands, *after)


def attention(resp_len, where, operands):
    rows = PROMPT_ROWS + BACK + OWN_ROWS
    bf16, f32 = jnp.bfloat16, jnp.float32
    return call(
        attention_kernel, (resp_len, where), operands,
        [((128, 2 * WIDE), bf16)] * 4 + [((n, 256), f32) for n in (512, 512, 512, 256, 256, BACK, OWN_ROWS)],
        "attention",
        scratch=[
            pltpu.VMEM((rows, 256), bf16),
            pltpu.VMEM((rows, 256), bf16),
            pltpu.VMEM((128, rows), bf16),
            pltpu.VMEM((144, rows), bf16),
            pltpu.VMEM((OWN_ROWS, 2 * WIDE), bf16),
            pltpu.VMEM((OWN_ROWS, 2 * WIDE), bf16),
            pltpu.VMEM((PROMPT_ROWS + SPAN, ROWS), f32),
            pltpu.VMEM((PROMPT_ROWS + SPAN, ROWS), bf16),
            pltpu.VMEM((rows, 128), f32),
            pltpu.VMEM((rows, 128), f32),
        ],
        limit=40,
        cost=pl.CostEstimate(
            flops=6 * 2 * 2560 * 2560 * 128, bytes_accessed=10_000_000, transcendentals=2560 * 2560
        ),
    )


def head_columns(x, distance, width):
    return pl.ds(pl.multiple_of(lax.rem(x + distance, 4) * width, 128), width)


def pack_small_kernel(where_ref, pk_ref, pv_ref, pk_far, pv_far, k_ref, v_ref, s0, s1, s2, s3):
    x = where_ref[1]
    for d, target in enumerate((s0, s1, s2, s3)):
        for at, keys, values in ((0, pk_ref, pv_ref), (64, pk_far, pv_far), (128, k_ref, v_ref)):
            target[at : at + keys.shape[0], :128] = keys[:, head_columns(x, d, 128)]
            target[at : at + keys.shape[0], 128:] = values[:, head_columns(x, d, 128)]


def pack_rows_kernel(where_ref, q_ref, g_ref, q0, q1, q2, q3):
    x = where_ref[1]
    for d, target in enumerate((q0, q1, q2, q3)):
        target[:, :WIDE] = q_ref[:, head_columns(x, d, WIDE)]
        target[:, WIDE:] = g_ref[:, head_columns(x, d, WIDE)]


def collect_kernel(where_ref, s0, s1, s2, s3, mine_ref, ahead_ref):
    x = where_ref[1]
    for d, source in enumerate((s0, s1, s2, s3)):
        mine_ref[d * 128 : d * 128 + 128, :] = source[:128, :]
        block = lax.rem(x + 4 - d, 4)

        @pl.when(block > 0)
        def _():
            ahead_ref[pl.ds(pl.multiple_of((block - 1) * 128, 128), 128), :] = source[128:, :]


def prompt_sum_kernel(stay, minus, plus, minus2, plus2, back, keep_ref, give_ref, back_ref):
    for d in range(4):
        for z, target in ((0, keep_ref), (1, give_ref)):
            at = (d * 2 + z) * 64
            total = stay[at : at + 64, :]
            if d < 2:
                total = total + minus2[at : at + 64, :] + plus[256 + at : 320 + at, :]
            else:
                total = total + plus2[at - 256 : at - 192, :] + minus[at : at + 64, :]
            target[d * 64 : d * 64 + 64, :] = total
    back_ref[...] = back[...]


def final_sum_kernel(where_ref, keep_ref, got_ref, own_ref, back_ref, f0, f1, f2, f3):
    x = where_ref[1]
    for d, target in enumerate((f0, f1, f2, f3)):
        at = slice(d * 64, d * 64 + 64)
        target[:64, :] = (keep_ref[at, :] + got_ref[at, :]).astype(jnp.bfloat16)
        block = lax.rem(x + 4 - d, 4)
        behind = pl.ds(pl.multiple_of(jnp.maximum(block - 1, 0) * 128, 128), 128)
        extra = jnp.where(block > 0, back_ref[behind, :], 0.0)
        target[64:, :] = (own_ref[block_at(x, d), :] + extra).astype(jnp.bfloat16)


def unpack_rows_kernel(where_ref, o0, o1, o2, o3, out_ref, dq_ref):
    x = where_ref[1]
    for d, source in enumerate((o0, o1, o2, o3)):
        out_ref[:, head_columns(x, d, WIDE)] = source[:, :WIDE]
        dq_ref[:, head_columns(x, d, WIDE)] = source[:, WIDE:]


def unpack_small_kernel(where_ref, f0, f1, f2, f3, k_ref, v_ref, pk_ref, pv_ref):
    x = where_ref[1]
    for d, source in enumerate((f0, f1, f2, f3)):
        at = head_columns(x, d, 128)
        pk_ref[:, at] = source[:64, :128]
        pv_ref[:, at] = source[:64, 128:]
        k_ref[:, at] = source[64:, :128]
        v_ref[:, at] = source[64:, 128:]


def along_x(value, step):
    return lax.ppermute(value, "seq", [(i, i // 4 * 4 + (i + step) % 4) for i in range(32)])


def along_y(value, step):
    return lax.ppermute(value, "seq", [(i, i // 16 * 16 + (i + 4 * step) % 16) for i in range(32)])


def along_z(value):
    return lax.ppermute(value, "seq", [(i, (i + 16) % 32) for i in range(32)])


def along_rows(value, step):
    return lax.ppermute(value, "seq", [(i, (i + 4 * step) % 32) for i in range(32)])


def local(resp_len, prompt_keys, prompt_values, resp_q, resp_k, resp_v, out_grad):
    me = lax.axis_index("seq").astype(jnp.int32)
    where = jnp.stack([me // 4 * OWN_ROWS, me % 4])
    rows, bf16, f32 = resp_q.shape[0], jnp.bfloat16, jnp.float32

    far_keys, far_values = along_z(prompt_keys), along_z(prompt_values)
    s = call(
        pack_small_kernel, (where,), (prompt_keys, prompt_values, far_keys, far_values, resp_k, resp_v),
        [((256, 256), bf16)] * 4, "pack_small",
    )
    queries = call(
        pack_rows_kernel, (where,), (resp_q, out_grad), [((rows, 2 * WIDE), bf16)] * 4, "pack_rows", after=(s[0],)
    )
    s = [s[0]] + [along_x(s[d], d) for d in (1, 2, 3)]
    queries = [queries[0]] + [along_x(queries[d], d) for d in (1, 2, 3)]
    mine, ahead = call(collect_kernel, (where,), s, [((512, 256), bf16), ((BACK, 256), bf16)], "collect")
    p1, p3 = along_y(mine, 1), along_y(mine, -1)
    before = along_rows(ahead, 1)
    p2a, p2b = along_y(p1[:256], 1), along_y(p3[256:], -1)

    results = attention(resp_len, where, (*queries, *s, before, mine, p1, p2a, p2b, p3))
    o, (stay, minus, plus, minus2, plus2, back_grad, own_grad) = results[:4], results[4:]

    minus, plus = along_y(minus, -1), along_y(plus, 1)
    o = [o[0]] + [along_x(o[d], -d) for d in (1, 2, 3)]
    minus2 = along_y(minus2 + minus[:256], -1)
    plus2 = along_y(plus2 + plus[:256], 1)
    keep, give, back_grad = call(
        prompt_sum_kernel, (), (stay, minus, plus, minus2, plus2, back_grad),
        [((256, 256), f32)] * 2 + [((BACK, 256), f32)], "prompt_sum", after=tuple(o[1:]),
    )
    got = along_z(give)
    back = along_rows(back_grad, -1)
    attn_out, q_grad = call(
        unpack_rows_kernel, (where,), o, [((rows, HEADS * HEAD_DIM), bf16)] * 2, "unpack_rows"
    )

    f = call(final_sum_kernel, (where,), (keep, got, own_grad, back), [((192, 256), bf16)] * 4, "final_sum")
    f = [f[0]] + [along_x(f[d], -d) for d in (1, 2, 3)]
    resp_k_grad, resp_v_grad, prompt_k_grad, prompt_v_grad = call(
        unpack_small_kernel, (where,), f, [((rows, 512), bf16)] * 2 + [((64, 512), bf16)] * 2, "unpack_small"
    )
    return attn_out, q_grad, resp_k_grad, resp_v_grad, prompt_k_grad, prompt_v_grad


def solution(mesh):
    split = P(("grp", "seq"), None)
    return jax.shard_map(
        local,
        mesh=mesh,
        in_specs=(P("grp"),) + (split,) * 6,
        out_specs=(split,) * 6,
        check_vma=False,
    )
```

time: 601 us -> 154 us (0.26)
  the two profiles are of different devices: /device:TPU:192 before, /device:TPU:32 now
where the time goes in v1:
time: 154 us; the launch traced here: 153 us
  waiting for transfers between devices  64.3 us (42%)
  starting transfers between devices  42.4 us (28%)
  Pallas kernels  40.4 us (26%)
  local copies, waits for them, and re-layouts  4.6 us (3%)
    pallas_call x8, Pallas kernels, call(): pl.pallas_call(kernel, in_specs=[smem] * len(scalars) + [vmem] * len(oper...  40.4 us
    ppermute x3, waiting for transfers between devices, along_z(): return lax.ppermute(value, 'seq', [(i, (i + 16) % 32) for i in range(32)])  29.3 us
    ppermute x8, waiting for transfers between devices, along_y(): lax.ppermute(value, 'seq', [(i, i // 16 * 16 + (i + 4 * step) % 16) for i...  19.8 us
    ppermute x12, starting transfers between devices, along_x(): lax.ppermute(value, 'seq', [(i, i // 4 * 4 + (i + step) % 4) for i in ran...  17.7 us
    ppermute x8, starting transfers between devices, along_y(): lax.ppermute(value, 'seq', [(i, i // 16 * 16 + (i + 4 * step) % 16) for i...  12.6 us
    ppermute x3, starting transfers between devices, along_z(): return lax.ppermute(value, 'seq', [(i, (i + 16) % 32) for i in range(32)])  11 us
    ppermute x2, waiting for transfers between devices, along_rows(): lax.ppermute(value, 'seq', [(i, (i + 4 * step) % 32) for i in range(32)])  7.9 us
    ppermute x12, waiting for transfers between devices, along_x(): lax.ppermute(value, 'seq', [(i, i // 4 * 4 + (i + step) % 4) for i in ran...  7.33 us
  transfers between devices with their start and end apart: 25, of which 14 were waited for; matrix products, arithmetic and copies ran while one was open for 0% of the time, Pallas kernels for 2%

profile of v1, /device:TPU:32, one launch (start us, length us, event | category | flops | bytes accessed | tf_op | source)
XLA Modules:
  0.0 152.6 jit_solution(7450194031444717956)
XLA Ops:
  0.6 6.4 %collective-permute-start = (bf16[64,512]{1,0:T(8,128)(2,1)}, bf16[64,512]{1,0:T(8,128)(2,1)S(1)}, u32[]{:S(2)}, u32[]{:S(2)}) collective-permute-start(bf16[64,512]{1,0:T(8,128)(2,1)} %refs_1_.2), channel_id=1, source_target_pairs={{0,16},{1,17},{2,18},{3,19},{4,20},{5,21},{6,22},{7,23},{8,24},{9,... | collective-permute-start | bytes 196616 | tf_op jit(solution)/shard_map/ppermute | solution.py:268
  7.2 5.0 %collective-permute-done.refs_3_ = bf16[64,512]{1,0:T(8,128)(2,1)S(1)} collective-permute-done((bf16[64,512]{1,0:T(8,128)(2,1)}, bf16[64,512]{1,0:T(8,128)(2,1)S(1)}, u32[]{:S(2)}, u32[]{:S(2)}) %collective-permute-start) | collective-permute-done | bytes 65568 | tf_op jit(solution)/shard_map/ppermute | solution.py:268
  12.2 4.3 %collective-permute-done.1.refs_4_ = bf16[64,512]{1,0:T(8,128)(2,1)S(1)} collective-permute-done((bf16[64,512]{1,0:T(8,128)(2,1)}, bf16[64,512]{1,0:T(8,128)(2,1)S(1)}, u32[]{:S(2)}, u32[]{:S(2)}) %collective-permute-start.1) | collective-permute-done | bytes 65568 | tf_op jit(solution)/shard_map/ppermute | solution.py:268
  20.7 1.6 %collective-permute-start.5 = (bf16[256,256]{1,0:T(8,128)(2,1)S(1)}, bf16[256,256]{1,0:T(8,128)(2,1)S(1)}, u32[]{:S(2)}, u32[]{:S(2)}) collective-permute-start(bf16[256,256]{1,0:T(8,128)(2,1)S(1)} %get-tuple-element.45), channel_id=1, source_target_pairs={{0,1},{1,2},{2,3},{3,0},{4,5},{5,6},{6,7},{7,4},{8,9},{9,10},{10,1... | collective-permute-start | bytes 393224 | tf_op jit(solution)/shard_map/ppermute | solution.py:260
  22.2 2.7 %collective-permute-start.6 = (bf16[256,256]{1,0:T(8,128)(2,1)S(1)}, bf16[256,256]{1,0:T(8,128)(2,1)S(1)}, u32[]{:S(2)}, u32[]{:S(2)}) collective-permute-start(bf16[256,256]{1,0:T(8,128)(2,1)S(1)} %get-tuple-element.46), channel_id=1, source_target_pairs={{0,2},{1,3},{2,0},{3,1},{4,6},{5,7},{6,4},{7,5},{8,10},{9,11},{10,... | collective-permute-start | bytes 393224 | tf_op jit(solution)/shard_map/ppermute | solution.py:260
  25.0 1.4 collective-permute-start.7
  27.0 2.3 %collective-permute-done.6.refs_3_.refs_8_ = bf16[256,256]{1,0:T(8,128)(2,1)S(1)} collective-permute-done((bf16[256,256]{1,0:T(8,128)(2,1)S(1)}, bf16[256,256]{1,0:T(8,128)(2,1)S(1)}, u32[]{:S(2)}, u32[]{:S(2)}) %collective-permute-start.6) | collective-permute-done | bytes 131104 | tf_op jit(solution)/shard_map/ppermute | solution.py:260
  30.5 3.1 %collective-permute-start.11 = (bf16[512,256]{1,0:T(8,128)(2,1)S(1)}, bf16[512,256]{1,0:T(8,128)(2,1)S(1)}, u32[]{:S(2)}, u32[]{:S(2)}) collective-permute-start(bf16[512,256]{1,0:T(8,128)(2,1)S(1)} %get-tuple-element.49.refs_11_), channel_id=1, source_target_pairs={{0,12},{1,13},{2,14},{3,15},{4,0},{5,1},{6,2},{7,3},{8,4},{9,5},{1... | collective-permute-start | bytes 786440 | tf_op jit(solution)/shard_map/ppermute | solution.py:264
  35.4 1.4 collective-permute-start.2
  36.7 2.8 %collective-permute-start.3 = (bf16[128,1280]{1,0:T(8,128)(2,1)S(1)}, bf16[128,1280]{1,0:T(8,128)(2,1)S(1)}, u32[]{:S(2)}, u32[]{:S(2)}) collective-permute-start(bf16[128,1280]{1,0:T(8,128)(2,1)S(1)} %get-tuple-element.43), channel_id=1, source_target_pairs={{0,2},{1,3},{2,0},{3,1},{4,6},{5,7},{6,4},{7,5},{8,10},{9,11},{10,... | collective-permute-start | bytes 983048 | tf_op jit(solution)/shard_map/ppermute | solution.py:260
  41.2 5.2 %collective-permute-start.12 = (bf16[256,256]{1,0:T(8,128)(2,1)S(1)}, bf16[256,256]{1,0:T(8,128)(2,1)S(1)}, u32[]{:S(2)}, u32[]{:S(2)}) collective-permute-start(bf16[256,256]{1,0:T(8,128)(2,1)S(1)} %slice.17), channel_id=1, source_target_pairs={{0,12},{1,13},{2,14},{3,15},{4,0},{5,1},{6,2},{7,3},{8,4},{9,5},{1... | collective-permute-start | bytes 393224 | tf_op jit(solution)/shard_map/ppermute | solution.py:264
  46.4 7.9 %collective-permute-done.8.refs_10_ = bf16[384,256]{1,0:T(8,128)(2,1)S(1)} collective-permute-done((bf16[384,256]{1,0:T(8,128)(2,1)S(1)}, bf16[384,256]{1,0:T(8,128)(2,1)S(1)}, u32[]{:S(2)}, u32[]{:S(2)}) %collective-permute-start.8) | collective-permute-done | bytes 196640 | tf_op jit(solution)/shard_map/ppermute | solution.py:272
  54.3 6.1 %collective-permute-done.10.refs_13_ = bf16[256,256]{1,0:T(8,128)(2,1)S(1)} collective-permute-done((bf16[256,256]{1,0:T(8,128)(2,1)S(1)}, bf16[256,256]{1,0:T(8,128)(2,1)S(1)}, u32[]{:S(2)}, u32[]{:S(2)}) %collective-permute-start.10) | collective-permute-done | bytes 131104 | tf_op jit(solution)/shard_map/ppermute | solution.py:264
  60.5 34.6 %attention.1 = (bf16[128,1280]{1,0:T(8,128)(2,1)S(1)}, bf16[128,1280]{1,0:T(8,128)(2,1)S(1)}, bf16[128,1280]{1,0:T(8,128)(2,1)S(1)}, bf16[128,1280]{1,0:T(8,128)...) custom-call(s32[16]{0:T(128)S(1)} %copy-done.6, ...), custom_call_target="tpu_custom_call" | custom-call | flops 10066329600 | bytes 10000000 | tf_op jit(solution)/shard_map/attention/pallas_call | solution.py:150
  95.2 2.0 %collective-permute-start.17 = (f32[512,256]{1,0:T(8,128)S(1)}, f32[512,256]{1,0:T(8,128)S(1)}, u32[]{:S(2)}, u32[]{:S(2)}) collective-permute-start(f32[512,256]{1,0:T(8,128)S(1)} %get-tuple-element.58), channel_id=1, source_target_pairs={{0,4},{1,5},{2,6},{3,7},{4,8},{5,9},{6,10},{7,11},{8,12},{9,13},{1... | collective-permute-start | bytes 1572872 | tf_op jit(solution)/shard_map/ppermute | solution.py:264
  97.6 2.8 %collective-permute-start.14 = (bf16[128,1280]{1,0:T(8,128)(2,1)S(1)}, bf16[128,1280]{1,0:T(8,128)(2,1)S(1)}, u32[]{:S(2)}, u32[]{:S(2)}) collective-permute-start(bf16[128,1280]{1,0:T(8,128)(2,1)S(1)} %get-tuple-element.52), channel_id=1, source_target_pairs={{0,2},{1,3},{2,0},{3,1},{4,6},{5,7},{6,4},{7,5},{8,10},{9,11},{10,... | collective-permute-start | bytes 983048 | tf_op jit(solution)/shard_map/ppermute | solution.py:260
  100.5 6.7 %collective-permute-done.16.refs_1_ = f32[512,256]{1,0:T(8,128)S(1)} collective-permute-done((f32[512,256]{1,0:T(8,128)S(1)}, f32[512,256]{1,0:T(8,128)S(1)}, u32[]{:S(2)}, u32[]{:S(2)}) %collective-permute-start.16) | collective-permute-done | bytes 524320 | tf_op jit(solution)/shard_map/ppermute | solution.py:264
  109.7 6.7 %collective-permute-done.18.refs_3_ = f32[256,256]{1,0:T(8,128)S(1)} collective-permute-done((f32[256,256]{1,0:T(8,128)S(1)}, f32[256,256]{1,0:T(8,128)S(1)}, u32[]{:S(2)}, u32[]{:S(2)}) %collective-permute-start.18) | collective-permute-done | bytes 262176 | tf_op jit(solution)/shard_map/ppermute | solution.py:264
  117.2 4.5 %collective-permute-start.20 = (f32[256,256]{1,0:T(8,128)S(1)}, f32[256,256]{1,0:T(8,128)S(1)}, u32[]{:S(2)}, u32[]{:S(2)}) collective-permute-start(f32[256,256]{1,0:T(8,128)S(1)} %get-tuple-element.63), channel_id=1, source_target_pairs={{0,16},{1,17},{2,18},{3,19},{4,20},{5,21},{6,22},{7,23},{8,24},{9,... | collective-permute-start | bytes 786440 | tf_op jit(solution)/shard_map/ppermute | solution.py:268
  121.7 20.0 %collective-permute-done.20.refs_2_ = f32[256,256]{1,0:T(8,128)S(1)} collective-permute-done((f32[256,256]{1,0:T(8,128)S(1)}, f32[256,256]{1,0:T(8,128)S(1)}, u32[]{:S(2)}, u32[]{:S(2)}) %collective-permute-start.20) | collective-permute-done | bytes 262176 | tf_op jit(solution)/shard_map/ppermute | solution.py:268
  143.2 2.0 %collective-permute-start.23 = (bf16[192,256]{1,0:T(8,128)(2,1)S(1)}, bf16[192,256]{1,0:T(8,128)(2,1)S(1)}, u32[]{:S(2)}, u32[]{:S(2)}) collective-permute-start(bf16[192,256]{1,0:T(8,128)(2,1)S(1)} %get-tuple-element.68), channel_id=1, source_target_pairs={{0,2},{1,3},{2,0},{3,1},{4,6},{5,7},{6,4},{7,5},{8,10},{9,11},{10,... | collective-permute-start | bytes 294920 | tf_op jit(solution)/shard_map/ppermute | solution.py:260
  146.0 1.7 %unpack_rows.1 = (bf16[128,2560]{1,0:T(8,128)(2,1)}, bf16[128,2560]{1,0:T(8,128)(2,1)}) custom-call(s32[2]{0:T(128)S(1)} %pad_add_fusion.refs_0_.refs_1_, bf16[128,1280]{1,0:T(8,128)(2,1)S(1)} %get-tuple-element.50.refs_1_, bf16[128,1280]{1,0:T(8,128)(2,1)S(1)} %collective-permute-done.13.refs_2_.refs_6_, ...), custom_call_target="tpu_custom_call" | custom-call | tf_op jit(solution)/shard_map/unpack_rows/pallas_call | solution.py:150
  147.8 2.5 %collective-permute-done.23.refs_3_ = bf16[192,256]{1,0:T(8,128)(2,1)S(1)} collective-permute-done((bf16[192,256]{1,0:T(8,128)(2,1)S(1)}, bf16[192,256]{1,0:T(8,128)(2,1)S(1)}, u32[]{:S(2)}, u32[]{:S(2)}) %collective-permute-start.23) | collective-permute-done | bytes 98336 | tf_op jit(solution)/shard_map/ppermute | solution.py:260
  151.3 1.3 unpack_small.1
  (53 shorter events, 16.7 us)
Async XLA Ops:
  0.6 11.6 %collective-permute-start = (bf16[64,512]{1,0:T(8,128)(2,1)}, bf16[64,512]{1,0:T(8,128)(2,1)S(1)}, u32[]{:S(2)}, u32[]{:S(2)}) collective-permute-start(bf16[64,512]{1,0:T(8,128)(2,1)} %refs_1_.2), channel_id=1, source_target_pairs={{0,16},{1,17},{2,18},{3,19},{4,20},{5,21},{6,22},{7,23},{8,24},{9,... | collective-permute-start | bytes 196616 | tf_op jit(solution)/shard_map/ppermute | solution.py:268
  7.0 9.5 %collective-permute-start.1 = (bf16[64,512]{1,0:T(8,128)(2,1)}, bf16[64,512]{1,0:T(8,128)(2,1)S(1)}, u32[]{:S(2)}, u32[]{:S(2)}) collective-permute-start(bf16[64,512]{1,0:T(8,128)(2,1)} %refs_2_.2), channel_id=1, source_target_pairs={{0,16},{1,17},{2,18},{3,19},{4,20},{5,21},{6,22},{7,23},{8,24},{9,... | collective-permute-start | bytes 196616 | tf_op jit(solution)/shard_map/ppermute | solution.py:268
  20.7 6.4 %collective-permute-start.5 = (bf16[256,256]{1,0:T(8,128)(2,1)S(1)}, bf16[256,256]{1,0:T(8,128)(2,1)S(1)}, u32[]{:S(2)}, u32[]{:S(2)}) collective-permute-start(bf16[256,256]{1,0:T(8,128)(2,1)S(1)} %get-tuple-element.45), channel_id=1, source_target_pairs={{0,1},{1,2},{2,3},{3,0},{4,5},{5,6},{6,7},{7,4},{8,9},{9,10},{10,1... | collective-permute-start | bytes 393224 | tf_op jit(solution)/shard_map/ppermute | solution.py:260
  22.2 7.1 %collective-permute-start.6 = (bf16[256,256]{1,0:T(8,128)(2,1)S(1)}, bf16[256,256]{1,0:T(8,128)(2,1)S(1)}, u32[]{:S(2)}, u32[]{:S(2)}) collective-permute-start(bf16[256,256]{1,0:T(8,128)(2,1)S(1)} %get-tuple-element.46), channel_id=1, source_target_pairs={{0,2},{1,3},{2,0},{3,1},{4,6},{5,7},{6,4},{7,5},{8,10},{9,11},{10,... | collective-permute-start | bytes 393224 | tf_op jit(solution)/shard_map/ppermute | solution.py:260
  30.5 9.9 %collective-permute-start.11 = (bf16[512,256]{1,0:T(8,128)(2,1)S(1)}, bf16[512,256]{1,0:T(8,128)(2,1)S(1)}, u32[]{:S(2)}, u32[]{:S(2)}) collective-permute-start(bf16[512,256]{1,0:T(8,128)(2,1)S(1)} %get-tuple-element.49.refs_11_), channel_id=1, source_target_pairs={{0,12},{1,13},{2,14},{3,15},{4,0},{5,1},{6,2},{7,3},{8,4},{9,5},{1... | collective-permute-start | bytes 786440 | tf_op jit(solution)/shard_map/ppermute | solution.py:264
  33.6 7.6 %collective-permute-start.9 = (bf16[512,256]{1,0:T(8,128)(2,1)S(1)}, bf16[512,256]{1,0:T(8,128)(2,1)S(1)}, u32[]{:S(2)}, u32[]{:S(2)}) collective-permute-start(bf16[512,256]{1,0:T(8,128)(2,1)S(1)} %get-tuple-element.49.refs_11_), channel_id=1, source_target_pairs={{0,4},{1,5},{2,6},{3,7},{4,8},{5,9},{6,10},{7,11},{8,12},{9,13},{1... | collective-permute-start | bytes 786440 | tf_op jit(solution)/shard_map/ppermute | solution.py:264
  35.4 18.9 %collective-permute-start.2 = (bf16[128,1280]{1,0:T(8,128)(2,1)S(1)}, bf16[128,1280]{1,0:T(8,128)(2,1)S(1)}, u32[]{:S(2)}, u32[]{:S(2)}) collective-permute-start(bf16[128,1280]{1,0:T(8,128)(2,1)S(1)} %get-tuple-element.42), channel_id=1, source_target_pairs={{0,1},{1,2},{2,3},{3,0},{4,5},{5,6},{6,7},{7,4},{8,9},{9,10},{10,1... | collective-permute-start | bytes 983048 | tf_op jit(solution)/shard_map/ppermute | solution.py:260
  36.7 17.6 %collective-permute-start.3 = (bf16[128,1280]{1,0:T(8,128)(2,1)S(1)}, bf16[128,1280]{1,0:T(8,128)(2,1)S(1)}, u32[]{:S(2)}, u32[]{:S(2)}) collective-permute-start(bf16[128,1280]{1,0:T(8,128)(2,1)S(1)} %get-tuple-element.43), channel_id=1, source_target_pairs={{0,2},{1,3},{2,0},{3,1},{4,6},{5,7},{6,4},{7,5},{8,10},{9,11},{10,... | collective-permute-start | bytes 983048 | tf_op jit(solution)/shard_map/ppermute | solution.py:260
  39.5 14.8 %collective-permute-start.4 = (bf16[128,1280]{1,0:T(8,128)(2,1)S(1)}, bf16[128,1280]{1,0:T(8,128)(2,1)S(1)}, u32[]{:S(2)}, u32[]{:S(2)}) collective-permute-start(bf16[128,1280]{1,0:T(8,128)(2,1)S(1)} %get-tuple-element.44), channel_id=1, source_target_pairs={{0,3},{1,0},{2,1},{3,2},{4,7},{5,4},{6,5},{7,6},{8,11},{9,8},{10,9... | collective-permute-start | bytes 983048 | tf_op jit(solution)/shard_map/ppermute | solution.py:260
  40.4 13.9 %collective-permute-start.8 = (bf16[384,256]{1,0:T(8,128)(2,1)S(1)}, bf16[384,256]{1,0:T(8,128)(2,1)S(1)}, u32[]{:S(2)}, u32[]{:S(2)}) collective-permute-start(bf16[384,256]{1,0:T(8,128)(2,1)S(1)} %get-tuple-element.48), channel_id=1, source_target_pairs={{0,4},{1,5},{2,6},{3,7},{4,8},{5,9},{6,10},{7,11},{8,12},{9,13},{1... | collective-permute-start | bytes 589832 | tf_op jit(solution)/shard_map/ppermute | solution.py:272
  41.2 13.1 %collective-permute-start.12 = (bf16[256,256]{1,0:T(8,128)(2,1)S(1)}, bf16[256,256]{1,0:T(8,128)(2,1)S(1)}, u32[]{:S(2)}, u32[]{:S(2)}) collective-permute-start(bf16[256,256]{1,0:T(8,128)(2,1)S(1)} %slice.17), channel_id=1, source_target_pairs={{0,12},{1,13},{2,14},{3,15},{4,0},{5,1},{6,2},{7,3},{8,4},{9,5},{1... | collective-permute-start | bytes 393224 | tf_op jit(solution)/shard_map/ppermute | solution.py:264
  54.3 6.2 %collective-permute-start.10 = (bf16[256,256]{1,0:T(8,128)(2,1)S(1)}, bf16[256,256]{1,0:T(8,128)(2,1)S(1)}, u32[]{:S(2)}, u32[]{:S(2)}) collective-permute-start(bf16[256,256]{1,0:T(8,128)(2,1)S(1)} %slice.16), channel_id=1, source_target_pairs={{0,4},{1,5},{2,6},{3,7},{4,8},{5,9},{6,10},{7,11},{8,12},{9,13},{1... | collective-permute-start | bytes 393224 | tf_op jit(solution)/shard_map/ppermute | solution.py:264
  95.1 12.1 %collective-permute-start.16 = (f32[512,256]{1,0:T(8,128)S(1)}, f32[512,256]{1,0:T(8,128)S(1)}, u32[]{:S(2)}, u32[]{:S(2)}) collective-permute-start(f32[512,256]{1,0:T(8,128)S(1)} %get-tuple-element.57), channel_id=1, source_target_pairs={{0,12},{1,13},{2,14},{3,15},{4,0},{5,1},{6,2},{7,3},{8,4},{9,5},{1... | collective-permute-start | bytes 1572872 | tf_op jit(solution)/shard_map/ppermute | solution.py:264
  95.2 13.3 %collective-permute-start.17 = (f32[512,256]{1,0:T(8,128)S(1)}, f32[512,256]{1,0:T(8,128)S(1)}, u32[]{:S(2)}, u32[]{:S(2)}) collective-permute-start(f32[512,256]{1,0:T(8,128)S(1)} %get-tuple-element.58), channel_id=1, source_target_pairs={{0,4},{1,5},{2,6},{3,7},{4,8},{5,9},{6,10},{7,11},{8,12},{9,13},{1... | collective-permute-start | bytes 1572872 | tf_op jit(solution)/shard_map/ppermute | solution.py:264
  97.2 12.2 %collective-permute-start.13 = (bf16[128,1280]{1,0:T(8,128)(2,1)S(1)}, bf16[128,1280]{1,0:T(8,128)(2,1)S(1)}, u32[]{:S(2)}, u32[]{:S(2)}) collective-permute-start(bf16[128,1280]{1,0:T(8,128)(2,1)S(1)} %get-tuple-element.51), channel_id=1, source_target_pairs={{0,3},{1,0},{2,1},{3,2},{4,7},{5,4},{6,5},{7,6},{8,11},{9,8},{10,9... | collective-permute-start | bytes 983048 | tf_op jit(solution)/shard_map/ppermute | solution.py:260
  97.6 11.8 %collective-permute-start.14 = (bf16[128,1280]{1,0:T(8,128)(2,1)S(1)}, bf16[128,1280]{1,0:T(8,128)(2,1)S(1)}, u32[]{:S(2)}, u32[]{:S(2)}) collective-permute-start(bf16[128,1280]{1,0:T(8,128)(2,1)S(1)} %get-tuple-element.52), channel_id=1, source_target_pairs={{0,2},{1,3},{2,0},{3,1},{4,6},{5,7},{6,4},{7,5},{8,10},{9,11},{10,... | collective-permute-start | bytes 983048 | tf_op jit(solution)/shard_map/ppermute | solution.py:260
  100.5 9.3 %collective-permute-start.15 = (bf16[128,1280]{1,0:T(8,128)(2,1)S(1)}, bf16[128,1280]{1,0:T(8,128)(2,1)S(1)}, u32[]{:S(2)}, u32[]{:S(2)}) collective-permute-start(bf16[128,1280]{1,0:T(8,128)(2,1)S(1)} %get-tuple-element.53), channel_id=1, source_target_pairs={{0,1},{1,2},{2,3},{3,0},{4,5},{5,6},{6,7},{7,4},{8,9},{9,10},{10,1... | collective-permute-start | bytes 983048 | tf_op jit(solution)/shard_map/ppermute | solution.py:260
  107.2 9.2 %collective-permute-start.18 = (f32[256,256]{1,0:T(8,128)S(1)}, f32[256,256]{1,0:T(8,128)S(1)}, u32[]{:S(2)}, u32[]{:S(2)}) collective-permute-start(f32[256,256]{1,0:T(8,128)S(1)} %slice_add_fusion.1), channel_id=1, source_target_pairs={{0,12},{1,13},{2,14},{3,15},{4,0},{5,1},{6,2},{7,3},{8,4},{9,5},{1... | collective-permute-start | bytes 786440 | tf_op jit(solution)/shard_map/ppermute | solution.py:264
  108.6 7.9 %collective-permute-start.19 = (f32[256,256]{1,0:T(8,128)S(1)}, f32[256,256]{1,0:T(8,128)S(1)}, u32[]{:S(2)}, u32[]{:S(2)}) collective-permute-start(f32[256,256]{1,0:T(8,128)S(1)} %slice_add_fusion), channel_id=1, source_target_pairs={{0,4},{1,5},{2,6},{3,7},{4,8},{5,9},{6,10},{7,11},{8,12},{9,13},{1... | collective-permute-start | bytes 786440 | tf_op jit(solution)/shard_map/ppermute | solution.py:264
  116.6 25.1 %collective-permute-start.21 = (f32[384,256]{1,0:T(8,128)S(1)}, f32[384,256]{1,0:T(8,128)S(1)}, u32[]{:S(2)}, u32[]{:S(2)}) collective-permute-start(f32[384,256]{1,0:T(8,128)S(1)} %get-tuple-element.65), channel_id=1, source_target_pairs={{0,28},{1,29},{2,30},{3,31},{4,0},{5,1},{6,2},{7,3},{8,4},{9,5},{1... | collective-permute-start | bytes 1179656 | tf_op jit(solution)/shard_map/ppermute | solution.py:272
  117.2 24.5 %collective-permute-start.20 = (f32[256,256]{1,0:T(8,128)S(1)}, f32[256,256]{1,0:T(8,128)S(1)}, u32[]{:S(2)}, u32[]{:S(2)}) collective-permute-start(f32[256,256]{1,0:T(8,128)S(1)} %get-tuple-element.63), channel_id=1, source_target_pairs={{0,16},{1,17},{2,18},{3,19},{4,20},{5,21},{6,22},{7,23},{8,24},{9,... | collective-permute-start | bytes 786440 | tf_op jit(solution)/shard_map/ppermute | solution.py:268
  142.3 5.4 %collective-permute-start.22 = (bf16[192,256]{1,0:T(8,128)(2,1)S(1)}, bf16[192,256]{1,0:T(8,128)(2,1)S(1)}, u32[]{:S(2)}, u32[]{:S(2)}) collective-permute-start(bf16[192,256]{1,0:T(8,128)(2,1)S(1)} %get-tuple-element.67), channel_id=1, source_target_pairs={{0,3},{1,0},{2,1},{3,2},{4,7},{5,4},{6,5},{7,6},{8,11},{9,8},{10,9... | collective-permute-start | bytes 294920 | tf_op jit(solution)/shard_map/ppermute | solution.py:260
  143.2 7.0 %collective-permute-start.23 = (bf16[192,256]{1,0:T(8,128)(2,1)S(1)}, bf16[192,256]{1,0:T(8,128)(2,1)S(1)}, u32[]{:S(2)}, u32[]{:S(2)}) collective-permute-start(bf16[192,256]{1,0:T(8,128)(2,1)S(1)} %get-tuple-element.68), channel_id=1, source_target_pairs={{0,2},{1,3},{2,0},{3,1},{4,6},{5,7},{6,4},{7,5},{8,10},{9,11},{10,... | collective-permute-start | bytes 294920 | tf_op jit(solution)/shard_map/ppermute | solution.py:260
  145.2 6.0 %collective-permute-start.24 = (bf16[192,256]{1,0:T(8,128)(2,1)S(1)}, bf16[192,256]{1,0:T(8,128)(2,1)S(1)}, u32[]{:S(2)}, u32[]{:S(2)}) collective-permute-start(bf16[192,256]{1,0:T(8,128)(2,1)S(1)} %get-tuple-element.69), channel_id=1, source_target_pairs={{0,1},{1,2},{2,3},{3,0},{4,5},{5,6},{6,7},{7,4},{8,9},{9,10},{10,1... | collective-permute-start | bytes 294920 | tf_op jit(solution)/shard_map/ppermute | solution.py:260
  (8 other events, 56.6 us)

commit v2 on v1

v2 whole, which is shorter than its diff:
```python
import jax
import jax.numpy as jnp
from jax import lax
from jax.experimental import pallas as pl
from jax.experimental.pallas import tpu as pltpu
from jax.sharding import PartitionSpec as P

HEADS = 20
KV_HEADS = 4
HEAD_DIM = 128
PER_GROUP = HEADS // KV_HEADS
BACK = 384
NEGATIVE = -1e30
LOG2E = 1.4426950408889634
FACTOR = HEAD_DIM ** (-0.5)

ROWS = 256
KEYS = 512
SPAN = 640
PROMPT_ROWS = 2048
OWN_ROWS = 512
WIDE = PER_GROUP * HEAD_DIM
LIMIT = 16


def nt(a, b):
    return lax.dot_general(a, b, (((1,), (1,)), ((), ())), preferred_element_type=jnp.float32)


def nn(a, b):
    return lax.dot_general(a, b, (((1,), (0,)), ((), ())), preferred_element_type=jnp.float32)


def block_at(x, distance):
    return pl.ds(pl.multiple_of(lax.rem(x + 4 - distance, 4) * 128, 128), 128)


def forward_kernel(
    len_ref, where_ref, q0, q1, q2, q3, s0, s1, s2, s3, before_ref, h0, h1, h2, h3, l0, l1, l2, l3,
    out_all, q_all, p_all, grad2_all, dq_all, key_t, value1, back_grad_ref, own_grad_ref,
    key2, value_t, wkey2, wvalue1, wkey_t, wvalue_t, s_first, s_second, key_sum, value_sum,
):
    base, x = where_ref[0], where_ref[1]
    window_rows = BACK + OWN_ROWS

    def place(keys, values, at, source):
        keys[at, :128] = source[:, :128]
        keys[at, 128:] = source[:, :128]
        values[at, :128] = source[:, 128:]

    for i, source in enumerate((h0, h1, h2, h3, l0, l1, l2, l3)):
        place(key2, value1, slice(i * 256, i * 256 + 256), source)
    place(wkey2, wvalue1, slice(0, BACK), before_ref)
    for d, source in enumerate((s0, s1, s2, s3)):
        first = BACK + lax.rem(x + 4 - d, 4) * 128
        place(wkey2, wvalue1, pl.ds(pl.multiple_of(first, 128), 128), source.at[64:192, :])
    for rows, keys, values, keys_t, values_t in (
        (PROMPT_ROWS, key2, value1, key_t, value_t), (window_rows, wkey2, wvalue1, wkey_t, wvalue_t),
    ):
        values[:, 128:] = jnp.ones((rows, 128), jnp.bfloat16)
        values_t[128:, :] = jnp.ones((16, rows), jnp.bfloat16)
        for c in range(0, rows, 128):
            at = slice(c, c + 128)
            keys_t[:, at] = keys[at, :128].astype(jnp.float32).T.astype(jnp.bfloat16)
            values_t[:128, at] = values[at, :128].astype(jnp.float32).T.astype(jnp.bfloat16)
    for d, source in enumerate((q0, q1, q2, q3)):
        q_all[block_at(x, d), :] = source[...]
    key_sum[...] = jnp.zeros_like(key_sum)
    value_sum[...] = jnp.zeros_like(value_sum)

    def one_head(head, carry):
        q_cols = pl.ds(pl.multiple_of(head * 128, 128), 128)
        g_cols = pl.ds(pl.multiple_of(WIDE + head * 128, 128), 128)
        state = []
        for block, s_ref in enumerate((s_first, s_second)):
            mine = slice(block * ROWS, block * ROWS + ROWS)
            q = q_all[mine, q_cols]
            scaled = q.astype(jnp.float32).T * (FACTOR * LOG2E)
            high = scaled.astype(jnp.bfloat16)
            low = (scaled - high.astype(jnp.float32)).astype(jnp.bfloat16)
            q2t = jnp.concatenate([high, low], 0)
            top = None
            for c in range(0, PROMPT_ROWS, KEYS):
                s = nn(key2[c : c + KEYS, :], q2t)
                s_ref[c : c + KEYS, :] = s
                tile_top = jnp.max(s, axis=0, keepdims=True)
                top = tile_top if top is None else jnp.maximum(top, tile_top)

            own = base + block * ROWS
            row_pos = own + lax.broadcasted_iota(jnp.int32, (1, ROWS), 1)
            seg_start = jnp.zeros((1, ROWS), jnp.int32)
            end = jnp.int32(0)
            for j in range(16):
                end = end + len_ref[j]
                seg_start = jnp.maximum(seg_start, jnp.where(row_pos >= end, end, 0))
            key_pos = own - BACK + lax.broadcasted_iota(jnp.int32, (SPAN, ROWS), 0)
            seen = (key_pos <= row_pos) & (key_pos >= seg_start)
            span = slice(block * ROWS, block * ROWS + SPAN)
            s = jnp.where(seen, nn(wkey2[span, :], q2t), NEGATIVE)
            s_ref[PROMPT_ROWS:, :] = s
            top = jnp.maximum(top, jnp.max(s, axis=0, keepdims=True))
            state.append((block, s_ref, mine, span, q, top))

        for block, s_ref, mine, span, q, top in state:
            item = block * PER_GROUP + head
            total = jnp.zeros((144, ROWS), jnp.float32)
            for c in range(0, PROMPT_ROWS, KEYS):
                p = jnp.exp2(s_ref[c : c + KEYS, :] - top).astype(jnp.bfloat16)
                p_all[item, c : c + KEYS, :] = p
                total = total + nn(value_t[:, c : c + KEYS], p)
            p = jnp.exp2(s_ref[PROMPT_ROWS:, :] - top).astype(jnp.bfloat16)
            total = total + nn(wvalue_t[:, span], p)

            inverse = 1.0 / total[128:129, :]
            out = (total[:128, :] * inverse).astype(jnp.bfloat16).astype(jnp.float32)
            out_all[mine, q_cols] = out.T.astype(jnp.bfloat16)
            grad_n = (q_all[mine, g_cols].astype(jnp.float32).T * inverse).astype(jnp.bfloat16)
            row_dot = -jnp.sum(grad_n.astype(jnp.float32) * out, axis=0, keepdims=True)
            dot_high = row_dot.astype(jnp.bfloat16).astype(jnp.float32)
            line = lax.broadcasted_iota(jnp.int32, (128, ROWS), 0)
            extra = jnp.where(line == 0, dot_high, jnp.where(line == 1, row_dot - dot_high, 0.0))
            grad2 = jnp.concatenate([grad_n, extra.astype(jnp.bfloat16)], 0)
            grad2_all[item] = grad2

            ds = (p.astype(jnp.float32) * nn(wvalue1[span, :], grad2)).astype(jnp.bfloat16)
            dq_all[item] = nn(wkey_t[:, span], ds)
            key_sum[span, :] += nn(ds, q)
            value_sum[span, :] += nt(p, grad_n)
        return carry

    lax.fori_loop(0, PER_GROUP, one_head, 0)

    for target, at in ((back_grad_ref, slice(0, BACK)), (own_grad_ref, slice(BACK, window_rows))):
        target[:, :128] = key_sum[at, :] * FACTOR
        target[:, 128:] = value_sum[at, :]


def backward(first, q_all, p_all, grad2_all, dq_all, key_t, value1, key_sum, value_sum, finish):
    key_sum[...] = jnp.zeros_like(key_sum)
    value_sum[...] = jnp.zeros_like(value_sum)

    def one_head(head, carry):
        q_cols = pl.ds(pl.multiple_of(head * 128, 128), 128)
        dq = [dq_all[block * PER_GROUP + head] for block in range(2)]
        for c in range(0, PROMPT_ROWS // 2, KEYS):
            at, keys = slice(c, c + KEYS), slice(first + c, first + c + KEYS)
            key_term, value_term = None, None
            for block in range(2):
                item = block * PER_GROUP + head
                grad2 = grad2_all[item]
                p = p_all[item, keys, :]
                ds = (p.astype(jnp.float32) * nn(value1[keys, :], grad2)).astype(jnp.bfloat16)
                dq[block] = dq[block] + nn(key_t[:, keys], ds)
                k = nn(ds, q_all[block * ROWS : block * ROWS + ROWS, q_cols])
                v = nt(p, grad2[:128, :])
                key_term = k if key_term is None else key_term + k
                value_term = v if value_term is None else value_term + v
            key_sum[at, :] += key_term
            value_sum[at, :] += value_term
        for block in range(2):
            finish(head, block, dq[block])
        return carry

    lax.fori_loop(0, PER_GROUP, one_head, 0)


def write_sums(key_sum, value_sum, targets):
    for i, target in enumerate(targets):
        at = slice(i * 256, i * 256 + 256)
        target[:, :128] = key_sum[at, :] * FACTOR
        target[:, 128:] = value_sum[at, :]


def far_backward_kernel(
    q_all, p_all, grad2_all, dq_in, key_t, value1, dq_out, g0, g1, g2, g3, key_sum, value_sum
):
    def finish(head, block, dq):
        dq_out[block * PER_GROUP + head] = dq

    backward(0, q_all, p_all, grad2_all, dq_in, key_t, value1, key_sum, value_sum, finish)
    write_sums(key_sum, value_sum, (g0, g1, g2, g3))


def near_backward_kernel(
    where_ref, q_all, p_all, grad2_all, dq_in, key_t, value1, out_all,
    g0, g1, g2, g3, o0, o1, o2, o3, dq_rows, key_sum, value_sum,
):
    def finish(head, block, dq):
        cols = pl.ds(pl.multiple_of(head * 128, 128), 128)
        dq_rows[block * ROWS : block * ROWS + ROWS, cols] = (dq * FACTOR).T.astype(jnp.bfloat16)

    backward(PROMPT_ROWS // 2, q_all, p_all, grad2_all, dq_in, key_t, value1, key_sum, value_sum, finish)
    write_sums(key_sum, value_sum, (g0, g1, g2, g3))
    for d, target in enumerate((o0, o1, o2, o3)):
        at = block_at(where_ref[1], d)
        target[:, :WIDE] = out_all[at, :]
        target[:, WIDE:] = dq_rows[at, :]


def call(body, scalars, operands, outs, name, scratch=(), limit=24, cost=None, space=pltpu.VMEM):
    vmem, smem = pl.BlockSpec(memory_space=pltpu.VMEM), pl.BlockSpec(memory_space=pltpu.SMEM)
    return pl.pallas_call(
        body,
        in_specs=[smem] * len(scalars) + [pl.BlockSpec(memory_space=space)] * len(operands),
        out_specs=[vmem] * len(outs),
        out_shape=[jax.ShapeDtypeStruct(shape, dtype) for shape, dtype in outs],
        scratch_shapes=list(scratch),
        compiler_params=pltpu.CompilerParams(vmem_limit_bytes=limit * 1024 * 1024),
        cost_estimate=cost,
        name=name,
    )(*scalars, *operands)


def work(share):
    total = int(share * 12 * 2560 * 2560 * 128)
    return pl.CostEstimate(flops=total, bytes_accessed=8_000_000, transcendentals=total // 1536)


def forward(resp_len, where, operands):
    bf16, f32 = jnp.bfloat16, jnp.float32
    window_rows, items = BACK + OWN_ROWS, OWN_ROWS // ROWS * PER_GROUP
    return call(
        forward_kernel, (resp_len, where), operands,
        [
            ((OWN_ROWS, WIDE), bf16), ((OWN_ROWS, 2 * WIDE), bf16), ((items, PROMPT_ROWS, ROWS), bf16),
            ((items, 256, ROWS), bf16), ((items, 128, ROWS), f32), ((128, PROMPT_ROWS), bf16),
            ((PROMPT_ROWS, 256), bf16), ((BACK, 256), f32), ((OWN_ROWS, 256), f32),
        ],
        "forward",
        scratch=[
            pltpu.VMEM((PROMPT_ROWS, 256), bf16),
            pltpu.VMEM((144, PROMPT_ROWS), bf16),
            pltpu.VMEM((window_rows, 256), bf16),
            pltpu.VMEM((window_rows, 256), bf16),
            pltpu.VMEM((128, window_rows), bf16),
            pltpu.VMEM((144, window_rows), bf16),
            pltpu.VMEM((PROMPT_ROWS + SPAN, ROWS), f32),
            pltpu.VMEM((PROMPT_ROWS + SPAN, ROWS), f32),
            pltpu.VMEM((window_rows, 128), f32),
            pltpu.VMEM((window_rows, 128), f32),
        ],
        limit=LIMIT, cost=work(0.5),
    )


SUMS = [pltpu.VMEM((PROMPT_ROWS // 2, 128), jnp.float32)] * 2


def head_columns(x, distance, width):
    return pl.ds(pl.multiple_of(lax.rem(x + distance, 4) * width, 128), width)


def pack_kernel(where_ref, pk, pv, k, v, q, g, s0, s1, s2, s3, q0, q1, q2, q3, sems):
    x = where_ref[1]
    copies = []
    for d, small, rows in ((0, s0, q0), (1, s1, q1), (2, s2, q2), (3, s3, q3)):
        narrow, wide = head_columns(x, d, 128), head_columns(x, d, WIDE)
        for source, target in (
            (pk.at[:, narrow], small.at[0:64, 0:128]),
            (pv.at[:, narrow], small.at[0:64, 128:256]),
            (k.at[:, narrow], small.at[64:192, 0:128]),
            (v.at[:, narrow], small.at[64:192, 128:256]),
            (q.at[:, wide], rows.at[:, 0:WIDE]),
            (g.at[:, wide], rows.at[:, WIDE : 2 * WIDE]),
        ):
            copies.append(pltpu.make_async_copy(source, target, sems.at[len(copies)]))
    for copy in copies:
        copy.start()
    for copy in copies:
        copy.wait()


def collect_kernel(where_ref, s0, s1, s2, s3, mine_ref, ahead_ref):
    x = where_ref[1]
    for d, source in enumerate((s0, s1, s2, s3)):
        mine_ref[d * 64 : d * 64 + 64, :] = source[:64, :]
        block = lax.rem(x + 4 - d, 4)

        @pl.when(block > 0)
        def _():
            ahead_ref[pl.ds(pl.multiple_of((block - 1) * 128, 128), 128), :] = source[64:, :]


def final_sum_kernel(where_ref, n0, n1, n2, got_ref, own_ref, back_ref, f0, f1, f2, f3):
    x = where_ref[1]
    for d, target in enumerate((f0, f1, f2, f3)):
        at = slice(d * 64, d * 64 + 64)
        total = (n0[at, :] + n1[at, :]) + (n2[at, :] + got_ref[at, :])
        target[:64, :] = total.astype(jnp.bfloat16)
        block = lax.rem(x + 4 - d, 4)
        behind = pl.ds(pl.multiple_of(jnp.maximum(block - 1, 0) * 128, 128), 128)
        extra = jnp.where(block > 0, back_ref[behind, :], 0.0)
        target[64:, :] = (own_ref[block_at(x, d), :] + extra).astype(jnp.bfloat16)


def unpack_rows_kernel(where_ref, o0, o1, o2, o3, out_ref, dq_ref):
    x = where_ref[1]
    for d, source in enumerate((o0, o1, o2, o3)):
        out_ref[:, head_columns(x, d, WIDE)] = source[:, :WIDE]
        dq_ref[:, head_columns(x, d, WIDE)] = source[:, WIDE:]


def unpack_small_kernel(where_ref, f0, f1, f2, f3, k_ref, v_ref, pk_ref, pv_ref):
    x = where_ref[1]
    for d, source in enumerate((f0, f1, f2, f3)):
        at = head_columns(x, d, 128)
        pk_ref[:, at] = source[:64, :128]
        pv_ref[:, at] = source[:64, 128:]
        k_ref[:, at] = source[64:, :128]
        v_ref[:, at] = source[64:, 128:]


def along_x(value, step):
    return lax.ppermute(value, "seq", [(i, i // 4 * 4 + (i + step) % 4) for i in range(32)])


def along_y(value, step):
    return lax.ppermute(value, "seq", [(i, i // 16 * 16 + (i + 4 * step) % 16) for i in range(32)])


def along_z(value):
    return lax.ppermute(value, "seq", [(i, (i + 16) % 32) for i in range(32)])


def along_rows(value, step):
    pairs = [(i, i + 4 * step) for i in range(32)]
    return lax.ppermute(value, "seq", [(i, j) for i, j in pairs if 0 <= j < 32])


def local(resp_len, prompt_keys, prompt_values, resp_q, resp_k, resp_v, out_grad):
    me = lax.axis_index("seq").astype(jnp.int32)
    where = jnp.stack([me // 4 * OWN_ROWS, me % 4])
    rows, bf16, f32 = resp_q.shape[0], jnp.bfloat16, jnp.float32

    packed = call(
        pack_kernel, (where,), (prompt_keys, prompt_values, resp_k, resp_v, resp_q, out_grad),
        [((192, 256), bf16)] * 4 + [((rows, 2 * WIDE), bf16)] * 4, "pack",
        scratch=[pltpu.SemaphoreType.DMA((24,))], space=pl.ANY, limit=60,
    )
    s = [packed[0]] + [along_x(packed[d], d) for d in (1, 2, 3)]
    queries = [packed[4]] + [along_x(packed[4 + d], d) for d in (1, 2, 3)]
    mine, ahead = call(collect_kernel, (where,), s, [((256, 256), bf16), ((BACK, 256), bf16)], "collect")
    far = along_z(mine)
    near_keys = [mine] + [along_y(mine, d) for d in (1, 2, 3)]
    before = along_rows(ahead, 1)
    far_keys = [far] + [along_y(far, d) for d in (1, 2, 3)]

    out_all, q_all, p_all, grad2, dq, key_t, value1, back_grad, own_grad = forward(
        resp_len, where, (*queries, *s, before, *far_keys, *near_keys)
    )
    back = along_rows(back_grad, -1)

    dq, stay, minus, through, plus = call(
        far_backward_kernel, (), (q_all, p_all, grad2, dq, key_t, value1),
        [((OWN_ROWS // ROWS * PER_GROUP, 128, ROWS), f32)]
        + [((256, 256), f32)] * 4, "far_backward", scratch=SUMS, limit=LIMIT, cost=work(0.25),
    )
    through = along_y(through, 1)
    minus = along_y(minus, -1)
    plus = along_y(plus + through, 1)
    got = along_z(stay + minus + plus)

    near = call(
        near_backward_kernel, (where,), (q_all, p_all, grad2, dq, key_t, value1, out_all),
        [((256, 256), f32)] * 4 + [((rows, 2 * WIDE), bf16)] * 4, "near_backward",
        scratch=[pltpu.VMEM((OWN_ROWS, WIDE), bf16)] + SUMS, limit=LIMIT, cost=work(0.25),
    )
    stay, minus, through, plus = near[:4]
    through = along_y(through, -1)
    plus = along_y(plus, 1)
    minus = along_y(minus + through, -1)

    o = [near[4]] + [along_x(near[4 + d], -d) for d in (1, 2, 3)]
    attn_out, q_grad = call(
        unpack_rows_kernel, (where,), o, [((rows, HEADS * HEAD_DIM), bf16)] * 2, "unpack_rows"
    )

    f = call(
        final_sum_kernel, (where,), (stay, minus, plus, got, own_grad, back), [((192, 256), bf16)] * 4, "final_sum"
    )
    f = [f[0]] + [along_x(f[d], -d) for d in (1, 2, 3)]
    resp_k_grad, resp_v_grad, prompt_k_grad, prompt_v_grad = call(
        unpack_small_kernel, (where,), f, [((rows, 512), bf16)] * 2 + [((64, 512), bf16)] * 2, "unpack_small"
    )
    return attn_out, q_grad, resp_k_grad, resp_v_grad, prompt_k_grad, prompt_v_grad


def solution(mesh):
    split = P(("grp", "seq"), None)
    return jax.shard_map(
        local,
        mesh=mesh,
        in_specs=(P("grp"),) + (split,) * 6,
        out_specs=(split,) * 6,
        check_vma=False,
    )
```

time: 154 us -> 144 us (0.935)
  waiting for transfers between devices: 64.3 us -> 35.6 us
  starting transfers between devices: 42.4 us -> 55.1 us
  Pallas kernels: 40.4 us -> 49 us
  local copies, waits for them, and re-layouts: 4.6 us -> 2.76 us
    ppermute x3 -> x2, waiting for transfers between devices: 29.3 us -> 13.9 us  [along_z(): return lax.ppermute(value, 'seq', [(i, (i + 16) % 32) for i in range(32)])]
    ppermute x8 -> x12, starting transfers between devices: 12.6 us -> 26 us  [along_y(): lax.ppermute(value, 'seq', [(i, i // 16 * 16 + (i + 4 * step) % 16) for i...]
    pallas_call x8, Pallas kernels: 40.4 us -> 49 us  [call(): pl.pallas_call(body, in_specs=[smem] * len(scalars) + [pl.BlockSpec(memor...]
    ppermute x2, waiting for transfers between devices: 7.9 us -> 0.01 us  [along_rows(): return lax.ppermute(value, 'seq', [(i, j) for i, j in pairs if 0 <= j < 32])]
    ppermute x8 -> x12, waiting for transfers between devices: 19.8 us -> 14.1 us  [along_y(): lax.ppermute(value, 'seq', [(i, i // 16 * 16 + (i + 4 * step) % 16) for i...]
    unnamed x14 -> x10, local copies, waits for them, and re-layouts: 4.58 us -> 2.76 us
    ppermute x2, starting transfers between devices: 1.17 us -> 2.8 us  [along_rows(): return lax.ppermute(value, 'seq', [(i, j) for i, j in pairs if 0 <= j < 32])]
    ppermute x3 -> x2, starting transfers between devices: 11 us -> 9.99 us  [along_z(): return lax.ppermute(value, 'seq', [(i, (i + 16) % 32) for i in range(32)])]
  transfers between devices with their start and end apart: 25 -> 28, of which waited for: 14 -> 10; matrix products, arithmetic and copies ran while one was open for 0% -> 0% of each run, Pallas kernels for 2% -> 9%
where the time goes in v2:
time: 144 us
  starting transfers between devices  55.1 us (38%)
  Pallas kernels  49 us (34%)
  waiting for transfers between devices  35.6 us (25%)
  local copies, waits for them, and re-layouts  2.76 us (2%)
    pallas_call x8, Pallas kernels, call(): pl.pallas_call(body, in_specs=[smem] * len(scalars) + [pl.BlockSpec(memor...  49 us
    ppermute x12, starting transfers between devices, along_y(): lax.ppermute(value, 'seq', [(i, i // 16 * 16 + (i + 4 * step) % 16) for i...  26 us
    ppermute x12, starting transfers between devices, along_x(): lax.ppermute(value, 'seq', [(i, i // 4 * 4 + (i + step) % 4) for i in ran...  16.3 us
    ppermute x12, waiting for transfers between devices, along_y(): lax.ppermute(value, 'seq', [(i, i // 16 * 16 + (i + 4 * step) % 16) for i...  14.1 us
    ppermute x2, waiting for transfers between devices, along_z(): return lax.ppermute(value, 'seq', [(i, (i + 16) % 32) for i in range(32)])  13.9 us
    ppermute x2, starting transfers between devices, along_z(): return lax.ppermute(value, 'seq', [(i, (i + 16) % 32) for i in range(32)])  9.99 us
    ppermute x12, waiting for transfers between devices, along_x(): lax.ppermute(value, 'seq', [(i, i // 4 * 4 + (i + step) % 4) for i in ran...  7.67 us
  transfers between devices with their start and end apart: 28, of which 10 were waited for; matrix products, arithmetic and copies ran while one was open for 0% of the time, Pallas kernels for 9%

profile of v2, /device:TPU:32, one launch (start us, length us, event | category | flops | bytes accessed | tf_op | source)
XLA Modules:
  0.0 144.0 jit_solution(3303592997156546975)
XLA Ops:
  1.3 3.7 %pack.1 = (bf16[192,256]{1,0:T(8,128)(2,1)}, bf16[192,256]{1,0:T(8,128)(2,1)}, bf16[192,256]{1,0:T(8,128)(2,1)}, bf16[192,256]{1,0:T(8,128)(2,1)}, bf16[128,1280...) custom-call(s32[2]{0:T(128)} %pad_add_fusion.where_ref, ...), custom_call_target="tpu_custom_call" | custom-call | tf_op jit(solution)/shard_map/pack/pallas_call | solution.py:202
  6.5 2.7 %collective-permute-start.4 = (bf16[192,256]{1,0:T(8,128)(2,1)}, bf16[192,256]{1,0:T(8,128)(2,1)S(1)}, u32[]{:S(2)}, u32[]{:S(2)}) collective-permute-start(bf16[192,256]{1,0:T(8,128)(2,1)} %get-tuple-element.54), channel_id=1, source_target_pairs={{0,2},{1,3},{2,0},{3,1},{4,6},{5,7},{6,4},{7,5},{8,10},{9,11},{10,... | collective-permute-start | bytes 294920 | tf_op jit(solution)/shard_map/ppermute | solution.py:314
  11.3 2.8 %collective-permute-done.4.s2 = bf16[192,256]{1,0:T(8,128)(2,1)S(1)} collective-permute-done((bf16[192,256]{1,0:T(8,128)(2,1)}, bf16[192,256]{1,0:T(8,128)(2,1)S(1)}, u32[]{:S(2)}, u32[]{:S(2)}) %collective-permute-start.4) | collective-permute-done | bytes 98336 | tf_op jit(solution)/shard_map/ppermute | solution.py:314
  15.6 6.4 %collective-permute-start.7 = (bf16[256,256]{1,0:T(8,128)(2,1)S(1)}, bf16[256,256]{1,0:T(8,128)(2,1)S(1)}, u32[]{:S(2)}, u32[]{:S(2)}) collective-permute-start(bf16[256,256]{1,0:T(8,128)(2,1)S(1)} %get-tuple-element.57.l0), channel_id=1, source_target_pairs={{0,16},{1,17},{2,18},{3,19},{4,20},{5,21},{6,22},{7,23},{8,24},{9,... | collective-permute-start | bytes 393224 | tf_op jit(solution)/shard_map/ppermute | solution.py:322
  21.9 1.6 %collective-permute-start.11 = (bf16[256,256]{1,0:T(8,128)(2,1)S(1)}, bf16[256,256]{1,0:T(8,128)(2,1)S(1)}, u32[]{:S(2)}, u32[]{:S(2)}) collective-permute-start(bf16[256,256]{1,0:T(8,128)(2,1)S(1)} %get-tuple-element.57.l0), channel_id=1, source_target_pairs={{0,4},{1,5},{2,6},{3,7},{4,8},{5,9},{6,10},{7,11},{8,12},{9,13},{1... | collective-permute-start | bytes 393224 | tf_op jit(solution)/shard_map/ppermute | solution.py:318
  24.9 2.9 %collective-permute-start.12 = (bf16[256,256]{1,0:T(8,128)(2,1)S(1)}, bf16[256,256]{1,0:T(8,128)(2,1)S(1)}, u32[]{:S(2)}, u32[]{:S(2)}) collective-permute-start(bf16[256,256]{1,0:T(8,128)(2,1)S(1)} %get-tuple-element.57.l0), channel_id=1, source_target_pairs={{0,8},{1,9},{2,10},{3,11},{4,12},{5,13},{6,14},{7,15},{8,0},{9,1},... | collective-permute-start | bytes 393224 | tf_op jit(solution)/shard_map/ppermute | solution.py:318
  27.8 2.8 %collective-permute-start.1 = (bf16[128,1280]{1,0:T(8,128)(2,1)}, bf16[128,1280]{1,0:T(8,128)(2,1)S(1)}, u32[]{:S(2)}, u32[]{:S(2)}) collective-permute-start(bf16[128,1280]{1,0:T(8,128)(2,1)} %get-tuple-element.50), channel_id=1, source_target_pairs={{0,2},{1,3},{2,0},{3,1},{4,6},{5,7},{6,4},{7,5},{8,10},{9,11},{10,... | collective-permute-start | bytes 983048 | tf_op jit(solution)/shard_map/ppermute | solution.py:314
  33.5 6.4 %collective-permute-start.13 = (bf16[256,256]{1,0:T(8,128)(2,1)S(1)}, bf16[256,256]{1,0:T(8,128)(2,1)S(1)}, u32[]{:S(2)}, u32[]{:S(2)}) collective-permute-start(bf16[256,256]{1,0:T(8,128)(2,1)S(1)} %get-tuple-element.57.l0), channel_id=1, source_target_pairs={{0,12},{1,13},{2,14},{3,15},{4,0},{5,1},{6,2},{7,3},{8,4},{9,5},{1... | collective-permute-start | bytes 393224 | tf_op jit(solution)/shard_map/ppermute | solution.py:318
  39.9 2.8 %collective-permute-done.13.l3 = bf16[256,256]{1,0:T(8,128)(2,1)S(1)} collective-permute-done((bf16[256,256]{1,0:T(8,128)(2,1)S(1)}, bf16[256,256]{1,0:T(8,128)(2,1)S(1)}, u32[]{:S(2)}, u32[]{:S(2)}) %collective-permute-start.13) | collective-permute-done | bytes 131104 | tf_op jit(solution)/shard_map/ppermute | solution.py:318
  42.7 3.7 %collective-permute-start.10 = (bf16[256,256]{1,0:T(8,128)(2,1)S(1)}, bf16[256,256]{1,0:T(8,128)(2,1)S(1)}, u32[]{:S(2)}, u32[]{:S(2)}) collective-permute-start(bf16[256,256]{1,0:T(8,128)(2,1)S(1)} %collective-permute-done.7.h0), channel_id=1, source_target_pairs={{0,12},{1,13},{2,14},{3,15},{4,0},{5,1},{6,2},{7,3},{8,4},{9,5},{1... | collective-permute-start | bytes 393224 | tf_op jit(solution)/shard_map/ppermute | solution.py:318
  48.9 5.1 %collective-permute-done.8.h1 = bf16[256,256]{1,0:T(8,128)(2,1)S(1)} collective-permute-done((bf16[256,256]{1,0:T(8,128)(2,1)S(1)}, bf16[256,256]{1,0:T(8,128)(2,1)S(1)}, u32[]{:S(2)}, u32[]{:S(2)}) %collective-permute-start.8) | collective-permute-done | bytes 131104 | tf_op jit(solution)/shard_map/ppermute | solution.py:318
  55.9 21.4 %forward.1 = (bf16[512,640]{1,0:T(8,128)(2,1)S(1)}, bf16[512,1280]{1,0:T(8,128)(2,1)S(1)}, bf16[10,2048,256]{2,1,0:T(8,128)(2,1)S(1)}, bf16[10,256,256]{2,1,0:T(...) custom-call(s32[16]{0:T(128)S(1)} %copy-done.4, ...), custom_call_target="tpu_custom_call" | custom-call | flops 5033164800 | bytes 8000000 | tf_op jit(solution)/shard_map/forward/pallas_call | solution.py:202
  77.3 9.5 %far_backward.1 = (f32[10,128,256]{2,1,0:T(8,128)S(1)}, f32[256,256]{1,0:T(8,128)S(1)}, f32[256,256]{1,0:T(8,128)S(1)}, f32[256,256]{1,0:T(8,128)S(1)}, f32[256,256]{1,0:T(8,128)S(1)}) custom-call(bf16[512,1280]{1,0:T(8,128)(2,1)S(1)} %get-tuple-element.58.q_all, bf16[10,2048,256]{2,1,0:T(8,128)(2,1)S(1)} %get-tuple-element.59.p_all, ...), custom_call_target="tpu_custom_call" | custom-call | flops 2516582400 | bytes 8000000 | tf_op jit(solution)/shard_map/far_backward/pallas_call | solution.py:202
  86.9 10.1 %near_backward.1 = (f32[256,256]{1,0:T(8,128)S(1)}, f32[256,256]{1,0:T(8,128)S(1)}, f32[256,256]{1,0:T(8,128)S(1)}, f32[256,256]{1,0:T(8,128)S(1)}, bf16[128,128...) custom-call(s32[2]{0:T(128)S(1)} %copy-done.2, ...), custom_call_target="tpu_custom_call" | custom-call | flops 2516582400 | bytes 8000000 | tf_op jit(solution)/shard_map/near_backward/pallas_call | solution.py:202
  97.0 3.3 %collective-permute-start.17 = (f32[256,256]{1,0:T(8,128)S(1)}, f32[256,256]{1,0:T(8,128)S(1)}, u32[]{:S(2)}, u32[]{:S(2)}) collective-permute-start(f32[256,256]{1,0:T(8,128)S(1)} %get-tuple-element.74), channel_id=1, source_target_pairs={{0,12},{1,13},{2,14},{3,15},{4,0},{5,1},{6,2},{7,3},{8,4},{9,5},{1... | collective-permute-start | bytes 786440 | tf_op jit(solution)/shard_map/ppermute | solution.py:318
  103.8 2.7 %collective-permute-start.19 = (f32[256,256]{1,0:T(8,128)S(1)}, f32[256,256]{1,0:T(8,128)S(1)}, u32[]{:S(2)}, u32[]{:S(2)}) collective-permute-start(f32[256,256]{1,0:T(8,128)S(1)} %get-tuple-element.75), channel_id=1, source_target_pairs={{0,4},{1,5},{2,6},{3,7},{4,8},{5,9},{6,10},{7,11},{8,12},{9,13},{1... | collective-permute-start | bytes 786440 | tf_op jit(solution)/shard_map/ppermute | solution.py:318
  106.7 5.1 %collective-permute-done.20 = f32[256,256]{1,0:T(8,128)S(1)} collective-permute-done((f32[256,256]{1,0:T(8,128)S(1)}, f32[256,256]{1,0:T(8,128)S(1)}, u32[]{:S(2)}, u32[]{:S(2)}) %collective-permute-start.20) | collective-permute-done | bytes 262176 | tf_op jit(solution)/shard_map/ppermute | solution.py:318
  111.9 1.8 %collective-permute-start.18 = (f32[256,256]{1,0:T(8,128)S(1)}, f32[256,256]{1,0:T(8,128)S(1)}, u32[]{:S(2)}, u32[]{:S(2)}) collective-permute-start(f32[256,256]{1,0:T(8,128)S(1)} %add.18), channel_id=1, source_target_pairs={{0,12},{1,13},{2,14},{3,15},{4,0},{5,1},{6,2},{7,3},{8,4},{9,5},{1... | collective-permute-start | bytes 786440 | tf_op jit(solution)/shard_map/ppermute | solution.py:318
  113.7 3.6 %collective-permute-start.23 = (f32[256,256]{1,0:T(8,128)S(1)}, f32[256,256]{1,0:T(8,128)S(1)}, u32[]{:S(2)}, u32[]{:S(2)}) collective-permute-start(f32[256,256]{1,0:T(8,128)S(1)} %add_add_fusion), channel_id=1, source_target_pairs={{0,16},{1,17},{2,18},{3,19},{4,20},{5,21},{6,22},{7,23},{8,24},{9,... | collective-permute-start | bytes 786440 | tf_op jit(solution)/shard_map/ppermute | solution.py:322
  117.3 1.9 %collective-permute-start.15 = (bf16[128,1280]{1,0:T(8,128)(2,1)S(1)}, bf16[128,1280]{1,0:T(8,128)(2,1)S(1)}, u32[]{:S(2)}, u32[]{:S(2)}) collective-permute-start(bf16[128,1280]{1,0:T(8,128)(2,1)S(1)} %get-tuple-element.68), channel_id=1, source_target_pairs={{0,2},{1,3},{2,0},{3,1},{4,6},{5,7},{6,4},{7,5},{8,10},{9,11},{10,... | collective-permute-start | bytes 983048 | tf_op jit(solution)/shard_map/ppermute | solution.py:314
  119.6 13.9 %collective-permute-done.23.got_ref = f32[256,256]{1,0:T(8,128)S(1)} collective-permute-done((f32[256,256]{1,0:T(8,128)S(1)}, f32[256,256]{1,0:T(8,128)S(1)}, u32[]{:S(2)}, u32[]{:S(2)}) %collective-permute-start.23) | collective-permute-done | bytes 262176 | tf_op jit(solution)/shard_map/ppermute | solution.py:322
  134.2 2.5 %collective-permute-start.26 = (bf16[192,256]{1,0:T(8,128)(2,1)S(1)}, bf16[192,256]{1,0:T(8,128)(2,1)S(1)}, u32[]{:S(2)}, u32[]{:S(2)}) collective-permute-start(bf16[192,256]{1,0:T(8,128)(2,1)S(1)} %get-tuple-element.84), channel_id=1, source_target_pairs={{0,2},{1,3},{2,0},{3,1},{4,6},{5,7},{6,4},{7,5},{8,10},{9,11},{10,... | collective-permute-start | bytes 294920 | tf_op jit(solution)/shard_map/ppermute | solution.py:314
  136.7 1.7 %unpack_rows.1 = (bf16[128,2560]{1,0:T(8,128)(2,1)}, bf16[128,2560]{1,0:T(8,128)(2,1)}) custom-call(s32[2]{0:T(128)S(1)} %copy-done.2, bf16[128,1280]{1,0:T(8,128)(2,1)S(1)} %get-tuple-element.66.o0, bf16[128,1280]{1,0:T(8,128)(2,1)S(1)} %collective-permute-done.14.o1, bf16[128,1280]{1,0:T(8,128)(2,1)S(1)} %collective-permute-done.15.o2, ...), custom_call_target="tpu_custom_call" | custom-call | tf_op jit(solution)/shard_map/unpack_rows/pallas_call | solution.py:202
  138.8 2.4 %collective-permute-done.26.f2 = bf16[192,256]{1,0:T(8,128)(2,1)S(1)} collective-permute-done((bf16[192,256]{1,0:T(8,128)(2,1)S(1)}, bf16[192,256]{1,0:T(8,128)(2,1)S(1)}, u32[]{:S(2)}, u32[]{:S(2)}) %collective-permute-start.26) | collective-permute-done | bytes 98336 | tf_op jit(solution)/shard_map/ppermute | solution.py:314
  (54 shorter events, 22.5 us)
Async XLA Ops:
  4.9 6.4 %collective-permute-start.3 = (bf16[192,256]{1,0:T(8,128)(2,1)}, bf16[192,256]{1,0:T(8,128)(2,1)S(1)}, u32[]{:S(2)}, u32[]{:S(2)}) collective-permute-start(bf16[192,256]{1,0:T(8,128)(2,1)} %get-tuple-element.53), channel_id=1, source_target_pairs={{0,1},{1,2},{2,3},{3,0},{4,5},{5,6},{6,7},{7,4},{8,9},{9,10},{10,1... | collective-permute-start | bytes 294920 | tf_op jit(solution)/shard_map/ppermute | solution.py:314
  6.5 7.6 %collective-permute-start.4 = (bf16[192,256]{1,0:T(8,128)(2,1)}, bf16[192,256]{1,0:T(8,128)(2,1)S(1)}, u32[]{:S(2)}, u32[]{:S(2)}) collective-permute-start(bf16[192,256]{1,0:T(8,128)(2,1)} %get-tuple-element.54), channel_id=1, source_target_pairs={{0,2},{1,3},{2,0},{3,1},{4,6},{5,7},{6,4},{7,5},{8,10},{9,11},{10,... | collective-permute-start | bytes 294920 | tf_op jit(solution)/shard_map/ppermute | solution.py:314
  15.6 15.0 %collective-permute-start.7 = (bf16[256,256]{1,0:T(8,128)(2,1)S(1)}, bf16[256,256]{1,0:T(8,128)(2,1)S(1)}, u32[]{:S(2)}, u32[]{:S(2)}) collective-permute-start(bf16[256,256]{1,0:T(8,128)(2,1)S(1)} %get-tuple-element.57.l0), channel_id=1, source_target_pairs={{0,16},{1,17},{2,18},{3,19},{4,20},{5,21},{6,22},{7,23},{8,24},{9,... | collective-permute-start | bytes 393224 | tf_op jit(solution)/shard_map/ppermute | solution.py:322
  21.9 10.1 %collective-permute-start.11 = (bf16[256,256]{1,0:T(8,128)(2,1)S(1)}, bf16[256,256]{1,0:T(8,128)(2,1)S(1)}, u32[]{:S(2)}, u32[]{:S(2)}) collective-permute-start(bf16[256,256]{1,0:T(8,128)(2,1)S(1)} %get-tuple-element.57.l0), channel_id=1, source_target_pairs={{0,4},{1,5},{2,6},{3,7},{4,8},{5,9},{6,10},{7,11},{8,12},{9,13},{1... | collective-permute-start | bytes 393224 | tf_op jit(solution)/shard_map/ppermute | solution.py:318
  23.5 22.9 %collective-permute-start = (bf16[128,1280]{1,0:T(8,128)(2,1)}, bf16[128,1280]{1,0:T(8,128)(2,1)S(1)}, u32[]{:S(2)}, u32[]{:S(2)}) collective-permute-start(bf16[128,1280]{1,0:T(8,128)(2,1)} %get-tuple-element.49), channel_id=1, source_target_pairs={{0,1},{1,2},{2,3},{3,0},{4,5},{5,6},{6,7},{7,4},{8,9},{9,10},{10,1... | collective-permute-start | bytes 983048 | tf_op jit(solution)/shard_map/ppermute | solution.py:314
  24.9 8.7 %collective-permute-start.12 = (bf16[256,256]{1,0:T(8,128)(2,1)S(1)}, bf16[256,256]{1,0:T(8,128)(2,1)S(1)}, u32[]{:S(2)}, u32[]{:S(2)}) collective-permute-start(bf16[256,256]{1,0:T(8,128)(2,1)S(1)} %get-tuple-element.57.l0), channel_id=1, source_target_pairs={{0,8},{1,9},{2,10},{3,11},{4,12},{5,13},{6,14},{7,15},{8,0},{9,1},... | collective-permute-start | bytes 393224 | tf_op jit(solution)/shard_map/ppermute | solution.py:318
  27.8 20.1 %collective-permute-start.1 = (bf16[128,1280]{1,0:T(8,128)(2,1)}, bf16[128,1280]{1,0:T(8,128)(2,1)S(1)}, u32[]{:S(2)}, u32[]{:S(2)}) collective-permute-start(bf16[128,1280]{1,0:T(8,128)(2,1)} %get-tuple-element.50), channel_id=1, source_target_pairs={{0,2},{1,3},{2,0},{3,1},{4,6},{5,7},{6,4},{7,5},{8,10},{9,11},{10,... | collective-permute-start | bytes 983048 | tf_op jit(solution)/shard_map/ppermute | solution.py:314
  30.5 15.9 %collective-permute-start.6 = (bf16[384,256]{1,0:T(8,128)(2,1)S(1)}, bf16[384,256]{1,0:T(8,128)(2,1)S(1)}, u32[]{:S(2)}, u32[]{:S(2)}) collective-permute-start(bf16[384,256]{1,0:T(8,128)(2,1)S(1)} %get-tuple-element.56), channel_id=1, source_target_pairs={{0,4},{1,5},{2,6},{3,7},{4,8},{5,9},{6,10},{7,11},{8,12},{9,13},{1... | collective-permute-start | bytes 589832 | tf_op jit(solution)/shard_map/ppermute | solution.py:327
  32.1 15.8 %collective-permute-start.2 = (bf16[128,1280]{1,0:T(8,128)(2,1)}, bf16[128,1280]{1,0:T(8,128)(2,1)S(1)}, u32[]{:S(2)}, u32[]{:S(2)}) collective-permute-start(bf16[128,1280]{1,0:T(8,128)(2,1)} %get-tuple-element.51), channel_id=1, source_target_pairs={{0,3},{1,0},{2,1},{3,2},{4,7},{5,4},{6,5},{7,6},{8,11},{9,8},{10,9... | collective-permute-start | bytes 983048 | tf_op jit(solution)/shard_map/ppermute | solution.py:314
  33.5 9.2 %collective-permute-start.13 = (bf16[256,256]{1,0:T(8,128)(2,1)S(1)}, bf16[256,256]{1,0:T(8,128)(2,1)S(1)}, u32[]{:S(2)}, u32[]{:S(2)}) collective-permute-start(bf16[256,256]{1,0:T(8,128)(2,1)S(1)} %get-tuple-element.57.l0), channel_id=1, source_target_pairs={{0,12},{1,13},{2,14},{3,15},{4,0},{5,1},{6,2},{7,3},{8,4},{9,5},{1... | collective-permute-start | bytes 393224 | tf_op jit(solution)/shard_map/ppermute | solution.py:318
  46.4 7.6 %collective-permute-start.8 = (bf16[256,256]{1,0:T(8,128)(2,1)S(1)}, bf16[256,256]{1,0:T(8,128)(2,1)S(1)}, u32[]{:S(2)}, u32[]{:S(2)}) collective-permute-start(bf16[256,256]{1,0:T(8,128)(2,1)S(1)} %collective-permute-done.7.h0), channel_id=1, source_target_pairs={{0,4},{1,5},{2,6},{3,7},{4,8},{5,9},{6,10},{7,11},{8,12},{9,13},{1... | collective-permute-start | bytes 393224 | tf_op jit(solution)/shard_map/ppermute | solution.py:318
  46.4 7.6 %collective-permute-start.9 = (bf16[256,256]{1,0:T(8,128)(2,1)S(1)}, bf16[256,256]{1,0:T(8,128)(2,1)S(1)}, u32[]{:S(2)}, u32[]{:S(2)}) collective-permute-start(bf16[256,256]{1,0:T(8,128)(2,1)S(1)} %collective-permute-done.7.h0), channel_id=1, source_target_pairs={{0,8},{1,9},{2,10},{3,11},{4,12},{5,13},{6,14},{7,15},{8,0},{9,1},... | collective-permute-start | bytes 393224 | tf_op jit(solution)/shard_map/ppermute | solution.py:318
  86.8 14.4 %collective-permute-start.21 = (f32[256,256]{1,0:T(8,128)S(1)}, f32[256,256]{1,0:T(8,128)S(1)}, u32[]{:S(2)}, u32[]{:S(2)}) collective-permute-start(f32[256,256]{1,0:T(8,128)S(1)} %get-tuple-element.79), channel_id=1, source_target_pairs={{0,4},{1,5},{2,6},{3,7},{4,8},{5,9},{6,10},{7,11},{8,12},{9,13},{1... | collective-permute-start | bytes 786440 | tf_op jit(solution)/shard_map/ppermute | solution.py:318
  97.0 9.5 %collective-permute-start.17 = (f32[256,256]{1,0:T(8,128)S(1)}, f32[256,256]{1,0:T(8,128)S(1)}, u32[]{:S(2)}, u32[]{:S(2)}) collective-permute-start(f32[256,256]{1,0:T(8,128)S(1)} %get-tuple-element.74), channel_id=1, source_target_pairs={{0,12},{1,13},{2,14},{3,15},{4,0},{5,1},{6,2},{7,3},{8,4},{9,5},{1... | collective-permute-start | bytes 786440 | tf_op jit(solution)/shard_map/ppermute | solution.py:318
  100.3 11.5 %collective-permute-start.20 = (f32[256,256]{1,0:T(8,128)S(1)}, f32[256,256]{1,0:T(8,128)S(1)}, u32[]{:S(2)}, u32[]{:S(2)}) collective-permute-start(f32[256,256]{1,0:T(8,128)S(1)} %get-tuple-element.77), channel_id=1, source_target_pairs={{0,12},{1,13},{2,14},{3,15},{4,0},{5,1},{6,2},{7,3},{8,4},{9,5},{1... | collective-permute-start | bytes 786440 | tf_op jit(solution)/shard_map/ppermute | solution.py:318
  101.3 12.4 %collective-permute-start.22 = (f32[256,256]{1,0:T(8,128)S(1)}, f32[256,256]{1,0:T(8,128)S(1)}, u32[]{:S(2)}, u32[]{:S(2)}) collective-permute-start(f32[256,256]{1,0:T(8,128)S(1)} %add.20), channel_id=1, source_target_pairs={{0,4},{1,5},{2,6},{3,7},{4,8},{5,9},{6,10},{7,11},{8,12},{9,13},{1... | collective-permute-start | bytes 786440 | tf_op jit(solution)/shard_map/ppermute | solution.py:318
  102.5 16.8 %collective-permute-start.24 = (f32[384,256]{1,0:T(8,128)S(1)}, f32[384,256]{1,0:T(8,128)S(1)}, u32[]{:S(2)}, u32[]{:S(2)}) collective-permute-start(f32[384,256]{1,0:T(8,128)S(1)} %get-tuple-element.81), channel_id=1, source_target_pairs={{4,0},{5,1},{6,2},{7,3},{8,4},{9,5},{10,6},{11,7},{12,8},{13,9},{1... | collective-permute-start | bytes 1179656 | tf_op jit(solution)/shard_map/ppermute | solution.py:327
  103.8 13.6 %collective-permute-start.19 = (f32[256,256]{1,0:T(8,128)S(1)}, f32[256,256]{1,0:T(8,128)S(1)}, u32[]{:S(2)}, u32[]{:S(2)}) collective-permute-start(f32[256,256]{1,0:T(8,128)S(1)} %get-tuple-element.75), channel_id=1, source_target_pairs={{0,4},{1,5},{2,6},{3,7},{4,8},{5,9},{6,10},{7,11},{8,12},{9,13},{1... | collective-permute-start | bytes 786440 | tf_op jit(solution)/shard_map/ppermute | solution.py:318
  106.5 30.2 %collective-permute-start.14 = (bf16[128,1280]{1,0:T(8,128)(2,1)S(1)}, bf16[128,1280]{1,0:T(8,128)(2,1)S(1)}, u32[]{:S(2)}, u32[]{:S(2)}) collective-permute-start(bf16[128,1280]{1,0:T(8,128)(2,1)S(1)} %get-tuple-element.67), channel_id=1, source_target_pairs={{0,3},{1,0},{2,1},{3,2},{4,7},{5,4},{6,5},{7,6},{8,11},{9,8},{10,9... | collective-permute-start | bytes 983048 | tf_op jit(solution)/shard_map/ppermute | solution.py:314
  111.9 7.7 %collective-permute-start.18 = (f32[256,256]{1,0:T(8,128)S(1)}, f32[256,256]{1,0:T(8,128)S(1)}, u32[]{:S(2)}, u32[]{:S(2)}) collective-permute-start(f32[256,256]{1,0:T(8,128)S(1)} %add.18), channel_id=1, source_target_pairs={{0,12},{1,13},{2,14},{3,15},{4,0},{5,1},{6,2},{7,3},{8,4},{9,5},{1... | collective-permute-start | bytes 786440 | tf_op jit(solution)/shard_map/ppermute | solution.py:318
  113.7 19.7 %collective-permute-start.23 = (f32[256,256]{1,0:T(8,128)S(1)}, f32[256,256]{1,0:T(8,128)S(1)}, u32[]{:S(2)}, u32[]{:S(2)}) collective-permute-start(f32[256,256]{1,0:T(8,128)S(1)} %add_add_fusion), channel_id=1, source_target_pairs={{0,16},{1,17},{2,18},{3,19},{4,20},{5,21},{6,22},{7,23},{8,24},{9,... | collective-permute-start | bytes 786440 | tf_op jit(solution)/shard_map/ppermute | solution.py:322
  117.3 19.3 %collective-permute-start.15 = (bf16[128,1280]{1,0:T(8,128)(2,1)S(1)}, bf16[128,1280]{1,0:T(8,128)(2,1)S(1)}, u32[]{:S(2)}, u32[]{:S(2)}) collective-permute-start(bf16[128,1280]{1,0:T(8,128)(2,1)S(1)} %get-tuple-element.68), channel_id=1, source_target_pairs={{0,2},{1,3},{2,0},{3,1},{4,6},{5,7},{6,4},{7,5},{8,10},{9,11},{10,... | collective-permute-start | bytes 983048 | tf_op jit(solution)/shard_map/ppermute | solution.py:314
  119.3 17.4 %collective-permute-start.16 = (bf16[128,1280]{1,0:T(8,128)(2,1)S(1)}, bf16[128,1280]{1,0:T(8,128)(2,1)S(1)}, u32[]{:S(2)}, u32[]{:S(2)}) collective-permute-start(bf16[128,1280]{1,0:T(8,128)(2,1)S(1)} %get-tuple-element.69), channel_id=1, source_target_pairs={{0,1},{1,2},{2,3},{3,0},{4,5},{5,6},{6,7},{7,4},{8,9},{9,10},{10,1... | collective-permute-start | bytes 983048 | tf_op jit(solution)/shard_map/ppermute | solution.py:314
  134.2 7.0 %collective-permute-start.26 = (bf16[192,256]{1,0:T(8,128)(2,1)S(1)}, bf16[192,256]{1,0:T(8,128)(2,1)S(1)}, u32[]{:S(2)}, u32[]{:S(2)}) collective-permute-start(bf16[192,256]{1,0:T(8,128)(2,1)S(1)} %get-tuple-element.84), channel_id=1, source_target_pairs={{0,2},{1,3},{2,0},{3,1},{4,6},{5,7},{6,4},{7,5},{8,10},{9,11},{10,... | collective-permute-start | bytes 294920 | tf_op jit(solution)/shard_map/ppermute | solution.py:314
  (9 other events, 90.7 us)

commit v3 on v2

--- a/solution.py
+++ b/solution.py
@@ -14,6 +14,7 @@
 LOG2E = 1.4426950408889634
 FACTOR = HEAD_DIM ** (-0.5)
 
+X_GROUPS = [[first + x for x in range(4)] for first in range(0, 32, 4)]
 ROWS = 256
 KEYS = 512
 SPAN = 640
@@ -21,6 +22,7 @@
 OWN_ROWS = 512
 WIDE = PER_GROUP * HEAD_DIM
 LIMIT = 16
+TILE = 1024
 
 
 def nt(a, b):
@@ -36,8 +38,8 @@
 
 
 def forward_kernel(
-    len_ref, where_ref, q0, q1, q2, q3, s0, s1, s2, s3, before_ref, h0, h1, h2, h3, l0, l1, l2, l3,
-    out_all, q_all, p_all, grad2_all, dq_all, key_t, value1, back_grad_ref, own_grad_ref,
+    len_ref, where_ref, q_all, s0, s1, s2, s3, before_ref, h0, h1, h2, h3, l0, l1, l2, l3,
+    out_all, p_all, grad2_all, dq_all, key_t, value1, back_grad_ref, own_grad_ref,
     key2, value_t, wkey2, wvalue1, wkey_t, wvalue_t, s_first, s_second, key_sum, value_sum,
 ):
     base, x = where_ref[0], where_ref[1]
@@ -63,8 +65,6 @@
             at = slice(c, c + 128)
             keys_t[:, at] = keys[at, :128].astype(jnp.float32).T.astype(jnp.bfloat16)
             values_t[:128, at] = values[at, :128].astype(jnp.float32).T.astype(jnp.bfloat16)
-    for d, source in enumerate((q0, q1, q2, q3)):
-        q_all[block_at(x, d), :] = source[...]
     key_sum[...] = jnp.zeros_like(key_sum)
     value_sum[...] = jnp.zeros_like(value_sum)
 
@@ -73,15 +73,15 @@
         g_cols = pl.ds(pl.multiple_of(WIDE + head * 128, 128), 128)
         state = []
         for block, s_ref in enumerate((s_first, s_second)):
-            mine = slice(block * ROWS, block * ROWS + ROWS)
-            q = q_all[mine, q_cols]
-            scaled = q.astype(jnp.float32).T * (FACTOR * LOG2E)
+            mine = slice(block * 2, block * 2 + 2)
+            q = q_all[mine, :, q_cols].reshape(ROWS, 128)
+            scaled = q.astype(jnp.float32) * (FACTOR * LOG2E)
             high = scaled.astype(jnp.bfloat16)
             low = (scaled - high.astype(jnp.float32)).astype(jnp.bfloat16)
-            q2t = jnp.concatenate([high, low], 0)
+            q2 = jnp.concatenate([high, low], 1)
             top = None
             for c in range(0, PROMPT_ROWS, KEYS):
-                s = nn(key2[c : c + KEYS, :], q2t)
+                s = nt(key2[c : c + KEYS, :], q2)
                 s_ref[c : c + KEYS, :] = s
                 tile_top = jnp.max(s, axis=0, keepdims=True)
                 top = tile_top if top is None else jnp.maximum(top, tile_top)
@@ -96,7 +96,7 @@
             key_pos = own - BACK + lax.broadcasted_iota(jnp.int32, (SPAN, ROWS), 0)
             seen = (key_pos <= row_pos) & (key_pos >= seg_start)
             span = slice(block * ROWS, block * ROWS + SPAN)
-            s = jnp.where(seen, nn(wkey2[span, :], q2t), NEGATIVE)
+            s = jnp.where(seen, nt(wkey2[span, :], q2), NEGATIVE)
             s_ref[PROMPT_ROWS:, :] = s
             top = jnp.maximum(top, jnp.max(s, axis=0, keepdims=True))
             state.append((block, s_ref, mine, span, q, top))
@@ -112,20 +112,22 @@
             total = total + nn(wvalue_t[:, span], p)
 
             inverse = 1.0 / total[128:129, :]
-            out = (total[:128, :] * inverse).astype(jnp.bfloat16).astype(jnp.float32)
-            out_all[mine, q_cols] = out.T.astype(jnp.bfloat16)
-            grad_n = (q_all[mine, g_cols].astype(jnp.float32).T * inverse).astype(jnp.bfloat16)
-            row_dot = -jnp.sum(grad_n.astype(jnp.float32) * out, axis=0, keepdims=True)
+            out = (total[:128, :] * inverse).T.astype(jnp.bfloat16)
+            out_all[mine, :, q_cols] = out.reshape(2, 128, 128)
+            column = jnp.broadcast_to(inverse, (8, ROWS)).T[:, :1]
+            grad = q_all[mine, :, g_cols].reshape(ROWS, 128)
+            grad_n = (grad.astype(jnp.float32) * column).astype(jnp.bfloat16)
+            row_dot = -jnp.sum(grad_n.astype(jnp.float32) * out.astype(jnp.float32), axis=1, keepdims=True)
             dot_high = row_dot.astype(jnp.bfloat16).astype(jnp.float32)
-            line = lax.broadcasted_iota(jnp.int32, (128, ROWS), 0)
-            extra = jnp.where(line == 0, dot_high, jnp.where(line == 1, row_dot - dot_high, 0.0))
-            grad2 = jnp.concatenate([grad_n, extra.astype(jnp.bfloat16)], 0)
+            lane = lax.broadcasted_iota(jnp.int32, (ROWS, 128), 1)
+            extra = jnp.where(lane == 0, dot_high, jnp.where(lane == 1, row_dot - dot_high, 0.0))
+            grad2 = jnp.concatenate([grad_n, extra.astype(jnp.bfloat16)], 1)
             grad2_all[item] = grad2
 
-            ds = (p.astype(jnp.float32) * nn(wvalue1[span, :], grad2)).astype(jnp.bfloat16)
+            ds = (p.astype(jnp.float32) * nt(wvalue1[span, :], grad2)).astype(jnp.bfloat16)
             dq_all[item] = nn(wkey_t[:, span], ds)
             key_sum[span, :] += nn(ds, q)
-            value_sum[span, :] += nt(p, grad_n)
+            value_sum[span, :] += nn(p, grad_n)
         return carry
 
     lax.fori_loop(0, PER_GROUP, one_head, 0)
@@ -142,17 +144,17 @@
     def one_head(head, carry):
         q_cols = pl.ds(pl.multiple_of(head * 128, 128), 128)
         dq = [dq_all[block * PER_GROUP + head] for block in range(2)]
-        for c in range(0, PROMPT_ROWS // 2, KEYS):
-            at, keys = slice(c, c + KEYS), slice(first + c, first + c + KEYS)
+        for c in range(0, PROMPT_ROWS // 2, TILE):
+            at, keys = slice(c, c + TILE), slice(first + c, first + c + TILE)
             key_term, value_term = None, None
             for block in range(2):
                 item = block * PER_GROUP + head
                 grad2 = grad2_all[item]
                 p = p_all[item, keys, :]
-                ds = (p.astype(jnp.float32) * nn(value1[keys, :], grad2)).astype(jnp.bfloat16)
+                ds = (p.astype(jnp.float32) * nt(value1[keys, :], grad2)).astype(jnp.bfloat16)
                 dq[block] = dq[block] + nn(key_t[:, keys], ds)
-                k = nn(ds, q_all[block * ROWS : block * ROWS + ROWS, q_cols])
-                v = nt(p, grad2[:128, :])
+                k = nn(ds, q_all[block * 2 : block * 2 + 2, :, q_cols].reshape(ROWS, 128))
+                v = nn(p, grad2[:, :128])
                 key_term = k if key_term is None else key_term + k
                 value_term = v if value_term is None else value_term + v
             key_sum[at, :] += key_term
@@ -182,33 +184,31 @@
 
 
 def near_backward_kernel(
-    where_ref, q_all, p_all, grad2_all, dq_in, key_t, value1, out_all,
-    g0, g1, g2, g3, o0, o1, o2, o3, dq_rows, key_sum, value_sum,
+    q_all, p_all, grad2_all, dq_in, key_t, value1, out_all, back, g0, g1, g2, g3, o_ref, key_sum, value_sum
 ):
     def finish(head, block, dq):
-        cols = pl.ds(pl.multiple_of(head * 128, 128), 128)
-        dq_rows[block * ROWS : block * ROWS + ROWS, cols] = (dq * FACTOR).T.astype(jnp.bfloat16)
+        cols = pl.ds(pl.multiple_of(WIDE + head * 128, 128), 128)
+        dq = (dq * FACTOR).T.astype(jnp.bfloat16)
+        o_ref[block * 2 : block * 2 + 2, :, cols] = dq.reshape(2, 128, 128)
 
     backward(PROMPT_ROWS // 2, q_all, p_all, grad2_all, dq_in, key_t, value1, key_sum, value_sum, finish)
     write_sums(key_sum, value_sum, (g0, g1, g2, g3))
-    for d, target in enumerate((o0, o1, o2, o3)):
-        at = block_at(where_ref[1], d)
-        target[:, :WIDE] = out_all[at, :]
-        target[:, WIDE:] = dq_rows[at, :]
-
-
-def call(body, scalars, operands, outs, name, scratch=(), limit=24, cost=None, space=pltpu.VMEM):
-    vmem, smem = pl.BlockSpec(memory_space=pltpu.VMEM), pl.BlockSpec(memory_space=pltpu.SMEM)
+    o_ref[:, :, :WIDE] = out_all[...]
+
+
+def call(body, scalars, operands, outs, name, scratch=(), limit=24, cost=None, space=pltpu.VMEM, extra=()):
+    smem = pl.BlockSpec(memory_space=pltpu.SMEM)
     return pl.pallas_call(
         body,
-        in_specs=[smem] * len(scalars) + [pl.BlockSpec(memory_space=space)] * len(operands),
-        out_specs=[vmem] * len(outs),
+        in_specs=[smem] * len(scalars) + [pl.BlockSpec(memory_space=space)] * len(operands)
+        + [pl.BlockSpec(memory_space=pl.ANY)] * len(extra),
+        out_specs=[pl.BlockSpec(memory_space=space)] * len(outs),
         out_shape=[jax.ShapeDtypeStruct(shape, dtype) for shape, dtype in outs],
         scratch_shapes=list(scratch),
         compiler_params=pltpu.CompilerParams(vmem_limit_bytes=limit * 1024 * 1024),
         cost_estimate=cost,
         name=name,
-    )(*scalars, *operands)
+    )(*scalars, *operands, *extra)
 
 
 def work(share):
@@ -222,7 +222,7 @@
     return call(
         forward_kernel, (resp_len, where), operands,
         [
-            ((OWN_ROWS, WIDE), bf16), ((OWN_ROWS, 2 * WIDE), bf16), ((items, PROMPT_ROWS, ROWS), bf16),
+            ((4, 128, WIDE), bf16), ((items, PROMPT_ROWS, ROWS), bf16),
             ((items, 256, ROWS), bf16), ((items, 128, ROWS), f32), ((128, PROMPT_ROWS), bf16),
             ((PROMPT_ROWS, 256), bf16), ((BACK, 256), f32), ((OWN_ROWS, 256), f32),
         ],
@@ -250,24 +250,29 @@
     return pl.ds(pl.multiple_of(lax.rem(x + distance, 4) * width, 128), width)
 
 
-def pack_kernel(where_ref, pk, pv, k, v, q, g, s0, s1, s2, s3, q0, q1, q2, q3, sems):
-    x = where_ref[1]
-    copies = []
-    for d, small, rows in ((0, s0, q0), (1, s1, q1), (2, s2, q2), (3, s3, q3)):
-        narrow, wide = head_columns(x, d, 128), head_columns(x, d, WIDE)
-        for source, target in (
-            (pk.at[:, narrow], small.at[0:64, 0:128]),
-            (pv.at[:, narrow], small.at[0:64, 128:256]),
-            (k.at[:, narrow], small.at[64:192, 0:128]),
-            (v.at[:, narrow], small.at[64:192, 128:256]),
-            (q.at[:, wide], rows.at[:, 0:WIDE]),
-            (g.at[:, wide], rows.at[:, WIDE : 2 * WIDE]),
-        ):
-            copies.append(pltpu.make_async_copy(source, target, sems.at[len(copies)]))
+def run_copies(pairs, sems):
+    copies = [pltpu.make_async_copy(source, target, sems.at[i]) for i, (source, target) in enumerate(pairs)]
     for copy in copies:
         copy.start()
     for copy in copies:
         copy.wait()
+
+
+def pack_small_kernel(where_ref, pk, pv, k, v, s0, s1, s2, s3, sems):
+    pairs = []
+    for d, target in enumerate((s0, s1, s2, s3)):
+        cols = head_columns(where_ref[1], d, 128)
+        for source, lines, lanes in ((pk, (0, 64), 0), (pv, (0, 64), 128), (k, (64, 192), 0), (v, (64, 192), 128)):
+            pairs.append((source.at[:, cols], target.at[slice(*lines), lanes : lanes + 128]))
+    run_copies(pairs, sems)
+
+
+def pack_rows_kernel(q, g, target, sems):
+    pairs = []
+    for h in range(KV_HEADS):
+        for source, first in ((q, 0), (g, WIDE)):
+            pairs.append((source.at[:, h * WIDE : h * WIDE + WIDE], target.at[h, :, first : first + WIDE]))
+    run_copies(pairs, sems)
 
 
 def collect_kernel(where_ref, s0, s1, s2, s3, mine_ref, ahead_ref):
@@ -293,11 +298,16 @@
         target[64:, :] = (own_ref[block_at(x, d), :] + extra).astype(jnp.bfloat16)
 
 
-def unpack_rows_kernel(where_ref, o0, o1, o2, o3, out_ref, dq_ref):
-    x = where_ref[1]
-    for d, source in enumerate((o0, o1, o2, o3)):
-        out_ref[:, head_columns(x, d, WIDE)] = source[:, :WIDE]
-        dq_ref[:, head_columns(x, d, WIDE)] = source[:, WIDE:]
+def add_kernel(a, b, c, d, after, ab_ref, cd_ref):
+    ab_ref[...] = a[...] + b[...]
+    cd_ref[...] = c[...] + d[...]
+
+
+def unpack_rows_kernel(o_ref, out_ref, dq_ref):
+    for h in range(KV_HEADS):
+        at = slice(h * WIDE, h * WIDE + WIDE)
+        out_ref[:, at] = o_ref[h, :, :WIDE]
+        dq_ref[:, at] = o_ref[h, :, WIDE:]
 
 
 def unpack_small_kernel(where_ref, f0, f1, f2, f3, k_ref, v_ref, pk_ref, pv_ref):
@@ -314,6 +324,10 @@
     return lax.ppermute(value, "seq", [(i, i // 4 * 4 + (i + step) % 4) for i in range(32)])
 
 
+def exchange_x(value):
+    return lax.all_to_all(value, "seq", 0, 0, axis_index_groups=X_GROUPS, tiled=True)
+
+
 def along_y(value, step):
     return lax.ppermute(value, "seq", [(i, i // 16 * 16 + (i + 4 * step) % 16) for i in range(32)])
 
@@ -332,21 +346,24 @@
     where = jnp.stack([me // 4 * OWN_ROWS, me % 4])
     rows, bf16, f32 = resp_q.shape[0], jnp.bfloat16, jnp.float32
 
-    packed = call(
-        pack_kernel, (where,), (prompt_keys, prompt_values, resp_k, resp_v, resp_q, out_grad),
-        [((192, 256), bf16)] * 4 + [((rows, 2 * WIDE), bf16)] * 4, "pack",
-        scratch=[pltpu.SemaphoreType.DMA((24,))], space=pl.ANY, limit=60,
-    )
-    s = [packed[0]] + [along_x(packed[d], d) for d in (1, 2, 3)]
-    queries = [packed[4]] + [along_x(packed[4 + d], d) for d in (1, 2, 3)]
+    s = call(
+        pack_small_kernel, (where,), (prompt_keys, prompt_values, resp_k, resp_v), [((192, 256), bf16)] * 4,
+        "pack_small", scratch=[pltpu.SemaphoreType.DMA((16,))], space=pl.ANY, limit=60,
+    )
+    (q_all,) = call(
+        pack_rows_kernel, (), (resp_q, out_grad), [((4, rows, 2 * WIDE), bf16)],
+        "pack_rows", scratch=[pltpu.SemaphoreType.DMA((8,))], space=pl.ANY, limit=60,
+    )
+    s = [s[0]] + [along_x(s[d], d) for d in (1, 2, 3)]
+    q_all = exchange_x(q_all)
     mine, ahead = call(collect_kernel, (where,), s, [((256, 256), bf16), ((BACK, 256), bf16)], "collect")
     far = along_z(mine)
     near_keys = [mine] + [along_y(mine, d) for d in (1, 2, 3)]
     before = along_rows(ahead, 1)
     far_keys = [far] + [along_y(far, d) for d in (1, 2, 3)]
 
-    out_all, q_all, p_all, grad2, dq, key_t, value1, back_grad, own_grad = forward(
-        resp_len, where, (*queries, *s, before, *far_keys, *near_keys)
+    out_all, p_all, grad2, dq, key_t, value1, back_grad, own_grad = forward(
+        resp_len, where, (q_all, *s, before, *far_keys, *near_keys)
     )
     back = along_rows(back_grad, -1)
 
@@ -357,22 +374,23 @@
     )
     through = along_y(through, 1)
     minus = along_y(minus, -1)
-    plus = along_y(plus + through, 1)
-    got = along_z(stay + minus + plus)
-
     near = call(
-        near_backward_kernel, (where,), (q_all, p_all, grad2, dq, key_t, value1, out_all),
-        [((256, 256), f32)] * 4 + [((rows, 2 * WIDE), bf16)] * 4, "near_backward",
-        scratch=[pltpu.VMEM((OWN_ROWS, WIDE), bf16)] + SUMS, limit=LIMIT, cost=work(0.25),
-    )
-    stay, minus, through, plus = near[:4]
+        near_backward_kernel, (), (q_all, p_all, grad2, dq, key_t, value1, out_all),
+        [((256, 256), f32)] * 4 + [((4, rows, 2 * WIDE), bf16)], "near_backward",
+        scratch=SUMS, limit=LIMIT, cost=work(0.25), extra=(back,),
+    )
+    plus, stay = call(
+        add_kernel, (), (plus, through, stay, minus), [((256, 256), f32)] * 2, "far_sum", extra=(near[0],)
+    )
+    plus = along_y(plus, 1)
+    got = along_z(stay + plus)
+    stay, minus, through, plus, o = near
     through = along_y(through, -1)
     plus = along_y(plus, 1)
     minus = along_y(minus + through, -1)
 
-    o = [near[4]] + [along_x(near[4 + d], -d) for d in (1, 2, 3)]
     attn_out, q_grad = call(
-        unpack_rows_kernel, (where,), o, [((rows, HEADS * HEAD_DIM), bf16)] * 2, "unpack_rows"
+        unpack_rows_kernel, (), (exchange_x(o),), [((rows, HEADS * HEAD_DIM), bf16)] * 2, "unpack_rows"
     )
 
     f = call(

time: 144 us -> 208 us (1.44)
  Pallas kernels: 49 us -> 100 us
  local copies, waits for them, and re-layouts: 2.76 us -> 9.95 us
  starting transfers between devices: 55.1 us -> 62 us
    pallas_call x8 -> x10, Pallas kernels: 49 us -> 100 us  [call(): pl.pallas_call(body, in_specs=[smem] * len(scalars) + [pl.BlockSpec(memor...]
    all_to_all x0 -> x2, starting transfers between devices: none -> 8.01 us  [exchange_x(): lax.all_to_all(value, 'seq', 0, 0, axis_index_groups=X_GROUPS, tiled=True)]
    unnamed x10 -> x30, local copies, waits for them, and re-layouts: 2.76 us -> 9.95 us
    ppermute x12, starting transfers between devices: 26 us -> 32.6 us  [along_y(): lax.ppermute(value, 'seq', [(i, i // 16 * 16 + (i + 4 * step) % 16) for i...]
    ppermute x2, waiting for transfers between devices: 13.9 us -> 7.59 us  [along_z(): return lax.ppermute(value, 'seq', [(i, (i + 16) % 32) for i in range(32)])]
    ppermute x12 -> x6, starting transfers between devices: 16.3 us -> 10.6 us  [along_x(): lax.ppermute(value, 'seq', [(i, i // 4 * 4 + (i + step) % 4) for i in ran...]
    ppermute x2, starting transfers between devices: 9.99 us -> 6.47 us  [along_z(): return lax.ppermute(value, 'seq', [(i, (i + 16) % 32) for i in range(32)])]
    ppermute x12, waiting for transfers between devices: 14.1 us -> 17.3 us  [along_y(): lax.ppermute(value, 'seq', [(i, i // 16 * 16 + (i + 4 * step) % 16) for i...]
  transfers between devices with their start and end apart: 28 -> 24, of which waited for: 10 -> 14; matrix products, arithmetic and copies ran while one was open for 0% -> 0% of each run, Pallas kernels for 9% -> 12%
where the time goes in v3:
time: 208 us; the launch traced here: 207 us
  Pallas kernels  100 us (48%)
  starting transfers between devices  62 us (30%)
  waiting for transfers between devices  33.7 us (16%)
  local copies, waits for them, and re-layouts  9.95 us (5%)
    pallas_call x10, Pallas kernels, call(): pl.pallas_call(body, in_specs=[smem] * len(scalars) + [pl.BlockSpec(memor...  100 us
    ppermute x12, starting transfers between devices, along_y(): lax.ppermute(value, 'seq', [(i, i // 16 * 16 + (i + 4 * step) % 16) for i...  32.6 us
    ppermute x12, waiting for transfers between devices, along_y(): lax.ppermute(value, 'seq', [(i, i // 16 * 16 + (i + 4 * step) % 16) for i...  17.3 us
    ppermute x6, starting transfers between devices, along_x(): lax.ppermute(value, 'seq', [(i, i // 4 * 4 + (i + step) % 4) for i in ran...  10.6 us
    unnamed x30, local copies, waits for them, and re-layouts  9.95 us
    ppermute x6, waiting for transfers between devices, along_x(): lax.ppermute(value, 'seq', [(i, i // 4 * 4 + (i + step) % 4) for i in ran...  8.82 us
    all_to_all x2, starting transfers between devices, exchange_x(): lax.all_to_all(value, 'seq', 0, 0, axis_index_groups=X_GROUPS, tiled=True)  8.01 us
    ppermute x2, waiting for transfers between devices, along_z(): return lax.ppermute(value, 'seq', [(i, (i + 16) % 32) for i in range(32)])  7.59 us
  transfers between devices with their start and end apart: 24, of which 14 were waited for; matrix products, arithmetic and copies ran while one was open for 0% of the time, Pallas kernels for 12%

profile of v3, /device:TPU:32, one launch (start us, length us, event | category | flops | bytes accessed | tf_op | source)
XLA Modules:
  0.0 207.4 jit_solution(3734516697156835486)
XLA Ops:
  0.6 40.9 %pack_rows.1 = bf16[4,128,1280]{2,1,0:T(8,128)(2,1)} custom-call(bf16[128,2560]{1,0:T(8,128)(2,1)} %q.1, bf16[128,2560]{1,0:T(8,128)(2,1)} %g.1), custom_call_target="tpu_custom_call" | custom-call | tf_op jit(solution)/shard_map/pack_rows/pallas_call | solution.py:201
  41.5 4.3 %all-to-all-start = ((bf16[4,128,1280]{2,1,0:T(8,128)(2,1)}), bf16[4,128,1280]{2,1,0:T(8,128)(2,1)S(1)}, u32[]{:S(2)}, u32[]{:S(2)}) async-start(bf16[4,128,1280]{2,1,0:T(8,128)(2,1)} %pack_rows.1), calls=%async_computation | async-start | bytes 2621440 | tf_op jit(solution)/shard_map/all_to_all | solution.py:328
  46.5 13.8 %pack_small.1 = (bf16[192,256]{1,0:T(8,128)(2,1)}, bf16[192,256]{1,0:T(8,128)(2,1)}, bf16[192,256]{1,0:T(8,128)(2,1)}, bf16[192,256]{1,0:T(8,128)(2,1)}) custom-call(s32[2]{0:T(128)} %pad_add_fusion.where_ref, bf16[64,512]{1,0:T(8,128)(2,1)} %pk.1, bf16[64,512]{1,0:T(8,128)(2,1)} %pv.1, bf16[128,512]{1,0:T(8,128)(2,1)} %k.1, bf16[128,512]{1,0:T(8,128)(2,1)} %v.1), custom_call_target="tpu_custom_call" | custom-call | tf_op jit(solution)/shard_map/pack_small/pallas_call | solution.py:201
  60.3 2.1 %collective-permute-start = (bf16[192,256]{1,0:T(8,128)(2,1)}, bf16[192,256]{1,0:T(8,128)(2,1)S(1)}, u32[]{:S(2)}, u32[]{:S(2)}) collective-permute-start(bf16[192,256]{1,0:T(8,128)(2,1)} %get-tuple-element.43), channel_id=1, source_target_pairs={{0,1},{1,2},{2,3},{3,0},{4,5},{5,6},{6,7},{7,4},{8,9},{9,10},{10,1... | collective-permute-start | bytes 294920 | tf_op jit(solution)/shard_map/ppermute | solution.py:324
  62.4 2.7 %collective-permute-start.1 = (bf16[192,256]{1,0:T(8,128)(2,1)}, bf16[192,256]{1,0:T(8,128)(2,1)S(1)}, u32[]{:S(2)}, u32[]{:S(2)}) collective-permute-start(bf16[192,256]{1,0:T(8,128)(2,1)} %get-tuple-element.44), channel_id=1, source_target_pairs={{0,2},{1,3},{2,0},{3,1},{4,6},{5,7},{6,4},{7,5},{8,10},{9,11},{10,... | collective-permute-start | bytes 294920 | tf_op jit(solution)/shard_map/ppermute | solution.py:324
  67.4 2.0 collective-permute-done.1.s2
  72.1 6.4 %collective-permute-start.4 = (bf16[256,256]{1,0:T(8,128)(2,1)S(1)}, bf16[256,256]{1,0:T(8,128)(2,1)S(1)}, u32[]{:S(2)}, u32[]{:S(2)}) collective-permute-start(bf16[256,256]{1,0:T(8,128)(2,1)S(1)} %get-tuple-element.47.l0), channel_id=1, source_target_pairs={{0,16},{1,17},{2,18},{3,19},{4,20},{5,21},{6,22},{7,23},{8,24},{9,... | collective-permute-start | bytes 393224 | tf_op jit(solution)/shard_map/ppermute | solution.py:336
  78.5 3.0 %collective-permute-start.10 = (bf16[256,256]{1,0:T(8,128)(2,1)S(1)}, bf16[256,256]{1,0:T(8,128)(2,1)S(1)}, u32[]{:S(2)}, u32[]{:S(2)}) collective-permute-start(bf16[256,256]{1,0:T(8,128)(2,1)S(1)} %get-tuple-element.47.l0), channel_id=1, source_target_pairs={{0,12},{1,13},{2,14},{3,15},{4,0},{5,1},{6,2},{7,3},{8,4},{9,5},{1... | collective-permute-start | bytes 393224 | tf_op jit(solution)/shard_map/ppermute | solution.py:332
  82.1 2.9 %collective-permute-start.3 = (bf16[384,256]{1,0:T(8,128)(2,1)S(1)}, bf16[384,256]{1,0:T(8,128)(2,1)S(1)}, u32[]{:S(2)}, u32[]{:S(2)}) collective-permute-start(bf16[384,256]{1,0:T(8,128)(2,1)S(1)} %get-tuple-element.46), channel_id=1, source_target_pairs={{0,4},{1,5},{2,6},{3,7},{4,8},{5,9},{6,10},{7,11},{8,12},{9,13},{1... | collective-permute-start | bytes 589832 | tf_op jit(solution)/shard_map/ppermute | solution.py:341
  90.3 3.4 %collective-permute-done.8.l1 = bf16[256,256]{1,0:T(8,128)(2,1)S(1)} collective-permute-done((bf16[256,256]{1,0:T(8,128)(2,1)S(1)}, bf16[256,256]{1,0:T(8,128)(2,1)S(1)}, u32[]{:S(2)}, u32[]{:S(2)}) %collective-permute-start.8) | collective-permute-done | bytes 131104 | tf_op jit(solution)/shard_map/ppermute | solution.py:332
  94.3 3.9 %collective-permute-done.6.h2 = bf16[256,256]{1,0:T(8,128)(2,1)S(1)} collective-permute-done((bf16[256,256]{1,0:T(8,128)(2,1)S(1)}, bf16[256,256]{1,0:T(8,128)(2,1)S(1)}, u32[]{:S(2)}, u32[]{:S(2)}) %collective-permute-start.6) | collective-permute-done | bytes 131104 | tf_op jit(solution)/shard_map/ppermute | solution.py:332
  103.8 24.0 %forward.1 = (bf16[4,128,640]{2,1,0:T(8,128)(2,1)S(1)}, bf16[10,2048,256]{2,1,0:T(8,128)(2,1)S(1)}, bf16[10,256,256]{2,1,0:T(8,128)(2,1)S(1)}, f32[10,128,256]{2...) custom-call(s32[16]{0:T(128)S(1)} %copy-done.14, ...), custom_call_target="tpu_custom_call" | custom-call | flops 5033164800 | bytes 8000000 | tf_op jit(solution)/shard_map/forward/pallas_call | solution.py:201
  129.3 8.3 %far_backward.1 = (f32[10,128,256]{2,1,0:T(8,128)S(1)}, f32[256,256]{1,0:T(8,128)S(1)}, f32[256,256]{1,0:T(8,128)S(1)}, f32[256,256]{1,0:T(8,128)S(1)}, f32[256,256]{1,0:T(8,128)S(1)}) custom-call(bf16[4,128,1280]{2,1,0:T(8,128)(2,1)S(1)} %all-to-all-done.q_all, bf16[10,2048,256]{2,1,0:T(8,128)(2,1)S(1)} %get-tuple-element.48.p_all, ...), custom_call_target="tpu_custom_call" | custom-call | flops 2516582400 | bytes 8000000 | tf_op jit(solution)/shard_map/far_backward/pallas_call | solution.py:201
  139.1 9.4 %near_backward.1 = (f32[256,256]{1,0:T(8,128)S(1)}, f32[256,256]{1,0:T(8,128)S(1)}, f32[256,256]{1,0:T(8,128)S(1)}, f32[256,256]{1,0:T(8,128)S(1)}, bf16[4,128,1280]{2,1,0:T(8,128)(2,1)}) custom-call(bf16[4,128,1280]{2,1,0:T(8,128)(2,1)S(1)} %all-to-all-done.q_all, bf16[10,2048,256]{2,1,0:T(8,128)(2,1)S(1)} %get-tuple-element.48.p_all, ...), custom_call_target="tpu_custom_call" | custom-call | flops 2516582400 | bytes 8000000 | tf_op jit(solution)/shard_map/near_backward/pallas_call | solution.py:201
  149.1 3.7 %all-to-all-start.1 = ((bf16[4,128,1280]{2,1,0:T(8,128)(2,1)}), bf16[4,128,1280]{2,1,0:T(8,128)(2,1)S(1)}, u32[]{:S(2)}, u32[]{:S(2)}) async-start(bf16[4,128,1280]{2,1,0:T(8,128)(2,1)} %get-tuple-element.56), calls=%async_computation.1 | async-start | bytes 2621440 | tf_op jit(solution)/shard_map/all_to_all | solution.py:328
  152.9 2.6 %collective-permute-start.15 = (f32[256,256]{1,0:T(8,128)}, f32[256,256]{1,0:T(8,128)S(1)}, u32[]{:S(2)}, u32[]{:S(2)}) collective-permute-start(f32[256,256]{1,0:T(8,128)} %copy-done.7), channel_id=1, source_target_pairs={{0,4},{1,5},{2,6},{3,7},{4,8},{5,9},{6,10},{7,11},{8,12},{9,13},{1... | collective-permute-start | bytes 786440 | tf_op jit(solution)/shard_map/ppermute | solution.py:332
  155.5 12.2 %collective-permute-start.16 = (f32[256,256]{1,0:T(8,128)}, f32[256,256]{1,0:T(8,128)S(1)}, u32[]{:S(2)}, u32[]{:S(2)}) collective-permute-start(f32[256,256]{1,0:T(8,128)} %copy-done.6), channel_id=1, source_target_pairs={{0,12},{1,13},{2,14},{3,15},{4,0},{5,1},{6,2},{7,3},{8,4},{9,5},{1... | collective-permute-start | bytes 786440 | tf_op jit(solution)/shard_map/ppermute | solution.py:332
  169.7 3.7 %collective-permute-done.15.b = f32[256,256]{1,0:T(8,128)S(1)} collective-permute-done((f32[256,256]{1,0:T(8,128)}, f32[256,256]{1,0:T(8,128)S(1)}, u32[]{:S(2)}, u32[]{:S(2)}) %collective-permute-start.15) | collective-permute-done | bytes 262176 | tf_op jit(solution)/shard_map/ppermute | solution.py:332
  176.6 2.0 collective-permute-start.14
  178.7 3.4 %collective-permute-start.13 = (f32[256,256]{1,0:T(8,128)S(1)}, f32[256,256]{1,0:T(8,128)S(1)}, u32[]{:S(2)}, u32[]{:S(2)}) collective-permute-start(f32[256,256]{1,0:T(8,128)S(1)} %add.12), channel_id=1, source_target_pairs={{0,12},{1,13},{2,14},{3,15},{4,0},{5,1},{6,2},{7,3},{8,4},{9,5},{1... | collective-permute-start | bytes 786440 | tf_op jit(solution)/shard_map/ppermute | solution.py:332
  184.2 2.7 %collective-permute-done.14.n2 = f32[256,256]{1,0:T(8,128)S(1)} collective-permute-done((f32[256,256]{1,0:T(8,128)S(1)}, f32[256,256]{1,0:T(8,128)S(1)}, u32[]{:S(2)}, u32[]{:S(2)}) %collective-permute-start.14) | collective-permute-done | bytes 262176 | tf_op jit(solution)/shard_map/ppermute | solution.py:332
  186.9 7.6 %collective-permute-done.18.got_ref = f32[256,256]{1,0:T(8,128)S(1)} collective-permute-done((f32[256,256]{1,0:T(8,128)S(1)}, f32[256,256]{1,0:T(8,128)S(1)}, u32[]{:S(2)}, u32[]{:S(2)}) %collective-permute-start.18) | collective-permute-done | bytes 262176 | tf_op jit(solution)/shard_map/ppermute | solution.py:336
  195.1 2.6 %collective-permute-start.19 = (bf16[192,256]{1,0:T(8,128)(2,1)S(1)}, bf16[192,256]{1,0:T(8,128)(2,1)S(1)}, u32[]{:S(2)}, u32[]{:S(2)}) collective-permute-start(bf16[192,256]{1,0:T(8,128)(2,1)S(1)} %get-tuple-element.71), channel_id=1, source_target_pairs={{0,3},{1,0},{2,1},{3,2},{4,7},{5,4},{6,5},{7,6},{8,11},{9,8},{10,9... | collective-permute-start | bytes 294920 | tf_op jit(solution)/shard_map/ppermute | solution.py:324
  200.0 4.0 %collective-permute-done.20.f2 = bf16[192,256]{1,0:T(8,128)(2,1)S(1)} collective-permute-done((bf16[192,256]{1,0:T(8,128)(2,1)S(1)}, bf16[192,256]{1,0:T(8,128)(2,1)S(1)}, u32[]{:S(2)}, u32[]{:S(2)}) %collective-permute-start.20) | collective-permute-done | bytes 98336 | tf_op jit(solution)/shard_map/ppermute | solution.py:324
  (67 shorter events, 35.1 us)
Async XLA Ops:
  41.5 58.0 %all-to-all-start = ((bf16[4,128,1280]{2,1,0:T(8,128)(2,1)}), bf16[4,128,1280]{2,1,0:T(8,128)(2,1)S(1)}, u32[]{:S(2)}, u32[]{:S(2)}) async-start(bf16[4,128,1280]{2,1,0:T(8,128)(2,1)} %pack_rows.1), calls=%async_computation | async-start | bytes 2621440 | tf_op jit(solution)/shard_map/all_to_all | solution.py:328
  60.3 7.1 %collective-permute-start = (bf16[192,256]{1,0:T(8,128)(2,1)}, bf16[192,256]{1,0:T(8,128)(2,1)S(1)}, u32[]{:S(2)}, u32[]{:S(2)}) collective-permute-start(bf16[192,256]{1,0:T(8,128)(2,1)} %get-tuple-element.43), channel_id=1, source_target_pairs={{0,1},{1,2},{2,3},{3,0},{4,5},{5,6},{6,7},{7,4},{8,9},{9,10},{10,1... | collective-permute-start | bytes 294920 | tf_op jit(solution)/shard_map/ppermute | solution.py:324
  62.4 6.9 %collective-permute-start.1 = (bf16[192,256]{1,0:T(8,128)(2,1)}, bf16[192,256]{1,0:T(8,128)(2,1)S(1)}, u32[]{:S(2)}, u32[]{:S(2)}) collective-permute-start(bf16[192,256]{1,0:T(8,128)(2,1)} %get-tuple-element.44), channel_id=1, source_target_pairs={{0,2},{1,3},{2,0},{3,1},{4,6},{5,7},{6,4},{7,5},{8,10},{9,11},{10,... | collective-permute-start | bytes 294920 | tf_op jit(solution)/shard_map/ppermute | solution.py:324
  65.1 4.8 %collective-permute-start.2 = (bf16[192,256]{1,0:T(8,128)(2,1)}, bf16[192,256]{1,0:T(8,128)(2,1)S(1)}, u32[]{:S(2)}, u32[]{:S(2)}) collective-permute-start(bf16[192,256]{1,0:T(8,128)(2,1)} %get-tuple-element.45), channel_id=1, source_target_pairs={{0,3},{1,0},{2,1},{3,2},{4,7},{5,4},{6,5},{7,6},{8,11},{9,8},{10,9... | collective-permute-start | bytes 294920 | tf_op jit(solution)/shard_map/ppermute | solution.py:324
  72.1 14.9 %collective-permute-start.4 = (bf16[256,256]{1,0:T(8,128)(2,1)S(1)}, bf16[256,256]{1,0:T(8,128)(2,1)S(1)}, u32[]{:S(2)}, u32[]{:S(2)}) collective-permute-start(bf16[256,256]{1,0:T(8,128)(2,1)S(1)} %get-tuple-element.47.l0), channel_id=1, source_target_pairs={{0,16},{1,17},{2,18},{3,19},{4,20},{5,21},{6,22},{7,23},{8,24},{9,... | collective-permute-start | bytes 393224 | tf_op jit(solution)/shard_map/ppermute | solution.py:336
  78.5 9.8 %collective-permute-start.10 = (bf16[256,256]{1,0:T(8,128)(2,1)S(1)}, bf16[256,256]{1,0:T(8,128)(2,1)S(1)}, u32[]{:S(2)}, u32[]{:S(2)}) collective-permute-start(bf16[256,256]{1,0:T(8,128)(2,1)S(1)} %get-tuple-element.47.l0), channel_id=1, source_target_pairs={{0,12},{1,13},{2,14},{3,15},{4,0},{5,1},{6,2},{7,3},{8,4},{9,5},{1... | collective-permute-start | bytes 393224 | tf_op jit(solution)/shard_map/ppermute | solution.py:332
  81.5 7.9 %collective-permute-start.9 = (bf16[256,256]{1,0:T(8,128)(2,1)S(1)}, bf16[256,256]{1,0:T(8,128)(2,1)S(1)}, u32[]{:S(2)}, u32[]{:S(2)}) collective-permute-start(bf16[256,256]{1,0:T(8,128)(2,1)S(1)} %get-tuple-element.47.l0), channel_id=1, source_target_pairs={{0,8},{1,9},{2,10},{3,11},{4,12},{5,13},{6,14},{7,15},{8,0},{9,1},... | collective-permute-start | bytes 393224 | tf_op jit(solution)/shard_map/ppermute | solution.py:332
  82.1 11.5 %collective-permute-start.3 = (bf16[384,256]{1,0:T(8,128)(2,1)S(1)}, bf16[384,256]{1,0:T(8,128)(2,1)S(1)}, u32[]{:S(2)}, u32[]{:S(2)}) collective-permute-start(bf16[384,256]{1,0:T(8,128)(2,1)S(1)} %get-tuple-element.46), channel_id=1, source_target_pairs={{0,4},{1,5},{2,6},{3,7},{4,8},{5,9},{6,10},{7,11},{8,12},{9,13},{1... | collective-permute-start | bytes 589832 | tf_op jit(solution)/shard_map/ppermute | solution.py:341
  85.0 8.6 %collective-permute-start.8 = (bf16[256,256]{1,0:T(8,128)(2,1)S(1)}, bf16[256,256]{1,0:T(8,128)(2,1)S(1)}, u32[]{:S(2)}, u32[]{:S(2)}) collective-permute-start(bf16[256,256]{1,0:T(8,128)(2,1)S(1)} %get-tuple-element.47.l0), channel_id=1, source_target_pairs={{0,4},{1,5},{2,6},{3,7},{4,8},{5,9},{6,10},{7,11},{8,12},{9,13},{1... | collective-permute-start | bytes 393224 | tf_op jit(solution)/shard_map/ppermute | solution.py:332
  87.0 6.7 %collective-permute-start.7 = (bf16[256,256]{1,0:T(8,128)(2,1)S(1)}, bf16[256,256]{1,0:T(8,128)(2,1)S(1)}, u32[]{:S(2)}, u32[]{:S(2)}) collective-permute-start(bf16[256,256]{1,0:T(8,128)(2,1)S(1)} %collective-permute-done.4.h0), channel_id=1, source_target_pairs={{0,12},{1,13},{2,14},{3,15},{4,0},{5,1},{6,2},{7,3},{8,4},{9,5},{1... | collective-permute-start | bytes 393224 | tf_op jit(solution)/shard_map/ppermute | solution.py:332
  88.3 9.9 %collective-permute-start.6 = (bf16[256,256]{1,0:T(8,128)(2,1)S(1)}, bf16[256,256]{1,0:T(8,128)(2,1)S(1)}, u32[]{:S(2)}, u32[]{:S(2)}) collective-permute-start(bf16[256,256]{1,0:T(8,128)(2,1)S(1)} %collective-permute-done.4.h0), channel_id=1, source_target_pairs={{0,8},{1,9},{2,10},{3,11},{4,12},{5,13},{6,14},{7,15},{8,0},{9,1},... | collective-permute-start | bytes 393224 | tf_op jit(solution)/shard_map/ppermute | solution.py:332
  89.4 9.5 %collective-permute-start.5 = (bf16[256,256]{1,0:T(8,128)(2,1)S(1)}, bf16[256,256]{1,0:T(8,128)(2,1)S(1)}, u32[]{:S(2)}, u32[]{:S(2)}) collective-permute-start(bf16[256,256]{1,0:T(8,128)(2,1)S(1)} %collective-permute-done.4.h0), channel_id=1, source_target_pairs={{0,4},{1,5},{2,6},{3,7},{4,8},{5,9},{6,10},{7,11},{8,12},{9,13},{1... | collective-permute-start | bytes 393224 | tf_op jit(solution)/shard_map/ppermute | solution.py:332
  127.8 11.2 %collective-permute-start.11 = (f32[384,256]{1,0:T(8,128)S(1)}, f32[384,256]{1,0:T(8,128)S(1)}, u32[]{:S(2)}, u32[]{:S(2)}) collective-permute-start(f32[384,256]{1,0:T(8,128)S(1)} %get-tuple-element.55), channel_id=1, source_target_pairs={{4,0},{5,1},{6,2},{7,3},{8,4},{9,5},{10,6},{11,7},{12,8},{13,9},{1... | collective-permute-start | bytes 1179656 | tf_op jit(solution)/shard_map/ppermute | solution.py:341
  149.1 57.1 %all-to-all-start.1 = ((bf16[4,128,1280]{2,1,0:T(8,128)(2,1)}), bf16[4,128,1280]{2,1,0:T(8,128)(2,1)S(1)}, u32[]{:S(2)}, u32[]{:S(2)}) async-start(bf16[4,128,1280]{2,1,0:T(8,128)(2,1)} %get-tuple-element.56), calls=%async_computation.1 | async-start | bytes 2621440 | tf_op jit(solution)/shard_map/all_to_all | solution.py:328
  152.9 20.5 %collective-permute-start.15 = (f32[256,256]{1,0:T(8,128)}, f32[256,256]{1,0:T(8,128)S(1)}, u32[]{:S(2)}, u32[]{:S(2)}) collective-permute-start(f32[256,256]{1,0:T(8,128)} %copy-done.7), channel_id=1, source_target_pairs={{0,4},{1,5},{2,6},{3,7},{4,8},{5,9},{6,10},{7,11},{8,12},{9,13},{1... | collective-permute-start | bytes 786440 | tf_op jit(solution)/shard_map/ppermute | solution.py:332
  155.5 19.3 %collective-permute-start.16 = (f32[256,256]{1,0:T(8,128)}, f32[256,256]{1,0:T(8,128)S(1)}, u32[]{:S(2)}, u32[]{:S(2)}) collective-permute-start(f32[256,256]{1,0:T(8,128)} %copy-done.6), channel_id=1, source_target_pairs={{0,12},{1,13},{2,14},{3,15},{4,0},{5,1},{6,2},{7,3},{8,4},{9,5},{1... | collective-permute-start | bytes 786440 | tf_op jit(solution)/shard_map/ppermute | solution.py:332
  167.7 10.9 %collective-permute-start.12 = (f32[256,256]{1,0:T(8,128)}, f32[256,256]{1,0:T(8,128)S(1)}, u32[]{:S(2)}, u32[]{:S(2)}) collective-permute-start(f32[256,256]{1,0:T(8,128)} %copy-done.5), channel_id=1, source_target_pairs={{0,12},{1,13},{2,14},{3,15},{4,0},{5,1},{6,2},{7,3},{8,4},{9,5},{1... | collective-permute-start | bytes 786440 | tf_op jit(solution)/shard_map/ppermute | solution.py:332
  174.9 9.2 %collective-permute-start.17 = (f32[256,256]{1,0:T(8,128)S(1)}, f32[256,256]{1,0:T(8,128)S(1)}, u32[]{:S(2)}, u32[]{:S(2)}) collective-permute-start(f32[256,256]{1,0:T(8,128)S(1)} %get-tuple-element.68), channel_id=1, source_target_pairs={{0,4},{1,5},{2,6},{3,7},{4,8},{5,9},{6,10},{7,11},{8,12},{9,13},{1... | collective-permute-start | bytes 786440 | tf_op jit(solution)/shard_map/ppermute | solution.py:332
  176.6 10.2 %collective-permute-start.14 = (f32[256,256]{1,0:T(8,128)S(1)}, f32[256,256]{1,0:T(8,128)S(1)}, u32[]{:S(2)}, u32[]{:S(2)}) collective-permute-start(f32[256,256]{1,0:T(8,128)S(1)} %get-tuple-element.62), channel_id=1, source_target_pairs={{0,4},{1,5},{2,6},{3,7},{4,8},{5,9},{6,10},{7,11},{8,12},{9,13},{1... | collective-permute-start | bytes 786440 | tf_op jit(solution)/shard_map/ppermute | solution.py:332
  178.7 8.2 %collective-permute-start.13 = (f32[256,256]{1,0:T(8,128)S(1)}, f32[256,256]{1,0:T(8,128)S(1)}, u32[]{:S(2)}, u32[]{:S(2)}) collective-permute-start(f32[256,256]{1,0:T(8,128)S(1)} %add.12), channel_id=1, source_target_pairs={{0,12},{1,13},{2,14},{3,15},{4,0},{5,1},{6,2},{7,3},{8,4},{9,5},{1... | collective-permute-start | bytes 786440 | tf_op jit(solution)/shard_map/ppermute | solution.py:332
  184.1 10.4 %collective-permute-start.18 = (f32[256,256]{1,0:T(8,128)S(1)}, f32[256,256]{1,0:T(8,128)S(1)}, u32[]{:S(2)}, u32[]{:S(2)}) collective-permute-start(f32[256,256]{1,0:T(8,128)S(1)} %add.13), channel_id=1, source_target_pairs={{0,16},{1,17},{2,18},{3,19},{4,20},{5,21},{6,22},{7,23},{8,24},{9,... | collective-permute-start | bytes 786440 | tf_op jit(solution)/shard_map/ppermute | solution.py:336
  195.1 4.8 %collective-permute-start.19 = (bf16[192,256]{1,0:T(8,128)(2,1)S(1)}, bf16[192,256]{1,0:T(8,128)(2,1)S(1)}, u32[]{:S(2)}, u32[]{:S(2)}) collective-permute-start(bf16[192,256]{1,0:T(8,128)(2,1)S(1)} %get-tuple-element.71), channel_id=1, source_target_pairs={{0,3},{1,0},{2,1},{3,2},{4,7},{5,4},{6,5},{7,6},{8,11},{9,8},{10,9... | collective-permute-start | bytes 294920 | tf_op jit(solution)/shard_map/ppermute | solution.py:324
  197.7 6.2 %collective-permute-start.20 = (bf16[192,256]{1,0:T(8,128)(2,1)S(1)}, bf16[192,256]{1,0:T(8,128)(2,1)S(1)}, u32[]{:S(2)}, u32[]{:S(2)}) collective-permute-start(bf16[192,256]{1,0:T(8,128)(2,1)S(1)} %get-tuple-element.72), channel_id=1, source_target_pairs={{0,2},{1,3},{2,0},{3,1},{4,6},{5,7},{6,4},{7,5},{8,10},{9,11},{10,... | collective-permute-start | bytes 294920 | tf_op jit(solution)/shard_map/ppermute | solution.py:324
  198.6 6.3 %collective-permute-start.21 = (bf16[192,256]{1,0:T(8,128)(2,1)S(1)}, bf16[192,256]{1,0:T(8,128)(2,1)S(1)}, u32[]{:S(2)}, u32[]{:S(2)}) collective-permute-start(bf16[192,256]{1,0:T(8,128)(2,1)S(1)} %get-tuple-element.73), channel_id=1, source_target_pairs={{0,1},{1,2},{2,3},{3,0},{4,5},{5,6},{6,7},{7,4},{8,9},{9,10},{10,1... | collective-permute-start | bytes 294920 | tf_op jit(solution)/shard_map/ppermute | solution.py:324
  (15 other events, 87.6 us)

commit v4 on v3

--- a/solution.py
+++ b/solution.py
@@ -1,3 +1,5 @@
+import functools
+
 import jax
 import jax.numpy as jnp
 from jax import lax
@@ -16,13 +18,13 @@
 
 X_GROUPS = [[first + x for x in range(4)] for first in range(0, 32, 4)]
 ROWS = 256
-KEYS = 512
+KEYS = 1024
 SPAN = 640
 PROMPT_ROWS = 2048
 OWN_ROWS = 512
 WIDE = PER_GROUP * HEAD_DIM
 LIMIT = 16
-TILE = 1024
+SHARE = 512
 
 
 def nt(a, b):
@@ -39,7 +41,7 @@
 
 def forward_kernel(
     len_ref, where_ref, q_all, s0, s1, s2, s3, before_ref, h0, h1, h2, h3, l0, l1, l2, l3,
-    out_all, p_all, grad2_all, dq_all, key_t, value1, back_grad_ref, own_grad_ref,
+    out_all, p_all, grad2_all, grad_all, dq_all, key_t, value1, back_grad_ref, own_grad_ref,
     key2, value_t, wkey2, wvalue1, wkey_t, wvalue_t, s_first, s_second, key_sum, value_sum,
 ):
     base, x = where_ref[0], where_ref[1]
@@ -50,7 +52,7 @@
         keys[at, 128:] = source[:, :128]
         values[at, :128] = source[:, 128:]
 
-    for i, source in enumerate((h0, h1, h2, h3, l0, l1, l2, l3)):
+    for i, source in enumerate((h2, h1, h0, h3, l2, l1, l0, l3)):
         place(key2, value1, slice(i * 256, i * 256 + 256), source)
     place(wkey2, wvalue1, slice(0, BACK), before_ref)
     for d, source in enumerate((s0, s1, s2, s3)):
@@ -75,13 +77,13 @@
         for block, s_ref in enumerate((s_first, s_second)):
             mine = slice(block * 2, block * 2 + 2)
             q = q_all[mine, :, q_cols].reshape(ROWS, 128)
-            scaled = q.astype(jnp.float32) * (FACTOR * LOG2E)
+            scaled = q.astype(jnp.float32).T * (FACTOR * LOG2E)
             high = scaled.astype(jnp.bfloat16)
             low = (scaled - high.astype(jnp.float32)).astype(jnp.bfloat16)
-            q2 = jnp.concatenate([high, low], 1)
+            q2t = jnp.concatenate([high, low], 0)
             top = None
             for c in range(0, PROMPT_ROWS, KEYS):
-                s = nt(key2[c : c + KEYS, :], q2)
+                s = nn(key2[c : c + KEYS, :], q2t)
                 s_ref[c : c + KEYS, :] = s
                 tile_top = jnp.max(s, axis=0, keepdims=True)
                 top = tile_top if top is None else jnp.maximum(top, tile_top)
@@ -96,7 +98,7 @@
             key_pos = own - BACK + lax.broadcasted_iota(jnp.int32, (SPAN, ROWS), 0)
             seen = (key_pos <= row_pos) & (key_pos >= seg_start)
             span = slice(block * ROWS, block * ROWS + SPAN)
-            s = jnp.where(seen, nt(wkey2[span, :], q2), NEGATIVE)
+            s = jnp.where(seen, nn(wkey2[span, :], q2t), NEGATIVE)
             s_ref[PROMPT_ROWS:, :] = s
             top = jnp.maximum(top, jnp.max(s, axis=0, keepdims=True))
             state.append((block, s_ref, mine, span, q, top))
@@ -112,22 +114,24 @@
             total = total + nn(wvalue_t[:, span], p)
 
             inverse = 1.0 / total[128:129, :]
-            out = (total[:128, :] * inverse).T.astype(jnp.bfloat16)
-            out_all[mine, :, q_cols] = out.reshape(2, 128, 128)
-            column = jnp.broadcast_to(inverse, (8, ROWS)).T[:, :1]
-            grad = q_all[mine, :, g_cols].reshape(ROWS, 128)
-            grad_n = (grad.astype(jnp.float32) * column).astype(jnp.bfloat16)
-            row_dot = -jnp.sum(grad_n.astype(jnp.float32) * out.astype(jnp.float32), axis=1, keepdims=True)
+            out = (total[:128, :] * inverse).astype(jnp.bfloat16).astype(jnp.float32)
+            out_all[mine, :, q_cols] = out.T.astype(jnp.bfloat16).reshape(2, 128, 128)
+            grad_t = q_all[mine, :, g_cols].reshape(ROWS, 128).astype(jnp.float32).T
+            grad_n = (grad_t * inverse).astype(jnp.bfloat16)
+            grad_wide = grad_n.astype(jnp.float32)
+            row_dot = -jnp.sum(grad_wide * out, axis=0, keepdims=True)
             dot_high = row_dot.astype(jnp.bfloat16).astype(jnp.float32)
-            lane = lax.broadcasted_iota(jnp.int32, (ROWS, 128), 1)
-            extra = jnp.where(lane == 0, dot_high, jnp.where(lane == 1, row_dot - dot_high, 0.0))
-            grad2 = jnp.concatenate([grad_n, extra.astype(jnp.bfloat16)], 1)
+            line = lax.broadcasted_iota(jnp.int32, (128, ROWS), 0)
+            extra = jnp.where(line == 0, dot_high, jnp.where(line == 1, row_dot - dot_high, 0.0))
+            grad2 = jnp.concatenate([grad_n, extra.astype(jnp.bfloat16)], 0)
+            grad_rows = grad_wide.T.astype(jnp.bfloat16)
+            grad_all[item] = grad_rows
             grad2_all[item] = grad2
 
-            ds = (p.astype(jnp.float32) * nt(wvalue1[span, :], grad2)).astype(jnp.bfloat16)
+            ds = (p.astype(jnp.float32) * nn(wvalue1[span, :], grad2)).astype(jnp.bfloat16)
             dq_all[item] = nn(wkey_t[:, span], ds)
             key_sum[span, :] += nn(ds, q)
-            value_sum[span, :] += nn(p, grad_n)
+            value_sum[span, :] += nn(p, grad_rows)
         return carry
 
     lax.fori_loop(0, PER_GROUP, one_head, 0)
@@ -137,30 +141,25 @@
         target[:, 128:] = value_sum[at, :]
 
 
-def backward(first, q_all, p_all, grad2_all, dq_all, key_t, value1, key_sum, value_sum, finish):
+def backward(first, q_all, p_all, grad2_all, grad_all, dq_all, key_t, value1, key_sum, value_sum, finish):
+    keys = slice(first, first + SHARE)
     key_sum[...] = jnp.zeros_like(key_sum)
     value_sum[...] = jnp.zeros_like(value_sum)
 
     def one_head(head, carry):
         q_cols = pl.ds(pl.multiple_of(head * 128, 128), 128)
-        dq = [dq_all[block * PER_GROUP + head] for block in range(2)]
-        for c in range(0, PROMPT_ROWS // 2, TILE):
-            at, keys = slice(c, c + TILE), slice(first + c, first + c + TILE)
-            key_term, value_term = None, None
-            for block in range(2):
-                item = block * PER_GROUP + head
-                grad2 = grad2_all[item]
-                p = p_all[item, keys, :]
-                ds = (p.astype(jnp.float32) * nt(value1[keys, :], grad2)).astype(jnp.bfloat16)
-                dq[block] = dq[block] + nn(key_t[:, keys], ds)
-                k = nn(ds, q_all[block * 2 : block * 2 + 2, :, q_cols].reshape(ROWS, 128))
-                v = nn(p, grad2[:, :128])
-                key_term = k if key_term is None else key_term + k
-                value_term = v if value_term is None else value_term + v
-            key_sum[at, :] += key_term
-            value_sum[at, :] += value_term
+        key_term, value_term = None, None
         for block in range(2):
-            finish(head, block, dq[block])
+            item = block * PER_GROUP + head
+            p = p_all[item, keys, :]
+            ds = (p.astype(jnp.float32) * nn(value1[keys, :], grad2_all[item])).astype(jnp.bfloat16)
+            finish(head, block, dq_all[item] + nn(key_t[:, keys], ds))
+            k = nn(ds, q_all[block * 2 : block * 2 + 2, :, q_cols].reshape(ROWS, 128))
+            v = nn(p, grad_all[item])
+            key_term = k if key_term is None else key_term + k
+            value_term = v if value_term is None else value_term + v
+        key_sum[...] += key_term
+        value_sum[...] += value_term
         return carry
 
     lax.fori_loop(0, PER_GROUP, one_head, 0)
@@ -173,26 +172,27 @@
         target[:, 128:] = value_sum[at, :]
 
 
-def far_backward_kernel(
-    q_all, p_all, grad2_all, dq_in, key_t, value1, dq_out, g0, g1, g2, g3, key_sum, value_sum
+def middle_backward_kernel(
+    first, q_all, p_all, grad2_all, grad_all, dq_in, key_t, value1, after, dq_out, a_ref, b_ref, key_sum, value_sum
 ):
     def finish(head, block, dq):
         dq_out[block * PER_GROUP + head] = dq
 
-    backward(0, q_all, p_all, grad2_all, dq_in, key_t, value1, key_sum, value_sum, finish)
-    write_sums(key_sum, value_sum, (g0, g1, g2, g3))
-
-
-def near_backward_kernel(
-    q_all, p_all, grad2_all, dq_in, key_t, value1, out_all, back, g0, g1, g2, g3, o_ref, key_sum, value_sum
+    backward(first, q_all, p_all, grad2_all, grad_all, dq_in, key_t, value1, key_sum, value_sum, finish)
+    write_sums(key_sum, value_sum, (a_ref, b_ref))
+
+
+def last_backward_kernel(
+    first, q_all, p_all, grad2_all, grad_all, dq_in, key_t, value1, out_all, after, a_ref, b_ref, o_ref,
+    key_sum, value_sum,
 ):
     def finish(head, block, dq):
         cols = pl.ds(pl.multiple_of(WIDE + head * 128, 128), 128)
         dq = (dq * FACTOR).T.astype(jnp.bfloat16)
         o_ref[block * 2 : block * 2 + 2, :, cols] = dq.reshape(2, 128, 128)
 
-    backward(PROMPT_ROWS // 2, q_all, p_all, grad2_all, dq_in, key_t, value1, key_sum, value_sum, finish)
-    write_sums(key_sum, value_sum, (g0, g1, g2, g3))
+    backward(first, q_all, p_all, grad2_all, grad_all, dq_in, key_t, value1, key_sum, value_sum, finish)
+    write_sums(key_sum, value_sum, (a_ref, b_ref))
     o_ref[:, :, :WIDE] = out_all[...]
 
 
@@ -202,7 +202,7 @@
         body,
         in_specs=[smem] * len(scalars) + [pl.BlockSpec(memory_space=space)] * len(operands)
         + [pl.BlockSpec(memory_space=pl.ANY)] * len(extra),
-        out_specs=[pl.BlockSpec(memory_space=space)] * len(outs),
+        out_specs=[pl.BlockSpec(memory_space=pltpu.VMEM)] * len(outs),
         out_shape=[jax.ShapeDtypeStruct(shape, dtype) for shape, dtype in outs],
         scratch_shapes=list(scratch),
         compiler_params=pltpu.CompilerParams(vmem_limit_bytes=limit * 1024 * 1024),
@@ -223,7 +223,7 @@
         forward_kernel, (resp_len, where), operands,
         [
             ((4, 128, WIDE), bf16), ((items, PROMPT_ROWS, ROWS), bf16),
-            ((items, 256, ROWS), bf16), ((items, 128, ROWS), f32), ((128, PROMPT_ROWS), bf16),
+            ((items, 256, ROWS), bf16), ((items, ROWS, 128), bf16), ((items, 128, ROWS), f32), ((128, PROMPT_ROWS), bf16),
             ((PROMPT_ROWS, 256), bf16), ((BACK, 256), f32), ((OWN_ROWS, 256), f32),
         ],
         "forward",
@@ -243,14 +243,22 @@
     )
 
 
-SUMS = [pltpu.VMEM((PROMPT_ROWS // 2, 128), jnp.float32)] * 2
+SUMS = [pltpu.VMEM((SHARE, 128), jnp.float32)] * 2
 
 
 def head_columns(x, distance, width):
     return pl.ds(pl.multiple_of(lax.rem(x + distance, 4) * width, 128), width)
 
 
-def run_copies(pairs, sems):
+def pack_kernel(where_ref, pk, pv, k, v, q, g, s0, s1, s2, s3, rows, sems):
+    pairs = []
+    for d, target in enumerate((s0, s1, s2, s3)):
+        cols = head_columns(where_ref[1], d, 128)
+        for source, lines, lanes in ((pk, (0, 64), 0), (pv, (0, 64), 128), (k, (64, 192), 0), (v, (64, 192), 128)):
+            pairs.append((source.at[:, cols], target.at[slice(*lines), lanes : lanes + 128]))
+    for h in range(KV_HEADS):
+        for source, first in ((q, 0), (g, WIDE)):
+            pairs.append((source.at[:, h * WIDE : h * WIDE + WIDE], rows.at[h, :, first : first + WIDE]))
     copies = [pltpu.make_async_copy(source, target, sems.at[i]) for i, (source, target) in enumerate(pairs)]
     for copy in copies:
         copy.start()
@@ -258,23 +266,6 @@
         copy.wait()
 
 
-def pack_small_kernel(where_ref, pk, pv, k, v, s0, s1, s2, s3, sems):
-    pairs = []
-    for d, target in enumerate((s0, s1, s2, s3)):
-        cols = head_columns(where_ref[1], d, 128)
-        for source, lines, lanes in ((pk, (0, 64), 0), (pv, (0, 64), 128), (k, (64, 192), 0), (v, (64, 192), 128)):
-            pairs.append((source.at[:, cols], target.at[slice(*lines), lanes : lanes + 128]))
-    run_copies(pairs, sems)
-
-
-def pack_rows_kernel(q, g, target, sems):
-    pairs = []
-    for h in range(KV_HEADS):
-        for source, first in ((q, 0), (g, WIDE)):
-            pairs.append((source.at[:, h * WIDE : h * WIDE + WIDE], target.at[h, :, first : first + WIDE]))
-    run_copies(pairs, sems)
-
-
 def collect_kernel(where_ref, s0, s1, s2, s3, mine_ref, ahead_ref):
     x = where_ref[1]
     for d, source in enumerate((s0, s1, s2, s3)):
@@ -286,11 +277,11 @@
             ahead_ref[pl.ds(pl.multiple_of((block - 1) * 128, 128), 128), :] = source[64:, :]
 
 
-def final_sum_kernel(where_ref, n0, n1, n2, got_ref, own_ref, back_ref, f0, f1, f2, f3):
+def final_sum_kernel(where_ref, n0, n1, n2, n3, got_ref, own_ref, back_ref, f0, f1, f2, f3):
     x = where_ref[1]
     for d, target in enumerate((f0, f1, f2, f3)):
         at = slice(d * 64, d * 64 + 64)
-        total = (n0[at, :] + n1[at, :]) + (n2[at, :] + got_ref[at, :])
+        total = (n0[at, :] + n1[at, :]) + (n2[at, :] + n3[at, :]) + got_ref[at, :]
         target[:64, :] = total.astype(jnp.bfloat16)
         block = lax.rem(x + 4 - d, 4)
         behind = pl.ds(pl.multiple_of(jnp.maximum(block - 1, 0) * 128, 128), 128)
@@ -298,7 +289,7 @@
         target[64:, :] = (own_ref[block_at(x, d), :] + extra).astype(jnp.bfloat16)
 
 
-def add_kernel(a, b, c, d, after, ab_ref, cd_ref):
+def add_kernel(a, b, c, d, ab_ref, cd_ref):
     ab_ref[...] = a[...] + b[...]
     cd_ref[...] = c[...] + d[...]
 
@@ -346,13 +337,10 @@
     where = jnp.stack([me // 4 * OWN_ROWS, me % 4])
     rows, bf16, f32 = resp_q.shape[0], jnp.bfloat16, jnp.float32
 
-    s = call(
-        pack_small_kernel, (where,), (prompt_keys, prompt_values, resp_k, resp_v), [((192, 256), bf16)] * 4,
-        "pack_small", scratch=[pltpu.SemaphoreType.DMA((16,))], space=pl.ANY, limit=60,
-    )
-    (q_all,) = call(
-        pack_rows_kernel, (), (resp_q, out_grad), [((4, rows, 2 * WIDE), bf16)],
-        "pack_rows", scratch=[pltpu.SemaphoreType.DMA((8,))], space=pl.ANY, limit=60,
+    *s, q_all = call(
+        pack_kernel, (where,), (prompt_keys, prompt_values, resp_k, resp_v, resp_q, out_grad),
+        [((192, 256), bf16)] * 4 + [((4, rows, 2 * WIDE), bf16)], "pack",
+        scratch=[pltpu.SemaphoreType.DMA((24,))], space=pl.ANY, limit=60,
     )
     s = [s[0]] + [along_x(s[d], d) for d in (1, 2, 3)]
     q_all = exchange_x(q_all)
@@ -362,39 +350,45 @@
     before = along_rows(ahead, 1)
     far_keys = [far] + [along_y(far, d) for d in (1, 2, 3)]
 
-    out_all, p_all, grad2, dq, key_t, value1, back_grad, own_grad = forward(
+    out_all, p_all, grad2, grad, dq, key_t, value1, back_grad, own_grad = forward(
         resp_len, where, (q_all, *s, before, *far_keys, *near_keys)
     )
     back = along_rows(back_grad, -1)
 
-    dq, stay, minus, through, plus = call(
-        far_backward_kernel, (), (q_all, p_all, grad2, dq, key_t, value1),
-        [((OWN_ROWS // ROWS * PER_GROUP, 128, ROWS), f32)]
-        + [((256, 256), f32)] * 4, "far_backward", scratch=SUMS, limit=LIMIT, cost=work(0.25),
-    )
+    def middle(share, dq, after):
+        return call(
+            functools.partial(middle_backward_kernel, share * SHARE), (),
+            (q_all, p_all, grad2, grad, dq, key_t, value1),
+            [(dq.shape, f32)] + [((256, 256), f32)] * 2, "backward%d" % share,
+            scratch=SUMS, limit=LIMIT, cost=work(0.12), extra=(after,),
+        )
+
+    dq, through, minus = middle(0, dq, grad)
     through = along_y(through, 1)
     minus = along_y(minus, -1)
-    near = call(
-        near_backward_kernel, (), (q_all, p_all, grad2, dq, key_t, value1, out_all),
-        [((256, 256), f32)] * 4 + [((4, rows, 2 * WIDE), bf16)], "near_backward",
-        scratch=SUMS, limit=LIMIT, cost=work(0.25), extra=(back,),
-    )
-    plus, stay = call(
-        add_kernel, (), (plus, through, stay, minus), [((256, 256), f32)] * 2, "far_sum", extra=(near[0],)
-    )
+    dq, stay, plus = middle(1, dq, back)
+    plus, stay = call(add_kernel, (), (plus, through, stay, minus), [((256, 256), f32)] * 2, "far_sum")
+    after = plus
     plus = along_y(plus, 1)
-    got = along_z(stay + plus)
-    stay, minus, through, plus, o = near
-    through = along_y(through, -1)
-    plus = along_y(plus, 1)
-    minus = along_y(minus + through, -1)
+
+    dq, two, one = middle(2, dq, after)
+    got = stay + plus
+    after = got
+    got = along_z(got)
+    stay, three, o = call(
+        functools.partial(last_backward_kernel, 3 * SHARE), (), (q_all, p_all, grad2, grad, dq, key_t, value1, out_all),
+        [((256, 256), f32)] * 2 + [((4, rows, 2 * WIDE), bf16)], "backward3",
+        scratch=SUMS, limit=LIMIT, cost=work(0.12), extra=(after,),
+    )
+    minus, through, plus = along_y(one, -1), along_y(two, -2), along_y(three, 1)
 
     attn_out, q_grad = call(
         unpack_rows_kernel, (), (exchange_x(o),), [((rows, HEADS * HEAD_DIM), bf16)] * 2, "unpack_rows"
     )
 
     f = call(
-        final_sum_kernel, (where,), (stay, minus, plus, got, own_grad, back), [((192, 256), bf16)] * 4, "final_sum"
+        final_sum_kernel, (where,), (stay, minus, through, plus, got, own_grad, back),
+        [((192, 256), bf16)] * 4, "final_sum",
     )
     f = [f[0]] + [along_x(f[d], -d) for d in (1, 2, 3)]
     resp_k_grad, resp_v_grad, prompt_k_grad, prompt_v_grad = call(

time: 208 us -> 154 us (0.74)
  Pallas kernels: 100 us -> 50.3 us
  waiting for transfers between devices: 33.7 us -> 55.5 us
  starting transfers between devices: 62 us -> 45.9 us
  local copies, waits for them, and re-layouts: 9.95 us -> 0.04 us
    pallas_call x10 -> x11, Pallas kernels: 100 us -> 50.3 us  [call(): pl.pallas_call(body, in_specs=[smem] * len(scalars) + [pl.BlockSpec(memor...]
    ppermute x12, starting transfers between devices: 32.6 us -> 16.8 us  [along_y(): lax.ppermute(value, 'seq', [(i, i // 16 * 16 + (i + 4 * step) % 16) for i...]
    ppermute x12, waiting for transfers between devices: 17.3 us -> 32.1 us  [along_y(): lax.ppermute(value, 'seq', [(i, i // 16 * 16 + (i + 4 * step) % 16) for i...]
    ppermute x6, waiting for transfers between devices: 8.82 us -> 21.7 us  [along_x(): lax.ppermute(value, 'seq', [(i, i // 4 * 4 + (i + step) % 4) for i in ran...]
    unnamed x30 -> x12, local copies, waits for them, and re-layouts: 9.95 us -> 0.04 us
    ppermute x2, waiting for transfers between devices: 7.59 us -> 0.01 us  [along_z(): return lax.ppermute(value, 'seq', [(i, (i + 16) % 32) for i in range(32)])]
where the time goes in v4:
time: 154 us; the launch traced here: 153 us
  waiting for transfers between devices  55.5 us (36%)
  Pallas kernels  50.3 us (33%)
  starting transfers between devices  45.9 us (30%)
    pallas_call x11, Pallas kernels, call(): pl.pallas_call(body, in_specs=[smem] * len(scalars) + [pl.BlockSpec(memor...  50.3 us
    ppermute x12, waiting for transfers between devices, along_y(): lax.ppermute(value, 'seq', [(i, i // 16 * 16 + (i + 4 * step) % 16) for i...  32.1 us
    ppermute x6, waiting for transfers between devices, along_x(): lax.ppermute(value, 'seq', [(i, i // 4 * 4 + (i + step) % 4) for i in ran...  21.7 us
    ppermute x12, starting transfers between devices, along_y(): lax.ppermute(value, 'seq', [(i, i // 16 * 16 + (i + 4 * step) % 16) for i...  16.8 us
    ppermute x6, starting transfers between devices, along_x(): lax.ppermute(value, 'seq', [(i, i // 4 * 4 + (i + step) % 4) for i in ran...  10.8 us
    all_to_all x2, starting transfers between devices, exchange_x(): lax.all_to_all(value, 'seq', 0, 0, axis_index_groups=X_GROUPS, tiled=True)  7.97 us
    ppermute x2, starting transfers between devices, along_z(): return lax.ppermute(value, 'seq', [(i, (i + 16) % 32) for i in range(32)])  6.38 us
    ppermute x2, starting transfers between devices, along_rows(): return lax.ppermute(value, 'seq', [(i, j) for i, j in pairs if 0 <= j < 32])  3.96 us
  transfers between devices with their start and end apart: 24, of which 14 were waited for; matrix products, arithmetic and copies ran while one was open for 0% of the time, Pallas kernels for 12%

profile of v4, /device:TPU:32, one launch (start us, length us, event | category | flops | bytes accessed | tf_op | source)
XLA Modules:
  0.0 153.2 jit_solution(1273994181637028122)
XLA Ops:
  1.3 3.7 %pack.1 = (bf16[192,256]{1,0:T(8,128)(2,1)}, bf16[192,256]{1,0:T(8,128)(2,1)}, bf16[192,256]{1,0:T(8,128)(2,1)}, bf16[192,256]{1,0:T(8,128)(2,1)}, bf16[4,128,1280]{2,1,0:T(8,128)(2,1)}) custom-call(s32[2]{0:T(128)} %pad_add_fusion.where_ref, bf16[64,512]{1,0:T(8,128)(2,1)} %pk.1, bf16[64,512]{1,0:T(8,128)(2,1)} %pv.1, bf16[128,512]{1,0:T(8,128)(2,1)} %k.1, ...), custom_call_target="tpu_custom_call" | custom-call | tf_op jit(solution)/shard_map/pack/pallas_call | solution.py:201
  5.0 4.4 %all-to-all-start = ((bf16[4,128,1280]{2,1,0:T(8,128)(2,1)}), bf16[4,128,1280]{2,1,0:T(8,128)(2,1)S(1)}, u32[]{:S(2)}, u32[]{:S(2)}) async-start(bf16[4,128,1280]{2,1,0:T(8,128)(2,1)} %get-tuple-element.46), calls=%async_computation | async-start | bytes 2621440 | tf_op jit(solution)/shard_map/all_to_all | solution.py:319
  11.5 2.7 %collective-permute-start.1 = (bf16[192,256]{1,0:T(8,128)(2,1)S(1)}, bf16[192,256]{1,0:T(8,128)(2,1)S(1)}, u32[]{:S(2)}, u32[]{:S(2)}) collective-permute-start(bf16[192,256]{1,0:T(8,128)(2,1)S(1)} %copy-done.4), channel_id=1, source_target_pairs={{0,2},{1,3},{2,0},{3,1},{4,6},{5,7},{6,4},{7,5},{8,10},{9,11},{10,... | collective-permute-start | bytes 294920 | tf_op jit(solution)/shard_map/ppermute | solution.py:315
  15.6 14.6 %collective-permute-done.s1 = bf16[192,256]{1,0:T(8,128)(2,1)S(1)} collective-permute-done((bf16[192,256]{1,0:T(8,128)(2,1)S(1)}, bf16[192,256]{1,0:T(8,128)(2,1)S(1)}, u32[]{:S(2)}, u32[]{:S(2)}) %collective-permute-start) | collective-permute-done | bytes 98336 | tf_op jit(solution)/shard_map/ppermute | solution.py:315
  32.2 6.4 %collective-permute-start.4 = (bf16[256,256]{1,0:T(8,128)(2,1)S(1)}, bf16[256,256]{1,0:T(8,128)(2,1)S(1)}, u32[]{:S(2)}, u32[]{:S(2)}) collective-permute-start(bf16[256,256]{1,0:T(8,128)(2,1)S(1)} %get-tuple-element.52.l0), channel_id=1, source_target_pairs={{0,16},{1,17},{2,18},{3,19},{4,20},{5,21},{6,22},{7,23},{8,24},{9,... | collective-permute-start | bytes 393224 | tf_op jit(solution)/shard_map/ppermute | solution.py:327
  38.6 3.0 %collective-permute-start.10 = (bf16[256,256]{1,0:T(8,128)(2,1)S(1)}, bf16[256,256]{1,0:T(8,128)(2,1)S(1)}, u32[]{:S(2)}, u32[]{:S(2)}) collective-permute-start(bf16[256,256]{1,0:T(8,128)(2,1)S(1)} %get-tuple-element.52.l0), channel_id=1, source_target_pairs={{0,12},{1,13},{2,14},{3,15},{4,0},{5,1},{6,2},{7,3},{8,4},{9,5},{1... | collective-permute-start | bytes 393224 | tf_op jit(solution)/shard_map/ppermute | solution.py:323
  41.6 2.5 %collective-permute-start.3 = (bf16[384,256]{1,0:T(8,128)(2,1)S(1)}, bf16[384,256]{1,0:T(8,128)(2,1)S(1)}, u32[]{:S(2)}, u32[]{:S(2)}) collective-permute-start(bf16[384,256]{1,0:T(8,128)(2,1)S(1)} %get-tuple-element.51), channel_id=1, source_target_pairs={{0,4},{1,5},{2,6},{3,7},{4,8},{5,9},{6,10},{7,11},{8,12},{9,13},{1... | collective-permute-start | bytes 589832 | tf_op jit(solution)/shard_map/ppermute | solution.py:332
  44.1 4.2 %collective-permute-start.9 = (bf16[256,256]{1,0:T(8,128)(2,1)S(1)}, bf16[256,256]{1,0:T(8,128)(2,1)S(1)}, u32[]{:S(2)}, u32[]{:S(2)}) collective-permute-start(bf16[256,256]{1,0:T(8,128)(2,1)S(1)} %get-tuple-element.52.l0), channel_id=1, source_target_pairs={{0,8},{1,9},{2,10},{3,11},{4,12},{5,13},{6,14},{7,15},{8,0},{9,1},... | collective-permute-start | bytes 393224 | tf_op jit(solution)/shard_map/ppermute | solution.py:323
  51.7 5.1 %collective-permute-done.9.l2 = bf16[256,256]{1,0:T(8,128)(2,1)S(1)} collective-permute-done((bf16[256,256]{1,0:T(8,128)(2,1)S(1)}, bf16[256,256]{1,0:T(8,128)(2,1)S(1)}, u32[]{:S(2)}, u32[]{:S(2)}) %collective-permute-start.9) | collective-permute-done | bytes 131104 | tf_op jit(solution)/shard_map/ppermute | solution.py:323
  59.5 21.3 %forward.1 = (bf16[4,128,640]{2,1,0:T(8,128)(2,1)S(1)}, bf16[10,2048,256]{2,1,0:T(8,128)(2,1)S(1)}, bf16[10,256,256]{2,1,0:T(8,128)(2,1)S(1)}, bf16[10,256,128]{...) custom-call(s32[16]{0:T(128)S(1)} %copy-done.2, ...), custom_call_target="tpu_custom_call" | custom-call | flops 5033164800 | bytes 8000000 | tf_op jit(solution)/shard_map/forward/pallas_call | solution.py:201
  82.3 5.1 %backward0.1 = (f32[10,128,256]{2,1,0:T(8,128)S(1)}, f32[256,256]{1,0:T(8,128)S(1)}, f32[256,256]{1,0:T(8,128)S(1)}) custom-call(bf16[4,128,1280]{2,1,0:T(8,128)(2,1)S(1)} %all-to-all-done.q_all, bf16[10,2048,256]{2,1,0:T(8,128)(2,1)S(1)} %get-tuple-element.53.p_all, bf16[10,256,256]{2,1,0:T(8,128)(2,1)S(1)} %get-tuple-element.54.grad2_all, ...), custom_call_target="tpu_custom_call" | custom-call | flops 1207959552 | bytes 8000000 | tf_op jit(solution)/shard_map/backward0/pallas_call | solution.py:201
  87.4 2.7 %collective-permute-start.12 = (f32[256,256]{1,0:T(8,128)S(1)}, f32[256,256]{1,0:T(8,128)S(1)}, u32[]{:S(2)}, u32[]{:S(2)}) collective-permute-start(f32[256,256]{1,0:T(8,128)S(1)} %get-tuple-element.63), channel_id=1, source_target_pairs={{0,4},{1,5},{2,6},{3,7},{4,8},{5,9},{6,10},{7,11},{8,12},{9,13},{1... | collective-permute-start | bytes 786440 | tf_op jit(solution)/shard_map/ppermute | solution.py:323
  92.3 5.1 %backward1.1 = (f32[10,128,256]{2,1,0:T(8,128)S(1)}, f32[256,256]{1,0:T(8,128)S(1)}, f32[256,256]{1,0:T(8,128)S(1)}) custom-call(bf16[4,128,1280]{2,1,0:T(8,128)(2,1)S(1)} %all-to-all-done.q_all, bf16[10,2048,256]{2,1,0:T(8,128)(2,1)S(1)} %get-tuple-element.53.p_all, bf16[10,256,256]{2,1,0:T(8,128)(2,1)S(1)} %get-tuple-element.54.grad2_all, ...), custom_call_target="tpu_custom_call" | custom-call | flops 1207959552 | bytes 8000000 | tf_op jit(solution)/shard_map/backward1/pallas_call | solution.py:201
  97.4 4.4 %collective-permute-done.13.d = f32[256,256]{1,0:T(8,128)S(1)} collective-permute-done((f32[256,256]{1,0:T(8,128)S(1)}, f32[256,256]{1,0:T(8,128)S(1)}, u32[]{:S(2)}, u32[]{:S(2)}) %collective-permute-start.13) | collective-permute-done | bytes 262176 | tf_op jit(solution)/shard_map/ppermute | solution.py:323
  102.0 5.1 %backward2.1 = (f32[10,128,256]{2,1,0:T(8,128)S(1)}, f32[256,256]{1,0:T(8,128)S(1)}, f32[256,256]{1,0:T(8,128)S(1)}) custom-call(bf16[4,128,1280]{2,1,0:T(8,128)(2,1)S(1)} %all-to-all-done.q_all, bf16[10,2048,256]{2,1,0:T(8,128)(2,1)S(1)} %get-tuple-element.53.p_all, bf16[10,256,256]{2,1,0:T(8,128)(2,1)S(1)} %get-tuple-element.54.grad2_all, ...), custom_call_target="tpu_custom_call" | custom-call | flops 1207959552 | bytes 8000000 | tf_op jit(solution)/shard_map/backward2/pallas_call | solution.py:201
  107.1 8.1 %collective-permute-done.14 = f32[256,256]{1,0:T(8,128)S(1)} collective-permute-done((f32[256,256]{1,0:T(8,128)S(1)}, f32[256,256]{1,0:T(8,128)S(1)}, u32[]{:S(2)}, u32[]{:S(2)}) %collective-permute-start.14) | collective-permute-done | bytes 262176 | tf_op jit(solution)/shard_map/ppermute | solution.py:323
  115.3 6.2 %backward3.1 = (f32[256,256]{1,0:T(8,128)S(1)}, f32[256,256]{1,0:T(8,128)S(1)}, bf16[4,128,1280]{2,1,0:T(8,128)(2,1)}) custom-call(bf16[4,128,1280]{2,1,0:T(8,128)(2,1)S(1)} %all-to-all-done.q_all, bf16[10,2048,256]{2,1,0:T(8,128)(2,1)S(1)} %get-tuple-element.53.p_all, bf16[10,256,256]{2,1,0:T(8,128)(2,1)S(1)} %get-tuple-element.54.grad2_all, ...), custom_call_target="tpu_custom_call" | custom-call | flops 1207959552 | bytes 8000000 | tf_op jit(solution)/shard_map/backward3/pallas_call | solution.py:201
  121.5 3.5 %all-to-all-start.1 = ((bf16[4,128,1280]{2,1,0:T(8,128)(2,1)}), bf16[4,128,1280]{2,1,0:T(8,128)(2,1)S(1)}, u32[]{:S(2)}, u32[]{:S(2)}) async-start(bf16[4,128,1280]{2,1,0:T(8,128)(2,1)} %get-tuple-element.70), calls=%async_computation.1 | async-start | bytes 2621440 | tf_op jit(solution)/shard_map/all_to_all | solution.py:319
  127.9 6.3 %collective-permute-done.15.n1 = f32[256,256]{1,0:T(8,128)S(1)} collective-permute-done((f32[256,256]{1,0:T(8,128)S(1)}, f32[256,256]{1,0:T(8,128)S(1)}, u32[]{:S(2)}, u32[]{:S(2)}) %collective-permute-start.15) | collective-permute-done | bytes 262176 | tf_op jit(solution)/shard_map/ppermute | solution.py:323
  134.2 2.8 %collective-permute-done.16.n2 = f32[256,256]{1,0:T(8,128)S(1)} collective-permute-done((f32[256,256]{1,0:T(8,128)S(1)}, f32[256,256]{1,0:T(8,128)S(1)}, u32[]{:S(2)}, u32[]{:S(2)}) %collective-permute-start.16) | collective-permute-done | bytes 262176 | tf_op jit(solution)/shard_map/ppermute | solution.py:323
  137.0 2.7 %collective-permute-done.17.n3 = f32[256,256]{1,0:T(8,128)S(1)} collective-permute-done((f32[256,256]{1,0:T(8,128)S(1)}, f32[256,256]{1,0:T(8,128)S(1)}, u32[]{:S(2)}, u32[]{:S(2)}) %collective-permute-start.17) | collective-permute-done | bytes 262176 | tf_op jit(solution)/shard_map/ppermute | solution.py:323
  140.4 2.9 %collective-permute-start.19 = (bf16[192,256]{1,0:T(8,128)(2,1)S(1)}, bf16[192,256]{1,0:T(8,128)(2,1)S(1)}, u32[]{:S(2)}, u32[]{:S(2)}) collective-permute-start(bf16[192,256]{1,0:T(8,128)(2,1)S(1)} %get-tuple-element.79), channel_id=1, source_target_pairs={{0,3},{1,0},{2,1},{3,2},{4,7},{5,4},{6,5},{7,6},{8,11},{9,8},{10,9... | collective-permute-start | bytes 294920 | tf_op jit(solution)/shard_map/ppermute | solution.py:315
  145.0 2.2 %collective-permute-done.19.f1 = bf16[192,256]{1,0:T(8,128)(2,1)S(1)} collective-permute-done((bf16[192,256]{1,0:T(8,128)(2,1)S(1)}, bf16[192,256]{1,0:T(8,128)(2,1)S(1)}, u32[]{:S(2)}, u32[]{:S(2)}) %collective-permute-start.19) | collective-permute-done | bytes 98336 | tf_op jit(solution)/shard_map/ppermute | solution.py:315
  147.2 2.5 %collective-permute-done.20.f2 = bf16[192,256]{1,0:T(8,128)(2,1)S(1)} collective-permute-done((bf16[192,256]{1,0:T(8,128)(2,1)S(1)}, bf16[192,256]{1,0:T(8,128)(2,1)S(1)}, u32[]{:S(2)}, u32[]{:S(2)}) %collective-permute-start.20) | collective-permute-done | bytes 98336 | tf_op jit(solution)/shard_map/ppermute | solution.py:315
  (49 shorter events, 24.9 us)
Async XLA Ops:
  5.0 54.4 %all-to-all-start = ((bf16[4,128,1280]{2,1,0:T(8,128)(2,1)}), bf16[4,128,1280]{2,1,0:T(8,128)(2,1)S(1)}, u32[]{:S(2)}, u32[]{:S(2)}) async-start(bf16[4,128,1280]{2,1,0:T(8,128)(2,1)} %get-tuple-element.46), calls=%async_computation | async-start | bytes 2621440 | tf_op jit(solution)/shard_map/all_to_all | solution.py:319
  9.5 20.8 %collective-permute-start = (bf16[192,256]{1,0:T(8,128)(2,1)S(1)}, bf16[192,256]{1,0:T(8,128)(2,1)S(1)}, u32[]{:S(2)}, u32[]{:S(2)}) collective-permute-start(bf16[192,256]{1,0:T(8,128)(2,1)S(1)} %copy-done.5), channel_id=1, source_target_pairs={{0,1},{1,2},{2,3},{3,0},{4,5},{5,6},{6,7},{7,4},{8,9},{9,10},{10,1... | collective-permute-start | bytes 294920 | tf_op jit(solution)/shard_map/ppermute | solution.py:315
  11.5 20.1 %collective-permute-start.1 = (bf16[192,256]{1,0:T(8,128)(2,1)S(1)}, bf16[192,256]{1,0:T(8,128)(2,1)S(1)}, u32[]{:S(2)}, u32[]{:S(2)}) collective-permute-start(bf16[192,256]{1,0:T(8,128)(2,1)S(1)} %copy-done.4), channel_id=1, source_target_pairs={{0,2},{1,3},{2,0},{3,1},{4,6},{5,7},{6,4},{7,5},{8,10},{9,11},{10,... | collective-permute-start | bytes 294920 | tf_op jit(solution)/shard_map/ppermute | solution.py:315
  14.2 17.5 %collective-permute-start.2 = (bf16[192,256]{1,0:T(8,128)(2,1)S(1)}, bf16[192,256]{1,0:T(8,128)(2,1)S(1)}, u32[]{:S(2)}, u32[]{:S(2)}) collective-permute-start(bf16[192,256]{1,0:T(8,128)(2,1)S(1)} %copy-done.3), channel_id=1, source_target_pairs={{0,3},{1,0},{2,1},{3,2},{4,7},{5,4},{6,5},{7,6},{8,11},{9,8},{10,9... | collective-permute-start | bytes 294920 | tf_op jit(solution)/shard_map/ppermute | solution.py:315
  32.2 16.1 %collective-permute-start.4 = (bf16[256,256]{1,0:T(8,128)(2,1)S(1)}, bf16[256,256]{1,0:T(8,128)(2,1)S(1)}, u32[]{:S(2)}, u32[]{:S(2)}) collective-permute-start(bf16[256,256]{1,0:T(8,128)(2,1)S(1)} %get-tuple-element.52.l0), channel_id=1, source_target_pairs={{0,16},{1,17},{2,18},{3,19},{4,20},{5,21},{6,22},{7,23},{8,24},{9,... | collective-permute-start | bytes 393224 | tf_op jit(solution)/shard_map/ppermute | solution.py:327
  38.6 9.7 %collective-permute-start.10 = (bf16[256,256]{1,0:T(8,128)(2,1)S(1)}, bf16[256,256]{1,0:T(8,128)(2,1)S(1)}, u32[]{:S(2)}, u32[]{:S(2)}) collective-permute-start(bf16[256,256]{1,0:T(8,128)(2,1)S(1)} %get-tuple-element.52.l0), channel_id=1, source_target_pairs={{0,12},{1,13},{2,14},{3,15},{4,0},{5,1},{6,2},{7,3},{8,4},{9,5},{1... | collective-permute-start | bytes 393224 | tf_op jit(solution)/shard_map/ppermute | solution.py:323
  41.6 8.3 %collective-permute-start.8 = (bf16[256,256]{1,0:T(8,128)(2,1)S(1)}, bf16[256,256]{1,0:T(8,128)(2,1)S(1)}, u32[]{:S(2)}, u32[]{:S(2)}) collective-permute-start(bf16[256,256]{1,0:T(8,128)(2,1)S(1)} %get-tuple-element.52.l0), channel_id=1, source_target_pairs={{0,4},{1,5},{2,6},{3,7},{4,8},{5,9},{6,10},{7,11},{8,12},{9,13},{1... | collective-permute-start | bytes 393224 | tf_op jit(solution)/shard_map/ppermute | solution.py:323
  41.6 15.1 %collective-permute-start.3 = (bf16[384,256]{1,0:T(8,128)(2,1)S(1)}, bf16[384,256]{1,0:T(8,128)(2,1)S(1)}, u32[]{:S(2)}, u32[]{:S(2)}) collective-permute-start(bf16[384,256]{1,0:T(8,128)(2,1)S(1)} %get-tuple-element.51), channel_id=1, source_target_pairs={{0,4},{1,5},{2,6},{3,7},{4,8},{5,9},{6,10},{7,11},{8,12},{9,13},{1... | collective-permute-start | bytes 589832 | tf_op jit(solution)/shard_map/ppermute | solution.py:332
  44.1 12.6 %collective-permute-start.9 = (bf16[256,256]{1,0:T(8,128)(2,1)S(1)}, bf16[256,256]{1,0:T(8,128)(2,1)S(1)}, u32[]{:S(2)}, u32[]{:S(2)}) collective-permute-start(bf16[256,256]{1,0:T(8,128)(2,1)S(1)} %get-tuple-element.52.l0), channel_id=1, source_target_pairs={{0,8},{1,9},{2,10},{3,11},{4,12},{5,13},{6,14},{7,15},{8,0},{9,1},... | collective-permute-start | bytes 393224 | tf_op jit(solution)/shard_map/ppermute | solution.py:323
  48.3 9.0 %collective-permute-start.5 = (bf16[256,256]{1,0:T(8,128)(2,1)S(1)}, bf16[256,256]{1,0:T(8,128)(2,1)S(1)}, u32[]{:S(2)}, u32[]{:S(2)}) collective-permute-start(bf16[256,256]{1,0:T(8,128)(2,1)S(1)} %collective-permute-done.4.h0), channel_id=1, source_target_pairs={{0,4},{1,5},{2,6},{3,7},{4,8},{5,9},{6,10},{7,11},{8,12},{9,13},{1... | collective-permute-start | bytes 393224 | tf_op jit(solution)/shard_map/ppermute | solution.py:323
  48.3 11.1 %collective-permute-start.6 = (bf16[256,256]{1,0:T(8,128)(2,1)S(1)}, bf16[256,256]{1,0:T(8,128)(2,1)S(1)}, u32[]{:S(2)}, u32[]{:S(2)}) collective-permute-start(bf16[256,256]{1,0:T(8,128)(2,1)S(1)} %collective-permute-done.4.h0), channel_id=1, source_target_pairs={{0,8},{1,9},{2,10},{3,11},{4,12},{5,13},{6,14},{7,15},{8,0},{9,1},... | collective-permute-start | bytes 393224 | tf_op jit(solution)/shard_map/ppermute | solution.py:323
  49.9 9.5 %collective-permute-start.7 = (bf16[256,256]{1,0:T(8,128)(2,1)S(1)}, bf16[256,256]{1,0:T(8,128)(2,1)S(1)}, u32[]{:S(2)}, u32[]{:S(2)}) collective-permute-start(bf16[256,256]{1,0:T(8,128)(2,1)S(1)} %collective-permute-done.4.h0), channel_id=1, source_target_pairs={{0,12},{1,13},{2,14},{3,15},{4,0},{5,1},{6,2},{7,3},{8,4},{9,5},{1... | collective-permute-start | bytes 393224 | tf_op jit(solution)/shard_map/ppermute | solution.py:323
  80.8 11.5 %collective-permute-start.11 = (f32[384,256]{1,0:T(8,128)S(1)}, f32[384,256]{1,0:T(8,128)S(1)}, u32[]{:S(2)}, u32[]{:S(2)}) collective-permute-start(f32[384,256]{1,0:T(8,128)S(1)} %get-tuple-element.60), channel_id=1, source_target_pairs={{4,0},{5,1},{6,2},{7,3},{8,4},{9,5},{10,6},{11,7},{12,8},{13,9},{1... | collective-permute-start | bytes 1179656 | tf_op jit(solution)/shard_map/ppermute | solution.py:332
  87.4 10.0 %collective-permute-start.12 = (f32[256,256]{1,0:T(8,128)S(1)}, f32[256,256]{1,0:T(8,128)S(1)}, u32[]{:S(2)}, u32[]{:S(2)}) collective-permute-start(f32[256,256]{1,0:T(8,128)S(1)} %get-tuple-element.63), channel_id=1, source_target_pairs={{0,4},{1,5},{2,6},{3,7},{4,8},{5,9},{6,10},{7,11},{8,12},{9,13},{1... | collective-permute-start | bytes 786440 | tf_op jit(solution)/shard_map/ppermute | solution.py:323
  90.1 11.8 %collective-permute-start.13 = (f32[256,256]{1,0:T(8,128)S(1)}, f32[256,256]{1,0:T(8,128)S(1)}, u32[]{:S(2)}, u32[]{:S(2)}) collective-permute-start(f32[256,256]{1,0:T(8,128)S(1)} %get-tuple-element.65), channel_id=1, source_target_pairs={{0,12},{1,13},{2,14},{3,15},{4,0},{5,1},{6,2},{7,3},{8,4},{9,5},{1... | collective-permute-start | bytes 786440 | tf_op jit(solution)/shard_map/ppermute | solution.py:323
  101.9 13.3 %collective-permute-start.14 = (f32[256,256]{1,0:T(8,128)S(1)}, f32[256,256]{1,0:T(8,128)S(1)}, u32[]{:S(2)}, u32[]{:S(2)}) collective-permute-start(f32[256,256]{1,0:T(8,128)S(1)} %get-tuple-element.66.after), channel_id=1, source_target_pairs={{0,4},{1,5},{2,6},{3,7},{4,8},{5,9},{6,10},{7,11},{8,12},{9,13},{1... | collective-permute-start | bytes 786440 | tf_op jit(solution)/shard_map/ppermute | solution.py:323
  121.5 30.6 %all-to-all-start.1 = ((bf16[4,128,1280]{2,1,0:T(8,128)(2,1)}), bf16[4,128,1280]{2,1,0:T(8,128)(2,1)S(1)}, u32[]{:S(2)}, u32[]{:S(2)}) async-start(bf16[4,128,1280]{2,1,0:T(8,128)(2,1)} %get-tuple-element.70), calls=%async_computation.1 | async-start | bytes 2621440 | tf_op jit(solution)/shard_map/all_to_all | solution.py:319
  125.0 9.2 %collective-permute-start.15 = (f32[256,256]{1,0:T(8,128)S(1)}, f32[256,256]{1,0:T(8,128)S(1)}, u32[]{:S(2)}, u32[]{:S(2)}) collective-permute-start(f32[256,256]{1,0:T(8,128)S(1)} %get-tuple-element.74), channel_id=1, source_target_pairs={{0,12},{1,13},{2,14},{3,15},{4,0},{5,1},{6,2},{7,3},{8,4},{9,5},{1... | collective-permute-start | bytes 786440 | tf_op jit(solution)/shard_map/ppermute | solution.py:323
  126.9 10.1 %collective-permute-start.16 = (f32[256,256]{1,0:T(8,128)S(1)}, f32[256,256]{1,0:T(8,128)S(1)}, u32[]{:S(2)}, u32[]{:S(2)}) collective-permute-start(f32[256,256]{1,0:T(8,128)S(1)} %get-tuple-element.75), channel_id=1, source_target_pairs={{0,8},{1,9},{2,10},{3,11},{4,12},{5,13},{6,14},{7,15},{8,0},{9,1},... | collective-permute-start | bytes 786440 | tf_op jit(solution)/shard_map/ppermute | solution.py:323
  126.9 12.8 %collective-permute-start.17 = (f32[256,256]{1,0:T(8,128)S(1)}, f32[256,256]{1,0:T(8,128)S(1)}, u32[]{:S(2)}, u32[]{:S(2)}) collective-permute-start(f32[256,256]{1,0:T(8,128)S(1)} %get-tuple-element.76), channel_id=1, source_target_pairs={{0,4},{1,5},{2,6},{3,7},{4,8},{5,9},{6,10},{7,11},{8,12},{9,13},{1... | collective-permute-start | bytes 786440 | tf_op jit(solution)/shard_map/ppermute | solution.py:323
  127.9 11.8 %collective-permute-start.18 = (f32[256,256]{1,0:T(8,128)S(1)}, f32[256,256]{1,0:T(8,128)S(1)}, u32[]{:S(2)}, u32[]{:S(2)}) collective-permute-start(f32[256,256]{1,0:T(8,128)S(1)} %add.9.after), channel_id=1, source_target_pairs={{0,16},{1,17},{2,18},{3,19},{4,20},{5,21},{6,22},{7,23},{8,24},{9,... | collective-permute-start | bytes 786440 | tf_op jit(solution)/shard_map/ppermute | solution.py:327
  140.4 6.8 %collective-permute-start.19 = (bf16[192,256]{1,0:T(8,128)(2,1)S(1)}, bf16[192,256]{1,0:T(8,128)(2,1)S(1)}, u32[]{:S(2)}, u32[]{:S(2)}) collective-permute-start(bf16[192,256]{1,0:T(8,128)(2,1)S(1)} %get-tuple-element.79), channel_id=1, source_target_pairs={{0,3},{1,0},{2,1},{3,2},{4,7},{5,4},{6,5},{7,6},{8,11},{9,8},{10,9... | collective-permute-start | bytes 294920 | tf_op jit(solution)/shard_map/ppermute | solution.py:315
  143.3 6.4 %collective-permute-start.20 = (bf16[192,256]{1,0:T(8,128)(2,1)S(1)}, bf16[192,256]{1,0:T(8,128)(2,1)S(1)}, u32[]{:S(2)}, u32[]{:S(2)}) collective-permute-start(bf16[192,256]{1,0:T(8,128)(2,1)S(1)} %get-tuple-element.80), channel_id=1, source_target_pairs={{0,2},{1,3},{2,0},{3,1},{4,6},{5,7},{6,4},{7,5},{8,10},{9,11},{10,... | collective-permute-start | bytes 294920 | tf_op jit(solution)/shard_map/ppermute | solution.py:315
  144.1 6.6 %collective-permute-start.21 = (bf16[192,256]{1,0:T(8,128)(2,1)S(1)}, bf16[192,256]{1,0:T(8,128)(2,1)S(1)}, u32[]{:S(2)}, u32[]{:S(2)}) collective-permute-start(bf16[192,256]{1,0:T(8,128)(2,1)S(1)} %get-tuple-element.81), channel_id=1, source_target_pairs={{0,1},{1,2},{2,3},{3,0},{4,5},{5,6},{6,7},{7,4},{8,9},{9,10},{10,1... | collective-permute-start | bytes 294920 | tf_op jit(solution)/shard_map/ppermute | solution.py:315
  (6 other events, 127.9 us)

commit v5 on v1

v5 whole, which is shorter than its diff:
```python
import jax
import jax.numpy as jnp
from jax import lax
from jax.experimental import pallas as pl
from jax.experimental.pallas import tpu as pltpu
from jax.sharding import PartitionSpec as P

HEADS = 20
KV_HEADS = 4
HEAD_DIM = 128
PER_GROUP = HEADS // KV_HEADS
BACK = 384
NEGATIVE = -1e30
LOG2E = 1.4426950408889634
FACTOR = HEAD_DIM ** (-0.5)

X_GROUPS = [[first + x for x in range(4)] for first in range(0, 32, 4)]
ROWS = 256
KEYS = 1024
SPAN = 640
PROMPT_ROWS = 2048
OWN_ROWS = 512
WIDE = PER_GROUP * HEAD_DIM


def nt(a, b):
    return lax.dot_general(a, b, (((1,), (1,)), ((), ())), preferred_element_type=jnp.float32)


def nn(a, b):
    return lax.dot_general(a, b, (((1,), (0,)), ((), ())), preferred_element_type=jnp.float32)


def block_at(x, distance):
    return pl.ds(pl.multiple_of(lax.rem(x + 4 - distance, 4) * 128, 128), 128)


def attention_kernel(
    len_ref, where_ref, q_all, s0, s1, s2, s3, before_ref, h0, h1, h2, h3, l0, l1, l2, l3,
    o_ref, g0, g1, g2, g3, g4, g5, g6, g7, back_grad_ref, own_grad_ref,
    key2, value1, key_t, value_t, s_first, s_second, p_first, p_second,
    grad2_first, grad2_second, rows_first, rows_second, key_sum, value_sum,
):
    base, x = where_ref[0], where_ref[1]
    all_rows = PROMPT_ROWS + BACK + OWN_ROWS

    def place(at, source):
        key2[at, :128] = source[:, :128]
        key2[at, 128:] = source[:, :128]
        value1[at, :128] = source[:, 128:]

    for i, source in enumerate((h2, h1, h0, h3, l2, l1, l0, l3)):
        place(slice(i * 256, i * 256 + 256), source)
    place(slice(PROMPT_ROWS, PROMPT_ROWS + BACK), before_ref)
    for d, source in enumerate((s0, s1, s2, s3)):
        first = PROMPT_ROWS + BACK + lax.rem(x + 4 - d, 4) * 128
        place(pl.ds(pl.multiple_of(first, 128), 128), source.at[64:192, :])
    value1[:, 128:] = jnp.ones((all_rows, 128), jnp.bfloat16)
    value_t[128:, :] = jnp.ones((16, all_rows), jnp.bfloat16)
    for c in range(0, all_rows, 128):
        at = slice(c, c + 128)
        key_t[:, at] = key2[at, :128].astype(jnp.float32).T.astype(jnp.bfloat16)
        value_t[:128, at] = value1[at, :128].astype(jnp.float32).T.astype(jnp.bfloat16)
    for ref in (key_sum, value_sum, p_second, grad2_second, rows_second):
        ref[...] = jnp.zeros_like(ref)

    s_refs, p_refs = (s_first, s_second), (p_first, p_second)
    grad2_refs, rows_refs = (grad2_first, grad2_second), (rows_first, rows_second)

    def tiles(block):
        span = PROMPT_ROWS + block * ROWS
        out = [(c, c, KEYS) for c in range(0, PROMPT_ROWS, KEYS)] + [(span, PROMPT_ROWS, SPAN)]
        return [(slice(keys, keys + size), slice(at, at + size)) for keys, at, size in out]

    def rows_of(block, head, first):
        cols = pl.ds(pl.multiple_of(first + head * 128, 128), 128)
        return q_all[block * 2 : block * 2 + 2, :, cols].reshape(ROWS, 128)

    def scores(block, head):
        scaled = rows_of(block, head, 0).astype(jnp.float32).T * (FACTOR * LOG2E)
        high = scaled.astype(jnp.bfloat16)
        low = (scaled - high.astype(jnp.float32)).astype(jnp.bfloat16)
        q2t = jnp.concatenate([high, low], 0)
        top = None
        for keys, at in tiles(block):
            s = nn(key2[keys, :], q2t)
            if at.start == PROMPT_ROWS:
                own = base + block * ROWS
                row_pos = own + lax.broadcasted_iota(jnp.int32, (1, ROWS), 1)
                seg_start = jnp.zeros((1, ROWS), jnp.int32)
                end = jnp.int32(0)
                for j in range(16):
                    end = end + len_ref[j]
                    seg_start = jnp.maximum(seg_start, jnp.where(row_pos >= end, end, 0))
                key_pos = own - BACK + lax.broadcasted_iota(jnp.int32, (SPAN, ROWS), 0)
                s = jnp.where((key_pos <= row_pos) & (key_pos >= seg_start), s, NEGATIVE)
            s_refs[block][at, :] = s
            tile_top = jnp.max(s, axis=0, keepdims=True)
            top = tile_top if top is None else jnp.maximum(top, tile_top)
            yield top

    def weigh(block, head, top):
        total = jnp.zeros((144, ROWS), jnp.float32)
        for i, (keys, at) in enumerate(tiles(block)):
            p = jnp.exp2(s_refs[block][at, :] - top).astype(jnp.bfloat16)
            p_refs[block][at, :] = p
            total = total + nn(value_t[:, keys], p)
            if i < len(tiles(block)) - 1:
                yield
        inverse = 1.0 / total[128:129, :]
        out = (total[:128, :] * inverse).astype(jnp.bfloat16).astype(jnp.float32)
        cols = pl.ds(pl.multiple_of(head * 128, 128), 128)
        o_ref[block * 2 : block * 2 + 2, :, cols] = out.T.astype(jnp.bfloat16).reshape(2, 128, 128)
        grad_n = (rows_of(block, head, WIDE).astype(jnp.float32).T * inverse).astype(jnp.bfloat16)
        wide = grad_n.astype(jnp.float32)
        row_dot = -jnp.sum(wide * out, axis=0, keepdims=True)
        dot_high = row_dot.astype(jnp.bfloat16).astype(jnp.float32)
        line = lax.broadcasted_iota(jnp.int32, (128, ROWS), 0)
        extra = jnp.where(line == 0, dot_high, jnp.where(line == 1, row_dot - dot_high, 0.0))
        grad2_refs[block][:128, :] = grad_n
        grad2_refs[block][128:, :] = extra.astype(jnp.bfloat16)
        rows_refs[block][...] = wide.T.astype(jnp.bfloat16)
        yield

    def backward(block, head):
        q = rows_of(block, head, 0)
        dq = jnp.zeros((HEAD_DIM, ROWS), jnp.float32)
        for i, (keys, at) in enumerate(tiles(block)):
            p = p_refs[block][at, :]
            ds = (p.astype(jnp.float32) * nn(value1[keys, :], grad2_refs[block][...])).astype(jnp.bfloat16)
            dq = dq + nn(key_t[:, keys], ds)
            key_sum[keys, :] += nn(ds, q)
            value_sum[keys, :] += nn(p, rows_refs[block][...])
            if i < len(tiles(block)) - 1:
                yield
        cols = pl.ds(pl.multiple_of(WIDE + head * 128, 128), 128)
        dq = (dq * FACTOR).T.astype(jnp.bfloat16)
        o_ref[block * 2 : block * 2 + 2, :, cols] = dq.reshape(2, 128, 128)
        yield

    def beside(one, other):
        last = None
        for _, last in zip(one, other):
            pass
        return last

    def step(head, carry):
        top_first = beside(backward(1, jnp.maximum(head - 1, 0)), scores(0, head))
        top_second = beside(weigh(0, head, top_first), scores(1, head))
        beside(backward(0, head), weigh(1, head, top_second))
        return carry

    lax.fori_loop(0, PER_GROUP, step, 0)
    for _ in backward(1, PER_GROUP - 1):
        pass

    outs = [(i * 256, i * 256 + 256, ref) for i, ref in enumerate((g0, g1, g2, g3, g4, g5, g6, g7))]
    outs += [(PROMPT_ROWS, PROMPT_ROWS + BACK, back_grad_ref), (PROMPT_ROWS + BACK, all_rows, own_grad_ref)]
    for first, last, target in outs:
        target[:, :128] = key_sum[first:last, :] * FACTOR
        target[:, 128:] = value_sum[first:last, :]


def call(body, scalars, operands, outs, name, scratch=(), limit=24, cost=None, space=pltpu.VMEM, extra=(), passed={}):
    smem = pl.BlockSpec(memory_space=pltpu.SMEM)
    return pl.pallas_call(
        body,
        in_specs=[smem] * len(scalars) + [pl.BlockSpec(memory_space=space)] * len(operands)
        + [pl.BlockSpec(memory_space=pl.ANY)] * len(extra),
        out_specs=[
            pl.BlockSpec(memory_space=pl.ANY if i in passed.values() else pltpu.VMEM) for i in range(len(outs))
        ],
        input_output_aliases=passed,
        out_shape=[jax.ShapeDtypeStruct(shape, dtype) for shape, dtype in outs],
        scratch_shapes=list(scratch),
        compiler_params=pltpu.CompilerParams(vmem_limit_bytes=limit * 1024 * 1024),
        cost_estimate=cost,
        name=name,
    )(*scalars, *operands, *extra)


def attention(resp_len, where, operands):
    bf16, f32 = jnp.bfloat16, jnp.float32
    rows = PROMPT_ROWS + BACK + OWN_ROWS
    flops = 12 * 2560 * 2560 * 128
    return call(
        attention_kernel, (resp_len, where), operands,
        [((4, 128, 2 * WIDE), bf16)] + [((256, 256), f32)] * 8 + [((BACK, 256), f32), ((OWN_ROWS, 256), f32)],
        "attention",
        scratch=[
            pltpu.VMEM((rows, 256), bf16),
            pltpu.VMEM((rows, 256), bf16),
            pltpu.VMEM((128, rows), bf16),
            pltpu.VMEM((144, rows), bf16),
            pltpu.VMEM((PROMPT_ROWS + SPAN, ROWS), f32),
            pltpu.VMEM((PROMPT_ROWS + SPAN, ROWS), f32),
            pltpu.VMEM((PROMPT_ROWS + SPAN, ROWS), bf16),
            pltpu.VMEM((PROMPT_ROWS + SPAN, ROWS), bf16),
            pltpu.VMEM((256, ROWS), bf16),
            pltpu.VMEM((256, ROWS), bf16),
            pltpu.VMEM((ROWS, 128), bf16),
            pltpu.VMEM((ROWS, 128), bf16),
            pltpu.VMEM((rows, 128), f32),
            pltpu.VMEM((rows, 128), f32),
        ],
        limit=32,
        cost=pl.CostEstimate(flops=flops, bytes_accessed=8_000_000, transcendentals=flops // 1536),
    )


def head_columns(x, distance, width):
    return pl.ds(pl.multiple_of(lax.rem(x + distance, 4) * width, 128), width)


def pack_kernel(where_ref, pk, pv, k, v, q, g, s0, s1, s2, s3, rows, sems):
    pairs = []
    for d, target in enumerate((s0, s1, s2, s3)):
        cols = head_columns(where_ref[1], d, 128)
        for source, lines, lanes in ((pk, (0, 64), 0), (pv, (0, 64), 128), (k, (64, 192), 0), (v, (64, 192), 128)):
            pairs.append((source.at[:, cols], target.at[slice(*lines), lanes : lanes + 128]))
    for h in range(KV_HEADS):
        for source, first in ((q, 0), (g, WIDE)):
            pairs.append((source.at[:, h * WIDE : h * WIDE + WIDE], rows.at[h, :, first : first + WIDE]))
    copies = [pltpu.make_async_copy(source, target, sems.at[i]) for i, (source, target) in enumerate(pairs)]
    for copy in copies:
        copy.start()
    for copy in copies:
        copy.wait()


def collect_kernel(where_ref, s0, s1, s2, s3, rows_in, mine_ref, ahead_ref, rows_out):
    x = where_ref[1]
    for d, source in enumerate((s0, s1, s2, s3)):
        mine_ref[d * 64 : d * 64 + 64, :] = source[:64, :]
        block = lax.rem(x + 4 - d, 4)

        @pl.when(block > 0)
        def _():
            ahead_ref[pl.ds(pl.multiple_of((block - 1) * 128, 128), 128), :] = source[64:, :]


def final_sum_kernel(where_ref, n0, n1, n2, n3, got_ref, own_ref, back_ref, f0, f1, f2, f3):
    x = where_ref[1]
    for d, target in enumerate((f0, f1, f2, f3)):
        at = slice(d * 64, d * 64 + 64)
        total = (n0[at, :] + n1[at, :]) + (n2[at, :] + n3[at, :]) + got_ref[at, :]
        target[:64, :] = total.astype(jnp.bfloat16)
        block = lax.rem(x + 4 - d, 4)
        behind = pl.ds(pl.multiple_of(jnp.maximum(block - 1, 0) * 128, 128), 128)
        extra = jnp.where(block > 0, back_ref[behind, :], 0.0)
        target[64:, :] = (own_ref[block_at(x, d), :] + extra).astype(jnp.bfloat16)


def unpack_rows_kernel(o_ref, out_ref, dq_ref):
    for h in range(KV_HEADS):
        at = slice(h * WIDE, h * WIDE + WIDE)
        out_ref[:, at] = o_ref[h, :, :WIDE]
        dq_ref[:, at] = o_ref[h, :, WIDE:]


def unpack_small_kernel(where_ref, f0, f1, f2, f3, k_ref, v_ref, pk_ref, pv_ref):
    x = where_ref[1]
    for d, source in enumerate((f0, f1, f2, f3)):
        at = head_columns(x, d, 128)
        pk_ref[:, at] = source[:64, :128]
        pv_ref[:, at] = source[:64, 128:]
        k_ref[:, at] = source[64:, :128]
        v_ref[:, at] = source[64:, 128:]


def along_x(value, step):
    return lax.ppermute(value, "seq", [(i, i // 4 * 4 + (i + step) % 4) for i in range(32)])


def exchange_x(value):
    return lax.all_to_all(value, "seq", 0, 0, axis_index_groups=X_GROUPS, tiled=True)


def along_y(value, step):
    return lax.ppermute(value, "seq", [(i, i // 16 * 16 + (i + 4 * step) % 16) for i in range(32)])


def along_z(value):
    return lax.ppermute(value, "seq", [(i, (i + 16) % 32) for i in range(32)])


def along_rows(value, step):
    pairs = [(i, i + 4 * step) for i in range(32)]
    return lax.ppermute(value, "seq", [(i, j) for i, j in pairs if 0 <= j < 32])


def local(resp_len, prompt_keys, prompt_values, resp_q, resp_k, resp_v, out_grad):
    me = lax.axis_index("seq").astype(jnp.int32)
    where = jnp.stack([me // 4 * OWN_ROWS, me % 4])
    rows, bf16, f32 = resp_q.shape[0], jnp.bfloat16, jnp.float32

    *s, q_all = call(
        pack_kernel, (where,), (prompt_keys, prompt_values, resp_k, resp_v, resp_q, out_grad),
        [((192, 256), bf16)] * 4 + [((4, rows, 2 * WIDE), bf16)], "pack",
        scratch=[pltpu.SemaphoreType.DMA((24,))], space=pl.ANY, limit=60,
    )
    s = [s[0]] + [along_x(s[d], d) for d in (1, 2, 3)]
    mine, ahead, q_all = call(
        collect_kernel, (where,), s, [((256, 256), bf16), ((BACK, 256), bf16), (q_all.shape, bf16)], "collect",
        extra=(q_all,), passed={5: 2},
    )
    q_all = exchange_x(q_all)
    far = along_z(mine)
    near_keys = [mine] + [along_y(mine, d) for d in (1, 2, 3)]
    before = along_rows(ahead, 1)
    far_keys = [far] + [along_y(far, d) for d in (1, 2, 3)]

    o, h2, h1, h0, h3, l2, l1, l0, l3, back_grad, own_grad = attention(
        resp_len, where, (q_all, *s, before, *far_keys, *near_keys)
    )

    through, minus = along_y(h2, 1), along_y(h1, -1)
    plus = along_y(h3 + through, 1)
    got = along_z(h0 + minus + plus)
    one, two, three = along_y(l1, -1), along_y(l2, -2), along_y(l3, 1)
    back = along_rows(back_grad, -1)

    attn_out, q_grad = call(
        unpack_rows_kernel, (), (exchange_x(o),), [((rows, HEADS * HEAD_DIM), bf16)] * 2, "unpack_rows"
    )

    f = call(
        final_sum_kernel, (where,), (l0, one, two, three, got, own_grad, back),
        [((192, 256), bf16)] * 4, "final_sum",
    )
    f = [f[0]] + [along_x(f[d], -d) for d in (1, 2, 3)]
    resp_k_grad, resp_v_grad, prompt_k_grad, prompt_v_grad = call(
        unpack_small_kernel, (where,), f, [((rows, 512), bf16)] * 2 + [((64, 512), bf16)] * 2, "unpack_small"
    )
    return attn_out, q_grad, resp_k_grad, resp_v_grad, prompt_k_grad, prompt_v_grad


def solution(mesh):
    split = P(("grp", "seq"), None)
    return jax.shard_map(
        local,
        mesh=mesh,
        in_specs=(P("grp"),) + (split,) * 6,
        out_specs=(split,) * 6,
        check_vma=False,
    )
```

time: 154 us -> 149 us (0.968)
  waiting for transfers between devices: 64.3 us -> 32.9 us
  starting transfers between devices: 42.4 us -> 58.8 us
  local copies, waits for them, and re-layouts: 4.6 us -> 16.5 us
  Pallas kernels: 40.4 us -> 37.6 us
    ppermute x3 -> x2, waiting for transfers between devices: 29.3 us -> 16 us  [along_z(): return lax.ppermute(value, 'seq', [(i, (i + 16) % 32) for i in range(32)])]
    ppermute x8 -> x12, waiting for transfers between devices: 19.8 us -> 7.67 us  [along_y(): lax.ppermute(value, 'seq', [(i, i // 16 * 16 + (i + 4 * step) % 16) for i...]
    unnamed x14 -> x54, local copies, waits for them, and re-layouts: 4.58 us -> 16.5 us
    all_to_all x0 -> x2, starting transfers between devices: none -> 8.72 us  [exchange_x(): lax.all_to_all(value, 'seq', 0, 0, axis_index_groups=X_GROUPS, tiled=True)]
    ppermute x2, waiting for transfers between devices: 7.9 us -> 0.01 us  [along_rows(): return lax.ppermute(value, 'seq', [(i, j) for i, j in pairs if 0 <= j < 32])]
    ppermute x12 -> x6, starting transfers between devices: 17.7 us -> 10.3 us  [along_x(): lax.ppermute(value, 'seq', [(i, i // 4 * 4 + (i + step) % 4) for i in ran...]
    ppermute x3 -> x2, starting transfers between devices: 11 us -> 17.7 us  [along_z(): return lax.ppermute(value, 'seq', [(i, (i + 16) % 32) for i in range(32)])]
    ppermute x8 -> x12, starting transfers between devices: 12.6 us -> 17.9 us  [along_y(): lax.ppermute(value, 'seq', [(i, i // 16 * 16 + (i + 4 * step) % 16) for i...]
  transfers between devices with their start and end apart: 25 -> 24, of which waited for: 14 -> 10; matrix products, arithmetic and copies ran while one was open for 0% -> 1% of each run, Pallas kernels for 2% -> 1%
where the time goes in v5:
time: 149 us; the launch traced here: 148 us
  starting transfers between devices  58.8 us (39%)
  Pallas kernels  37.6 us (25%)
  waiting for transfers between devices  32.9 us (22%)
  local copies, waits for them, and re-layouts  16.5 us (11%)
  other arithmetic  1.62 us (1%)
    pallas_call x6, Pallas kernels, call(): pl.pallas_call(body, in_specs=[smem] * len(scalars) + [pl.BlockSpec(memor...  37.6 us
    ppermute x12, starting transfers between devices, along_y(): lax.ppermute(value, 'seq', [(i, i // 16 * 16 + (i + 4 * step) % 16) for i...  17.9 us
    ppermute x2, starting transfers between devices, along_z(): return lax.ppermute(value, 'seq', [(i, (i + 16) % 32) for i in range(32)])  17.7 us
    unnamed x54, local copies, waits for them, and re-layouts  16.5 us
    ppermute x2, waiting for transfers between devices, along_z(): return lax.ppermute(value, 'seq', [(i, (i + 16) % 32) for i in range(32)])  16 us
    ppermute x6, starting transfers between devices, along_x(): lax.ppermute(value, 'seq', [(i, i // 4 * 4 + (i + step) % 4) for i in ran...  10.3 us
    ppermute x6, waiting for transfers between devices, along_x(): lax.ppermute(value, 'seq', [(i, i // 4 * 4 + (i + step) % 4) for i in ran...  9.15 us
    all_to_all x2, starting transfers between devices, exchange_x(): lax.all_to_all(value, 'seq', 0, 0, axis_index_groups=X_GROUPS, tiled=True)  8.72 us
  transfers between devices with their start and end apart: 24, of which 10 were waited for; matrix products, arithmetic and copies ran while one was open for 1% of the time, Pallas kernels for 1%

profile of v5, /device:TPU:32, one launch (start us, length us, event | category | flops | bytes accessed | tf_op | source)
XLA Modules:
  0.0 148.2 jit_solution(3893476685276893110)
XLA Ops:
  1.2 3.8 %pack.1 = (bf16[192,256]{1,0:T(8,128)(2,1)}, bf16[192,256]{1,0:T(8,128)(2,1)}, bf16[192,256]{1,0:T(8,128)(2,1)}, bf16[192,256]{1,0:T(8,128)(2,1)}, bf16[4,128,1280]{2,1,0:T(8,128)(2,1)}) custom-call(s32[2]{0:T(128)} %pad_add_fusion.where_ref, bf16[64,512]{1,0:T(8,128)(2,1)} %pk.1, bf16[64,512]{1,0:T(8,128)(2,1)} %pv.1, bf16[128,512]{1,0:T(8,128)(2,1)} %k.1, ...), custom_call_target="tpu_custom_call" | custom-call | tf_op jit(solution)/shard_map/pack/pallas_call | solution.py:166
  5.0 1.6 %collective-permute-start = (bf16[192,256]{1,0:T(8,128)(2,1)}, bf16[192,256]{1,0:T(8,128)(2,1)S(1)}, u32[]{:S(2)}, u32[]{:S(2)}) collective-permute-start(bf16[192,256]{1,0:T(8,128)(2,1)} %get-tuple-element.36), channel_id=1, source_target_pairs={{0,1},{1,2},{2,3},{3,0},{4,5},{5,6},{6,7},{7,4},{8,9},{9,10},{10,1... | collective-permute-start | bytes 294920 | tf_op jit(solution)/shard_map/ppermute | solution.py:272
  6.6 2.7 %collective-permute-start.1 = (bf16[192,256]{1,0:T(8,128)(2,1)}, bf16[192,256]{1,0:T(8,128)(2,1)S(1)}, u32[]{:S(2)}, u32[]{:S(2)}) collective-permute-start(bf16[192,256]{1,0:T(8,128)(2,1)} %get-tuple-element.37), channel_id=1, source_target_pairs={{0,2},{1,3},{2,0},{3,1},{4,6},{5,7},{6,4},{7,5},{8,10},{9,11},{10,... | collective-permute-start | bytes 294920 | tf_op jit(solution)/shard_map/ppermute | solution.py:272
  9.3 1.4 collective-permute-start.2
  11.4 2.8 %collective-permute-done.1.s2 = bf16[192,256]{1,0:T(8,128)(2,1)S(1)} collective-permute-done((bf16[192,256]{1,0:T(8,128)(2,1)}, bf16[192,256]{1,0:T(8,128)(2,1)S(1)}, u32[]{:S(2)}, u32[]{:S(2)}) %collective-permute-start.1) | collective-permute-done | bytes 98336 | tf_op jit(solution)/shard_map/ppermute | solution.py:272
  18.1 4.1 %all-to-all-start = ((bf16[4,128,1280]{2,1,0:T(8,128)(2,1)}), bf16[4,128,1280]{2,1,0:T(8,128)(2,1)S(1)}, u32[]{:S(2)}, u32[]{:S(2)}) async-start(bf16[4,128,1280]{2,1,0:T(8,128)(2,1)} %copy-done.1), calls=%async_computation | async-start | bytes 2621440 | tf_op jit(solution)/shard_map/all_to_all | solution.py:276
  22.1 6.3 %collective-permute-start.4 = (bf16[256,256]{1,0:T(8,128)(2,1)S(1)}, bf16[256,256]{1,0:T(8,128)(2,1)S(1)}, u32[]{:S(2)}, u32[]{:S(2)}) collective-permute-start(bf16[256,256]{1,0:T(8,128)(2,1)S(1)} %get-tuple-element.42.l0), channel_id=1, source_target_pairs={{0,16},{1,17},{2,18},{3,19},{4,20},{5,21},{6,22},{7,23},{8,24},{9,... | collective-permute-start | bytes 393224 | tf_op jit(solution)/shard_map/ppermute | solution.py:284
  28.4 3.0 %collective-permute-start.10 = (bf16[256,256]{1,0:T(8,128)(2,1)S(1)}, bf16[256,256]{1,0:T(8,128)(2,1)S(1)}, u32[]{:S(2)}, u32[]{:S(2)}) collective-permute-start(bf16[256,256]{1,0:T(8,128)(2,1)S(1)} %get-tuple-element.42.l0), channel_id=1, source_target_pairs={{0,12},{1,13},{2,14},{3,15},{4,0},{5,1},{6,2},{7,3},{8,4},{9,5},{1... | collective-permute-start | bytes 393224 | tf_op jit(solution)/shard_map/ppermute | solution.py:280
  32.1 2.9 %collective-permute-start.3 = (bf16[384,256]{1,0:T(8,128)(2,1)S(1)}, bf16[384,256]{1,0:T(8,128)(2,1)S(1)}, u32[]{:S(2)}, u32[]{:S(2)}) collective-permute-start(bf16[384,256]{1,0:T(8,128)(2,1)S(1)} %get-tuple-element.41), channel_id=1, source_target_pairs={{0,4},{1,5},{2,6},{3,7},{4,8},{5,9},{6,10},{7,11},{8,12},{9,13},{1... | collective-permute-start | bytes 589832 | tf_op jit(solution)/shard_map/ppermute | solution.py:289
  34.9 2.0 %collective-permute-start.8 = (bf16[256,256]{1,0:T(8,128)(2,1)S(1)}, bf16[256,256]{1,0:T(8,128)(2,1)S(1)}, u32[]{:S(2)}, u32[]{:S(2)}) collective-permute-start(bf16[256,256]{1,0:T(8,128)(2,1)S(1)} %get-tuple-element.42.l0), channel_id=1, source_target_pairs={{0,4},{1,5},{2,6},{3,7},{4,8},{5,9},{6,10},{7,11},{8,12},{9,13},{1... | collective-permute-start | bytes 393224 | tf_op jit(solution)/shard_map/ppermute | solution.py:280
  36.9 1.4 collective-permute-start.7
  45.1 2.9 %collective-permute-done.6.h2 = bf16[256,256]{1,0:T(8,128)(2,1)S(1)} collective-permute-done((bf16[256,256]{1,0:T(8,128)(2,1)S(1)}, bf16[256,256]{1,0:T(8,128)(2,1)S(1)}, u32[]{:S(2)}, u32[]{:S(2)}) %collective-permute-start.6) | collective-permute-done | bytes 131104 | tf_op jit(solution)/shard_map/ppermute | solution.py:280
  56.6 30.1 %attention.1 = (bf16[4,128,1280]{2,1,0:T(8,128)(2,1)}, f32[256,256]{1,0:T(8,128)}, f32[256,256]{1,0:T(8,128)S(1)}, f32[256,256]{1,0:T(8,128)S(1)}, f32[256,256]{...) custom-call(s32[16]{0:T(128)S(1)} %copy-done.26, ...), custom_call_target="tpu_custom_call" | custom-call | flops 10066329600 | bytes 8000000 | tf_op jit(solution)/shard_map/attention/pallas_call | solution.py:166
  88.6 4.7 %all-to-all-start.1 = ((bf16[4,128,1280]{2,1,0:T(8,128)(2,1)}), bf16[4,128,1280]{2,1,0:T(8,128)(2,1)S(1)}, u32[]{:S(2)}, u32[]{:S(2)}) async-start(bf16[4,128,1280]{2,1,0:T(8,128)(2,1)} %get-tuple-element.43), calls=%async_computation.1 | async-start | bytes 2621440 | tf_op jit(solution)/shard_map/all_to_all | solution.py:276
  93.2 2.1 %collective-permute-start.14 = (f32[256,256]{1,0:T(8,128)}, f32[256,256]{1,0:T(8,128)S(1)}, u32[]{:S(2)}, u32[]{:S(2)}) collective-permute-start(f32[256,256]{1,0:T(8,128)} %copy-done.9), channel_id=1, source_target_pairs={{0,12},{1,13},{2,14},{3,15},{4,0},{5,1},{6,2},{7,3},{8,4},{9,5},{1... | collective-permute-start | bytes 786440 | tf_op jit(solution)/shard_map/ppermute | solution.py:280
  97.6 2.1 %collective-permute-start.11 = (f32[256,256]{1,0:T(8,128)}, f32[256,256]{1,0:T(8,128)S(1)}, u32[]{:S(2)}, u32[]{:S(2)}) collective-permute-start(f32[256,256]{1,0:T(8,128)} %copy-done.8), channel_id=1, source_target_pairs={{0,12},{1,13},{2,14},{3,15},{4,0},{5,1},{6,2},{7,3},{8,4},{9,5},{1... | collective-permute-start | bytes 786440 | tf_op jit(solution)/shard_map/ppermute | solution.py:280
  99.7 2.5 %collective-permute-start.12 = (f32[256,256]{1,0:T(8,128)}, f32[256,256]{1,0:T(8,128)S(1)}, u32[]{:S(2)}, u32[]{:S(2)}) collective-permute-start(f32[256,256]{1,0:T(8,128)} %copy-done.7), channel_id=1, source_target_pairs={{0,8},{1,9},{2,10},{3,11},{4,12},{5,13},{6,14},{7,15},{8,0},{9,1},... | collective-permute-start | bytes 786440 | tf_op jit(solution)/shard_map/ppermute | solution.py:280
  102.1 1.6 %collective-permute-done.14 = f32[256,256]{1,0:T(8,128)S(1)} collective-permute-done((f32[256,256]{1,0:T(8,128)}, f32[256,256]{1,0:T(8,128)S(1)}, u32[]{:S(2)}, u32[]{:S(2)}) %collective-permute-start.14) | collective-permute-done | bytes 262176 | tf_op jit(solution)/shard_map/ppermute | solution.py:280
  105.0 2.1 %collective-permute-done.16 = f32[256,256]{1,0:T(8,128)S(1)} collective-permute-done((f32[256,256]{1,0:T(8,128)S(1)}, f32[256,256]{1,0:T(8,128)S(1)}, u32[]{:S(2)}, u32[]{:S(2)}) %collective-permute-start.16) | collective-permute-done | bytes 262176 | tf_op jit(solution)/shard_map/ppermute | solution.py:280
  107.2 11.4 %collective-permute-start.17 = (f32[256,256]{1,0:T(8,128)S(1)}, f32[256,256]{1,0:T(8,128)S(1)}, u32[]{:S(2)}, u32[]{:S(2)}) collective-permute-start(f32[256,256]{1,0:T(8,128)S(1)} %add_add_fusion), channel_id=1, source_target_pairs={{0,16},{1,17},{2,18},{3,19},{4,20},{5,21},{6,22},{7,23},{8,24},{9,... | collective-permute-start | bytes 786440 | tf_op jit(solution)/shard_map/ppermute | solution.py:284
  118.6 16.0 %collective-permute-done.17.got_ref = f32[256,256]{1,0:T(8,128)S(1)} collective-permute-done((f32[256,256]{1,0:T(8,128)S(1)}, f32[256,256]{1,0:T(8,128)S(1)}, u32[]{:S(2)}, u32[]{:S(2)}) %collective-permute-start.17) | collective-permute-done | bytes 262176 | tf_op jit(solution)/shard_map/ppermute | solution.py:284
  135.3 3.2 %collective-permute-start.19 = (bf16[192,256]{1,0:T(8,128)(2,1)S(1)}, bf16[192,256]{1,0:T(8,128)(2,1)S(1)}, u32[]{:S(2)}, u32[]{:S(2)}) collective-permute-start(bf16[192,256]{1,0:T(8,128)(2,1)S(1)} %get-tuple-element.57), channel_id=1, source_target_pairs={{0,3},{1,0},{2,1},{3,2},{4,7},{5,4},{6,5},{7,6},{8,11},{9,8},{10,9... | collective-permute-start | bytes 294920 | tf_op jit(solution)/shard_map/ppermute | solution.py:272
  140.7 4.0 %collective-permute-done.20.f2 = bf16[192,256]{1,0:T(8,128)(2,1)S(1)} collective-permute-done((bf16[192,256]{1,0:T(8,128)(2,1)S(1)}, bf16[192,256]{1,0:T(8,128)(2,1)S(1)}, u32[]{:S(2)}, u32[]{:S(2)}) %collective-permute-start.20) | collective-permute-done | bytes 98336 | tf_op jit(solution)/shard_map/ppermute | solution.py:272
  145.7 1.3 unpack_small.1
  (87 shorter events, 31.6 us)
Async XLA Ops:
  5.0 6.4 %collective-permute-start = (bf16[192,256]{1,0:T(8,128)(2,1)}, bf16[192,256]{1,0:T(8,128)(2,1)S(1)}, u32[]{:S(2)}, u32[]{:S(2)}) collective-permute-start(bf16[192,256]{1,0:T(8,128)(2,1)} %get-tuple-element.36), channel_id=1, source_target_pairs={{0,1},{1,2},{2,3},{3,0},{4,5},{5,6},{6,7},{7,4},{8,9},{9,10},{10,1... | collective-permute-start | bytes 294920 | tf_op jit(solution)/shard_map/ppermute | solution.py:272
  6.6 7.6 %collective-permute-start.1 = (bf16[192,256]{1,0:T(8,128)(2,1)}, bf16[192,256]{1,0:T(8,128)(2,1)S(1)}, u32[]{:S(2)}, u32[]{:S(2)}) collective-permute-start(bf16[192,256]{1,0:T(8,128)(2,1)} %get-tuple-element.37), channel_id=1, source_target_pairs={{0,2},{1,3},{2,0},{3,1},{4,6},{5,7},{6,4},{7,5},{8,10},{9,11},{10,... | collective-permute-start | bytes 294920 | tf_op jit(solution)/shard_map/ppermute | solution.py:272
  9.3 4.8 %collective-permute-start.2 = (bf16[192,256]{1,0:T(8,128)(2,1)}, bf16[192,256]{1,0:T(8,128)(2,1)S(1)}, u32[]{:S(2)}, u32[]{:S(2)}) collective-permute-start(bf16[192,256]{1,0:T(8,128)(2,1)} %get-tuple-element.38), channel_id=1, source_target_pairs={{0,3},{1,0},{2,1},{3,2},{4,7},{5,4},{6,5},{7,6},{8,11},{9,8},{10,9... | collective-permute-start | bytes 294920 | tf_op jit(solution)/shard_map/ppermute | solution.py:272
  18.1 31.2 %all-to-all-start = ((bf16[4,128,1280]{2,1,0:T(8,128)(2,1)}), bf16[4,128,1280]{2,1,0:T(8,128)(2,1)S(1)}, u32[]{:S(2)}, u32[]{:S(2)}) async-start(bf16[4,128,1280]{2,1,0:T(8,128)(2,1)} %copy-done.1), calls=%async_computation | async-start | bytes 2621440 | tf_op jit(solution)/shard_map/all_to_all | solution.py:276
  22.1 14.8 %collective-permute-start.4 = (bf16[256,256]{1,0:T(8,128)(2,1)S(1)}, bf16[256,256]{1,0:T(8,128)(2,1)S(1)}, u32[]{:S(2)}, u32[]{:S(2)}) collective-permute-start(bf16[256,256]{1,0:T(8,128)(2,1)S(1)} %get-tuple-element.42.l0), channel_id=1, source_target_pairs={{0,16},{1,17},{2,18},{3,19},{4,20},{5,21},{6,22},{7,23},{8,24},{9,... | collective-permute-start | bytes 393224 | tf_op jit(solution)/shard_map/ppermute | solution.py:284
  28.4 9.8 %collective-permute-start.10 = (bf16[256,256]{1,0:T(8,128)(2,1)S(1)}, bf16[256,256]{1,0:T(8,128)(2,1)S(1)}, u32[]{:S(2)}, u32[]{:S(2)}) collective-permute-start(bf16[256,256]{1,0:T(8,128)(2,1)S(1)} %get-tuple-element.42.l0), channel_id=1, source_target_pairs={{0,12},{1,13},{2,14},{3,15},{4,0},{5,1},{6,2},{7,3},{8,4},{9,5},{1... | collective-permute-start | bytes 393224 | tf_op jit(solution)/shard_map/ppermute | solution.py:280
  31.4 8.3 %collective-permute-start.9 = (bf16[256,256]{1,0:T(8,128)(2,1)S(1)}, bf16[256,256]{1,0:T(8,128)(2,1)S(1)}, u32[]{:S(2)}, u32[]{:S(2)}) collective-permute-start(bf16[256,256]{1,0:T(8,128)(2,1)S(1)} %get-tuple-element.42.l0), channel_id=1, source_target_pairs={{0,8},{1,9},{2,10},{3,11},{4,12},{5,13},{6,14},{7,15},{8,0},{9,1},... | collective-permute-start | bytes 393224 | tf_op jit(solution)/shard_map/ppermute | solution.py:280
  32.1 11.7 %collective-permute-start.3 = (bf16[384,256]{1,0:T(8,128)(2,1)S(1)}, bf16[384,256]{1,0:T(8,128)(2,1)S(1)}, u32[]{:S(2)}, u32[]{:S(2)}) collective-permute-start(bf16[384,256]{1,0:T(8,128)(2,1)S(1)} %get-tuple-element.41), channel_id=1, source_target_pairs={{0,4},{1,5},{2,6},{3,7},{4,8},{5,9},{6,10},{7,11},{8,12},{9,13},{1... | collective-permute-start | bytes 589832 | tf_op jit(solution)/shard_map/ppermute | solution.py:289
  34.9 8.1 %collective-permute-start.8 = (bf16[256,256]{1,0:T(8,128)(2,1)S(1)}, bf16[256,256]{1,0:T(8,128)(2,1)S(1)}, u32[]{:S(2)}, u32[]{:S(2)}) collective-permute-start(bf16[256,256]{1,0:T(8,128)(2,1)S(1)} %get-tuple-element.42.l0), channel_id=1, source_target_pairs={{0,4},{1,5},{2,6},{3,7},{4,8},{5,9},{6,10},{7,11},{8,12},{9,13},{1... | collective-permute-start | bytes 393224 | tf_op jit(solution)/shard_map/ppermute | solution.py:280
  36.9 7.5 %collective-permute-start.7 = (bf16[256,256]{1,0:T(8,128)(2,1)S(1)}, bf16[256,256]{1,0:T(8,128)(2,1)S(1)}, u32[]{:S(2)}, u32[]{:S(2)}) collective-permute-start(bf16[256,256]{1,0:T(8,128)(2,1)S(1)} %collective-permute-done.4.h0), channel_id=1, source_target_pairs={{0,12},{1,13},{2,14},{3,15},{4,0},{5,1},{6,2},{7,3},{8,4},{9,5},{1... | collective-permute-start | bytes 393224 | tf_op jit(solution)/shard_map/ppermute | solution.py:280
  38.9 9.0 %collective-permute-start.6 = (bf16[256,256]{1,0:T(8,128)(2,1)S(1)}, bf16[256,256]{1,0:T(8,128)(2,1)S(1)}, u32[]{:S(2)}, u32[]{:S(2)}) collective-permute-start(bf16[256,256]{1,0:T(8,128)(2,1)S(1)} %collective-permute-done.4.h0), channel_id=1, source_target_pairs={{0,8},{1,9},{2,10},{3,11},{4,12},{5,13},{6,14},{7,15},{8,0},{9,1},... | collective-permute-start | bytes 393224 | tf_op jit(solution)/shard_map/ppermute | solution.py:280
  40.4 8.2 %collective-permute-start.5 = (bf16[256,256]{1,0:T(8,128)(2,1)S(1)}, bf16[256,256]{1,0:T(8,128)(2,1)S(1)}, u32[]{:S(2)}, u32[]{:S(2)}) collective-permute-start(bf16[256,256]{1,0:T(8,128)(2,1)S(1)} %collective-permute-done.4.h0), channel_id=1, source_target_pairs={{0,4},{1,5},{2,6},{3,7},{4,8},{5,9},{6,10},{7,11},{8,12},{9,13},{1... | collective-permute-start | bytes 393224 | tf_op jit(solution)/shard_map/ppermute | solution.py:280
  87.3 8.0 %collective-permute-start.15 = (f32[256,256]{1,0:T(8,128)}, f32[256,256]{1,0:T(8,128)}, u32[]{:S(2)}, u32[]{:S(2)}) collective-permute-start(f32[256,256]{1,0:T(8,128)} %get-tuple-element.53), channel_id=1, source_target_pairs={{0,4},{1,5},{2,6},{3,7},{4,8},{5,9},{6,10},{7,11},{8,12},{9,13},{1... | collective-permute-start | bytes 786440 | tf_op jit(solution)/shard_map/ppermute | solution.py:280
  88.6 58.5 %all-to-all-start.1 = ((bf16[4,128,1280]{2,1,0:T(8,128)(2,1)}), bf16[4,128,1280]{2,1,0:T(8,128)(2,1)S(1)}, u32[]{:S(2)}, u32[]{:S(2)}) async-start(bf16[4,128,1280]{2,1,0:T(8,128)(2,1)} %get-tuple-element.43), calls=%async_computation.1 | async-start | bytes 2621440 | tf_op jit(solution)/shard_map/all_to_all | solution.py:276
  93.2 10.4 %collective-permute-start.14 = (f32[256,256]{1,0:T(8,128)}, f32[256,256]{1,0:T(8,128)S(1)}, u32[]{:S(2)}, u32[]{:S(2)}) collective-permute-start(f32[256,256]{1,0:T(8,128)} %copy-done.9), channel_id=1, source_target_pairs={{0,12},{1,13},{2,14},{3,15},{4,0},{5,1},{6,2},{7,3},{8,4},{9,5},{1... | collective-permute-start | bytes 786440 | tf_op jit(solution)/shard_map/ppermute | solution.py:280
  96.3 10.8 %collective-permute-start.16 = (f32[256,256]{1,0:T(8,128)S(1)}, f32[256,256]{1,0:T(8,128)S(1)}, u32[]{:S(2)}, u32[]{:S(2)}) collective-permute-start(f32[256,256]{1,0:T(8,128)S(1)} %add.16), channel_id=1, source_target_pairs={{0,4},{1,5},{2,6},{3,7},{4,8},{5,9},{6,10},{7,11},{8,12},{9,13},{1... | collective-permute-start | bytes 786440 | tf_op jit(solution)/shard_map/ppermute | solution.py:280
  97.6 21.0 %collective-permute-start.11 = (f32[256,256]{1,0:T(8,128)}, f32[256,256]{1,0:T(8,128)S(1)}, u32[]{:S(2)}, u32[]{:S(2)}) collective-permute-start(f32[256,256]{1,0:T(8,128)} %copy-done.8), channel_id=1, source_target_pairs={{0,12},{1,13},{2,14},{3,15},{4,0},{5,1},{6,2},{7,3},{8,4},{9,5},{1... | collective-permute-start | bytes 786440 | tf_op jit(solution)/shard_map/ppermute | solution.py:280
  99.7 19.0 %collective-permute-start.12 = (f32[256,256]{1,0:T(8,128)}, f32[256,256]{1,0:T(8,128)S(1)}, u32[]{:S(2)}, u32[]{:S(2)}) collective-permute-start(f32[256,256]{1,0:T(8,128)} %copy-done.7), channel_id=1, source_target_pairs={{0,8},{1,9},{2,10},{3,11},{4,12},{5,13},{6,14},{7,15},{8,0},{9,1},... | collective-permute-start | bytes 786440 | tf_op jit(solution)/shard_map/ppermute | solution.py:280
  102.1 16.5 %collective-permute-start.13 = (f32[256,256]{1,0:T(8,128)S(1)}, f32[256,256]{1,0:T(8,128)S(1)}, u32[]{:S(2)}, u32[]{:S(2)}) collective-permute-start(f32[256,256]{1,0:T(8,128)S(1)} %copy-done.6), channel_id=1, source_target_pairs={{0,4},{1,5},{2,6},{3,7},{4,8},{5,9},{6,10},{7,11},{8,12},{9,13},{1... | collective-permute-start | bytes 786440 | tf_op jit(solution)/shard_map/ppermute | solution.py:280
  103.7 14.9 %collective-permute-start.18 = (f32[384,256]{1,0:T(8,128)S(1)}, f32[384,256]{1,0:T(8,128)S(1)}, u32[]{:S(2)}, u32[]{:S(2)}) collective-permute-start(f32[384,256]{1,0:T(8,128)S(1)} %get-tuple-element.55), channel_id=1, source_target_pairs={{4,0},{5,1},{6,2},{7,3},{8,4},{9,5},{10,6},{11,7},{12,8},{13,9},{1... | collective-permute-start | bytes 1179656 | tf_op jit(solution)/shard_map/ppermute | solution.py:289
  107.2 27.5 %collective-permute-start.17 = (f32[256,256]{1,0:T(8,128)S(1)}, f32[256,256]{1,0:T(8,128)S(1)}, u32[]{:S(2)}, u32[]{:S(2)}) collective-permute-start(f32[256,256]{1,0:T(8,128)S(1)} %add_add_fusion), channel_id=1, source_target_pairs={{0,16},{1,17},{2,18},{3,19},{4,20},{5,21},{6,22},{7,23},{8,24},{9,... | collective-permute-start | bytes 786440 | tf_op jit(solution)/shard_map/ppermute | solution.py:284
  135.3 5.4 %collective-permute-start.19 = (bf16[192,256]{1,0:T(8,128)(2,1)S(1)}, bf16[192,256]{1,0:T(8,128)(2,1)S(1)}, u32[]{:S(2)}, u32[]{:S(2)}) collective-permute-start(bf16[192,256]{1,0:T(8,128)(2,1)S(1)} %get-tuple-element.57), channel_id=1, source_target_pairs={{0,3},{1,0},{2,1},{3,2},{4,7},{5,4},{6,5},{7,6},{8,11},{9,8},{10,9... | collective-permute-start | bytes 294920 | tf_op jit(solution)/shard_map/ppermute | solution.py:272
  138.5 6.2 %collective-permute-start.20 = (bf16[192,256]{1,0:T(8,128)(2,1)S(1)}, bf16[192,256]{1,0:T(8,128)(2,1)S(1)}, u32[]{:S(2)}, u32[]{:S(2)}) collective-permute-start(bf16[192,256]{1,0:T(8,128)(2,1)S(1)} %get-tuple-element.58), channel_id=1, source_target_pairs={{0,2},{1,3},{2,0},{3,1},{4,6},{5,7},{6,4},{7,5},{8,10},{9,11},{10,... | collective-permute-start | bytes 294920 | tf_op jit(solution)/shard_map/ppermute | solution.py:272
  139.1 6.6 %collective-permute-start.21 = (bf16[192,256]{1,0:T(8,128)(2,1)S(1)}, bf16[192,256]{1,0:T(8,128)(2,1)S(1)}, u32[]{:S(2)}, u32[]{:S(2)}) collective-permute-start(bf16[192,256]{1,0:T(8,128)(2,1)S(1)} %get-tuple-element.59), channel_id=1, source_target_pairs={{0,1},{1,2},{2,3},{3,0},{4,5},{5,6},{6,7},{7,4},{8,9},{9,10},{10,1... | collective-permute-start | bytes 294920 | tf_op jit(solution)/shard_map/ppermute | solution.py:272
  (27 other events, 109.2 us)

commit v6 on v5

--- a/solution.py
+++ b/solution.py
@@ -36,10 +36,10 @@
 
 
 def attention_kernel(
-    len_ref, where_ref, q_all, s0, s1, s2, s3, before_ref, h0, h1, h2, h3, l0, l1, l2, l3,
+    len_ref, where_ref, q_in, s0, s1, s2, s3, before_in, h0, h1, h2, h3, l0, l1, l2, l3,
     o_ref, g0, g1, g2, g3, g4, g5, g6, g7, back_grad_ref, own_grad_ref,
     key2, value1, key_t, value_t, s_first, s_second, p_first, p_second,
-    grad2_first, grad2_second, rows_first, rows_second, key_sum, value_sum,
+    grad2_first, grad2_second, rows_first, rows_second, key_sum, value_sum, q_all, staged, sems,
 ):
     base, x = where_ref[0], where_ref[1]
     all_rows = PROMPT_ROWS + BACK + OWN_ROWS
@@ -49,12 +49,22 @@
         key2[at, 128:] = source[:, :128]
         value1[at, :128] = source[:, 128:]
 
+    copies = []
+
+    def load(source, target):
+        copies.append(pltpu.make_async_copy(source, target, sems.at[len(copies)]))
+        copies[-1].start()
+
     for i, source in enumerate((h2, h1, h0, h3, l2, l1, l0, l3)):
-        place(slice(i * 256, i * 256 + 256), source)
-    place(slice(PROMPT_ROWS, PROMPT_ROWS + BACK), before_ref)
+        load(source, staged.at[i * 256 : i * 256 + 256, :])
+    load(before_in, staged.at[PROMPT_ROWS : PROMPT_ROWS + BACK, :])
     for d, source in enumerate((s0, s1, s2, s3)):
         first = PROMPT_ROWS + BACK + lax.rem(x + 4 - d, 4) * 128
-        place(pl.ds(pl.multiple_of(first, 128), 128), source.at[64:192, :])
+        load(source.at[64:192, :], staged.at[pl.ds(pl.multiple_of(first, 128), 128), :])
+    load(q_in, q_all)
+    for copy in copies:
+        copy.wait()
+    place(slice(0, all_rows), staged)
     value1[:, 128:] = jnp.ones((all_rows, 128), jnp.bfloat16)
     value_t[128:, :] = jnp.ones((16, all_rows), jnp.bfloat16)
     for c in range(0, all_rows, 128):
@@ -161,16 +171,13 @@
         target[:, 128:] = value_sum[first:last, :]
 
 
-def call(body, scalars, operands, outs, name, scratch=(), limit=24, cost=None, space=pltpu.VMEM, extra=(), passed={}):
+def call(body, scalars, operands, outs, name, scratch=(), limit=24, cost=None, space=pltpu.VMEM, extra=()):
     smem = pl.BlockSpec(memory_space=pltpu.SMEM)
     return pl.pallas_call(
         body,
         in_specs=[smem] * len(scalars) + [pl.BlockSpec(memory_space=space)] * len(operands)
         + [pl.BlockSpec(memory_space=pl.ANY)] * len(extra),
-        out_specs=[
-            pl.BlockSpec(memory_space=pl.ANY if i in passed.values() else pltpu.VMEM) for i in range(len(outs))
-        ],
-        input_output_aliases=passed,
+        out_specs=[pl.BlockSpec(memory_space=pltpu.VMEM)] * len(outs),
         out_shape=[jax.ShapeDtypeStruct(shape, dtype) for shape, dtype in outs],
         scratch_shapes=list(scratch),
         compiler_params=pltpu.CompilerParams(vmem_limit_bytes=limit * 1024 * 1024),
@@ -202,8 +209,11 @@
             pltpu.VMEM((ROWS, 128), bf16),
             pltpu.VMEM((rows, 128), f32),
             pltpu.VMEM((rows, 128), f32),
+            pltpu.VMEM((4, 128, 2 * WIDE), bf16),
+            pltpu.VMEM((rows, 256), bf16),
+            pltpu.SemaphoreType.DMA((14,)),
         ],
-        limit=32,
+        space=pl.ANY, limit=60,
         cost=pl.CostEstimate(flops=flops, bytes_accessed=8_000_000, transcendentals=flops // 1536),
     )
 
@@ -228,7 +238,7 @@
         copy.wait()
 
 
-def collect_kernel(where_ref, s0, s1, s2, s3, rows_in, mine_ref, ahead_ref, rows_out):
+def collect_kernel(where_ref, s0, s1, s2, s3, mine_ref, ahead_ref):
     x = where_ref[1]
     for d, source in enumerate((s0, s1, s2, s3)):
         mine_ref[d * 64 : d * 64 + 64, :] = source[:64, :]
@@ -251,6 +261,10 @@
         target[64:, :] = (own_ref[block_at(x, d), :] + extra).astype(jnp.bfloat16)
 
 
+def far_sum_kernel(a, b, c, after, out_ref):
+    out_ref[...] = a[...] + b[...] + c[...]
+
+
 def unpack_rows_kernel(o_ref, out_ref, dq_ref):
     for h in range(KV_HEADS):
         at = slice(h * WIDE, h * WIDE + WIDE)
@@ -300,11 +314,9 @@
         scratch=[pltpu.SemaphoreType.DMA((24,))], space=pl.ANY, limit=60,
     )
     s = [s[0]] + [along_x(s[d], d) for d in (1, 2, 3)]
-    mine, ahead, q_all = call(
-        collect_kernel, (where,), s, [((256, 256), bf16), ((BACK, 256), bf16), (q_all.shape, bf16)], "collect",
-        extra=(q_all,), passed={5: 2},
-    )
+    *s, q_all = lax.optimization_barrier((*s, q_all))
     q_all = exchange_x(q_all)
+    mine, ahead = call(collect_kernel, (where,), s, [((256, 256), bf16), ((BACK, 256), bf16)], "collect")
     far = along_z(mine)
     near_keys = [mine] + [along_y(mine, d) for d in (1, 2, 3)]
     before = along_rows(ahead, 1)
@@ -316,9 +328,10 @@
 
     through, minus = along_y(h2, 1), along_y(h1, -1)
     plus = along_y(h3 + through, 1)
-    got = along_z(h0 + minus + plus)
+    back = along_rows(back_grad, -1)
+    (got,) = call(far_sum_kernel, (), (h0, minus, plus), [((256, 256), f32)], "far_sum", extra=(back,))
+    got = along_z(got)
     one, two, three = along_y(l1, -1), along_y(l2, -2), along_y(l3, 1)
-    back = along_rows(back_grad, -1)
 
     attn_out, q_grad = call(
         unpack_rows_kernel, (), (exchange_x(o),), [((rows, HEADS * HEAD_DIM), bf16)] * 2, "unpack_rows"

time: 149 us -> 138 us (0.926)
  the two profiles are of different devices: /device:TPU:32 before, /device:TPU:56 now
where the time goes in v6:
time: 138 us
  starting transfers between devices  49.8 us (36%)
  waiting for transfers between devices  44.6 us (32%)
  Pallas kernels  39.9 us (29%)
  local copies, waits for them, and re-layouts  1.74 us (1%)
    pallas_call x7, Pallas kernels, call(): pl.pallas_call(body, in_specs=[smem] * len(scalars) + [pl.BlockSpec(memor...  39.9 us
    ppermute x12, starting transfers between devices, along_y(): lax.ppermute(value, 'seq', [(i, i // 16 * 16 + (i + 4 * step) % 16) for i...  17.9 us
    ppermute x12, waiting for transfers between devices, along_y(): lax.ppermute(value, 'seq', [(i, i // 16 * 16 + (i + 4 * step) % 16) for i...  17.6 us
    ppermute x2, waiting for transfers between devices, along_z(): return lax.ppermute(value, 'seq', [(i, (i + 16) % 32) for i in range(32)])  11.2 us
    ppermute x6, starting transfers between devices, along_x(): lax.ppermute(value, 'seq', [(i, i // 4 * 4 + (i + step) % 4) for i in ran...  10.5 us
    ppermute x6, waiting for transfers between devices, along_x(): lax.ppermute(value, 'seq', [(i, i // 4 * 4 + (i + step) % 4) for i in ran...  8.9 us
    all_to_all x2, starting transfers between devices, exchange_x(): lax.all_to_all(value, 'seq', 0, 0, axis_index_groups=X_GROUPS, tiled=True)  8.71 us
    ppermute x2, waiting for transfers between devices, along_rows(): return lax.ppermute(value, 'seq', [(i, j) for i, j in pairs if 0 <= j < 32])  6.88 us
  transfers between devices with their start and end apart: 24, of which 13 were waited for; matrix products, arithmetic and copies ran while one was open for 0% of the time, Pallas kernels for 2%

profile of v6, /device:TPU:56, one launch (start us, length us, event | category | flops | bytes accessed | tf_op | source)
XLA Modules:
  0.0 137.7 jit_solution(11909827248776398345)
XLA Ops:
  1.3 3.7 %pack.1 = (bf16[192,256]{1,0:T(8,128)(2,1)}, bf16[192,256]{1,0:T(8,128)(2,1)}, bf16[192,256]{1,0:T(8,128)(2,1)}, bf16[192,256]{1,0:T(8,128)(2,1)}, bf16[4,128,1280]{2,1,0:T(8,128)(2,1)}) custom-call(s32[2]{0:T(128)} %pad_add_fusion.where_ref, bf16[64,512]{1,0:T(8,128)(2,1)} %pk.1, bf16[64,512]{1,0:T(8,128)(2,1)} %pv.1, bf16[128,512]{1,0:T(8,128)(2,1)} %k.1, ...), custom_call_target="tpu_custom_call" | custom-call | tf_op jit(solution)/shard_map/pack/pallas_call | solution.py:176
  5.0 1.6 %collective-permute-start = (bf16[192,256]{1,0:T(8,128)(2,1)}, bf16[192,256]{1,0:T(8,128)(2,1)S(1)}, u32[]{:S(2)}, u32[]{:S(2)}) collective-permute-start(bf16[192,256]{1,0:T(8,128)(2,1)} %get-tuple-element.40), channel_id=1, source_target_pairs={{0,1},{1,2},{2,3},{3,0},{4,5},{5,6},{6,7},{7,4},{8,9},{9,10},{10,1... | collective-permute-start | bytes 294920 | tf_op jit(solution)/shard_map/ppermute | solution.py:286
  6.5 2.7 %collective-permute-start.1 = (bf16[192,256]{1,0:T(8,128)(2,1)}, bf16[192,256]{1,0:T(8,128)(2,1)S(1)}, u32[]{:S(2)}, u32[]{:S(2)}) collective-permute-start(bf16[192,256]{1,0:T(8,128)(2,1)} %get-tuple-element.41), channel_id=1, source_target_pairs={{0,2},{1,3},{2,0},{3,1},{4,6},{5,7},{6,4},{7,5},{8,10},{9,11},{10,... | collective-permute-start | bytes 294920 | tf_op jit(solution)/shard_map/ppermute | solution.py:286
  11.3 2.8 %collective-permute-done.1.s2 = bf16[192,256]{1,0:T(8,128)(2,1)S(1)} collective-permute-done((bf16[192,256]{1,0:T(8,128)(2,1)}, bf16[192,256]{1,0:T(8,128)(2,1)S(1)}, u32[]{:S(2)}, u32[]{:S(2)}) %collective-permute-start.1) | collective-permute-done | bytes 98336 | tf_op jit(solution)/shard_map/ppermute | solution.py:286
  14.1 4.0 %all-to-all-start = ((bf16[4,128,1280]{2,1,0:T(8,128)(2,1)}), bf16[4,128,1280]{2,1,0:T(8,128)(2,1)S(1)}, u32[]{:S(2)}, u32[]{:S(2)}) async-start(bf16[4,128,1280]{2,1,0:T(8,128)(2,1)} %get-tuple-element.44), calls=%async_computation | async-start | bytes 2621440 | tf_op jit(solution)/shard_map/all_to_all | solution.py:290
  18.8 6.4 %collective-permute-start.4 = (bf16[256,256]{1,0:T(8,128)(2,1)S(1)}, bf16[256,256]{1,0:T(8,128)(2,1)S(1)}, u32[]{:S(2)}, u32[]{:S(2)}) collective-permute-start(bf16[256,256]{1,0:T(8,128)(2,1)S(1)} %get-tuple-element.50.l0), channel_id=1, source_target_pairs={{0,16},{1,17},{2,18},{3,19},{4,20},{5,21},{6,22},{7,23},{8,24},{9,... | collective-permute-start | bytes 393224 | tf_op jit(solution)/shard_map/ppermute | solution.py:298
  26.8 3.6 %collective-permute-start.3 = (bf16[384,256]{1,0:T(8,128)(2,1)S(1)}, bf16[384,256]{1,0:T(8,128)(2,1)S(1)}, u32[]{:S(2)}, u32[]{:S(2)}) collective-permute-start(bf16[384,256]{1,0:T(8,128)(2,1)S(1)} %get-tuple-element.49), channel_id=1, source_target_pairs={{0,4},{1,5},{2,6},{3,7},{4,8},{5,9},{6,10},{7,11},{8,12},{9,13},{1... | collective-permute-start | bytes 589832 | tf_op jit(solution)/shard_map/ppermute | solution.py:303
  32.9 2.4 %collective-permute-start.6 = (bf16[256,256]{1,0:T(8,128)(2,1)S(1)}, bf16[256,256]{1,0:T(8,128)(2,1)S(1)}, u32[]{:S(2)}, u32[]{:S(2)}) collective-permute-start(bf16[256,256]{1,0:T(8,128)(2,1)S(1)} %collective-permute-done.4.h0), channel_id=1, source_target_pairs={{0,8},{1,9},{2,10},{3,11},{4,12},{5,13},{6,14},{7,15},{8,0},{9,1},... | collective-permute-start | bytes 393224 | tf_op jit(solution)/shard_map/ppermute | solution.py:294
  36.3 4.3 %collective-permute-done.8.l1 = bf16[256,256]{1,0:T(8,128)(2,1)S(1)} collective-permute-done((bf16[256,256]{1,0:T(8,128)(2,1)S(1)}, bf16[256,256]{1,0:T(8,128)(2,1)S(1)}, u32[]{:S(2)}, u32[]{:S(2)}) %collective-permute-start.8) | collective-permute-done | bytes 131104 | tf_op jit(solution)/shard_map/ppermute | solution.py:294
  40.7 3.0 %collective-permute-done.5.h1 = bf16[256,256]{1,0:T(8,128)(2,1)S(1)} collective-permute-done((bf16[256,256]{1,0:T(8,128)(2,1)S(1)}, bf16[256,256]{1,0:T(8,128)(2,1)S(1)}, u32[]{:S(2)}, u32[]{:S(2)}) %collective-permute-start.5) | collective-permute-done | bytes 131104 | tf_op jit(solution)/shard_map/ppermute | solution.py:294
  45.4 32.5 %attention.1 = (bf16[4,128,1280]{2,1,0:T(8,128)(2,1)}, f32[256,256]{1,0:T(8,128)}, f32[256,256]{1,0:T(8,128)}, f32[256,256]{1,0:T(8,128)}, f32[256,256]{1,0:T(8,...) custom-call(s32[16]{0:T(128)} %len_ref.1, ...), custom_call_target="tpu_custom_call" | custom-call | flops 10066329600 | bytes 8000000 | tf_op jit(solution)/shard_map/attention/pallas_call | solution.py:176
  78.0 4.7 %all-to-all-start.1 = ((bf16[4,128,1280]{2,1,0:T(8,128)(2,1)}), bf16[4,128,1280]{2,1,0:T(8,128)(2,1)S(1)}, u32[]{:S(2)}, u32[]{:S(2)}) async-start(bf16[4,128,1280]{2,1,0:T(8,128)(2,1)} %get-tuple-element.51), calls=%async_computation.1 | async-start | bytes 2621440 | tf_op jit(solution)/shard_map/all_to_all | solution.py:290
  84.0 2.6 %collective-permute-start.17 = (f32[384,256]{1,0:T(8,128)S(1)}, f32[384,256]{1,0:T(8,128)S(1)}, u32[]{:S(2)}, u32[]{:S(2)}) collective-permute-start(f32[384,256]{1,0:T(8,128)S(1)} %copy-done.12), channel_id=1, source_target_pairs={{4,0},{5,1},{6,2},{7,3},{8,4},{9,5},{10,6},{11,7},{12,8},{13,9},{1... | collective-permute-start | bytes 1179656 | tf_op jit(solution)/shard_map/ppermute | solution.py:303
  86.7 1.8 %collective-permute-start.14 = (f32[256,256]{1,0:T(8,128)S(1)}, f32[256,256]{1,0:T(8,128)S(1)}, u32[]{:S(2)}, u32[]{:S(2)}) collective-permute-start(f32[256,256]{1,0:T(8,128)S(1)} %copy-done.16), channel_id=1, source_target_pairs={{0,12},{1,13},{2,14},{3,15},{4,0},{5,1},{6,2},{7,3},{8,4},{9,5},{1... | collective-permute-start | bytes 786440 | tf_op jit(solution)/shard_map/ppermute | solution.py:294
  88.5 2.1 %collective-permute-done.15 = f32[256,256]{1,0:T(8,128)S(1)} collective-permute-done((f32[256,256]{1,0:T(8,128)S(1)}, f32[256,256]{1,0:T(8,128)S(1)}, u32[]{:S(2)}, u32[]{:S(2)}) %collective-permute-start.15) | collective-permute-done | bytes 262176 | tf_op jit(solution)/shard_map/ppermute | solution.py:294
  90.6 2.1 %collective-permute-start.16 = (f32[256,256]{1,0:T(8,128)S(1)}, f32[256,256]{1,0:T(8,128)S(1)}, u32[]{:S(2)}, u32[]{:S(2)}) collective-permute-start(f32[256,256]{1,0:T(8,128)S(1)} %add.9), channel_id=1, source_target_pairs={{0,4},{1,5},{2,6},{3,7},{4,8},{5,9},{6,10},{7,11},{8,12},{9,13},{1... | collective-permute-start | bytes 786440 | tf_op jit(solution)/shard_map/ppermute | solution.py:294
  93.2 2.1 %collective-permute-start.12 = (f32[256,256]{1,0:T(8,128)S(1)}, f32[256,256]{1,0:T(8,128)S(1)}, u32[]{:S(2)}, u32[]{:S(2)}) collective-permute-start(f32[256,256]{1,0:T(8,128)S(1)} %copy-done.14), channel_id=1, source_target_pairs={{0,8},{1,9},{2,10},{3,11},{4,12},{5,13},{6,14},{7,15},{8,0},{9,1},... | collective-permute-start | bytes 786440 | tf_op jit(solution)/shard_map/ppermute | solution.py:294
  95.3 6.5 %collective-permute-done.14.b = f32[256,256]{1,0:T(8,128)S(1)} collective-permute-done((f32[256,256]{1,0:T(8,128)S(1)}, f32[256,256]{1,0:T(8,128)S(1)}, u32[]{:S(2)}, u32[]{:S(2)}) %collective-permute-start.14) | collective-permute-done | bytes 262176 | tf_op jit(solution)/shard_map/ppermute | solution.py:294
  101.8 2.9 %collective-permute-start.13 = (f32[256,256]{1,0:T(8,128)S(1)}, f32[256,256]{1,0:T(8,128)S(1)}, u32[]{:S(2)}, u32[]{:S(2)}) collective-permute-start(f32[256,256]{1,0:T(8,128)S(1)} %copy-done.13), channel_id=1, source_target_pairs={{0,4},{1,5},{2,6},{3,7},{4,8},{5,9},{6,10},{7,11},{8,12},{9,13},{1... | collective-permute-start | bytes 786440 | tf_op jit(solution)/shard_map/ppermute | solution.py:294
  104.8 6.9 %collective-permute-done.17.after.back_ref = f32[384,256]{1,0:T(8,128)S(1)} collective-permute-done((f32[384,256]{1,0:T(8,128)S(1)}, f32[384,256]{1,0:T(8,128)S(1)}, u32[]{:S(2)}, u32[]{:S(2)}) %collective-permute-start.17) | collective-permute-done | bytes 393248 | tf_op jit(solution)/shard_map/ppermute | solution.py:303
  113.1 11.1 %collective-permute-done.18.got_ref = f32[256,256]{1,0:T(8,128)S(1)} collective-permute-done((f32[256,256]{1,0:T(8,128)S(1)}, f32[256,256]{1,0:T(8,128)S(1)}, u32[]{:S(2)}, u32[]{:S(2)}) %collective-permute-start.18) | collective-permute-done | bytes 262176 | tf_op jit(solution)/shard_map/ppermute | solution.py:298
  124.9 3.1 %collective-permute-start.19 = (bf16[192,256]{1,0:T(8,128)(2,1)S(1)}, bf16[192,256]{1,0:T(8,128)(2,1)S(1)}, u32[]{:S(2)}, u32[]{:S(2)}) collective-permute-start(bf16[192,256]{1,0:T(8,128)(2,1)S(1)} %get-tuple-element.65), channel_id=1, source_target_pairs={{0,3},{1,0},{2,1},{3,2},{4,7},{5,4},{6,5},{7,6},{8,11},{9,8},{10,9... | collective-permute-start | bytes 294920 | tf_op jit(solution)/shard_map/ppermute | solution.py:286
  129.6 2.0 %collective-permute-done.19.f1 = bf16[192,256]{1,0:T(8,128)(2,1)S(1)} collective-permute-done((bf16[192,256]{1,0:T(8,128)(2,1)S(1)}, bf16[192,256]{1,0:T(8,128)(2,1)S(1)}, u32[]{:S(2)}, u32[]{:S(2)}) %collective-permute-start.19) | collective-permute-done | bytes 98336 | tf_op jit(solution)/shard_map/ppermute | solution.py:286
  131.6 2.5 %collective-permute-done.20.f2 = bf16[192,256]{1,0:T(8,128)(2,1)S(1)} collective-permute-done((bf16[192,256]{1,0:T(8,128)(2,1)S(1)}, bf16[192,256]{1,0:T(8,128)(2,1)S(1)}, u32[]{:S(2)}, u32[]{:S(2)}) %collective-permute-start.20) | collective-permute-done | bytes 98336 | tf_op jit(solution)/shard_map/ppermute | solution.py:286
  (85 shorter events, 19.3 us)
Async XLA Ops:
  5.0 6.4 %collective-permute-start = (bf16[192,256]{1,0:T(8,128)(2,1)}, bf16[192,256]{1,0:T(8,128)(2,1)S(1)}, u32[]{:S(2)}, u32[]{:S(2)}) collective-permute-start(bf16[192,256]{1,0:T(8,128)(2,1)} %get-tuple-element.40), channel_id=1, source_target_pairs={{0,1},{1,2},{2,3},{3,0},{4,5},{5,6},{6,7},{7,4},{8,9},{9,10},{10,1... | collective-permute-start | bytes 294920 | tf_op jit(solution)/shard_map/ppermute | solution.py:286
  6.5 7.6 %collective-permute-start.1 = (bf16[192,256]{1,0:T(8,128)(2,1)}, bf16[192,256]{1,0:T(8,128)(2,1)S(1)}, u32[]{:S(2)}, u32[]{:S(2)}) collective-permute-start(bf16[192,256]{1,0:T(8,128)(2,1)} %get-tuple-element.41), channel_id=1, source_target_pairs={{0,2},{1,3},{2,0},{3,1},{4,6},{5,7},{6,4},{7,5},{8,10},{9,11},{10,... | collective-permute-start | bytes 294920 | tf_op jit(solution)/shard_map/ppermute | solution.py:286
  9.3 4.8 %collective-permute-start.2 = (bf16[192,256]{1,0:T(8,128)(2,1)}, bf16[192,256]{1,0:T(8,128)(2,1)S(1)}, u32[]{:S(2)}, u32[]{:S(2)}) collective-permute-start(bf16[192,256]{1,0:T(8,128)(2,1)} %get-tuple-element.42), channel_id=1, source_target_pairs={{0,3},{1,0},{2,1},{3,2},{4,7},{5,4},{6,5},{7,6},{8,11},{9,8},{10,9... | collective-permute-start | bytes 294920 | tf_op jit(solution)/shard_map/ppermute | solution.py:286
  14.1 29.6 %all-to-all-start = ((bf16[4,128,1280]{2,1,0:T(8,128)(2,1)}), bf16[4,128,1280]{2,1,0:T(8,128)(2,1)S(1)}, u32[]{:S(2)}, u32[]{:S(2)}) async-start(bf16[4,128,1280]{2,1,0:T(8,128)(2,1)} %get-tuple-element.44), calls=%async_computation | async-start | bytes 2621440 | tf_op jit(solution)/shard_map/all_to_all | solution.py:290
  18.8 13.2 %collective-permute-start.4 = (bf16[256,256]{1,0:T(8,128)(2,1)S(1)}, bf16[256,256]{1,0:T(8,128)(2,1)S(1)}, u32[]{:S(2)}, u32[]{:S(2)}) collective-permute-start(bf16[256,256]{1,0:T(8,128)(2,1)S(1)} %get-tuple-element.50.l0), channel_id=1, source_target_pairs={{0,16},{1,17},{2,18},{3,19},{4,20},{5,21},{6,22},{7,23},{8,24},{9,... | collective-permute-start | bytes 393224 | tf_op jit(solution)/shard_map/ppermute | solution.py:298
  25.2 7.8 %collective-permute-start.10 = (bf16[256,256]{1,0:T(8,128)(2,1)S(1)}, bf16[256,256]{1,0:T(8,128)(2,1)S(1)}, u32[]{:S(2)}, u32[]{:S(2)}) collective-permute-start(bf16[256,256]{1,0:T(8,128)(2,1)S(1)} %get-tuple-element.50.l0), channel_id=1, source_target_pairs={{0,12},{1,13},{2,14},{3,15},{4,0},{5,1},{6,2},{7,3},{8,4},{9,5},{1... | collective-permute-start | bytes 393224 | tf_op jit(solution)/shard_map/ppermute | solution.py:294
  25.9 9.4 %collective-permute-start.9 = (bf16[256,256]{1,0:T(8,128)(2,1)S(1)}, bf16[256,256]{1,0:T(8,128)(2,1)S(1)}, u32[]{:S(2)}, u32[]{:S(2)}) collective-permute-start(bf16[256,256]{1,0:T(8,128)(2,1)S(1)} %get-tuple-element.50.l0), channel_id=1, source_target_pairs={{0,8},{1,9},{2,10},{3,11},{4,12},{5,13},{6,14},{7,15},{8,0},{9,1},... | collective-permute-start | bytes 393224 | tf_op jit(solution)/shard_map/ppermute | solution.py:294
  26.8 13.8 %collective-permute-start.3 = (bf16[384,256]{1,0:T(8,128)(2,1)S(1)}, bf16[384,256]{1,0:T(8,128)(2,1)S(1)}, u32[]{:S(2)}, u32[]{:S(2)}) collective-permute-start(bf16[384,256]{1,0:T(8,128)(2,1)S(1)} %get-tuple-element.49), channel_id=1, source_target_pairs={{0,4},{1,5},{2,6},{3,7},{4,8},{5,9},{6,10},{7,11},{8,12},{9,13},{1... | collective-permute-start | bytes 589832 | tf_op jit(solution)/shard_map/ppermute | solution.py:303
  30.5 10.2 %collective-permute-start.8 = (bf16[256,256]{1,0:T(8,128)(2,1)S(1)}, bf16[256,256]{1,0:T(8,128)(2,1)S(1)}, u32[]{:S(2)}, u32[]{:S(2)}) collective-permute-start(bf16[256,256]{1,0:T(8,128)(2,1)S(1)} %get-tuple-element.50.l0), channel_id=1, source_target_pairs={{0,4},{1,5},{2,6},{3,7},{4,8},{5,9},{6,10},{7,11},{8,12},{9,13},{1... | collective-permute-start | bytes 393224 | tf_op jit(solution)/shard_map/ppermute | solution.py:294
  32.0 8.7 %collective-permute-start.7 = (bf16[256,256]{1,0:T(8,128)(2,1)S(1)}, bf16[256,256]{1,0:T(8,128)(2,1)S(1)}, u32[]{:S(2)}, u32[]{:S(2)}) collective-permute-start(bf16[256,256]{1,0:T(8,128)(2,1)S(1)} %collective-permute-done.4.h0), channel_id=1, source_target_pairs={{0,12},{1,13},{2,14},{3,15},{4,0},{5,1},{6,2},{7,3},{8,4},{9,5},{1... | collective-permute-start | bytes 393224 | tf_op jit(solution)/shard_map/ppermute | solution.py:294
  32.9 7.7 %collective-permute-start.6 = (bf16[256,256]{1,0:T(8,128)(2,1)S(1)}, bf16[256,256]{1,0:T(8,128)(2,1)S(1)}, u32[]{:S(2)}, u32[]{:S(2)}) collective-permute-start(bf16[256,256]{1,0:T(8,128)(2,1)S(1)} %collective-permute-done.4.h0), channel_id=1, source_target_pairs={{0,8},{1,9},{2,10},{3,11},{4,12},{5,13},{6,14},{7,15},{8,0},{9,1},... | collective-permute-start | bytes 393224 | tf_op jit(solution)/shard_map/ppermute | solution.py:294
  35.3 8.3 %collective-permute-start.5 = (bf16[256,256]{1,0:T(8,128)(2,1)S(1)}, bf16[256,256]{1,0:T(8,128)(2,1)S(1)}, u32[]{:S(2)}, u32[]{:S(2)}) collective-permute-start(bf16[256,256]{1,0:T(8,128)(2,1)S(1)} %collective-permute-done.4.h0), channel_id=1, source_target_pairs={{0,4},{1,5},{2,6},{3,7},{4,8},{5,9},{6,10},{7,11},{8,12},{9,13},{1... | collective-permute-start | bytes 393224 | tf_op jit(solution)/shard_map/ppermute | solution.py:294
  78.0 58.5 %all-to-all-start.1 = ((bf16[4,128,1280]{2,1,0:T(8,128)(2,1)}), bf16[4,128,1280]{2,1,0:T(8,128)(2,1)S(1)}, u32[]{:S(2)}, u32[]{:S(2)}) async-start(bf16[4,128,1280]{2,1,0:T(8,128)(2,1)} %get-tuple-element.51), calls=%async_computation.1 | async-start | bytes 2621440 | tf_op jit(solution)/shard_map/all_to_all | solution.py:290
  82.6 7.9 %collective-permute-start.15 = (f32[256,256]{1,0:T(8,128)S(1)}, f32[256,256]{1,0:T(8,128)S(1)}, u32[]{:S(2)}, u32[]{:S(2)}) collective-permute-start(f32[256,256]{1,0:T(8,128)S(1)} %copy-done.17), channel_id=1, source_target_pairs={{0,4},{1,5},{2,6},{3,7},{4,8},{5,9},{6,10},{7,11},{8,12},{9,13},{1... | collective-permute-start | bytes 786440 | tf_op jit(solution)/shard_map/ppermute | solution.py:294
  84.0 27.6 %collective-permute-start.17 = (f32[384,256]{1,0:T(8,128)S(1)}, f32[384,256]{1,0:T(8,128)S(1)}, u32[]{:S(2)}, u32[]{:S(2)}) collective-permute-start(f32[384,256]{1,0:T(8,128)S(1)} %copy-done.12), channel_id=1, source_target_pairs={{4,0},{5,1},{6,2},{7,3},{8,4},{9,5},{10,6},{11,7},{12,8},{13,9},{1... | collective-permute-start | bytes 1179656 | tf_op jit(solution)/shard_map/ppermute | solution.py:303
  86.7 15.2 %collective-permute-start.14 = (f32[256,256]{1,0:T(8,128)S(1)}, f32[256,256]{1,0:T(8,128)S(1)}, u32[]{:S(2)}, u32[]{:S(2)}) collective-permute-start(f32[256,256]{1,0:T(8,128)S(1)} %copy-done.16), channel_id=1, source_target_pairs={{0,12},{1,13},{2,14},{3,15},{4,0},{5,1},{6,2},{7,3},{8,4},{9,5},{1... | collective-permute-start | bytes 786440 | tf_op jit(solution)/shard_map/ppermute | solution.py:294
  90.6 21.0 %collective-permute-start.16 = (f32[256,256]{1,0:T(8,128)S(1)}, f32[256,256]{1,0:T(8,128)S(1)}, u32[]{:S(2)}, u32[]{:S(2)}) collective-permute-start(f32[256,256]{1,0:T(8,128)S(1)} %add.9), channel_id=1, source_target_pairs={{0,4},{1,5},{2,6},{3,7},{4,8},{5,9},{6,10},{7,11},{8,12},{9,13},{1... | collective-permute-start | bytes 786440 | tf_op jit(solution)/shard_map/ppermute | solution.py:294
  92.7 19.1 %collective-permute-start.11 = (f32[256,256]{1,0:T(8,128)S(1)}, f32[256,256]{1,0:T(8,128)S(1)}, u32[]{:S(2)}, u32[]{:S(2)}) collective-permute-start(f32[256,256]{1,0:T(8,128)S(1)} %copy-done.15), channel_id=1, source_target_pairs={{0,12},{1,13},{2,14},{3,15},{4,0},{5,1},{6,2},{7,3},{8,4},{9,5},{1... | collective-permute-start | bytes 786440 | tf_op jit(solution)/shard_map/ppermute | solution.py:294
  93.2 19.9 %collective-permute-start.12 = (f32[256,256]{1,0:T(8,128)S(1)}, f32[256,256]{1,0:T(8,128)S(1)}, u32[]{:S(2)}, u32[]{:S(2)}) collective-permute-start(f32[256,256]{1,0:T(8,128)S(1)} %copy-done.14), channel_id=1, source_target_pairs={{0,8},{1,9},{2,10},{3,11},{4,12},{5,13},{6,14},{7,15},{8,0},{9,1},... | collective-permute-start | bytes 786440 | tf_op jit(solution)/shard_map/ppermute | solution.py:294
  101.8 11.3 %collective-permute-start.13 = (f32[256,256]{1,0:T(8,128)S(1)}, f32[256,256]{1,0:T(8,128)S(1)}, u32[]{:S(2)}, u32[]{:S(2)}) collective-permute-start(f32[256,256]{1,0:T(8,128)S(1)} %copy-done.13), channel_id=1, source_target_pairs={{0,4},{1,5},{2,6},{3,7},{4,8},{5,9},{6,10},{7,11},{8,12},{9,13},{1... | collective-permute-start | bytes 786440 | tf_op jit(solution)/shard_map/ppermute | solution.py:294
  111.7 12.5 %collective-permute-start.18 = (f32[256,256]{1,0:T(8,128)S(1)}, f32[256,256]{1,0:T(8,128)S(1)}, u32[]{:S(2)}, u32[]{:S(2)}) collective-permute-start(f32[256,256]{1,0:T(8,128)S(1)} %far_sum.1), channel_id=1, source_target_pairs={{0,16},{1,17},{2,18},{3,19},{4,20},{5,21},{6,22},{7,23},{8,24},{9,... | collective-permute-start | bytes 786440 | tf_op jit(solution)/shard_map/ppermute | solution.py:298
  124.9 6.7 %collective-permute-start.19 = (bf16[192,256]{1,0:T(8,128)(2,1)S(1)}, bf16[192,256]{1,0:T(8,128)(2,1)S(1)}, u32[]{:S(2)}, u32[]{:S(2)}) collective-permute-start(bf16[192,256]{1,0:T(8,128)(2,1)S(1)} %get-tuple-element.65), channel_id=1, source_target_pairs={{0,3},{1,0},{2,1},{3,2},{4,7},{5,4},{6,5},{7,6},{8,11},{9,8},{10,9... | collective-permute-start | bytes 294920 | tf_op jit(solution)/shard_map/ppermute | solution.py:286
  128.0 6.2 %collective-permute-start.20 = (bf16[192,256]{1,0:T(8,128)(2,1)S(1)}, bf16[192,256]{1,0:T(8,128)(2,1)S(1)}, u32[]{:S(2)}, u32[]{:S(2)}) collective-permute-start(bf16[192,256]{1,0:T(8,128)(2,1)S(1)} %get-tuple-element.66), channel_id=1, source_target_pairs={{0,2},{1,3},{2,0},{3,1},{4,6},{5,7},{6,4},{7,5},{8,10},{9,11},{10,... | collective-permute-start | bytes 294920 | tf_op jit(solution)/shard_map/ppermute | solution.py:286
  128.8 6.4 %collective-permute-start.21 = (bf16[192,256]{1,0:T(8,128)(2,1)S(1)}, bf16[192,256]{1,0:T(8,128)(2,1)S(1)}, u32[]{:S(2)}, u32[]{:S(2)}) collective-permute-start(bf16[192,256]{1,0:T(8,128)(2,1)S(1)} %get-tuple-element.67), channel_id=1, source_target_pairs={{0,1},{1,2},{2,3},{3,0},{4,5},{5,6},{6,7},{7,4},{8,9},{9,10},{10,1... | collective-permute-start | bytes 294920 | tf_op jit(solution)/shard_map/ppermute | solution.py:286
  (26 other events, 337.6 us)

commit v7 on v6

--- a/solution.py
+++ b/solution.py
@@ -249,7 +249,7 @@
             ahead_ref[pl.ds(pl.multiple_of((block - 1) * 128, 128), 128), :] = source[64:, :]
 
 
-def final_sum_kernel(where_ref, n0, n1, n2, n3, got_ref, own_ref, back_ref, f0, f1, f2, f3):
+def final_sum_kernel(where_ref, n0, n1, n2, n3, got_ref, own_ref, crossing_ref, within_ref, f0, f1, f2, f3):
     x = where_ref[1]
     for d, target in enumerate((f0, f1, f2, f3)):
         at = slice(d * 64, d * 64 + 64)
@@ -257,7 +257,7 @@
         target[:64, :] = total.astype(jnp.bfloat16)
         block = lax.rem(x + 4 - d, 4)
         behind = pl.ds(pl.multiple_of(jnp.maximum(block - 1, 0) * 128, 128), 128)
-        extra = jnp.where(block > 0, back_ref[behind, :], 0.0)
+        extra = jnp.where(block > 0, crossing_ref[behind, :] + within_ref[behind, :], 0.0)
         target[64:, :] = (own_ref[block_at(x, d), :] + extra).astype(jnp.bfloat16)
 
 
@@ -314,9 +314,9 @@
         scratch=[pltpu.SemaphoreType.DMA((24,))], space=pl.ANY, limit=60,
     )
     s = [s[0]] + [along_x(s[d], d) for d in (1, 2, 3)]
-    *s, q_all = lax.optimization_barrier((*s, q_all))
+    mine, ahead = call(collect_kernel, (where,), s, [((256, 256), bf16), ((BACK, 256), bf16)], "collect")
+    mine, ahead, q_all = lax.optimization_barrier((mine, ahead, q_all))
     q_all = exchange_x(q_all)
-    mine, ahead = call(collect_kernel, (where,), s, [((256, 256), bf16), ((BACK, 256), bf16)], "collect")
     far = along_z(mine)
     near_keys = [mine] + [along_y(mine, d) for d in (1, 2, 3)]
     before = along_rows(ahead, 1)
@@ -328,17 +328,20 @@
 
     through, minus = along_y(h2, 1), along_y(h1, -1)
     plus = along_y(h3 + through, 1)
-    back = along_rows(back_grad, -1)
-    (got,) = call(far_sum_kernel, (), (h0, minus, plus), [((256, 256), f32)], "far_sum", extra=(back,))
+    crossing = lax.ppermute(back_grad, "seq", [(i, i - 4) for i in range(16, 20)])
+    back_grad, plus = lax.optimization_barrier((back_grad, plus))
+    within = lax.ppermute(back_grad, "seq", [(i, i - 4) for i in range(4, 32) if i // 4 != 4])
+    (got,) = call(far_sum_kernel, (), (h0, minus, plus), [((256, 256), f32)], "far_sum", extra=(crossing,))
     got = along_z(got)
     one, two, three = along_y(l1, -1), along_y(l2, -2), along_y(l3, 1)
 
     attn_out, q_grad = call(
         unpack_rows_kernel, (), (exchange_x(o),), [((rows, HEADS * HEAD_DIM), bf16)] * 2, "unpack_rows"
     )
+    l0, attn_out, q_grad = lax.optimization_barrier((l0, attn_out, q_grad))
 
     f = call(
-        final_sum_kernel, (where,), (l0, one, two, three, got, own_grad, back),
+        final_sum_kernel, (where,), (l0, one, two, three, got, own_grad, crossing, within),
         [((192, 256), bf16)] * 4, "final_sum",
     )
     f = [f[0]] + [along_x(f[d], -d) for d in (1, 2, 3)]

time: 138 us -> 136 us (0.986)
  the two profiles are of different devices: /device:TPU:56 before, /device:TPU:32 now
where the time goes in v7:
time: 136 us; the launch traced here: 134 us
  starting transfers between devices  52.5 us (39%)
  Pallas kernels  40.7 us (30%)
  waiting for transfers between devices  36.1 us (27%)
  local copies, waits for them, and re-layouts  2.72 us (2%)
    pallas_call x7, Pallas kernels, call(): pl.pallas_call(body, in_specs=[smem] * len(scalars) + [pl.BlockSpec(memor...  40.7 us
    ppermute x12, waiting for transfers between devices, along_y(): lax.ppermute(value, 'seq', [(i, i // 16 * 16 + (i + 4 * step) % 16) for i...  24.9 us
    ppermute x12, starting transfers between devices, along_y(): lax.ppermute(value, 'seq', [(i, i // 16 * 16 + (i + 4 * step) % 16) for i...  17.8 us
    ppermute x6, starting transfers between devices, along_x(): lax.ppermute(value, 'seq', [(i, i // 4 * 4 + (i + step) % 4) for i in ran...  11.4 us
    ppermute x2, starting transfers between devices, along_z(): return lax.ppermute(value, 'seq', [(i, (i + 16) % 32) for i in range(32)])  9.91 us
    all_to_all x2, starting transfers between devices, exchange_x(): lax.all_to_all(value, 'seq', 0, 0, axis_index_groups=X_GROUPS, tiled=True)  8.56 us
    ppermute x6, waiting for transfers between devices, along_x(): lax.ppermute(value, 'seq', [(i, i // 4 * 4 + (i + step) % 4) for i in ran...  8.52 us
    ppermute x1, starting transfers between devices, along_rows(): return lax.ppermute(value, 'seq', [(i, j) for i, j in pairs if 0 <= j < 32])  2.87 us
  transfers between devices with their start and end apart: 25, of which 12 were waited for; matrix products, arithmetic and copies ran while one was open for 0% of the time, Pallas kernels for 1%

profile of v7, /device:TPU:32, one launch (start us, length us, event | category | flops | bytes accessed | tf_op | source)
XLA Modules:
  0.0 133.7 jit_solution(6597341018747478628)
XLA Ops:
  1.3 3.7 %pack.1 = (bf16[192,256]{1,0:T(8,128)(2,1)}, bf16[192,256]{1,0:T(8,128)(2,1)}, bf16[192,256]{1,0:T(8,128)(2,1)}, bf16[192,256]{1,0:T(8,128)(2,1)}, bf16[4,128,1280]{2,1,0:T(8,128)(2,1)}) custom-call(s32[2]{0:T(128)} %pad_add_fusion.where_ref, bf16[64,512]{1,0:T(8,128)(2,1)} %pk.1, bf16[64,512]{1,0:T(8,128)(2,1)} %pv.1, bf16[128,512]{1,0:T(8,128)(2,1)} %k.1, ...), custom_call_target="tpu_custom_call" | custom-call | tf_op jit(solution)/shard_map/pack/pallas_call | solution.py:176
  5.1 1.6 %collective-permute-start = (bf16[192,256]{1,0:T(8,128)(2,1)}, bf16[192,256]{1,0:T(8,128)(2,1)S(1)}, u32[]{:S(2)}, u32[]{:S(2)}) collective-permute-start(bf16[192,256]{1,0:T(8,128)(2,1)} %get-tuple-element.43), channel_id=1, source_target_pairs={{0,1},{1,2},{2,3},{3,0},{4,5},{5,6},{6,7},{7,4},{8,9},{9,10},{10,1... | collective-permute-start | bytes 294920 | tf_op jit(solution)/shard_map/ppermute | solution.py:286
  6.6 2.7 %collective-permute-start.1 = (bf16[192,256]{1,0:T(8,128)(2,1)}, bf16[192,256]{1,0:T(8,128)(2,1)S(1)}, u32[]{:S(2)}, u32[]{:S(2)}) collective-permute-start(bf16[192,256]{1,0:T(8,128)(2,1)} %get-tuple-element.44), channel_id=1, source_target_pairs={{0,2},{1,3},{2,0},{3,1},{4,6},{5,7},{6,4},{7,5},{8,10},{9,11},{10,... | collective-permute-start | bytes 294920 | tf_op jit(solution)/shard_map/ppermute | solution.py:286
  9.4 1.4 %collective-permute-start.2 = (bf16[192,256]{1,0:T(8,128)(2,1)}, bf16[192,256]{1,0:T(8,128)(2,1)S(1)}, u32[]{:S(2)}, u32[]{:S(2)}) collective-permute-start(bf16[192,256]{1,0:T(8,128)(2,1)} %get-tuple-element.45), channel_id=1, source_target_pairs={{0,3},{1,0},{2,1},{3,2},{4,7},{5,4},{6,5},{7,6},{8,11},{9,8},{10,9... | collective-permute-start | bytes 294920 | tf_op jit(solution)/shard_map/ppermute | solution.py:286
  11.4 2.8 %collective-permute-done.1.s2 = bf16[192,256]{1,0:T(8,128)(2,1)S(1)} collective-permute-done((bf16[192,256]{1,0:T(8,128)(2,1)}, bf16[192,256]{1,0:T(8,128)(2,1)S(1)}, u32[]{:S(2)}, u32[]{:S(2)}) %collective-permute-start.1) | collective-permute-done | bytes 98336 | tf_op jit(solution)/shard_map/ppermute | solution.py:286
  15.8 3.9 %all-to-all-start = ((bf16[4,128,1280]{2,1,0:T(8,128)(2,1)}), bf16[4,128,1280]{2,1,0:T(8,128)(2,1)S(1)}, u32[]{:S(2)}, u32[]{:S(2)}) async-start(bf16[4,128,1280]{2,1,0:T(8,128)(2,1)} %get-tuple-element.49), calls=%async_computation | async-start | bytes 2621440 | tf_op jit(solution)/shard_map/all_to_all | solution.py:290
  19.7 6.3 %collective-permute-start.4 = (bf16[256,256]{1,0:T(8,128)(2,1)S(1)}, bf16[256,256]{1,0:T(8,128)(2,1)S(1)}, u32[]{:S(2)}, u32[]{:S(2)}) collective-permute-start(bf16[256,256]{1,0:T(8,128)(2,1)S(1)} %get-tuple-element.51.l0), channel_id=1, source_target_pairs={{0,16},{1,17},{2,18},{3,19},{4,20},{5,21},{6,22},{7,23},{8,24},{9,... | collective-permute-start | bytes 393224 | tf_op jit(solution)/shard_map/ppermute | solution.py:298
  26.0 3.0 %collective-permute-start.10 = (bf16[256,256]{1,0:T(8,128)(2,1)S(1)}, bf16[256,256]{1,0:T(8,128)(2,1)S(1)}, u32[]{:S(2)}, u32[]{:S(2)}) collective-permute-start(bf16[256,256]{1,0:T(8,128)(2,1)S(1)} %get-tuple-element.51.l0), channel_id=1, source_target_pairs={{0,12},{1,13},{2,14},{3,15},{4,0},{5,1},{6,2},{7,3},{8,4},{9,5},{1... | collective-permute-start | bytes 393224 | tf_op jit(solution)/shard_map/ppermute | solution.py:294
  29.6 2.9 %collective-permute-start.3 = (bf16[384,256]{1,0:T(8,128)(2,1)S(1)}, bf16[384,256]{1,0:T(8,128)(2,1)S(1)}, u32[]{:S(2)}, u32[]{:S(2)}) collective-permute-start(bf16[384,256]{1,0:T(8,128)(2,1)S(1)} %get-tuple-element.50), channel_id=1, source_target_pairs={{0,4},{1,5},{2,6},{3,7},{4,8},{5,9},{6,10},{7,11},{8,12},{9,13},{1... | collective-permute-start | bytes 589832 | tf_op jit(solution)/shard_map/ppermute | solution.py:303
  32.5 2.0 %collective-permute-start.8 = (bf16[256,256]{1,0:T(8,128)(2,1)S(1)}, bf16[256,256]{1,0:T(8,128)(2,1)S(1)}, u32[]{:S(2)}, u32[]{:S(2)}) collective-permute-start(bf16[256,256]{1,0:T(8,128)(2,1)S(1)} %get-tuple-element.51.l0), channel_id=1, source_target_pairs={{0,4},{1,5},{2,6},{3,7},{4,8},{5,9},{6,10},{7,11},{8,12},{9,13},{1... | collective-permute-start | bytes 393224 | tf_op jit(solution)/shard_map/ppermute | solution.py:294
  37.6 3.8 %collective-permute-done.8.l1 = bf16[256,256]{1,0:T(8,128)(2,1)S(1)} collective-permute-done((bf16[256,256]{1,0:T(8,128)(2,1)S(1)}, bf16[256,256]{1,0:T(8,128)(2,1)S(1)}, u32[]{:S(2)}, u32[]{:S(2)}) %collective-permute-start.8) | collective-permute-done | bytes 131104 | tf_op jit(solution)/shard_map/ppermute | solution.py:294
  41.4 4.1 %collective-permute-done.6.h2 = bf16[256,256]{1,0:T(8,128)(2,1)S(1)} collective-permute-done((bf16[256,256]{1,0:T(8,128)(2,1)S(1)}, bf16[256,256]{1,0:T(8,128)(2,1)S(1)}, u32[]{:S(2)}, u32[]{:S(2)}) %collective-permute-start.6) | collective-permute-done | bytes 131104 | tf_op jit(solution)/shard_map/ppermute | solution.py:294
  47.3 32.5 %attention.1 = (bf16[4,128,1280]{2,1,0:T(8,128)(2,1)}, f32[256,256]{1,0:T(8,128)}, f32[256,256]{1,0:T(8,128)}, f32[256,256]{1,0:T(8,128)}, f32[256,256]{1,0:T(8,...) custom-call(s32[16]{0:T(128)} %len_ref.1, ...), custom_call_target="tpu_custom_call" | custom-call | flops 10066329600 | bytes 8000000 | tf_op jit(solution)/shard_map/attention/pallas_call | solution.py:176
  79.8 4.7 %all-to-all-start.1 = ((bf16[4,128,1280]{2,1,0:T(8,128)(2,1)}), bf16[4,128,1280]{2,1,0:T(8,128)(2,1)S(1)}, u32[]{:S(2)}, u32[]{:S(2)}) async-start(bf16[4,128,1280]{2,1,0:T(8,128)(2,1)} %get-tuple-element.53), calls=%async_computation.1 | async-start | bytes 2621440 | tf_op jit(solution)/shard_map/all_to_all | solution.py:290
  86.3 6.7 %collective-permute-done.15 = f32[256,256]{1,0:T(8,128)S(1)} collective-permute-done((f32[256,256]{1,0:T(8,128)S(1)}, f32[256,256]{1,0:T(8,128)S(1)}, u32[]{:S(2)}, u32[]{:S(2)}) %collective-permute-start.15) | collective-permute-done | bytes 262176 | tf_op jit(solution)/shard_map/ppermute | solution.py:294
  93.6 2.7 %collective-permute-start.14 = (f32[256,256]{1,0:T(8,128)S(1)}, f32[256,256]{1,0:T(8,128)S(1)}, u32[]{:S(2)}, u32[]{:S(2)}) collective-permute-start(f32[256,256]{1,0:T(8,128)S(1)} %copy-done.12), channel_id=1, source_target_pairs={{0,12},{1,13},{2,14},{3,15},{4,0},{5,1},{6,2},{7,3},{8,4},{9,5},{1... | collective-permute-start | bytes 786440 | tf_op jit(solution)/shard_map/ppermute | solution.py:294
  96.4 4.3 %collective-permute-done.16.c = f32[256,256]{1,0:T(8,128)S(1)} collective-permute-done((f32[256,256]{1,0:T(8,128)S(1)}, f32[256,256]{1,0:T(8,128)S(1)}, u32[]{:S(2)}, u32[]{:S(2)}) %collective-permute-start.16) | collective-permute-done | bytes 262176 | tf_op jit(solution)/shard_map/ppermute | solution.py:294
  102.0 3.1 %collective-permute-start.11 = (f32[256,256]{1,0:T(8,128)}, f32[256,256]{1,0:T(8,128)}, u32[]{:S(2)}, u32[]{:S(2)}) collective-permute-start(f32[256,256]{1,0:T(8,128)} %get-tuple-element.59), channel_id=1, source_target_pairs={{0,12},{1,13},{2,14},{3,15},{4,0},{5,1},{6,2},{7,3},{8,4},{9,5},{1... | collective-permute-start | bytes 786440 | tf_op jit(solution)/shard_map/ppermute | solution.py:294
  105.1 1.7 %collective-permute-start.12 = (f32[256,256]{1,0:T(8,128)}, f32[256,256]{1,0:T(8,128)}, u32[]{:S(2)}, u32[]{:S(2)}) collective-permute-start(f32[256,256]{1,0:T(8,128)} %get-tuple-element.60), channel_id=1, source_target_pairs={{0,8},{1,9},{2,10},{3,11},{4,12},{5,13},{6,14},{7,15},{8,0},{9,1},... | collective-permute-start | bytes 786440 | tf_op jit(solution)/shard_map/ppermute | solution.py:294
  106.9 3.6 %collective-permute-start.18 = (f32[256,256]{1,0:T(8,128)S(1)}, f32[256,256]{1,0:T(8,128)S(1)}, u32[]{:S(2)}, u32[]{:S(2)}) collective-permute-start(f32[256,256]{1,0:T(8,128)S(1)} %far_sum.1), channel_id=1, source_target_pairs={{0,16},{1,17},{2,18},{3,19},{4,20},{5,21},{6,22},{7,23},{8,24},{9,... | collective-permute-start | bytes 786440 | tf_op jit(solution)/shard_map/ppermute | solution.py:298
  111.7 5.7 %collective-permute-done.11.n1 = f32[256,256]{1,0:T(8,128)} collective-permute-done((f32[256,256]{1,0:T(8,128)}, f32[256,256]{1,0:T(8,128)}, u32[]{:S(2)}, u32[]{:S(2)}) %collective-permute-start.11) | collective-permute-done | bytes 262176 | tf_op jit(solution)/shard_map/ppermute | solution.py:294
  117.4 2.7 %collective-permute-done.18.got_ref = f32[256,256]{1,0:T(8,128)S(1)} collective-permute-done((f32[256,256]{1,0:T(8,128)S(1)}, f32[256,256]{1,0:T(8,128)S(1)}, u32[]{:S(2)}, u32[]{:S(2)}) %collective-permute-start.18) | collective-permute-done | bytes 262176 | tf_op jit(solution)/shard_map/ppermute | solution.py:298
  121.5 3.7 %collective-permute-start.20 = (bf16[192,256]{1,0:T(8,128)(2,1)S(1)}, bf16[192,256]{1,0:T(8,128)(2,1)S(1)}, u32[]{:S(2)}, u32[]{:S(2)}) collective-permute-start(bf16[192,256]{1,0:T(8,128)(2,1)S(1)} %get-tuple-element.71), channel_id=1, source_target_pairs={{0,3},{1,0},{2,1},{3,2},{4,7},{5,4},{6,5},{7,6},{8,11},{9,8},{10,9... | collective-permute-start | bytes 294920 | tf_op jit(solution)/shard_map/ppermute | solution.py:286
  127.4 3.9 %collective-permute-done.21.f2 = bf16[192,256]{1,0:T(8,128)(2,1)S(1)} collective-permute-done((bf16[192,256]{1,0:T(8,128)(2,1)S(1)}, bf16[192,256]{1,0:T(8,128)(2,1)S(1)}, u32[]{:S(2)}, u32[]{:S(2)}) %collective-permute-start.21) | collective-permute-done | bytes 98336 | tf_op jit(solution)/shard_map/ppermute | solution.py:286
  (79 shorter events, 19.2 us)
Async XLA Ops:
  5.1 6.4 %collective-permute-start = (bf16[192,256]{1,0:T(8,128)(2,1)}, bf16[192,256]{1,0:T(8,128)(2,1)S(1)}, u32[]{:S(2)}, u32[]{:S(2)}) collective-permute-start(bf16[192,256]{1,0:T(8,128)(2,1)} %get-tuple-element.43), channel_id=1, source_target_pairs={{0,1},{1,2},{2,3},{3,0},{4,5},{5,6},{6,7},{7,4},{8,9},{9,10},{10,1... | collective-permute-start | bytes 294920 | tf_op jit(solution)/shard_map/ppermute | solution.py:286
  6.6 7.6 %collective-permute-start.1 = (bf16[192,256]{1,0:T(8,128)(2,1)}, bf16[192,256]{1,0:T(8,128)(2,1)S(1)}, u32[]{:S(2)}, u32[]{:S(2)}) collective-permute-start(bf16[192,256]{1,0:T(8,128)(2,1)} %get-tuple-element.44), channel_id=1, source_target_pairs={{0,2},{1,3},{2,0},{3,1},{4,6},{5,7},{6,4},{7,5},{8,10},{9,11},{10,... | collective-permute-start | bytes 294920 | tf_op jit(solution)/shard_map/ppermute | solution.py:286
  15.8 29.7 %all-to-all-start = ((bf16[4,128,1280]{2,1,0:T(8,128)(2,1)}), bf16[4,128,1280]{2,1,0:T(8,128)(2,1)S(1)}, u32[]{:S(2)}, u32[]{:S(2)}) async-start(bf16[4,128,1280]{2,1,0:T(8,128)(2,1)} %get-tuple-element.49), calls=%async_computation | async-start | bytes 2621440 | tf_op jit(solution)/shard_map/all_to_all | solution.py:290
  19.7 14.8 %collective-permute-start.4 = (bf16[256,256]{1,0:T(8,128)(2,1)S(1)}, bf16[256,256]{1,0:T(8,128)(2,1)S(1)}, u32[]{:S(2)}, u32[]{:S(2)}) collective-permute-start(bf16[256,256]{1,0:T(8,128)(2,1)S(1)} %get-tuple-element.51.l0), channel_id=1, source_target_pairs={{0,16},{1,17},{2,18},{3,19},{4,20},{5,21},{6,22},{7,23},{8,24},{9,... | collective-permute-start | bytes 393224 | tf_op jit(solution)/shard_map/ppermute | solution.py:298
  26.0 9.9 %collective-permute-start.10 = (bf16[256,256]{1,0:T(8,128)(2,1)S(1)}, bf16[256,256]{1,0:T(8,128)(2,1)S(1)}, u32[]{:S(2)}, u32[]{:S(2)}) collective-permute-start(bf16[256,256]{1,0:T(8,128)(2,1)S(1)} %get-tuple-element.51.l0), channel_id=1, source_target_pairs={{0,12},{1,13},{2,14},{3,15},{4,0},{5,1},{6,2},{7,3},{8,4},{9,5},{1... | collective-permute-start | bytes 393224 | tf_op jit(solution)/shard_map/ppermute | solution.py:294
  29.0 7.9 %collective-permute-start.9 = (bf16[256,256]{1,0:T(8,128)(2,1)S(1)}, bf16[256,256]{1,0:T(8,128)(2,1)S(1)}, u32[]{:S(2)}, u32[]{:S(2)}) collective-permute-start(bf16[256,256]{1,0:T(8,128)(2,1)S(1)} %get-tuple-element.51.l0), channel_id=1, source_target_pairs={{0,8},{1,9},{2,10},{3,11},{4,12},{5,13},{6,14},{7,15},{8,0},{9,1},... | collective-permute-start | bytes 393224 | tf_op jit(solution)/shard_map/ppermute | solution.py:294
  29.6 11.8 %collective-permute-start.3 = (bf16[384,256]{1,0:T(8,128)(2,1)S(1)}, bf16[384,256]{1,0:T(8,128)(2,1)S(1)}, u32[]{:S(2)}, u32[]{:S(2)}) collective-permute-start(bf16[384,256]{1,0:T(8,128)(2,1)S(1)} %get-tuple-element.50), channel_id=1, source_target_pairs={{0,4},{1,5},{2,6},{3,7},{4,8},{5,9},{6,10},{7,11},{8,12},{9,13},{1... | collective-permute-start | bytes 589832 | tf_op jit(solution)/shard_map/ppermute | solution.py:303
  32.5 8.9 %collective-permute-start.8 = (bf16[256,256]{1,0:T(8,128)(2,1)S(1)}, bf16[256,256]{1,0:T(8,128)(2,1)S(1)}, u32[]{:S(2)}, u32[]{:S(2)}) collective-permute-start(bf16[256,256]{1,0:T(8,128)(2,1)S(1)} %get-tuple-element.51.l0), channel_id=1, source_target_pairs={{0,4},{1,5},{2,6},{3,7},{4,8},{5,9},{6,10},{7,11},{8,12},{9,13},{1... | collective-permute-start | bytes 393224 | tf_op jit(solution)/shard_map/ppermute | solution.py:294
  34.5 6.9 %collective-permute-start.7 = (bf16[256,256]{1,0:T(8,128)(2,1)S(1)}, bf16[256,256]{1,0:T(8,128)(2,1)S(1)}, u32[]{:S(2)}, u32[]{:S(2)}) collective-permute-start(bf16[256,256]{1,0:T(8,128)(2,1)S(1)} %collective-permute-done.4.h0), channel_id=1, source_target_pairs={{0,12},{1,13},{2,14},{3,15},{4,0},{5,1},{6,2},{7,3},{8,4},{9,5},{1... | collective-permute-start | bytes 393224 | tf_op jit(solution)/shard_map/ppermute | solution.py:294
  35.8 9.7 %collective-permute-start.6 = (bf16[256,256]{1,0:T(8,128)(2,1)S(1)}, bf16[256,256]{1,0:T(8,128)(2,1)S(1)}, u32[]{:S(2)}, u32[]{:S(2)}) collective-permute-start(bf16[256,256]{1,0:T(8,128)(2,1)S(1)} %collective-permute-done.4.h0), channel_id=1, source_target_pairs={{0,8},{1,9},{2,10},{3,11},{4,12},{5,13},{6,14},{7,15},{8,0},{9,1},... | collective-permute-start | bytes 393224 | tf_op jit(solution)/shard_map/ppermute | solution.py:294
  36.9 8.6 %collective-permute-start.5 = (bf16[256,256]{1,0:T(8,128)(2,1)S(1)}, bf16[256,256]{1,0:T(8,128)(2,1)S(1)}, u32[]{:S(2)}, u32[]{:S(2)}) collective-permute-start(bf16[256,256]{1,0:T(8,128)(2,1)S(1)} %collective-permute-done.4.h0), channel_id=1, source_target_pairs={{0,4},{1,5},{2,6},{3,7},{4,8},{5,9},{6,10},{7,11},{8,12},{9,13},{1... | collective-permute-start | bytes 393224 | tf_op jit(solution)/shard_map/ppermute | solution.py:294
  79.8 30.7 %all-to-all-start.1 = ((bf16[4,128,1280]{2,1,0:T(8,128)(2,1)}), bf16[4,128,1280]{2,1,0:T(8,128)(2,1)S(1)}, u32[]{:S(2)}, u32[]{:S(2)}) async-start(bf16[4,128,1280]{2,1,0:T(8,128)(2,1)} %get-tuple-element.53), calls=%async_computation.1 | async-start | bytes 2621440 | tf_op jit(solution)/shard_map/all_to_all | solution.py:290
  84.5 8.5 %collective-permute-start.15 = (f32[256,256]{1,0:T(8,128)S(1)}, f32[256,256]{1,0:T(8,128)S(1)}, u32[]{:S(2)}, u32[]{:S(2)}) collective-permute-start(f32[256,256]{1,0:T(8,128)S(1)} %copy-done.13), channel_id=1, source_target_pairs={{0,4},{1,5},{2,6},{3,7},{4,8},{5,9},{6,10},{7,11},{8,12},{9,13},{1... | collective-permute-start | bytes 786440 | tf_op jit(solution)/shard_map/ppermute | solution.py:294
  85.6 21.1 %collective-permute-start.17 = (f32[384,256]{1,0:T(8,128)}, f32[384,256]{1,0:T(8,128)S(1)}, u32[]{:S(2)}, u32[]{:S(2)}) collective-permute-start(f32[384,256]{1,0:T(8,128)} %get-tuple-element.69), channel_id=1, source_target_pairs={{16,12},{17,13},{18,14},{19,15},{48,44},{49,45},{50,46},{51,47},{8... | collective-permute-start | bytes 1179656 | tf_op jit(solution)/shard_map/ppermute | solution.py:331
  93.1 7.7 %collective-permute-start.16 = (f32[256,256]{1,0:T(8,128)S(1)}, f32[256,256]{1,0:T(8,128)S(1)}, u32[]{:S(2)}, u32[]{:S(2)}) collective-permute-start(f32[256,256]{1,0:T(8,128)S(1)} %add.9), channel_id=1, source_target_pairs={{0,4},{1,5},{2,6},{3,7},{4,8},{5,9},{6,10},{7,11},{8,12},{9,13},{1... | collective-permute-start | bytes 786440 | tf_op jit(solution)/shard_map/ppermute | solution.py:294
  93.6 13.2 %collective-permute-start.14 = (f32[256,256]{1,0:T(8,128)S(1)}, f32[256,256]{1,0:T(8,128)S(1)}, u32[]{:S(2)}, u32[]{:S(2)}) collective-permute-start(f32[256,256]{1,0:T(8,128)S(1)} %copy-done.12), channel_id=1, source_target_pairs={{0,12},{1,13},{2,14},{3,15},{4,0},{5,1},{6,2},{7,3},{8,4},{9,5},{1... | collective-permute-start | bytes 786440 | tf_op jit(solution)/shard_map/ppermute | solution.py:294
  100.7 19.4 %collective-permute-start.19 = (f32[384,256]{1,0:T(8,128)}, f32[384,256]{1,0:T(8,128)S(1)}, u32[]{:S(2)}, u32[]{:S(2)}) collective-permute-start(f32[384,256]{1,0:T(8,128)} %get-tuple-element.69), channel_id=1, source_target_pairs={{4,0},{5,1},{6,2},{7,3},{8,4},{9,5},{10,6},{11,7},{12,8},{13,9},{1... | collective-permute-start | bytes 1179656 | tf_op jit(solution)/shard_map/ppermute | solution.py:333
  102.0 15.4 %collective-permute-start.11 = (f32[256,256]{1,0:T(8,128)}, f32[256,256]{1,0:T(8,128)}, u32[]{:S(2)}, u32[]{:S(2)}) collective-permute-start(f32[256,256]{1,0:T(8,128)} %get-tuple-element.59), channel_id=1, source_target_pairs={{0,12},{1,13},{2,14},{3,15},{4,0},{5,1},{6,2},{7,3},{8,4},{9,5},{1... | collective-permute-start | bytes 786440 | tf_op jit(solution)/shard_map/ppermute | solution.py:294
  105.1 12.3 %collective-permute-start.12 = (f32[256,256]{1,0:T(8,128)}, f32[256,256]{1,0:T(8,128)}, u32[]{:S(2)}, u32[]{:S(2)}) collective-permute-start(f32[256,256]{1,0:T(8,128)} %get-tuple-element.60), channel_id=1, source_target_pairs={{0,8},{1,9},{2,10},{3,11},{4,12},{5,13},{6,14},{7,15},{8,0},{9,1},... | collective-permute-start | bytes 786440 | tf_op jit(solution)/shard_map/ppermute | solution.py:294
  106.8 10.6 %collective-permute-start.13 = (f32[256,256]{1,0:T(8,128)}, f32[256,256]{1,0:T(8,128)}, u32[]{:S(2)}, u32[]{:S(2)}) collective-permute-start(f32[256,256]{1,0:T(8,128)} %get-tuple-element.61), channel_id=1, source_target_pairs={{0,4},{1,5},{2,6},{3,7},{4,8},{5,9},{6,10},{7,11},{8,12},{9,13},{1... | collective-permute-start | bytes 786440 | tf_op jit(solution)/shard_map/ppermute | solution.py:294
  106.9 13.3 %collective-permute-start.18 = (f32[256,256]{1,0:T(8,128)S(1)}, f32[256,256]{1,0:T(8,128)S(1)}, u32[]{:S(2)}, u32[]{:S(2)}) collective-permute-start(f32[256,256]{1,0:T(8,128)S(1)} %far_sum.1), channel_id=1, source_target_pairs={{0,16},{1,17},{2,18},{3,19},{4,20},{5,21},{6,22},{7,23},{8,24},{9,... | collective-permute-start | bytes 786440 | tf_op jit(solution)/shard_map/ppermute | solution.py:298
  121.5 5.9 %collective-permute-start.20 = (bf16[192,256]{1,0:T(8,128)(2,1)S(1)}, bf16[192,256]{1,0:T(8,128)(2,1)S(1)}, u32[]{:S(2)}, u32[]{:S(2)}) collective-permute-start(bf16[192,256]{1,0:T(8,128)(2,1)S(1)} %get-tuple-element.71), channel_id=1, source_target_pairs={{0,3},{1,0},{2,1},{3,2},{4,7},{5,4},{6,5},{7,6},{8,11},{9,8},{10,9... | collective-permute-start | bytes 294920 | tf_op jit(solution)/shard_map/ppermute | solution.py:286
  125.1 6.1 %collective-permute-start.21 = (bf16[192,256]{1,0:T(8,128)(2,1)S(1)}, bf16[192,256]{1,0:T(8,128)(2,1)S(1)}, u32[]{:S(2)}, u32[]{:S(2)}) collective-permute-start(bf16[192,256]{1,0:T(8,128)(2,1)S(1)} %get-tuple-element.72), channel_id=1, source_target_pairs={{0,2},{1,3},{2,0},{3,1},{4,6},{5,7},{6,4},{7,5},{8,10},{9,11},{10,... | collective-permute-start | bytes 294920 | tf_op jit(solution)/shard_map/ppermute | solution.py:286
  126.3 6.0 %collective-permute-start.22 = (bf16[192,256]{1,0:T(8,128)(2,1)S(1)}, bf16[192,256]{1,0:T(8,128)(2,1)S(1)}, u32[]{:S(2)}, u32[]{:S(2)}) collective-permute-start(bf16[192,256]{1,0:T(8,128)(2,1)S(1)} %get-tuple-element.73), channel_id=1, source_target_pairs={{0,1},{1,2},{2,3},{3,0},{4,5},{5,6},{6,7},{7,4},{8,9},{9,10},{10,1... | collective-permute-start | bytes 294920 | tf_op jit(solution)/shard_map/ppermute | solution.py:286
  (23 other events, 186.1 us)

commit v8 on v7

--- a/solution.py
+++ b/solution.py
@@ -62,7 +62,7 @@
         first = PROMPT_ROWS + BACK + lax.rem(x + 4 - d, 4) * 128
         load(source.at[64:192, :], staged.at[pl.ds(pl.multiple_of(first, 128), 128), :])
     load(q_in, q_all)
-    for copy in copies:
+    for copy in copies[:-1]:
         copy.wait()
     place(slice(0, all_rows), staged)
     value1[:, 128:] = jnp.ones((all_rows, 128), jnp.bfloat16)
@@ -73,6 +73,7 @@
         value_t[:128, at] = value1[at, :128].astype(jnp.float32).T.astype(jnp.bfloat16)
     for ref in (key_sum, value_sum, p_second, grad2_second, rows_second):
         ref[...] = jnp.zeros_like(ref)
+    copies[-1].wait()
 
     s_refs, p_refs = (s_first, s_second), (p_first, p_second)
     grad2_refs, rows_refs = (grad2_first, grad2_second), (rows_first, rows_second)
@@ -249,11 +250,11 @@
             ahead_ref[pl.ds(pl.multiple_of((block - 1) * 128, 128), 128), :] = source[64:, :]
 
 
-def final_sum_kernel(where_ref, n0, n1, n2, n3, got_ref, own_ref, crossing_ref, within_ref, f0, f1, f2, f3):
+def final_sum_kernel(where_ref, n0, n1, n2, n3, own_ref, crossing_ref, within_ref, f0, f1, f2, f3):
     x = where_ref[1]
     for d, target in enumerate((f0, f1, f2, f3)):
         at = slice(d * 64, d * 64 + 64)
-        total = (n0[at, :] + n1[at, :]) + (n2[at, :] + n3[at, :]) + got_ref[at, :]
+        total = (n0[at, :] + n1[at, :]) + (n2[at, :] + n3[at, :])
         target[:64, :] = total.astype(jnp.bfloat16)
         block = lax.rem(x + 4 - d, 4)
         behind = pl.ds(pl.multiple_of(jnp.maximum(block - 1, 0) * 128, 128), 128)
@@ -261,8 +262,13 @@
         target[64:, :] = (own_ref[block_at(x, d), :] + extra).astype(jnp.bfloat16)
 
 
-def far_sum_kernel(a, b, c, after, out_ref):
-    out_ref[...] = a[...] + b[...] + c[...]
+def two_sums_kernel(a, b, c, d, ab_ref, cd_ref):
+    ab_ref[...] = a[...] + b[...]
+    cd_ref[...] = c[...] + d[...]
+
+
+def sum_kernel(a, b, *refs):
+    refs[-1][...] = a[...] + b[...]
 
 
 def unpack_rows_kernel(o_ref, out_ref, dq_ref):
@@ -327,21 +333,24 @@
     )
 
     through, minus = along_y(h2, 1), along_y(h1, -1)
-    plus = along_y(h3 + through, 1)
     crossing = lax.ppermute(back_grad, "seq", [(i, i - 4) for i in range(16, 20)])
-    back_grad, plus = lax.optimization_barrier((back_grad, plus))
+    part = [((256, 256), f32)]
+    plus, stay = call(two_sums_kernel, (), (h3, through, h0, minus), part * 2, "two_sums")
+    plus = along_y(plus, 1)
+    (give,) = call(sum_kernel, (), (stay, plus), part, "far_sum", extra=(crossing,))
+    give, back_grad, l1, l2, l3 = lax.optimization_barrier((give, back_grad, l1, l2, l3))
+    got = along_z(give)
+    one, two, three = along_y(l1, -1), along_y(l2, -2), along_y(l3, 1)
     within = lax.ppermute(back_grad, "seq", [(i, i - 4) for i in range(4, 32) if i // 4 != 4])
-    (got,) = call(far_sum_kernel, (), (h0, minus, plus), [((256, 256), f32)], "far_sum", extra=(crossing,))
-    got = along_z(got)
-    one, two, three = along_y(l1, -1), along_y(l2, -2), along_y(l3, 1)
 
     attn_out, q_grad = call(
         unpack_rows_kernel, (), (exchange_x(o),), [((rows, HEADS * HEAD_DIM), bf16)] * 2, "unpack_rows"
     )
     l0, attn_out, q_grad = lax.optimization_barrier((l0, attn_out, q_grad))
+    (stay,) = call(sum_kernel, (), (l0, got), part, "near_sum")
 
     f = call(
-        final_sum_kernel, (where,), (l0, one, two, three, got, own_grad, crossing, within),
+        final_sum_kernel, (where,), (stay, one, two, three, own_grad, crossing, within),
         [((192, 256), bf16)] * 4, "final_sum",
     )
     f = [f[0]] + [along_x(f[d], -d) for d in (1, 2, 3)]

time: 136 us -> 152 us (1.12)
  the two profiles are of different devices: /device:TPU:32 before, /device:TPU:40 now
where the time goes in v8:
time: 152 us; the launch traced here: 151 us
  starting transfers between devices  64 us (42%)
  Pallas kernels  41.7 us (27%)
  waiting for transfers between devices  41.3 us (27%)
  local copies, waits for them, and re-layouts  2.68 us (2%)
    pallas_call x9, Pallas kernels, call(): pl.pallas_call(body, in_specs=[smem] * len(scalars) + [pl.BlockSpec(memor...  41.7 us
    ppermute x12, waiting for transfers between devices, along_y(): lax.ppermute(value, 'seq', [(i, i // 16 * 16 + (i + 4 * step) % 16) for i...  32.3 us
    ppermute x2, starting transfers between devices, along_z(): return lax.ppermute(value, 'seq', [(i, (i + 16) % 32) for i in range(32)])  21.3 us
    ppermute x12, starting transfers between devices, along_y(): lax.ppermute(value, 'seq', [(i, i // 16 * 16 + (i + 4 * step) % 16) for i...  15.6 us
    ppermute x6, starting transfers between devices, along_x(): lax.ppermute(value, 'seq', [(i, i // 4 * 4 + (i + step) % 4) for i in ran...  10.5 us
    ppermute x6, waiting for transfers between devices, along_x(): lax.ppermute(value, 'seq', [(i, i // 4 * 4 + (i + step) % 4) for i in ran...  8.85 us
    all_to_all x2, starting transfers between devices, exchange_x(): lax.all_to_all(value, 'seq', 0, 0, axis_index_groups=X_GROUPS, tiled=True)  8.56 us
    ppermute x1, starting transfers between devices, along_rows(): return lax.ppermute(value, 'seq', [(i, j) for i, j in pairs if 0 <= j < 32])  3.78 us
  transfers between devices with their start and end apart: 25, of which 13 were waited for; matrix products, arithmetic and copies ran while one was open for 0% of the time, Pallas kernels for 2%

profile of v8, /device:TPU:40, one launch (start us, length us, event | category | flops | bytes accessed | tf_op | source)
XLA Modules:
  0.0 151.3 jit_solution(9497852163646744355)
XLA Ops:
  1.3 3.7 %pack.1 = (bf16[192,256]{1,0:T(8,128)(2,1)}, bf16[192,256]{1,0:T(8,128)(2,1)}, bf16[192,256]{1,0:T(8,128)(2,1)}, bf16[192,256]{1,0:T(8,128)(2,1)}, bf16[4,128,1280]{2,1,0:T(8,128)(2,1)}) custom-call(s32[2]{0:T(128)} %pad_add_fusion.where_ref, bf16[64,512]{1,0:T(8,128)(2,1)} %pk.1, bf16[64,512]{1,0:T(8,128)(2,1)} %pv.1, bf16[128,512]{1,0:T(8,128)(2,1)} %k.1, ...), custom_call_target="tpu_custom_call" | custom-call | tf_op jit(solution)/shard_map/pack/pallas_call | solution.py:177
  5.1 1.6 %collective-permute-start = (bf16[192,256]{1,0:T(8,128)(2,1)}, bf16[192,256]{1,0:T(8,128)(2,1)S(1)}, u32[]{:S(2)}, u32[]{:S(2)}) collective-permute-start(bf16[192,256]{1,0:T(8,128)(2,1)} %get-tuple-element.48), channel_id=1, source_target_pairs={{0,1},{1,2},{2,3},{3,0},{4,5},{5,6},{6,7},{7,4},{8,9},{9,10},{10,1... | collective-permute-start | bytes 294920 | tf_op jit(solution)/shard_map/ppermute | solution.py:292
  6.6 2.7 %collective-permute-start.1 = (bf16[192,256]{1,0:T(8,128)(2,1)}, bf16[192,256]{1,0:T(8,128)(2,1)S(1)}, u32[]{:S(2)}, u32[]{:S(2)}) collective-permute-start(bf16[192,256]{1,0:T(8,128)(2,1)} %get-tuple-element.49), channel_id=1, source_target_pairs={{0,2},{1,3},{2,0},{3,1},{4,6},{5,7},{6,4},{7,5},{8,10},{9,11},{10,... | collective-permute-start | bytes 294920 | tf_op jit(solution)/shard_map/ppermute | solution.py:292
  11.4 2.8 %collective-permute-done.1.s2 = bf16[192,256]{1,0:T(8,128)(2,1)S(1)} collective-permute-done((bf16[192,256]{1,0:T(8,128)(2,1)}, bf16[192,256]{1,0:T(8,128)(2,1)S(1)}, u32[]{:S(2)}, u32[]{:S(2)}) %collective-permute-start.1) | collective-permute-done | bytes 98336 | tf_op jit(solution)/shard_map/ppermute | solution.py:292
  15.8 3.9 %all-to-all-start = ((bf16[4,128,1280]{2,1,0:T(8,128)(2,1)}), bf16[4,128,1280]{2,1,0:T(8,128)(2,1)S(1)}, u32[]{:S(2)}, u32[]{:S(2)}) async-start(bf16[4,128,1280]{2,1,0:T(8,128)(2,1)} %get-tuple-element.54), calls=%async_computation | async-start | bytes 2621440 | tf_op jit(solution)/shard_map/all_to_all | solution.py:296
  19.7 6.3 %collective-permute-start.4 = (bf16[256,256]{1,0:T(8,128)(2,1)S(1)}, bf16[256,256]{1,0:T(8,128)(2,1)S(1)}, u32[]{:S(2)}, u32[]{:S(2)}) collective-permute-start(bf16[256,256]{1,0:T(8,128)(2,1)S(1)} %get-tuple-element.56.l0), channel_id=1, source_target_pairs={{0,16},{1,17},{2,18},{3,19},{4,20},{5,21},{6,22},{7,23},{8,24},{9,... | collective-permute-start | bytes 393224 | tf_op jit(solution)/shard_map/ppermute | solution.py:304
  26.4 2.6 %collective-permute-start.9 = (bf16[256,256]{1,0:T(8,128)(2,1)S(1)}, bf16[256,256]{1,0:T(8,128)(2,1)S(1)}, u32[]{:S(2)}, u32[]{:S(2)}) collective-permute-start(bf16[256,256]{1,0:T(8,128)(2,1)S(1)} %get-tuple-element.56.l0), channel_id=1, source_target_pairs={{0,8},{1,9},{2,10},{3,11},{4,12},{5,13},{6,14},{7,15},{8,0},{9,1},... | collective-permute-start | bytes 393224 | tf_op jit(solution)/shard_map/ppermute | solution.py:300
  29.0 3.8 %collective-permute-start.3 = (bf16[384,256]{1,0:T(8,128)(2,1)S(1)}, bf16[384,256]{1,0:T(8,128)(2,1)S(1)}, u32[]{:S(2)}, u32[]{:S(2)}) collective-permute-start(bf16[384,256]{1,0:T(8,128)(2,1)S(1)} %get-tuple-element.55), channel_id=1, source_target_pairs={{0,4},{1,5},{2,6},{3,7},{4,8},{5,9},{6,10},{7,11},{8,12},{9,13},{1... | collective-permute-start | bytes 589832 | tf_op jit(solution)/shard_map/ppermute | solution.py:309
  32.9 2.0 %collective-permute-start.7 = (bf16[256,256]{1,0:T(8,128)(2,1)S(1)}, bf16[256,256]{1,0:T(8,128)(2,1)S(1)}, u32[]{:S(2)}, u32[]{:S(2)}) collective-permute-start(bf16[256,256]{1,0:T(8,128)(2,1)S(1)} %collective-permute-done.4.h0), channel_id=1, source_target_pairs={{0,12},{1,13},{2,14},{3,15},{4,0},{5,1},{6,2},{7,3},{8,4},{9,5},{1... | collective-permute-start | bytes 393224 | tf_op jit(solution)/shard_map/ppermute | solution.py:300
  36.0 1.7 %collective-permute-start.5 = (bf16[256,256]{1,0:T(8,128)(2,1)S(1)}, bf16[256,256]{1,0:T(8,128)(2,1)S(1)}, u32[]{:S(2)}, u32[]{:S(2)}) collective-permute-start(bf16[256,256]{1,0:T(8,128)(2,1)S(1)} %collective-permute-done.4.h0), channel_id=1, source_target_pairs={{0,4},{1,5},{2,6},{3,7},{4,8},{5,9},{6,10},{7,11},{8,12},{9,13},{1... | collective-permute-start | bytes 393224 | tf_op jit(solution)/shard_map/ppermute | solution.py:300
  37.8 5.4 %collective-permute-done.8.l1 = bf16[256,256]{1,0:T(8,128)(2,1)S(1)} collective-permute-done((bf16[256,256]{1,0:T(8,128)(2,1)S(1)}, bf16[256,256]{1,0:T(8,128)(2,1)S(1)}, u32[]{:S(2)}, u32[]{:S(2)}) %collective-permute-start.8) | collective-permute-done | bytes 131104 | tf_op jit(solution)/shard_map/ppermute | solution.py:300
  43.2 1.9 %collective-permute-done.5.h1 = bf16[256,256]{1,0:T(8,128)(2,1)S(1)} collective-permute-done((bf16[256,256]{1,0:T(8,128)(2,1)S(1)}, bf16[256,256]{1,0:T(8,128)(2,1)S(1)}, u32[]{:S(2)}, u32[]{:S(2)}) %collective-permute-start.5) | collective-permute-done | bytes 131104 | tf_op jit(solution)/shard_map/ppermute | solution.py:300
  46.9 32.0 %attention.1 = (bf16[4,128,1280]{2,1,0:T(8,128)(2,1)}, f32[256,256]{1,0:T(8,128)}, f32[256,256]{1,0:T(8,128)}, f32[256,256]{1,0:T(8,128)}, f32[256,256]{1,0:T(8,...) custom-call(s32[16]{0:T(128)} %len_ref.1, ...), custom_call_target="tpu_custom_call" | custom-call | flops 10066329600 | bytes 8000000 | tf_op jit(solution)/shard_map/attention/pallas_call | solution.py:177
  78.9 4.7 %all-to-all-start.1 = ((bf16[4,128,1280]{2,1,0:T(8,128)(2,1)}), bf16[4,128,1280]{2,1,0:T(8,128)(2,1)S(1)}, u32[]{:S(2)}, u32[]{:S(2)}) async-start(bf16[4,128,1280]{2,1,0:T(8,128)(2,1)} %get-tuple-element.58), calls=%async_computation.1 | async-start | bytes 2621440 | tf_op jit(solution)/shard_map/all_to_all | solution.py:296
  83.5 1.9 %collective-permute-start.11 = (f32[256,256]{1,0:T(8,128)S(1)}, f32[256,256]{1,0:T(8,128)S(1)}, u32[]{:S(2)}, u32[]{:S(2)}) collective-permute-start(f32[256,256]{1,0:T(8,128)S(1)} %copy-done.13), channel_id=1, source_target_pairs={{0,4},{1,5},{2,6},{3,7},{4,8},{5,9},{6,10},{7,11},{8,12},{9,13},{1... | collective-permute-start | bytes 786440 | tf_op jit(solution)/shard_map/ppermute | solution.py:300
  86.2 4.5 %collective-permute-done.11.b = f32[256,256]{1,0:T(8,128)S(1)} collective-permute-done((f32[256,256]{1,0:T(8,128)S(1)}, f32[256,256]{1,0:T(8,128)S(1)}, u32[]{:S(2)}, u32[]{:S(2)}) %collective-permute-start.11) | collective-permute-done | bytes 262176 | tf_op jit(solution)/shard_map/ppermute | solution.py:300
  93.4 4.9 %collective-permute-done.13.b = f32[256,256]{1,0:T(8,128)S(1)} collective-permute-done((f32[256,256]{1,0:T(8,128)S(1)}, f32[256,256]{1,0:T(8,128)S(1)}, u32[]{:S(2)}, u32[]{:S(2)}) %collective-permute-start.13) | collective-permute-done | bytes 262176 | tf_op jit(solution)/shard_map/ppermute | solution.py:300
  99.1 3.6 %collective-permute-start.19 = (f32[384,256]{1,0:T(8,128)}, f32[384,256]{1,0:T(8,128)S(1)}, u32[]{:S(2)}, u32[]{:S(2)}) collective-permute-start(f32[384,256]{1,0:T(8,128)} %get-tuple-element.79), channel_id=1, source_target_pairs={{4,0},{5,1},{6,2},{7,3},{8,4},{9,5},{10,6},{11,7},{12,8},{13,9},{1... | collective-permute-start | bytes 1179656 | tf_op jit(solution)/shard_map/ppermute | solution.py:344
  102.7 15.0 %collective-permute-start.15 = (f32[256,256]{1,0:T(8,128)}, f32[256,256]{1,0:T(8,128)}, u32[]{:S(2)}, u32[]{:S(2)}) collective-permute-start(f32[256,256]{1,0:T(8,128)} %far_sum.1), channel_id=1, source_target_pairs={{0,16},{1,17},{2,18},{3,19},{4,20},{5,21},{6,22},{7,23},{8,24},{9,... | collective-permute-start | bytes 786440 | tf_op jit(solution)/shard_map/ppermute | solution.py:304
  117.7 1.8 %collective-permute-start.17 = (f32[256,256]{1,0:T(8,128)}, f32[256,256]{1,0:T(8,128)S(1)}, u32[]{:S(2)}, u32[]{:S(2)}) collective-permute-start(f32[256,256]{1,0:T(8,128)} %get-tuple-element.76), channel_id=1, source_target_pairs={{0,8},{1,9},{2,10},{3,11},{4,12},{5,13},{6,14},{7,15},{8,0},{9,1},... | collective-permute-start | bytes 786440 | tf_op jit(solution)/shard_map/ppermute | solution.py:300
  119.5 2.3 %collective-permute-start.18 = (f32[256,256]{1,0:T(8,128)}, f32[256,256]{1,0:T(8,128)}, u32[]{:S(2)}, u32[]{:S(2)}) collective-permute-start(f32[256,256]{1,0:T(8,128)} %get-tuple-element.77), channel_id=1, source_target_pairs={{0,4},{1,5},{2,6},{3,7},{4,8},{5,9},{6,10},{7,11},{8,12},{9,13},{1... | collective-permute-start | bytes 786440 | tf_op jit(solution)/shard_map/ppermute | solution.py:300
  124.8 13.8 %collective-permute-done.17.n2 = f32[256,256]{1,0:T(8,128)S(1)} collective-permute-done((f32[256,256]{1,0:T(8,128)}, f32[256,256]{1,0:T(8,128)S(1)}, u32[]{:S(2)}, u32[]{:S(2)}) %collective-permute-start.17) | collective-permute-done | bytes 262176 | tf_op jit(solution)/shard_map/ppermute | solution.py:300
  139.7 3.0 %collective-permute-start.20 = (bf16[192,256]{1,0:T(8,128)(2,1)S(1)}, bf16[192,256]{1,0:T(8,128)(2,1)S(1)}, u32[]{:S(2)}, u32[]{:S(2)}) collective-permute-start(bf16[192,256]{1,0:T(8,128)(2,1)S(1)} %get-tuple-element.81), channel_id=1, source_target_pairs={{0,3},{1,0},{2,1},{3,2},{4,7},{5,4},{6,5},{7,6},{8,11},{9,8},{10,9... | collective-permute-start | bytes 294920 | tf_op jit(solution)/shard_map/ppermute | solution.py:292
  144.9 4.0 %collective-permute-done.21.f2 = bf16[192,256]{1,0:T(8,128)(2,1)S(1)} collective-permute-done((bf16[192,256]{1,0:T(8,128)(2,1)S(1)}, bf16[192,256]{1,0:T(8,128)(2,1)S(1)}, u32[]{:S(2)}, u32[]{:S(2)}) %collective-permute-start.21) | collective-permute-done | bytes 98336 | tf_op jit(solution)/shard_map/ppermute | solution.py:292
  (80 shorter events, 20.5 us)
Async XLA Ops:
  5.1 6.4 %collective-permute-start = (bf16[192,256]{1,0:T(8,128)(2,1)}, bf16[192,256]{1,0:T(8,128)(2,1)S(1)}, u32[]{:S(2)}, u32[]{:S(2)}) collective-permute-start(bf16[192,256]{1,0:T(8,128)(2,1)} %get-tuple-element.48), channel_id=1, source_target_pairs={{0,1},{1,2},{2,3},{3,0},{4,5},{5,6},{6,7},{7,4},{8,9},{9,10},{10,1... | collective-permute-start | bytes 294920 | tf_op jit(solution)/shard_map/ppermute | solution.py:292
  6.6 7.6 %collective-permute-start.1 = (bf16[192,256]{1,0:T(8,128)(2,1)}, bf16[192,256]{1,0:T(8,128)(2,1)S(1)}, u32[]{:S(2)}, u32[]{:S(2)}) collective-permute-start(bf16[192,256]{1,0:T(8,128)(2,1)} %get-tuple-element.49), channel_id=1, source_target_pairs={{0,2},{1,3},{2,0},{3,1},{4,6},{5,7},{6,4},{7,5},{8,10},{9,11},{10,... | collective-permute-start | bytes 294920 | tf_op jit(solution)/shard_map/ppermute | solution.py:292
  15.8 29.4 %all-to-all-start = ((bf16[4,128,1280]{2,1,0:T(8,128)(2,1)}), bf16[4,128,1280]{2,1,0:T(8,128)(2,1)S(1)}, u32[]{:S(2)}, u32[]{:S(2)}) async-start(bf16[4,128,1280]{2,1,0:T(8,128)(2,1)} %get-tuple-element.54), calls=%async_computation | async-start | bytes 2621440 | tf_op jit(solution)/shard_map/all_to_all | solution.py:296
  19.7 13.2 %collective-permute-start.4 = (bf16[256,256]{1,0:T(8,128)(2,1)S(1)}, bf16[256,256]{1,0:T(8,128)(2,1)S(1)}, u32[]{:S(2)}, u32[]{:S(2)}) collective-permute-start(bf16[256,256]{1,0:T(8,128)(2,1)S(1)} %get-tuple-element.56.l0), channel_id=1, source_target_pairs={{0,16},{1,17},{2,18},{3,19},{4,20},{5,21},{6,22},{7,23},{8,24},{9,... | collective-permute-start | bytes 393224 | tf_op jit(solution)/shard_map/ppermute | solution.py:304
  26.0 9.0 %collective-permute-start.10 = (bf16[256,256]{1,0:T(8,128)(2,1)S(1)}, bf16[256,256]{1,0:T(8,128)(2,1)S(1)}, u32[]{:S(2)}, u32[]{:S(2)}) collective-permute-start(bf16[256,256]{1,0:T(8,128)(2,1)S(1)} %get-tuple-element.56.l0), channel_id=1, source_target_pairs={{0,12},{1,13},{2,14},{3,15},{4,0},{5,1},{6,2},{7,3},{8,4},{9,5},{1... | collective-permute-start | bytes 393224 | tf_op jit(solution)/shard_map/ppermute | solution.py:300
  26.4 9.6 %collective-permute-start.9 = (bf16[256,256]{1,0:T(8,128)(2,1)S(1)}, bf16[256,256]{1,0:T(8,128)(2,1)S(1)}, u32[]{:S(2)}, u32[]{:S(2)}) collective-permute-start(bf16[256,256]{1,0:T(8,128)(2,1)S(1)} %get-tuple-element.56.l0), channel_id=1, source_target_pairs={{0,8},{1,9},{2,10},{3,11},{4,12},{5,13},{6,14},{7,15},{8,0},{9,1},... | collective-permute-start | bytes 393224 | tf_op jit(solution)/shard_map/ppermute | solution.py:300
  29.0 14.2 %collective-permute-start.3 = (bf16[384,256]{1,0:T(8,128)(2,1)S(1)}, bf16[384,256]{1,0:T(8,128)(2,1)S(1)}, u32[]{:S(2)}, u32[]{:S(2)}) collective-permute-start(bf16[384,256]{1,0:T(8,128)(2,1)S(1)} %get-tuple-element.55), channel_id=1, source_target_pairs={{0,4},{1,5},{2,6},{3,7},{4,8},{5,9},{6,10},{7,11},{8,12},{9,13},{1... | collective-permute-start | bytes 589832 | tf_op jit(solution)/shard_map/ppermute | solution.py:309
  32.8 10.4 %collective-permute-start.8 = (bf16[256,256]{1,0:T(8,128)(2,1)S(1)}, bf16[256,256]{1,0:T(8,128)(2,1)S(1)}, u32[]{:S(2)}, u32[]{:S(2)}) collective-permute-start(bf16[256,256]{1,0:T(8,128)(2,1)S(1)} %get-tuple-element.56.l0), channel_id=1, source_target_pairs={{0,4},{1,5},{2,6},{3,7},{4,8},{5,9},{6,10},{7,11},{8,12},{9,13},{1... | collective-permute-start | bytes 393224 | tf_op jit(solution)/shard_map/ppermute | solution.py:300
  32.9 10.3 %collective-permute-start.7 = (bf16[256,256]{1,0:T(8,128)(2,1)S(1)}, bf16[256,256]{1,0:T(8,128)(2,1)S(1)}, u32[]{:S(2)}, u32[]{:S(2)}) collective-permute-start(bf16[256,256]{1,0:T(8,128)(2,1)S(1)} %collective-permute-done.4.h0), channel_id=1, source_target_pairs={{0,12},{1,13},{2,14},{3,15},{4,0},{5,1},{6,2},{7,3},{8,4},{9,5},{1... | collective-permute-start | bytes 393224 | tf_op jit(solution)/shard_map/ppermute | solution.py:300
  34.9 8.3 %collective-permute-start.6 = (bf16[256,256]{1,0:T(8,128)(2,1)S(1)}, bf16[256,256]{1,0:T(8,128)(2,1)S(1)}, u32[]{:S(2)}, u32[]{:S(2)}) collective-permute-start(bf16[256,256]{1,0:T(8,128)(2,1)S(1)} %collective-permute-done.4.h0), channel_id=1, source_target_pairs={{0,8},{1,9},{2,10},{3,11},{4,12},{5,13},{6,14},{7,15},{8,0},{9,1},... | collective-permute-start | bytes 393224 | tf_op jit(solution)/shard_map/ppermute | solution.py:300
  36.0 9.1 %collective-permute-start.5 = (bf16[256,256]{1,0:T(8,128)(2,1)S(1)}, bf16[256,256]{1,0:T(8,128)(2,1)S(1)}, u32[]{:S(2)}, u32[]{:S(2)}) collective-permute-start(bf16[256,256]{1,0:T(8,128)(2,1)S(1)} %collective-permute-done.4.h0), channel_id=1, source_target_pairs={{0,4},{1,5},{2,6},{3,7},{4,8},{5,9},{6,10},{7,11},{8,12},{9,13},{1... | collective-permute-start | bytes 393224 | tf_op jit(solution)/shard_map/ppermute | solution.py:300
  78.9 42.9 %all-to-all-start.1 = ((bf16[4,128,1280]{2,1,0:T(8,128)(2,1)}), bf16[4,128,1280]{2,1,0:T(8,128)(2,1)S(1)}, u32[]{:S(2)}, u32[]{:S(2)}) async-start(bf16[4,128,1280]{2,1,0:T(8,128)(2,1)} %get-tuple-element.58), calls=%async_computation.1 | async-start | bytes 2621440 | tf_op jit(solution)/shard_map/all_to_all | solution.py:296
  83.5 7.2 %collective-permute-start.11 = (f32[256,256]{1,0:T(8,128)S(1)}, f32[256,256]{1,0:T(8,128)S(1)}, u32[]{:S(2)}, u32[]{:S(2)}) collective-permute-start(f32[256,256]{1,0:T(8,128)S(1)} %copy-done.13), channel_id=1, source_target_pairs={{0,4},{1,5},{2,6},{3,7},{4,8},{5,9},{6,10},{7,11},{8,12},{9,13},{1... | collective-permute-start | bytes 786440 | tf_op jit(solution)/shard_map/ppermute | solution.py:300
  85.4 6.4 %collective-permute-start.12 = (f32[256,256]{1,0:T(8,128)S(1)}, f32[256,256]{1,0:T(8,128)S(1)}, u32[]{:S(2)}, u32[]{:S(2)}) collective-permute-start(f32[256,256]{1,0:T(8,128)S(1)} %copy-done.12), channel_id=1, source_target_pairs={{0,12},{1,13},{2,14},{3,15},{4,0},{5,1},{6,2},{7,3},{8,4},{9,5},{1... | collective-permute-start | bytes 786440 | tf_op jit(solution)/shard_map/ppermute | solution.py:300
  85.6 7.8 %collective-permute-start.14 = (f32[384,256]{1,0:T(8,128)}, f32[384,256]{1,0:T(8,128)S(1)}, u32[]{:S(2)}, u32[]{:S(2)}) collective-permute-start(f32[384,256]{1,0:T(8,128)} %get-tuple-element.79), channel_id=1, source_target_pairs={{16,12},{17,13},{18,14},{19,15},{48,44},{49,45},{50,46},{51,47},{8... | collective-permute-start | bytes 1179656 | tf_op jit(solution)/shard_map/ppermute | solution.py:336
  91.9 6.4 %collective-permute-start.13 = (f32[256,256]{1,0:T(8,128)S(1)}, f32[256,256]{1,0:T(8,128)S(1)}, u32[]{:S(2)}, u32[]{:S(2)}) collective-permute-start(f32[256,256]{1,0:T(8,128)S(1)} %get-tuple-element.69), channel_id=1, source_target_pairs={{0,4},{1,5},{2,6},{3,7},{4,8},{5,9},{6,10},{7,11},{8,12},{9,13},{1... | collective-permute-start | bytes 786440 | tf_op jit(solution)/shard_map/ppermute | solution.py:300
  99.1 39.5 %collective-permute-start.19 = (f32[384,256]{1,0:T(8,128)}, f32[384,256]{1,0:T(8,128)S(1)}, u32[]{:S(2)}, u32[]{:S(2)}) collective-permute-start(f32[384,256]{1,0:T(8,128)} %get-tuple-element.79), channel_id=1, source_target_pairs={{4,0},{5,1},{6,2},{7,3},{8,4},{9,5},{10,6},{11,7},{12,8},{13,9},{1... | collective-permute-start | bytes 1179656 | tf_op jit(solution)/shard_map/ppermute | solution.py:344
  102.7 20.4 %collective-permute-start.15 = (f32[256,256]{1,0:T(8,128)}, f32[256,256]{1,0:T(8,128)}, u32[]{:S(2)}, u32[]{:S(2)}) collective-permute-start(f32[256,256]{1,0:T(8,128)} %far_sum.1), channel_id=1, source_target_pairs={{0,16},{1,17},{2,18},{3,19},{4,20},{5,21},{6,22},{7,23},{8,24},{9,... | collective-permute-start | bytes 786440 | tf_op jit(solution)/shard_map/ppermute | solution.py:304
  117.7 7.1 %collective-permute-start.16 = (f32[256,256]{1,0:T(8,128)}, f32[256,256]{1,0:T(8,128)S(1)}, u32[]{:S(2)}, u32[]{:S(2)}) collective-permute-start(f32[256,256]{1,0:T(8,128)} %get-tuple-element.75), channel_id=1, source_target_pairs={{0,12},{1,13},{2,14},{3,15},{4,0},{5,1},{6,2},{7,3},{8,4},{9,5},{1... | collective-permute-start | bytes 786440 | tf_op jit(solution)/shard_map/ppermute | solution.py:300
  117.7 20.8 %collective-permute-start.17 = (f32[256,256]{1,0:T(8,128)}, f32[256,256]{1,0:T(8,128)S(1)}, u32[]{:S(2)}, u32[]{:S(2)}) collective-permute-start(f32[256,256]{1,0:T(8,128)} %get-tuple-element.76), channel_id=1, source_target_pairs={{0,8},{1,9},{2,10},{3,11},{4,12},{5,13},{6,14},{7,15},{8,0},{9,1},... | collective-permute-start | bytes 786440 | tf_op jit(solution)/shard_map/ppermute | solution.py:300
  119.5 19.1 %collective-permute-start.18 = (f32[256,256]{1,0:T(8,128)}, f32[256,256]{1,0:T(8,128)}, u32[]{:S(2)}, u32[]{:S(2)}) collective-permute-start(f32[256,256]{1,0:T(8,128)} %get-tuple-element.77), channel_id=1, source_target_pairs={{0,4},{1,5},{2,6},{3,7},{4,8},{5,9},{6,10},{7,11},{8,12},{9,13},{1... | collective-permute-start | bytes 786440 | tf_op jit(solution)/shard_map/ppermute | solution.py:300
  139.7 5.2 %collective-permute-start.20 = (bf16[192,256]{1,0:T(8,128)(2,1)S(1)}, bf16[192,256]{1,0:T(8,128)(2,1)S(1)}, u32[]{:S(2)}, u32[]{:S(2)}) collective-permute-start(bf16[192,256]{1,0:T(8,128)(2,1)S(1)} %get-tuple-element.81), channel_id=1, source_target_pairs={{0,3},{1,0},{2,1},{3,2},{4,7},{5,4},{6,5},{7,6},{8,11},{9,8},{10,9... | collective-permute-start | bytes 294920 | tf_op jit(solution)/shard_map/ppermute | solution.py:292
  142.7 6.2 %collective-permute-start.21 = (bf16[192,256]{1,0:T(8,128)(2,1)S(1)}, bf16[192,256]{1,0:T(8,128)(2,1)S(1)}, u32[]{:S(2)}, u32[]{:S(2)}) collective-permute-start(bf16[192,256]{1,0:T(8,128)(2,1)S(1)} %get-tuple-element.82), channel_id=1, source_target_pairs={{0,2},{1,3},{2,0},{3,1},{4,6},{5,7},{6,4},{7,5},{8,10},{9,11},{10,... | collective-permute-start | bytes 294920 | tf_op jit(solution)/shard_map/ppermute | solution.py:292
  143.6 6.3 %collective-permute-start.22 = (bf16[192,256]{1,0:T(8,128)(2,1)S(1)}, bf16[192,256]{1,0:T(8,128)(2,1)S(1)}, u32[]{:S(2)}, u32[]{:S(2)}) collective-permute-start(bf16[192,256]{1,0:T(8,128)(2,1)S(1)} %get-tuple-element.83), channel_id=1, source_target_pairs={{0,1},{1,2},{2,3},{3,0},{4,5},{5,6},{6,7},{7,4},{8,9},{9,10},{10,1... | collective-permute-start | bytes 294920 | tf_op jit(solution)/shard_map/ppermute | solution.py:292
  (23 other events, 231.9 us)

commit v9 on v8

--- a/solution.py
+++ b/solution.py
@@ -37,7 +37,7 @@
 
 def attention_kernel(
     len_ref, where_ref, q_in, s0, s1, s2, s3, before_in, h0, h1, h2, h3, l0, l1, l2, l3,
-    o_ref, g0, g1, g2, g3, g4, g5, g6, g7, back_grad_ref, own_grad_ref,
+    o_ref, g0, g1, g2, g3, g4, g5, g6, g7, own_grad_ref, back_k_ref, back_v_ref,
     key2, value1, key_t, value_t, s_first, s_second, p_first, p_second,
     grad2_first, grad2_second, rows_first, rows_second, key_sum, value_sum, q_all, staged, sems,
 ):
@@ -166,10 +166,13 @@
         pass
 
     outs = [(i * 256, i * 256 + 256, ref) for i, ref in enumerate((g0, g1, g2, g3, g4, g5, g6, g7))]
-    outs += [(PROMPT_ROWS, PROMPT_ROWS + BACK, back_grad_ref), (PROMPT_ROWS + BACK, all_rows, own_grad_ref)]
+    outs += [(PROMPT_ROWS + BACK, all_rows, own_grad_ref)]
     for first, last, target in outs:
         target[:, :128] = key_sum[first:last, :] * FACTOR
         target[:, 128:] = value_sum[first:last, :]
+    before = slice(PROMPT_ROWS, PROMPT_ROWS + BACK)
+    back_k_ref[...] = key_sum[before, :] * FACTOR
+    back_v_ref[...] = value_sum[before, :]
 
 
 def call(body, scalars, operands, outs, name, scratch=(), limit=24, cost=None, space=pltpu.VMEM, extra=()):
@@ -193,7 +196,8 @@
     flops = 12 * 2560 * 2560 * 128
     return call(
         attention_kernel, (resp_len, where), operands,
-        [((4, 128, 2 * WIDE), bf16)] + [((256, 256), f32)] * 8 + [((BACK, 256), f32), ((OWN_ROWS, 256), f32)],
+        [((4, 128, 2 * WIDE), bf16)] + [((256, 256), f32)] * 8
+        + [((OWN_ROWS, 256), f32)] + [((BACK, 128), f32)] * 2,
         "attention",
         scratch=[
             pltpu.VMEM((rows, 256), bf16),
@@ -258,13 +262,23 @@
         target[:64, :] = total.astype(jnp.bfloat16)
         block = lax.rem(x + 4 - d, 4)
         behind = pl.ds(pl.multiple_of(jnp.maximum(block - 1, 0) * 128, 128), 128)
-        extra = jnp.where(block > 0, crossing_ref[behind, :] + within_ref[behind, :], 0.0)
-        target[64:, :] = (own_ref[block_at(x, d), :] + extra).astype(jnp.bfloat16)
+        for lanes, extra in (
+            (slice(0, 128), crossing_ref[behind, :] + within_ref[behind, :128]),
+            (slice(128, 256), within_ref[behind, 128:]),
+        ):
+            total = own_ref[block_at(x, d), lanes] + jnp.where(block > 0, extra, 0.0)
+            target[64:, lanes] = total.astype(jnp.bfloat16)
 
 
 def two_sums_kernel(a, b, c, d, ab_ref, cd_ref):
     ab_ref[...] = a[...] + b[...]
     cd_ref[...] = c[...] + d[...]
+
+
+def pack_window_kernel(where_ref, k_ref, v_ref, over_z, out_ref):
+    first = where_ref[0] == 0
+    out_ref[:, :128] = jnp.where(first, 0.0, k_ref[...])
+    out_ref[:, 128:] = jnp.where(first, over_z[...], v_ref[...])
 
 
 def sum_kernel(a, b, *refs):
@@ -328,20 +342,22 @@
     before = along_rows(ahead, 1)
     far_keys = [far] + [along_y(far, d) for d in (1, 2, 3)]
 
-    o, h2, h1, h0, h3, l2, l1, l0, l3, back_grad, own_grad = attention(
+    o, h2, h1, h0, h3, l2, l1, l0, l3, own_grad, back_k, back_v = attention(
         resp_len, where, (q_all, *s, before, *far_keys, *near_keys)
     )
 
     through, minus = along_y(h2, 1), along_y(h1, -1)
-    crossing = lax.ppermute(back_grad, "seq", [(i, i - 4) for i in range(16, 20)])
+    crossing = lax.ppermute(back_k, "seq", [(i, i - 4) for i in range(16, 20)])
+    over_z = lax.ppermute(back_v, "seq", [(i, i - 16) for i in range(16, 20)])
     part = [((256, 256), f32)]
     plus, stay = call(two_sums_kernel, (), (h3, through, h0, minus), part * 2, "two_sums")
     plus = along_y(plus, 1)
-    (give,) = call(sum_kernel, (), (stay, plus), part, "far_sum", extra=(crossing,))
-    give, back_grad, l1, l2, l3 = lax.optimization_barrier((give, back_grad, l1, l2, l3))
+    (give,) = call(sum_kernel, (), (stay, plus), part, "far_sum", extra=(crossing, over_z))
     got = along_z(give)
     one, two, three = along_y(l1, -1), along_y(l2, -2), along_y(l3, 1)
-    within = lax.ppermute(back_grad, "seq", [(i, i - 4) for i in range(4, 32) if i // 4 != 4])
+    (back,) = call(pack_window_kernel, (where,), (back_k, back_v, over_z), [((BACK, 256), f32)], "pack_window")
+    pairs = [(i, i - 4) for i in range(4, 32) if i // 4 != 4] + [(i, i + 12) for i in range(4)]
+    within = lax.ppermute(back, "seq", pairs)
 
     attn_out, q_grad = call(
         unpack_rows_kernel, (), (exchange_x(o),), [((rows, HEADS * HEAD_DIM), bf16)] * 2, "unpack_rows"

time: 152 us -> 143 us (0.941)
  the two profiles are of different devices: /device:TPU:40 before, /device:TPU:32 now
where the time goes in v9:
time: 143 us
  starting transfers between devices  58.6 us (41%)
  Pallas kernels  42.3 us (30%)
  waiting for transfers between devices  37.6 us (26%)
  local copies, waits for them, and re-layouts  2.73 us (2%)
    pallas_call x10, Pallas kernels, call(): pl.pallas_call(body, in_specs=[smem] * len(scalars) + [pl.BlockSpec(memor...  42.3 us
    ppermute x12, waiting for transfers between devices, along_y(): lax.ppermute(value, 'seq', [(i, i // 16 * 16 + (i + 4 * step) % 16) for i...  19 us
    ppermute x12, starting transfers between devices, along_y(): lax.ppermute(value, 'seq', [(i, i // 16 * 16 + (i + 4 * step) % 16) for i...  17.6 us
    ppermute x2, starting transfers between devices, along_z(): return lax.ppermute(value, 'seq', [(i, (i + 16) % 32) for i in range(32)])  14.8 us
    ppermute x6, starting transfers between devices, along_x(): lax.ppermute(value, 'seq', [(i, i // 4 * 4 + (i + step) % 4) for i in ran...  10.8 us
    ppermute x1, waiting for transfers between devices, local(): over_z = lax.ppermute(back_v, 'seq', [(i, i - 16) for i in range(16, 20)])  9.7 us
    ppermute x6, waiting for transfers between devices, along_x(): lax.ppermute(value, 'seq', [(i, i // 4 * 4 + (i + step) % 4) for i in ran...  8.85 us
    all_to_all x2, starting transfers between devices, exchange_x(): lax.all_to_all(value, 'seq', 0, 0, axis_index_groups=X_GROUPS, tiled=True)  8.56 us
  transfers between devices with their start and end apart: 26, of which 13 were waited for; matrix products, arithmetic and copies ran while one was open for 0% of the time, Pallas kernels for 2%

profile of v9, /device:TPU:32, one launch (start us, length us, event | category | flops | bytes accessed | tf_op | source)
XLA Modules:
  0.0 142.8 jit_solution(17044517490591714283)
XLA Ops:
  1.3 3.7 %pack.1 = (bf16[192,256]{1,0:T(8,128)(2,1)}, bf16[192,256]{1,0:T(8,128)(2,1)}, bf16[192,256]{1,0:T(8,128)(2,1)}, bf16[192,256]{1,0:T(8,128)(2,1)}, bf16[4,128,1280]{2,1,0:T(8,128)(2,1)}) custom-call(s32[2]{0:T(128)} %pad_add_fusion.where_ref, bf16[64,512]{1,0:T(8,128)(2,1)} %pk.1, bf16[64,512]{1,0:T(8,128)(2,1)} %pv.1, bf16[128,512]{1,0:T(8,128)(2,1)} %k.1, ...), custom_call_target="tpu_custom_call" | custom-call | tf_op jit(solution)/shard_map/pack/pallas_call | solution.py:180
  5.0 1.6 %collective-permute-start = (bf16[192,256]{1,0:T(8,128)(2,1)}, bf16[192,256]{1,0:T(8,128)(2,1)S(1)}, u32[]{:S(2)}, u32[]{:S(2)}) collective-permute-start(bf16[192,256]{1,0:T(8,128)(2,1)} %get-tuple-element.44), channel_id=1, source_target_pairs={{0,1},{1,2},{2,3},{3,0},{4,5},{5,6},{6,7},{7,4},{8,9},{9,10},{10,1... | collective-permute-start | bytes 294920 | tf_op jit(solution)/shard_map/ppermute | solution.py:306
  6.6 2.7 %collective-permute-start.1 = (bf16[192,256]{1,0:T(8,128)(2,1)}, bf16[192,256]{1,0:T(8,128)(2,1)S(1)}, u32[]{:S(2)}, u32[]{:S(2)}) collective-permute-start(bf16[192,256]{1,0:T(8,128)(2,1)} %get-tuple-element.45), channel_id=1, source_target_pairs={{0,2},{1,3},{2,0},{3,1},{4,6},{5,7},{6,4},{7,5},{8,10},{9,11},{10,... | collective-permute-start | bytes 294920 | tf_op jit(solution)/shard_map/ppermute | solution.py:306
  11.4 2.8 %collective-permute-done.1.s2 = bf16[192,256]{1,0:T(8,128)(2,1)S(1)} collective-permute-done((bf16[192,256]{1,0:T(8,128)(2,1)}, bf16[192,256]{1,0:T(8,128)(2,1)S(1)}, u32[]{:S(2)}, u32[]{:S(2)}) %collective-permute-start.1) | collective-permute-done | bytes 98336 | tf_op jit(solution)/shard_map/ppermute | solution.py:306
  15.8 3.9 %all-to-all-start = ((bf16[4,128,1280]{2,1,0:T(8,128)(2,1)}), bf16[4,128,1280]{2,1,0:T(8,128)(2,1)S(1)}, u32[]{:S(2)}, u32[]{:S(2)}) async-start(bf16[4,128,1280]{2,1,0:T(8,128)(2,1)} %get-tuple-element.50), calls=%async_computation | async-start | bytes 2621440 | tf_op jit(solution)/shard_map/all_to_all | solution.py:310
  19.7 6.3 %collective-permute-start.4 = (bf16[256,256]{1,0:T(8,128)(2,1)S(1)}, bf16[256,256]{1,0:T(8,128)(2,1)S(1)}, u32[]{:S(2)}, u32[]{:S(2)}) collective-permute-start(bf16[256,256]{1,0:T(8,128)(2,1)S(1)} %get-tuple-element.52.l0), channel_id=1, source_target_pairs={{0,16},{1,17},{2,18},{3,19},{4,20},{5,21},{6,22},{7,23},{8,24},{9,... | collective-permute-start | bytes 393224 | tf_op jit(solution)/shard_map/ppermute | solution.py:318
  25.9 3.0 %collective-permute-start.10 = (bf16[256,256]{1,0:T(8,128)(2,1)S(1)}, bf16[256,256]{1,0:T(8,128)(2,1)S(1)}, u32[]{:S(2)}, u32[]{:S(2)}) collective-permute-start(bf16[256,256]{1,0:T(8,128)(2,1)S(1)} %get-tuple-element.52.l0), channel_id=1, source_target_pairs={{0,12},{1,13},{2,14},{3,15},{4,0},{5,1},{6,2},{7,3},{8,4},{9,5},{1... | collective-permute-start | bytes 393224 | tf_op jit(solution)/shard_map/ppermute | solution.py:314
  29.6 2.9 %collective-permute-start.3 = (bf16[384,256]{1,0:T(8,128)(2,1)S(1)}, bf16[384,256]{1,0:T(8,128)(2,1)S(1)}, u32[]{:S(2)}, u32[]{:S(2)}) collective-permute-start(bf16[384,256]{1,0:T(8,128)(2,1)S(1)} %get-tuple-element.51), channel_id=1, source_target_pairs={{0,4},{1,5},{2,6},{3,7},{4,8},{5,9},{6,10},{7,11},{8,12},{9,13},{1... | collective-permute-start | bytes 589832 | tf_op jit(solution)/shard_map/ppermute | solution.py:323
  32.5 2.0 %collective-permute-start.8 = (bf16[256,256]{1,0:T(8,128)(2,1)S(1)}, bf16[256,256]{1,0:T(8,128)(2,1)S(1)}, u32[]{:S(2)}, u32[]{:S(2)}) collective-permute-start(bf16[256,256]{1,0:T(8,128)(2,1)S(1)} %get-tuple-element.52.l0), channel_id=1, source_target_pairs={{0,4},{1,5},{2,6},{3,7},{4,8},{5,9},{6,10},{7,11},{8,12},{9,13},{1... | collective-permute-start | bytes 393224 | tf_op jit(solution)/shard_map/ppermute | solution.py:314
  37.6 3.8 %collective-permute-done.8.l1 = bf16[256,256]{1,0:T(8,128)(2,1)S(1)} collective-permute-done((bf16[256,256]{1,0:T(8,128)(2,1)S(1)}, bf16[256,256]{1,0:T(8,128)(2,1)S(1)}, u32[]{:S(2)}, u32[]{:S(2)}) %collective-permute-start.8) | collective-permute-done | bytes 131104 | tf_op jit(solution)/shard_map/ppermute | solution.py:314
  41.4 4.1 %collective-permute-done.6.h2 = bf16[256,256]{1,0:T(8,128)(2,1)S(1)} collective-permute-done((bf16[256,256]{1,0:T(8,128)(2,1)S(1)}, bf16[256,256]{1,0:T(8,128)(2,1)S(1)}, u32[]{:S(2)}, u32[]{:S(2)}) %collective-permute-start.6) | collective-permute-done | bytes 131104 | tf_op jit(solution)/shard_map/ppermute | solution.py:314
  47.2 32.0 %attention.1 = (bf16[4,128,1280]{2,1,0:T(8,128)(2,1)}, f32[256,256]{1,0:T(8,128)}, f32[256,256]{1,0:T(8,128)}, f32[256,256]{1,0:T(8,128)}, f32[256,256]{1,0:T(8,...) custom-call(s32[16]{0:T(128)} %len_ref.1, ...), custom_call_target="tpu_custom_call" | custom-call | flops 10066329600 | bytes 8000000 | tf_op jit(solution)/shard_map/attention/pallas_call | solution.py:180
  79.3 4.7 %all-to-all-start.1 = ((bf16[4,128,1280]{2,1,0:T(8,128)(2,1)}), bf16[4,128,1280]{2,1,0:T(8,128)(2,1)S(1)}, u32[]{:S(2)}, u32[]{:S(2)}) async-start(bf16[4,128,1280]{2,1,0:T(8,128)(2,1)} %get-tuple-element.54), calls=%async_computation.1 | async-start | bytes 2621440 | tf_op jit(solution)/shard_map/all_to_all | solution.py:310
  85.2 2.1 %collective-permute-start.12 = (f32[256,256]{1,0:T(8,128)S(1)}, f32[256,256]{1,0:T(8,128)S(1)}, u32[]{:S(2)}, u32[]{:S(2)}) collective-permute-start(f32[256,256]{1,0:T(8,128)S(1)} %copy-done.14), channel_id=1, source_target_pairs={{0,12},{1,13},{2,14},{3,15},{4,0},{5,1},{6,2},{7,3},{8,4},{9,5},{1... | collective-permute-start | bytes 786440 | tf_op jit(solution)/shard_map/ppermute | solution.py:314
  88.5 3.3 %collective-permute-done.11.b = f32[256,256]{1,0:T(8,128)S(1)} collective-permute-done((f32[256,256]{1,0:T(8,128)S(1)}, f32[256,256]{1,0:T(8,128)S(1)}, u32[]{:S(2)}, u32[]{:S(2)}) %collective-permute-start.11) | collective-permute-done | bytes 262176 | tf_op jit(solution)/shard_map/ppermute | solution.py:314
  91.9 1.7 %collective-permute-start.13 = (f32[256,256]{1,0:T(8,128)S(1)}, f32[256,256]{1,0:T(8,128)S(1)}, u32[]{:S(2)}, u32[]{:S(2)}) collective-permute-start(f32[256,256]{1,0:T(8,128)S(1)} %get-tuple-element.65), channel_id=1, source_target_pairs={{0,4},{1,5},{2,6},{3,7},{4,8},{5,9},{6,10},{7,11},{8,12},{9,13},{1... | collective-permute-start | bytes 786440 | tf_op jit(solution)/shard_map/ppermute | solution.py:314
  94.2 9.7 %collective-permute-done.15.refs_1_.over_z = f32[384,128]{1,0:T(8,128)S(1)} collective-permute-done((f32[384,128]{1,0:T(8,128)S(1)}, f32[384,128]{1,0:T(8,128)S(1)}, u32[]{:S(2)}, u32[]{:S(2)}) %collective-permute-start.15) | collective-permute-done | bytes 196640 | tf_op jit(solution)/shard_map/ppermute | solution.py:351
  104.5 2.1 %collective-permute-start.20 = (f32[384,256]{1,0:T(8,128)S(1)}, f32[384,256]{1,0:T(8,128)S(1)}, u32[]{:S(2)}, u32[]{:S(2)}) collective-permute-start(f32[384,256]{1,0:T(8,128)S(1)} %pack_window.1), channel_id=1, source_target_pairs={{4,0},{5,1},{6,2},{7,3},{8,4},{9,5},{10,6},{11,7},{12,8},{13,9},{1... | collective-permute-start | bytes 1179656 | tf_op jit(solution)/shard_map/ppermute | solution.py:360
  107.4 8.5 %collective-permute-start.16 = (f32[256,256]{1,0:T(8,128)}, f32[256,256]{1,0:T(8,128)}, u32[]{:S(2)}, u32[]{:S(2)}) collective-permute-start(f32[256,256]{1,0:T(8,128)} %far_sum.1), channel_id=1, source_target_pairs={{0,16},{1,17},{2,18},{3,19},{4,20},{5,21},{6,22},{7,23},{8,24},{9,... | collective-permute-start | bytes 786440 | tf_op jit(solution)/shard_map/ppermute | solution.py:318
  115.8 3.2 %collective-permute-start.17 = (f32[256,256]{1,0:T(8,128)}, f32[256,256]{1,0:T(8,128)S(1)}, u32[]{:S(2)}, u32[]{:S(2)}) collective-permute-start(f32[256,256]{1,0:T(8,128)} %get-tuple-element.68), channel_id=1, source_target_pairs={{0,12},{1,13},{2,14},{3,15},{4,0},{5,1},{6,2},{7,3},{8,4},{9,5},{1... | collective-permute-start | bytes 786440 | tf_op jit(solution)/shard_map/ppermute | solution.py:314
  122.2 3.9 %collective-permute-done.17.n1 = f32[256,256]{1,0:T(8,128)S(1)} collective-permute-done((f32[256,256]{1,0:T(8,128)}, f32[256,256]{1,0:T(8,128)S(1)}, u32[]{:S(2)}, u32[]{:S(2)}) %collective-permute-start.17) | collective-permute-done | bytes 262176 | tf_op jit(solution)/shard_map/ppermute | solution.py:314
  127.4 2.4 %collective-permute-done.19.n3 = f32[256,256]{1,0:T(8,128)} collective-permute-done((f32[256,256]{1,0:T(8,128)}, f32[256,256]{1,0:T(8,128)}, u32[]{:S(2)}, u32[]{:S(2)}) %collective-permute-start.19) | collective-permute-done | bytes 262176 | tf_op jit(solution)/shard_map/ppermute | solution.py:314
  130.9 3.3 %collective-permute-start.21 = (bf16[192,256]{1,0:T(8,128)(2,1)S(1)}, bf16[192,256]{1,0:T(8,128)(2,1)S(1)}, u32[]{:S(2)}, u32[]{:S(2)}) collective-permute-start(bf16[192,256]{1,0:T(8,128)(2,1)S(1)} %get-tuple-element.73), channel_id=1, source_target_pairs={{0,3},{1,0},{2,1},{3,2},{4,7},{5,4},{6,5},{7,6},{8,11},{9,8},{10,9... | collective-permute-start | bytes 294920 | tf_op jit(solution)/shard_map/ppermute | solution.py:306
  136.5 4.0 %collective-permute-done.22.f2 = bf16[192,256]{1,0:T(8,128)(2,1)S(1)} collective-permute-done((bf16[192,256]{1,0:T(8,128)(2,1)S(1)}, bf16[192,256]{1,0:T(8,128)(2,1)S(1)}, u32[]{:S(2)}, u32[]{:S(2)}) %collective-permute-start.22) | collective-permute-done | bytes 98336 | tf_op jit(solution)/shard_map/ppermute | solution.py:306
  (87 shorter events, 24.4 us)
Async XLA Ops:
  5.0 6.4 %collective-permute-start = (bf16[192,256]{1,0:T(8,128)(2,1)}, bf16[192,256]{1,0:T(8,128)(2,1)S(1)}, u32[]{:S(2)}, u32[]{:S(2)}) collective-permute-start(bf16[192,256]{1,0:T(8,128)(2,1)} %get-tuple-element.44), channel_id=1, source_target_pairs={{0,1},{1,2},{2,3},{3,0},{4,5},{5,6},{6,7},{7,4},{8,9},{9,10},{10,1... | collective-permute-start | bytes 294920 | tf_op jit(solution)/shard_map/ppermute | solution.py:306
  6.6 7.6 %collective-permute-start.1 = (bf16[192,256]{1,0:T(8,128)(2,1)}, bf16[192,256]{1,0:T(8,128)(2,1)S(1)}, u32[]{:S(2)}, u32[]{:S(2)}) collective-permute-start(bf16[192,256]{1,0:T(8,128)(2,1)} %get-tuple-element.45), channel_id=1, source_target_pairs={{0,2},{1,3},{2,0},{3,1},{4,6},{5,7},{6,4},{7,5},{8,10},{9,11},{10,... | collective-permute-start | bytes 294920 | tf_op jit(solution)/shard_map/ppermute | solution.py:306
  15.8 29.7 %all-to-all-start = ((bf16[4,128,1280]{2,1,0:T(8,128)(2,1)}), bf16[4,128,1280]{2,1,0:T(8,128)(2,1)S(1)}, u32[]{:S(2)}, u32[]{:S(2)}) async-start(bf16[4,128,1280]{2,1,0:T(8,128)(2,1)} %get-tuple-element.50), calls=%async_computation | async-start | bytes 2621440 | tf_op jit(solution)/shard_map/all_to_all | solution.py:310
  19.7 14.8 %collective-permute-start.4 = (bf16[256,256]{1,0:T(8,128)(2,1)S(1)}, bf16[256,256]{1,0:T(8,128)(2,1)S(1)}, u32[]{:S(2)}, u32[]{:S(2)}) collective-permute-start(bf16[256,256]{1,0:T(8,128)(2,1)S(1)} %get-tuple-element.52.l0), channel_id=1, source_target_pairs={{0,16},{1,17},{2,18},{3,19},{4,20},{5,21},{6,22},{7,23},{8,24},{9,... | collective-permute-start | bytes 393224 | tf_op jit(solution)/shard_map/ppermute | solution.py:318
  25.9 9.9 %collective-permute-start.10 = (bf16[256,256]{1,0:T(8,128)(2,1)S(1)}, bf16[256,256]{1,0:T(8,128)(2,1)S(1)}, u32[]{:S(2)}, u32[]{:S(2)}) collective-permute-start(bf16[256,256]{1,0:T(8,128)(2,1)S(1)} %get-tuple-element.52.l0), channel_id=1, source_target_pairs={{0,12},{1,13},{2,14},{3,15},{4,0},{5,1},{6,2},{7,3},{8,4},{9,5},{1... | collective-permute-start | bytes 393224 | tf_op jit(solution)/shard_map/ppermute | solution.py:314
  29.0 7.9 %collective-permute-start.9 = (bf16[256,256]{1,0:T(8,128)(2,1)S(1)}, bf16[256,256]{1,0:T(8,128)(2,1)S(1)}, u32[]{:S(2)}, u32[]{:S(2)}) collective-permute-start(bf16[256,256]{1,0:T(8,128)(2,1)S(1)} %get-tuple-element.52.l0), channel_id=1, source_target_pairs={{0,8},{1,9},{2,10},{3,11},{4,12},{5,13},{6,14},{7,15},{8,0},{9,1},... | collective-permute-start | bytes 393224 | tf_op jit(solution)/shard_map/ppermute | solution.py:314
  29.6 11.8 %collective-permute-start.3 = (bf16[384,256]{1,0:T(8,128)(2,1)S(1)}, bf16[384,256]{1,0:T(8,128)(2,1)S(1)}, u32[]{:S(2)}, u32[]{:S(2)}) collective-permute-start(bf16[384,256]{1,0:T(8,128)(2,1)S(1)} %get-tuple-element.51), channel_id=1, source_target_pairs={{0,4},{1,5},{2,6},{3,7},{4,8},{5,9},{6,10},{7,11},{8,12},{9,13},{1... | collective-permute-start | bytes 589832 | tf_op jit(solution)/shard_map/ppermute | solution.py:323
  32.5 8.9 %collective-permute-start.8 = (bf16[256,256]{1,0:T(8,128)(2,1)S(1)}, bf16[256,256]{1,0:T(8,128)(2,1)S(1)}, u32[]{:S(2)}, u32[]{:S(2)}) collective-permute-start(bf16[256,256]{1,0:T(8,128)(2,1)S(1)} %get-tuple-element.52.l0), channel_id=1, source_target_pairs={{0,4},{1,5},{2,6},{3,7},{4,8},{5,9},{6,10},{7,11},{8,12},{9,13},{1... | collective-permute-start | bytes 393224 | tf_op jit(solution)/shard_map/ppermute | solution.py:314
  34.4 6.9 %collective-permute-start.7 = (bf16[256,256]{1,0:T(8,128)(2,1)S(1)}, bf16[256,256]{1,0:T(8,128)(2,1)S(1)}, u32[]{:S(2)}, u32[]{:S(2)}) collective-permute-start(bf16[256,256]{1,0:T(8,128)(2,1)S(1)} %collective-permute-done.4.h0), channel_id=1, source_target_pairs={{0,12},{1,13},{2,14},{3,15},{4,0},{5,1},{6,2},{7,3},{8,4},{9,5},{1... | collective-permute-start | bytes 393224 | tf_op jit(solution)/shard_map/ppermute | solution.py:314
  35.8 9.7 %collective-permute-start.6 = (bf16[256,256]{1,0:T(8,128)(2,1)S(1)}, bf16[256,256]{1,0:T(8,128)(2,1)S(1)}, u32[]{:S(2)}, u32[]{:S(2)}) collective-permute-start(bf16[256,256]{1,0:T(8,128)(2,1)S(1)} %collective-permute-done.4.h0), channel_id=1, source_target_pairs={{0,8},{1,9},{2,10},{3,11},{4,12},{5,13},{6,14},{7,15},{8,0},{9,1},... | collective-permute-start | bytes 393224 | tf_op jit(solution)/shard_map/ppermute | solution.py:314
  36.9 8.6 %collective-permute-start.5 = (bf16[256,256]{1,0:T(8,128)(2,1)S(1)}, bf16[256,256]{1,0:T(8,128)(2,1)S(1)}, u32[]{:S(2)}, u32[]{:S(2)}) collective-permute-start(bf16[256,256]{1,0:T(8,128)(2,1)S(1)} %collective-permute-done.4.h0), channel_id=1, source_target_pairs={{0,4},{1,5},{2,6},{3,7},{4,8},{5,9},{6,10},{7,11},{8,12},{9,13},{1... | collective-permute-start | bytes 393224 | tf_op jit(solution)/shard_map/ppermute | solution.py:314
  79.3 40.7 %all-to-all-start.1 = ((bf16[4,128,1280]{2,1,0:T(8,128)(2,1)}), bf16[4,128,1280]{2,1,0:T(8,128)(2,1)S(1)}, u32[]{:S(2)}, u32[]{:S(2)}) async-start(bf16[4,128,1280]{2,1,0:T(8,128)(2,1)} %get-tuple-element.54), calls=%async_computation.1 | async-start | bytes 2621440 | tf_op jit(solution)/shard_map/all_to_all | solution.py:310
  84.0 7.8 %collective-permute-start.11 = (f32[256,256]{1,0:T(8,128)S(1)}, f32[256,256]{1,0:T(8,128)S(1)}, u32[]{:S(2)}, u32[]{:S(2)}) collective-permute-start(f32[256,256]{1,0:T(8,128)S(1)} %copy-done.15), channel_id=1, source_target_pairs={{0,4},{1,5},{2,6},{3,7},{4,8},{5,9},{6,10},{7,11},{8,12},{9,13},{1... | collective-permute-start | bytes 786440 | tf_op jit(solution)/shard_map/ppermute | solution.py:314
  85.2 6.6 %collective-permute-start.12 = (f32[256,256]{1,0:T(8,128)S(1)}, f32[256,256]{1,0:T(8,128)S(1)}, u32[]{:S(2)}, u32[]{:S(2)}) collective-permute-start(f32[256,256]{1,0:T(8,128)S(1)} %copy-done.14), channel_id=1, source_target_pairs={{0,12},{1,13},{2,14},{3,15},{4,0},{5,1},{6,2},{7,3},{8,4},{9,5},{1... | collective-permute-start | bytes 786440 | tf_op jit(solution)/shard_map/ppermute | solution.py:314
  87.2 16.7 %collective-permute-start.15 = (f32[384,128]{1,0:T(8,128)S(1)}, f32[384,128]{1,0:T(8,128)S(1)}, u32[]{:S(2)}, u32[]{:S(2)}) collective-permute-start(f32[384,128]{1,0:T(8,128)S(1)} %copy-done.5), channel_id=1, source_target_pairs={{16,0},{17,1},{18,2},{19,3},{48,32},{49,33},{50,34},{51,35},{80,64... | collective-permute-start | bytes 589832 | tf_op jit(solution)/shard_map/ppermute | solution.py:351
  91.9 14.8 %collective-permute-start.13 = (f32[256,256]{1,0:T(8,128)S(1)}, f32[256,256]{1,0:T(8,128)S(1)}, u32[]{:S(2)}, u32[]{:S(2)}) collective-permute-start(f32[256,256]{1,0:T(8,128)S(1)} %get-tuple-element.65), channel_id=1, source_target_pairs={{0,4},{1,5},{2,6},{3,7},{4,8},{5,9},{6,10},{7,11},{8,12},{9,13},{1... | collective-permute-start | bytes 786440 | tf_op jit(solution)/shard_map/ppermute | solution.py:314
  93.6 13.0 %collective-permute-start.14 = (f32[384,128]{1,0:T(8,128)S(1)}, f32[384,128]{1,0:T(8,128)S(1)}, u32[]{:S(2)}, u32[]{:S(2)}) collective-permute-start(f32[384,128]{1,0:T(8,128)S(1)} %copy-done.4), channel_id=1, source_target_pairs={{16,12},{17,13},{18,14},{19,15},{48,44},{49,45},{50,46},{51,47},{8... | collective-permute-start | bytes 589832 | tf_op jit(solution)/shard_map/ppermute | solution.py:350
  104.5 25.2 %collective-permute-start.20 = (f32[384,256]{1,0:T(8,128)S(1)}, f32[384,256]{1,0:T(8,128)S(1)}, u32[]{:S(2)}, u32[]{:S(2)}) collective-permute-start(f32[384,256]{1,0:T(8,128)S(1)} %pack_window.1), channel_id=1, source_target_pairs={{4,0},{5,1},{6,2},{7,3},{8,4},{9,5},{10,6},{11,7},{12,8},{13,9},{1... | collective-permute-start | bytes 1179656 | tf_op jit(solution)/shard_map/ppermute | solution.py:360
  107.4 13.8 %collective-permute-start.16 = (f32[256,256]{1,0:T(8,128)}, f32[256,256]{1,0:T(8,128)}, u32[]{:S(2)}, u32[]{:S(2)}) collective-permute-start(f32[256,256]{1,0:T(8,128)} %far_sum.1), channel_id=1, source_target_pairs={{0,16},{1,17},{2,18},{3,19},{4,20},{5,21},{6,22},{7,23},{8,24},{9,... | collective-permute-start | bytes 786440 | tf_op jit(solution)/shard_map/ppermute | solution.py:318
  115.8 10.3 %collective-permute-start.17 = (f32[256,256]{1,0:T(8,128)}, f32[256,256]{1,0:T(8,128)S(1)}, u32[]{:S(2)}, u32[]{:S(2)}) collective-permute-start(f32[256,256]{1,0:T(8,128)} %get-tuple-element.68), channel_id=1, source_target_pairs={{0,12},{1,13},{2,14},{3,15},{4,0},{5,1},{6,2},{7,3},{8,4},{9,5},{1... | collective-permute-start | bytes 786440 | tf_op jit(solution)/shard_map/ppermute | solution.py:314
  119.1 8.3 %collective-permute-start.18 = (f32[256,256]{1,0:T(8,128)}, f32[256,256]{1,0:T(8,128)}, u32[]{:S(2)}, u32[]{:S(2)}) collective-permute-start(f32[256,256]{1,0:T(8,128)} %get-tuple-element.69), channel_id=1, source_target_pairs={{0,8},{1,9},{2,10},{3,11},{4,12},{5,13},{6,14},{7,15},{8,0},{9,1},... | collective-permute-start | bytes 786440 | tf_op jit(solution)/shard_map/ppermute | solution.py:314
  119.1 10.7 %collective-permute-start.19 = (f32[256,256]{1,0:T(8,128)}, f32[256,256]{1,0:T(8,128)}, u32[]{:S(2)}, u32[]{:S(2)}) collective-permute-start(f32[256,256]{1,0:T(8,128)} %get-tuple-element.70), channel_id=1, source_target_pairs={{0,4},{1,5},{2,6},{3,7},{4,8},{5,9},{6,10},{7,11},{8,12},{9,13},{1... | collective-permute-start | bytes 786440 | tf_op jit(solution)/shard_map/ppermute | solution.py:314
  134.3 6.2 %collective-permute-start.22 = (bf16[192,256]{1,0:T(8,128)(2,1)S(1)}, bf16[192,256]{1,0:T(8,128)(2,1)S(1)}, u32[]{:S(2)}, u32[]{:S(2)}) collective-permute-start(bf16[192,256]{1,0:T(8,128)(2,1)S(1)} %get-tuple-element.74), channel_id=1, source_target_pairs={{0,2},{1,3},{2,0},{3,1},{4,6},{5,7},{6,4},{7,5},{8,10},{9,11},{10,... | collective-permute-start | bytes 294920 | tf_op jit(solution)/shard_map/ppermute | solution.py:306
  135.1 6.3 %collective-permute-start.23 = (bf16[192,256]{1,0:T(8,128)(2,1)S(1)}, bf16[192,256]{1,0:T(8,128)(2,1)S(1)}, u32[]{:S(2)}, u32[]{:S(2)}) collective-permute-start(bf16[192,256]{1,0:T(8,128)(2,1)S(1)} %get-tuple-element.75), channel_id=1, source_target_pairs={{0,1},{1,2},{2,3},{3,0},{4,5},{5,6},{6,7},{7,4},{8,9},{9,10},{10,1... | collective-permute-start | bytes 294920 | tf_op jit(solution)/shard_map/ppermute | solution.py:306
  (26 other events, 214.3 us)

commit v10 on v9

--- a/solution.py
+++ b/solution.py
@@ -275,7 +275,7 @@
     cd_ref[...] = c[...] + d[...]
 
 
-def pack_window_kernel(where_ref, k_ref, v_ref, over_z, out_ref):
+def pack_window_kernel(where_ref, k_ref, v_ref, over_z, after, out_ref):
     first = where_ref[0] == 0
     out_ref[:, :128] = jnp.where(first, 0.0, k_ref[...])
     out_ref[:, 128:] = jnp.where(first, over_z[...], v_ref[...])
@@ -351,11 +351,12 @@
     over_z = lax.ppermute(back_v, "seq", [(i, i - 16) for i in range(16, 20)])
     part = [((256, 256), f32)]
     plus, stay = call(two_sums_kernel, (), (h3, through, h0, minus), part * 2, "two_sums")
+    plus, stay, o = lax.optimization_barrier((plus, stay, o))
     plus = along_y(plus, 1)
     (give,) = call(sum_kernel, (), (stay, plus), part, "far_sum", extra=(crossing, over_z))
     got = along_z(give)
     one, two, three = along_y(l1, -1), along_y(l2, -2), along_y(l3, 1)
-    (back,) = call(pack_window_kernel, (where,), (back_k, back_v, over_z), [((BACK, 256), f32)], "pack_window")
+    (back,) = call(pack_window_kernel, (where,), (back_k, back_v, over_z), [((BACK, 256), f32)], "pack_window", extra=(crossing,))
     pairs = [(i, i - 4) for i in range(4, 32) if i // 4 != 4] + [(i, i + 12) for i in range(4)]
     within = lax.ppermute(back, "seq", pairs)
 

time: 143 us -> 152 us (1.063)
  the two profiles are of different devices: /device:TPU:32 before, /device:TPU:56 now
where the time goes in v10:
time: 152 us; the launch traced here: 151 us
  waiting for transfers between devices  51.6 us (34%)
  starting transfers between devices  51.4 us (34%)
  Pallas kernels  42.4 us (28%)
  local copies, waits for them, and re-layouts  4.58 us (3%)
    pallas_call x10, Pallas kernels, call(): pl.pallas_call(body, in_specs=[smem] * len(scalars) + [pl.BlockSpec(memor...  42.4 us
    ppermute x12, waiting for transfers between devices, along_y(): lax.ppermute(value, 'seq', [(i, i // 16 * 16 + (i + 4 * step) % 16) for i...  24.7 us
    ppermute x12, starting transfers between devices, along_y(): lax.ppermute(value, 'seq', [(i, i // 16 * 16 + (i + 4 * step) % 16) for i...  19 us
    ppermute x1, waiting for transfers between devices, local(): crossing = lax.ppermute(back_k, 'seq', [(i, i - 4) for i in range(16, 20)])  18 us
    ppermute x6, starting transfers between devices, along_x(): lax.ppermute(value, 'seq', [(i, i // 4 * 4 + (i + step) % 4) for i in ran...  10 us
    ppermute x6, waiting for transfers between devices, along_x(): lax.ppermute(value, 'seq', [(i, i // 4 * 4 + (i + step) % 4) for i in ran...  8.85 us
    all_to_all x2, starting transfers between devices, exchange_x(): lax.all_to_all(value, 'seq', 0, 0, axis_index_groups=X_GROUPS, tiled=True)  8.56 us
    ppermute x2, starting transfers between devices, along_z(): return lax.ppermute(value, 'seq', [(i, (i + 16) % 32) for i in range(32)])  6.29 us
  transfers between devices with their start and end apart: 26, of which 13 were waited for; matrix products, arithmetic and copies ran while one was open for 0% of the time, Pallas kernels for 2%

profile of v10, /device:TPU:56, one launch (start us, length us, event | category | flops | bytes accessed | tf_op | source)
XLA Modules:
  0.0 151.5 jit_solution(587907645519463504)
XLA Ops:
  1.3 3.7 %pack.1 = (bf16[192,256]{1,0:T(8,128)(2,1)}, bf16[192,256]{1,0:T(8,128)(2,1)}, bf16[192,256]{1,0:T(8,128)(2,1)}, bf16[192,256]{1,0:T(8,128)(2,1)}, bf16[4,128,1280]{2,1,0:T(8,128)(2,1)}) custom-call(s32[2]{0:T(128)} %pad_add_fusion.where_ref, bf16[64,512]{1,0:T(8,128)(2,1)} %pk.1, bf16[64,512]{1,0:T(8,128)(2,1)} %pv.1, bf16[128,512]{1,0:T(8,128)(2,1)} %k.1, ...), custom_call_target="tpu_custom_call" | custom-call | tf_op jit(solution)/shard_map/pack/pallas_call | solution.py:180
  5.0 1.6 %collective-permute-start = (bf16[192,256]{1,0:T(8,128)(2,1)}, bf16[192,256]{1,0:T(8,128)(2,1)S(1)}, u32[]{:S(2)}, u32[]{:S(2)}) collective-permute-start(bf16[192,256]{1,0:T(8,128)(2,1)} %get-tuple-element.47), channel_id=1, source_target_pairs={{0,1},{1,2},{2,3},{3,0},{4,5},{5,6},{6,7},{7,4},{8,9},{9,10},{10,1... | collective-permute-start | bytes 294920 | tf_op jit(solution)/shard_map/ppermute | solution.py:306
  6.6 2.7 %collective-permute-start.1 = (bf16[192,256]{1,0:T(8,128)(2,1)}, bf16[192,256]{1,0:T(8,128)(2,1)S(1)}, u32[]{:S(2)}, u32[]{:S(2)}) collective-permute-start(bf16[192,256]{1,0:T(8,128)(2,1)} %get-tuple-element.48), channel_id=1, source_target_pairs={{0,2},{1,3},{2,0},{3,1},{4,6},{5,7},{6,4},{7,5},{8,10},{9,11},{10,... | collective-permute-start | bytes 294920 | tf_op jit(solution)/shard_map/ppermute | solution.py:306
  9.3 1.4 collective-permute-start.2
  11.4 2.8 %collective-permute-done.1.s2 = bf16[192,256]{1,0:T(8,128)(2,1)S(1)} collective-permute-done((bf16[192,256]{1,0:T(8,128)(2,1)}, bf16[192,256]{1,0:T(8,128)(2,1)S(1)}, u32[]{:S(2)}, u32[]{:S(2)}) %collective-permute-start.1) | collective-permute-done | bytes 98336 | tf_op jit(solution)/shard_map/ppermute | solution.py:306
  15.7 3.9 %all-to-all-start = ((bf16[4,128,1280]{2,1,0:T(8,128)(2,1)}), bf16[4,128,1280]{2,1,0:T(8,128)(2,1)S(1)}, u32[]{:S(2)}, u32[]{:S(2)}) async-start(bf16[4,128,1280]{2,1,0:T(8,128)(2,1)} %get-tuple-element.53), calls=%async_computation | async-start | bytes 2621440 | tf_op jit(solution)/shard_map/all_to_all | solution.py:310
  19.6 6.3 %collective-permute-start.4 = (bf16[256,256]{1,0:T(8,128)(2,1)S(1)}, bf16[256,256]{1,0:T(8,128)(2,1)S(1)}, u32[]{:S(2)}, u32[]{:S(2)}) collective-permute-start(bf16[256,256]{1,0:T(8,128)(2,1)S(1)} %get-tuple-element.55.l0), channel_id=1, source_target_pairs={{0,16},{1,17},{2,18},{3,19},{4,20},{5,21},{6,22},{7,23},{8,24},{9,... | collective-permute-start | bytes 393224 | tf_op jit(solution)/shard_map/ppermute | solution.py:318
  27.6 3.5 %collective-permute-start.3 = (bf16[384,256]{1,0:T(8,128)(2,1)S(1)}, bf16[384,256]{1,0:T(8,128)(2,1)S(1)}, u32[]{:S(2)}, u32[]{:S(2)}) collective-permute-start(bf16[384,256]{1,0:T(8,128)(2,1)S(1)} %get-tuple-element.54), channel_id=1, source_target_pairs={{0,4},{1,5},{2,6},{3,7},{4,8},{5,9},{6,10},{7,11},{8,12},{9,13},{1... | collective-permute-start | bytes 589832 | tf_op jit(solution)/shard_map/ppermute | solution.py:323
  31.2 1.6 %collective-permute-start.8 = (bf16[256,256]{1,0:T(8,128)(2,1)S(1)}, bf16[256,256]{1,0:T(8,128)(2,1)S(1)}, u32[]{:S(2)}, u32[]{:S(2)}) collective-permute-start(bf16[256,256]{1,0:T(8,128)(2,1)S(1)} %get-tuple-element.55.l0), channel_id=1, source_target_pairs={{0,4},{1,5},{2,6},{3,7},{4,8},{5,9},{6,10},{7,11},{8,12},{9,13},{1... | collective-permute-start | bytes 393224 | tf_op jit(solution)/shard_map/ppermute | solution.py:314
  33.7 2.4 %collective-permute-start.6 = (bf16[256,256]{1,0:T(8,128)(2,1)S(1)}, bf16[256,256]{1,0:T(8,128)(2,1)S(1)}, u32[]{:S(2)}, u32[]{:S(2)}) collective-permute-start(bf16[256,256]{1,0:T(8,128)(2,1)S(1)} %collective-permute-done.4.h0), channel_id=1, source_target_pairs={{0,8},{1,9},{2,10},{3,11},{4,12},{5,13},{6,14},{7,15},{8,0},{9,1},... | collective-permute-start | bytes 393224 | tf_op jit(solution)/shard_map/ppermute | solution.py:314
  37.1 4.3 %collective-permute-done.8.l1 = bf16[256,256]{1,0:T(8,128)(2,1)S(1)} collective-permute-done((bf16[256,256]{1,0:T(8,128)(2,1)S(1)}, bf16[256,256]{1,0:T(8,128)(2,1)S(1)}, u32[]{:S(2)}, u32[]{:S(2)}) %collective-permute-start.8) | collective-permute-done | bytes 131104 | tf_op jit(solution)/shard_map/ppermute | solution.py:314
  41.5 3.0 %collective-permute-done.5.h1 = bf16[256,256]{1,0:T(8,128)(2,1)S(1)} collective-permute-done((bf16[256,256]{1,0:T(8,128)(2,1)S(1)}, bf16[256,256]{1,0:T(8,128)(2,1)S(1)}, u32[]{:S(2)}, u32[]{:S(2)}) %collective-permute-start.5) | collective-permute-done | bytes 131104 | tf_op jit(solution)/shard_map/ppermute | solution.py:314
  46.1 32.0 %attention.1 = (bf16[4,128,1280]{2,1,0:T(8,128)(2,1)}, f32[256,256]{1,0:T(8,128)}, f32[256,256]{1,0:T(8,128)}, f32[256,256]{1,0:T(8,128)}, f32[256,256]{1,0:T(8,...) custom-call(s32[16]{0:T(128)} %len_ref.1, ...), custom_call_target="tpu_custom_call" | custom-call | flops 10066329600 | bytes 8000000 | tf_op jit(solution)/shard_map/attention/pallas_call | solution.py:180
  80.3 4.6 %collective-permute-done.11.b = f32[256,256]{1,0:T(8,128)S(1)} collective-permute-done((f32[256,256]{1,0:T(8,128)}, f32[256,256]{1,0:T(8,128)S(1)}, u32[]{:S(2)}, u32[]{:S(2)}) %collective-permute-start.11) | collective-permute-done | bytes 262176 | tf_op jit(solution)/shard_map/ppermute | solution.py:314
  84.8 2.5 %collective-permute-done.12.d = f32[256,256]{1,0:T(8,128)S(1)} collective-permute-done((f32[256,256]{1,0:T(8,128)}, f32[256,256]{1,0:T(8,128)S(1)}, u32[]{:S(2)}, u32[]{:S(2)}) %collective-permute-start.12) | collective-permute-done | bytes 262176 | tf_op jit(solution)/shard_map/ppermute | solution.py:314
  89.3 4.7 %all-to-all-start.1 = ((bf16[4,128,1280]{2,1,0:T(8,128)(2,1)}), bf16[4,128,1280]{2,1,0:T(8,128)(2,1)S(1)}, u32[]{:S(2)}, u32[]{:S(2)}) async-start(bf16[4,128,1280]{2,1,0:T(8,128)(2,1)} %get-tuple-element.64), calls=%async_computation.1 | async-start | bytes 2621440 | tf_op jit(solution)/shard_map/all_to_all | solution.py:310
  96.1 18.0 %collective-permute-done.14.refs_0_.after.crossing_ref = f32[384,128]{1,0:T(8,128)S(1)} collective-permute-done((f32[384,128]{1,0:T(8,128)S(1)}, f32[384,128]{1,0:T(8,128)S(1)}, u32[]{:S(2)}, u32[]{:S(2)}) %collective-permute-start.14) | collective-permute-done | bytes 196640 | tf_op jit(solution)/shard_map/ppermute | solution.py:350
  114.7 2.1 %collective-permute-start.20 = (f32[384,256]{1,0:T(8,128)S(1)}, f32[384,256]{1,0:T(8,128)S(1)}, u32[]{:S(2)}, u32[]{:S(2)}) collective-permute-start(f32[384,256]{1,0:T(8,128)S(1)} %pack_window.1), channel_id=1, source_target_pairs={{4,0},{5,1},{6,2},{7,3},{8,4},{9,5},{10,6},{11,7},{12,8},{13,9},{1... | collective-permute-start | bytes 1179656 | tf_op jit(solution)/shard_map/ppermute | solution.py:361
  117.5 7.1 %collective-permute-start.18 = (f32[256,256]{1,0:T(8,128)}, f32[256,256]{1,0:T(8,128)}, u32[]{:S(2)}, u32[]{:S(2)}) collective-permute-start(f32[256,256]{1,0:T(8,128)} %get-tuple-element.75), channel_id=1, source_target_pairs={{0,8},{1,9},{2,10},{3,11},{4,12},{5,13},{6,14},{7,15},{8,0},{9,1},... | collective-permute-start | bytes 786440 | tf_op jit(solution)/shard_map/ppermute | solution.py:314
  124.6 2.5 %collective-permute-start.19 = (f32[256,256]{1,0:T(8,128)}, f32[256,256]{1,0:T(8,128)}, u32[]{:S(2)}, u32[]{:S(2)}) collective-permute-start(f32[256,256]{1,0:T(8,128)} %get-tuple-element.76), channel_id=1, source_target_pairs={{0,4},{1,5},{2,6},{3,7},{4,8},{5,9},{6,10},{7,11},{8,12},{9,13},{1... | collective-permute-start | bytes 786440 | tf_op jit(solution)/shard_map/ppermute | solution.py:314
  129.3 5.8 %collective-permute-done.17.n1 = f32[256,256]{1,0:T(8,128)S(1)} collective-permute-done((f32[256,256]{1,0:T(8,128)}, f32[256,256]{1,0:T(8,128)S(1)}, u32[]{:S(2)}, u32[]{:S(2)}) %collective-permute-start.17) | collective-permute-done | bytes 262176 | tf_op jit(solution)/shard_map/ppermute | solution.py:314
  135.1 4.1 %collective-permute-done.18.n2 = f32[256,256]{1,0:T(8,128)} collective-permute-done((f32[256,256]{1,0:T(8,128)}, f32[256,256]{1,0:T(8,128)}, u32[]{:S(2)}, u32[]{:S(2)}) %collective-permute-start.18) | collective-permute-done | bytes 262176 | tf_op jit(solution)/shard_map/ppermute | solution.py:314
  140.4 2.6 %collective-permute-start.21 = (bf16[192,256]{1,0:T(8,128)(2,1)S(1)}, bf16[192,256]{1,0:T(8,128)(2,1)S(1)}, u32[]{:S(2)}, u32[]{:S(2)}) collective-permute-start(bf16[192,256]{1,0:T(8,128)(2,1)S(1)} %get-tuple-element.79), channel_id=1, source_target_pairs={{0,3},{1,0},{2,1},{3,2},{4,7},{5,4},{6,5},{7,6},{8,11},{9,8},{10,9... | collective-permute-start | bytes 294920 | tf_op jit(solution)/shard_map/ppermute | solution.py:306
  145.2 4.0 %collective-permute-done.22.f2 = bf16[192,256]{1,0:T(8,128)(2,1)S(1)} collective-permute-done((bf16[192,256]{1,0:T(8,128)(2,1)S(1)}, bf16[192,256]{1,0:T(8,128)(2,1)S(1)}, u32[]{:S(2)}, u32[]{:S(2)}) %collective-permute-start.22) | collective-permute-done | bytes 98336 | tf_op jit(solution)/shard_map/ppermute | solution.py:306
  (83 shorter events, 23.4 us)
Async XLA Ops:
  5.0 6.4 %collective-permute-start = (bf16[192,256]{1,0:T(8,128)(2,1)}, bf16[192,256]{1,0:T(8,128)(2,1)S(1)}, u32[]{:S(2)}, u32[]{:S(2)}) collective-permute-start(bf16[192,256]{1,0:T(8,128)(2,1)} %get-tuple-element.47), channel_id=1, source_target_pairs={{0,1},{1,2},{2,3},{3,0},{4,5},{5,6},{6,7},{7,4},{8,9},{9,10},{10,1... | collective-permute-start | bytes 294920 | tf_op jit(solution)/shard_map/ppermute | solution.py:306
  6.6 7.6 %collective-permute-start.1 = (bf16[192,256]{1,0:T(8,128)(2,1)}, bf16[192,256]{1,0:T(8,128)(2,1)S(1)}, u32[]{:S(2)}, u32[]{:S(2)}) collective-permute-start(bf16[192,256]{1,0:T(8,128)(2,1)} %get-tuple-element.48), channel_id=1, source_target_pairs={{0,2},{1,3},{2,0},{3,1},{4,6},{5,7},{6,4},{7,5},{8,10},{9,11},{10,... | collective-permute-start | bytes 294920 | tf_op jit(solution)/shard_map/ppermute | solution.py:306
  15.7 28.7 %all-to-all-start = ((bf16[4,128,1280]{2,1,0:T(8,128)(2,1)}), bf16[4,128,1280]{2,1,0:T(8,128)(2,1)S(1)}, u32[]{:S(2)}, u32[]{:S(2)}) async-start(bf16[4,128,1280]{2,1,0:T(8,128)(2,1)} %get-tuple-element.53), calls=%async_computation | async-start | bytes 2621440 | tf_op jit(solution)/shard_map/all_to_all | solution.py:310
  19.6 13.1 %collective-permute-start.4 = (bf16[256,256]{1,0:T(8,128)(2,1)S(1)}, bf16[256,256]{1,0:T(8,128)(2,1)S(1)}, u32[]{:S(2)}, u32[]{:S(2)}) collective-permute-start(bf16[256,256]{1,0:T(8,128)(2,1)S(1)} %get-tuple-element.55.l0), channel_id=1, source_target_pairs={{0,16},{1,17},{2,18},{3,19},{4,20},{5,21},{6,22},{7,23},{8,24},{9,... | collective-permute-start | bytes 393224 | tf_op jit(solution)/shard_map/ppermute | solution.py:318
  25.9 7.8 %collective-permute-start.10 = (bf16[256,256]{1,0:T(8,128)(2,1)S(1)}, bf16[256,256]{1,0:T(8,128)(2,1)S(1)}, u32[]{:S(2)}, u32[]{:S(2)}) collective-permute-start(bf16[256,256]{1,0:T(8,128)(2,1)S(1)} %get-tuple-element.55.l0), channel_id=1, source_target_pairs={{0,12},{1,13},{2,14},{3,15},{4,0},{5,1},{6,2},{7,3},{8,4},{9,5},{1... | collective-permute-start | bytes 393224 | tf_op jit(solution)/shard_map/ppermute | solution.py:314
  26.7 9.5 %collective-permute-start.9 = (bf16[256,256]{1,0:T(8,128)(2,1)S(1)}, bf16[256,256]{1,0:T(8,128)(2,1)S(1)}, u32[]{:S(2)}, u32[]{:S(2)}) collective-permute-start(bf16[256,256]{1,0:T(8,128)(2,1)S(1)} %get-tuple-element.55.l0), channel_id=1, source_target_pairs={{0,8},{1,9},{2,10},{3,11},{4,12},{5,13},{6,14},{7,15},{8,0},{9,1},... | collective-permute-start | bytes 393224 | tf_op jit(solution)/shard_map/ppermute | solution.py:314
  27.6 13.8 %collective-permute-start.3 = (bf16[384,256]{1,0:T(8,128)(2,1)S(1)}, bf16[384,256]{1,0:T(8,128)(2,1)S(1)}, u32[]{:S(2)}, u32[]{:S(2)}) collective-permute-start(bf16[384,256]{1,0:T(8,128)(2,1)S(1)} %get-tuple-element.54), channel_id=1, source_target_pairs={{0,4},{1,5},{2,6},{3,7},{4,8},{5,9},{6,10},{7,11},{8,12},{9,13},{1... | collective-permute-start | bytes 589832 | tf_op jit(solution)/shard_map/ppermute | solution.py:323
  31.2 10.3 %collective-permute-start.8 = (bf16[256,256]{1,0:T(8,128)(2,1)S(1)}, bf16[256,256]{1,0:T(8,128)(2,1)S(1)}, u32[]{:S(2)}, u32[]{:S(2)}) collective-permute-start(bf16[256,256]{1,0:T(8,128)(2,1)S(1)} %get-tuple-element.55.l0), channel_id=1, source_target_pairs={{0,4},{1,5},{2,6},{3,7},{4,8},{5,9},{6,10},{7,11},{8,12},{9,13},{1... | collective-permute-start | bytes 393224 | tf_op jit(solution)/shard_map/ppermute | solution.py:314
  32.8 8.6 %collective-permute-start.7 = (bf16[256,256]{1,0:T(8,128)(2,1)S(1)}, bf16[256,256]{1,0:T(8,128)(2,1)S(1)}, u32[]{:S(2)}, u32[]{:S(2)}) collective-permute-start(bf16[256,256]{1,0:T(8,128)(2,1)S(1)} %collective-permute-done.4.h0), channel_id=1, source_target_pairs={{0,12},{1,13},{2,14},{3,15},{4,0},{5,1},{6,2},{7,3},{8,4},{9,5},{1... | collective-permute-start | bytes 393224 | tf_op jit(solution)/shard_map/ppermute | solution.py:314
  33.7 7.7 %collective-permute-start.6 = (bf16[256,256]{1,0:T(8,128)(2,1)S(1)}, bf16[256,256]{1,0:T(8,128)(2,1)S(1)}, u32[]{:S(2)}, u32[]{:S(2)}) collective-permute-start(bf16[256,256]{1,0:T(8,128)(2,1)S(1)} %collective-permute-done.4.h0), channel_id=1, source_target_pairs={{0,8},{1,9},{2,10},{3,11},{4,12},{5,13},{6,14},{7,15},{8,0},{9,1},... | collective-permute-start | bytes 393224 | tf_op jit(solution)/shard_map/ppermute | solution.py:314
  36.1 8.3 %collective-permute-start.5 = (bf16[256,256]{1,0:T(8,128)(2,1)S(1)}, bf16[256,256]{1,0:T(8,128)(2,1)S(1)}, u32[]{:S(2)}, u32[]{:S(2)}) collective-permute-start(bf16[256,256]{1,0:T(8,128)(2,1)S(1)} %collective-permute-done.4.h0), channel_id=1, source_target_pairs={{0,4},{1,5},{2,6},{3,7},{4,8},{5,9},{6,10},{7,11},{8,12},{9,13},{1... | collective-permute-start | bytes 393224 | tf_op jit(solution)/shard_map/ppermute | solution.py:314
  78.2 6.7 %collective-permute-start.11 = (f32[256,256]{1,0:T(8,128)}, f32[256,256]{1,0:T(8,128)S(1)}, u32[]{:S(2)}, u32[]{:S(2)}) collective-permute-start(f32[256,256]{1,0:T(8,128)} %get-tuple-element.58), channel_id=1, source_target_pairs={{0,4},{1,5},{2,6},{3,7},{4,8},{5,9},{6,10},{7,11},{8,12},{9,13},{1... | collective-permute-start | bytes 786440 | tf_op jit(solution)/shard_map/ppermute | solution.py:314
  79.5 7.8 %collective-permute-start.12 = (f32[256,256]{1,0:T(8,128)}, f32[256,256]{1,0:T(8,128)S(1)}, u32[]{:S(2)}, u32[]{:S(2)}) collective-permute-start(f32[256,256]{1,0:T(8,128)} %get-tuple-element.60), channel_id=1, source_target_pairs={{0,12},{1,13},{2,14},{3,15},{4,0},{5,1},{6,2},{7,3},{8,4},{9,5},{1... | collective-permute-start | bytes 786440 | tf_op jit(solution)/shard_map/ppermute | solution.py:314
  89.3 37.8 %all-to-all-start.1 = ((bf16[4,128,1280]{2,1,0:T(8,128)(2,1)}), bf16[4,128,1280]{2,1,0:T(8,128)(2,1)S(1)}, u32[]{:S(2)}, u32[]{:S(2)}) async-start(bf16[4,128,1280]{2,1,0:T(8,128)(2,1)} %get-tuple-element.64), calls=%async_computation.1 | async-start | bytes 2621440 | tf_op jit(solution)/shard_map/all_to_all | solution.py:310
  94.0 20.1 %collective-permute-start.14 = (f32[384,128]{1,0:T(8,128)S(1)}, f32[384,128]{1,0:T(8,128)S(1)}, u32[]{:S(2)}, u32[]{:S(2)}) collective-permute-start(f32[384,128]{1,0:T(8,128)S(1)} %copy-done.4), channel_id=1, source_target_pairs={{16,12},{17,13},{18,14},{19,15},{48,44},{49,45},{50,46},{51,47},{8... | collective-permute-start | bytes 589832 | tf_op jit(solution)/shard_map/ppermute | solution.py:350
  95.3 18.8 %collective-permute-start.15 = (f32[384,128]{1,0:T(8,128)S(1)}, f32[384,128]{1,0:T(8,128)S(1)}, u32[]{:S(2)}, u32[]{:S(2)}) collective-permute-start(f32[384,128]{1,0:T(8,128)S(1)} %copy-done.5), channel_id=1, source_target_pairs={{16,0},{17,1},{18,2},{19,3},{48,32},{49,33},{50,34},{51,35},{80,64... | collective-permute-start | bytes 589832 | tf_op jit(solution)/shard_map/ppermute | solution.py:351
  96.0 20.7 %collective-permute-start.13 = (f32[256,256]{1,0:T(8,128)S(1)}, f32[256,256]{1,0:T(8,128)S(1)}, u32[]{:S(2)}, u32[]{:S(2)}) collective-permute-start(f32[256,256]{1,0:T(8,128)S(1)} %get-tuple-element.71), channel_id=1, source_target_pairs={{0,4},{1,5},{2,6},{3,7},{4,8},{5,9},{6,10},{7,11},{8,12},{9,13},{1... | collective-permute-start | bytes 786440 | tf_op jit(solution)/shard_map/ppermute | solution.py:314
  114.7 24.5 %collective-permute-start.20 = (f32[384,256]{1,0:T(8,128)S(1)}, f32[384,256]{1,0:T(8,128)S(1)}, u32[]{:S(2)}, u32[]{:S(2)}) collective-permute-start(f32[384,256]{1,0:T(8,128)S(1)} %pack_window.1), channel_id=1, source_target_pairs={{4,0},{5,1},{6,2},{7,3},{8,4},{9,5},{10,6},{11,7},{12,8},{13,9},{1... | collective-permute-start | bytes 1179656 | tf_op jit(solution)/shard_map/ppermute | solution.py:361
  117.5 10.8 %collective-permute-start.16 = (f32[256,256]{1,0:T(8,128)}, f32[256,256]{1,0:T(8,128)}, u32[]{:S(2)}, u32[]{:S(2)}) collective-permute-start(f32[256,256]{1,0:T(8,128)} %far_sum.1), channel_id=1, source_target_pairs={{0,16},{1,17},{2,18},{3,19},{4,20},{5,21},{6,22},{7,23},{8,24},{9,... | collective-permute-start | bytes 786440 | tf_op jit(solution)/shard_map/ppermute | solution.py:318
  117.5 17.6 %collective-permute-start.17 = (f32[256,256]{1,0:T(8,128)}, f32[256,256]{1,0:T(8,128)S(1)}, u32[]{:S(2)}, u32[]{:S(2)}) collective-permute-start(f32[256,256]{1,0:T(8,128)} %get-tuple-element.74), channel_id=1, source_target_pairs={{0,12},{1,13},{2,14},{3,15},{4,0},{5,1},{6,2},{7,3},{8,4},{9,5},{1... | collective-permute-start | bytes 786440 | tf_op jit(solution)/shard_map/ppermute | solution.py:314
  117.5 21.7 %collective-permute-start.18 = (f32[256,256]{1,0:T(8,128)}, f32[256,256]{1,0:T(8,128)}, u32[]{:S(2)}, u32[]{:S(2)}) collective-permute-start(f32[256,256]{1,0:T(8,128)} %get-tuple-element.75), channel_id=1, source_target_pairs={{0,8},{1,9},{2,10},{3,11},{4,12},{5,13},{6,14},{7,15},{8,0},{9,1},... | collective-permute-start | bytes 786440 | tf_op jit(solution)/shard_map/ppermute | solution.py:314
  124.6 14.6 %collective-permute-start.19 = (f32[256,256]{1,0:T(8,128)}, f32[256,256]{1,0:T(8,128)}, u32[]{:S(2)}, u32[]{:S(2)}) collective-permute-start(f32[256,256]{1,0:T(8,128)} %get-tuple-element.76), channel_id=1, source_target_pairs={{0,4},{1,5},{2,6},{3,7},{4,8},{5,9},{6,10},{7,11},{8,12},{9,13},{1... | collective-permute-start | bytes 786440 | tf_op jit(solution)/shard_map/ppermute | solution.py:314
  142.9 6.2 %collective-permute-start.22 = (bf16[192,256]{1,0:T(8,128)(2,1)S(1)}, bf16[192,256]{1,0:T(8,128)(2,1)S(1)}, u32[]{:S(2)}, u32[]{:S(2)}) collective-permute-start(bf16[192,256]{1,0:T(8,128)(2,1)S(1)} %get-tuple-element.80), channel_id=1, source_target_pairs={{0,2},{1,3},{2,0},{3,1},{4,6},{5,7},{6,4},{7,5},{8,10},{9,11},{10,... | collective-permute-start | bytes 294920 | tf_op jit(solution)/shard_map/ppermute | solution.py:306
  143.8 6.3 %collective-permute-start.23 = (bf16[192,256]{1,0:T(8,128)(2,1)S(1)}, bf16[192,256]{1,0:T(8,128)(2,1)S(1)}, u32[]{:S(2)}, u32[]{:S(2)}) collective-permute-start(bf16[192,256]{1,0:T(8,128)(2,1)S(1)} %get-tuple-element.81), channel_id=1, source_target_pairs={{0,1},{1,2},{2,3},{3,0},{4,5},{5,6},{6,7},{7,4},{8,9},{9,10},{10,1... | collective-permute-start | bytes 294920 | tf_op jit(solution)/shard_map/ppermute | solution.py:306
  (24 other events, 163.7 us)

commit v11 on v7

--- a/solution.py
+++ b/solution.py
@@ -62,7 +62,7 @@
         first = PROMPT_ROWS + BACK + lax.rem(x + 4 - d, 4) * 128
         load(source.at[64:192, :], staged.at[pl.ds(pl.multiple_of(first, 128), 128), :])
     load(q_in, q_all)
-    for copy in copies:
+    for copy in copies[:-1]:
         copy.wait()
     place(slice(0, all_rows), staged)
     value1[:, 128:] = jnp.ones((all_rows, 128), jnp.bfloat16)
@@ -73,6 +73,7 @@
         value_t[:128, at] = value1[at, :128].astype(jnp.float32).T.astype(jnp.bfloat16)
     for ref in (key_sum, value_sum, p_second, grad2_second, rows_second):
         ref[...] = jnp.zeros_like(ref)
+    copies[-1].wait()
 
     s_refs, p_refs = (s_first, s_second), (p_first, p_second)
     grad2_refs, rows_refs = (grad2_first, grad2_second), (rows_first, rows_second)
@@ -261,7 +262,7 @@
         target[64:, :] = (own_ref[block_at(x, d), :] + extra).astype(jnp.bfloat16)
 
 
-def far_sum_kernel(a, b, c, after, out_ref):
+def far_sum_kernel(a, b, c, out_ref):
     out_ref[...] = a[...] + b[...] + c[...]
 
 
@@ -331,12 +332,13 @@
     crossing = lax.ppermute(back_grad, "seq", [(i, i - 4) for i in range(16, 20)])
     back_grad, plus = lax.optimization_barrier((back_grad, plus))
     within = lax.ppermute(back_grad, "seq", [(i, i - 4) for i in range(4, 32) if i // 4 != 4])
-    (got,) = call(far_sum_kernel, (), (h0, minus, plus), [((256, 256), f32)], "far_sum", extra=(crossing,))
+    (got,) = call(far_sum_kernel, (), (h0, minus, plus), [((256, 256), f32)], "far_sum")
     got = along_z(got)
     one, two, three = along_y(l1, -1), along_y(l2, -2), along_y(l3, 1)
 
+    o, crossing = lax.optimization_barrier((exchange_x(o), crossing))
     attn_out, q_grad = call(
-        unpack_rows_kernel, (), (exchange_x(o),), [((rows, HEADS * HEAD_DIM), bf16)] * 2, "unpack_rows"
+        unpack_rows_kernel, (), (o,), [((rows, HEADS * HEAD_DIM), bf16)] * 2, "unpack_rows"
     )
     l0, attn_out, q_grad = lax.optimization_barrier((l0, attn_out, q_grad))
 

time: 136 us -> 145 us (1.066)
  the two profiles are of different devices: /device:TPU:32 before, /device:TPU:56 now
where the time goes in v11:
time: 145 us; the launch traced here: 144 us
  waiting for transfers between devices  53.2 us (37%)
  starting transfers between devices  46.7 us (32%)
  Pallas kernels  40.1 us (28%)
  local copies, waits for them, and re-layouts  2.68 us (2%)
    pallas_call x7, Pallas kernels, call(): pl.pallas_call(body, in_specs=[smem] * len(scalars) + [pl.BlockSpec(memor...  40.1 us
    ppermute x12, waiting for transfers between devices, along_y(): lax.ppermute(value, 'seq', [(i, i // 16 * 16 + (i + 4 * step) % 16) for i...  20.5 us
    ppermute x1, waiting for transfers between devices, local(): lax.ppermute(back_grad, 'seq', [(i, i - 4) for i in range(16, 20)])  14.2 us
    ppermute x12, starting transfers between devices, along_y(): lax.ppermute(value, 'seq', [(i, i // 16 * 16 + (i + 4 * step) % 16) for i...  13.1 us
    ppermute x6, starting transfers between devices, along_x(): lax.ppermute(value, 'seq', [(i, i // 4 * 4 + (i + step) % 4) for i in ran...  10.1 us
    ppermute x6, waiting for transfers between devices, along_x(): lax.ppermute(value, 'seq', [(i, i // 4 * 4 + (i + step) % 4) for i in ran...  9.41 us
    ppermute x2, waiting for transfers between devices, along_z(): return lax.ppermute(value, 'seq', [(i, (i + 16) % 32) for i in range(32)])  9.11 us
    all_to_all x2, starting transfers between devices, exchange_x(): lax.all_to_all(value, 'seq', 0, 0, axis_index_groups=X_GROUPS, tiled=True)  8.57 us
  transfers between devices with their start and end apart: 25, of which 13 were waited for; matrix products, arithmetic and copies ran while one was open for 0% of the time, Pallas kernels for 1%

profile of v11, /device:TPU:56, one launch (start us, length us, event | category | flops | bytes accessed | tf_op | source)
XLA Modules:
  0.0 144.4 jit_solution(10299602556247369302)
XLA Ops:
  1.3 3.7 %pack.1 = (bf16[192,256]{1,0:T(8,128)(2,1)}, bf16[192,256]{1,0:T(8,128)(2,1)}, bf16[192,256]{1,0:T(8,128)(2,1)}, bf16[192,256]{1,0:T(8,128)(2,1)}, bf16[4,128,1280]{2,1,0:T(8,128)(2,1)}) custom-call(s32[2]{0:T(128)} %pad_add_fusion.where_ref, bf16[64,512]{1,0:T(8,128)(2,1)} %pk.1, bf16[64,512]{1,0:T(8,128)(2,1)} %pv.1, bf16[128,512]{1,0:T(8,128)(2,1)} %k.1, ...), custom_call_target="tpu_custom_call" | custom-call | tf_op jit(solution)/shard_map/pack/pallas_call | solution.py:177
  5.1 1.6 %collective-permute-start = (bf16[192,256]{1,0:T(8,128)(2,1)}, bf16[192,256]{1,0:T(8,128)(2,1)S(1)}, u32[]{:S(2)}, u32[]{:S(2)}) collective-permute-start(bf16[192,256]{1,0:T(8,128)(2,1)} %get-tuple-element.45), channel_id=1, source_target_pairs={{0,1},{1,2},{2,3},{3,0},{4,5},{5,6},{6,7},{7,4},{8,9},{9,10},{10,1... | collective-permute-start | bytes 294920 | tf_op jit(solution)/shard_map/ppermute | solution.py:287
  6.6 2.7 %collective-permute-start.1 = (bf16[192,256]{1,0:T(8,128)(2,1)}, bf16[192,256]{1,0:T(8,128)(2,1)S(1)}, u32[]{:S(2)}, u32[]{:S(2)}) collective-permute-start(bf16[192,256]{1,0:T(8,128)(2,1)} %get-tuple-element.46), channel_id=1, source_target_pairs={{0,2},{1,3},{2,0},{3,1},{4,6},{5,7},{6,4},{7,5},{8,10},{9,11},{10,... | collective-permute-start | bytes 294920 | tf_op jit(solution)/shard_map/ppermute | solution.py:287
  11.4 2.8 %collective-permute-done.1.s2 = bf16[192,256]{1,0:T(8,128)(2,1)S(1)} collective-permute-done((bf16[192,256]{1,0:T(8,128)(2,1)}, bf16[192,256]{1,0:T(8,128)(2,1)S(1)}, u32[]{:S(2)}, u32[]{:S(2)}) %collective-permute-start.1) | collective-permute-done | bytes 98336 | tf_op jit(solution)/shard_map/ppermute | solution.py:287
  15.8 3.9 %all-to-all-start = ((bf16[4,128,1280]{2,1,0:T(8,128)(2,1)}), bf16[4,128,1280]{2,1,0:T(8,128)(2,1)S(1)}, u32[]{:S(2)}, u32[]{:S(2)}) async-start(bf16[4,128,1280]{2,1,0:T(8,128)(2,1)} %get-tuple-element.51), calls=%async_computation | async-start | bytes 2621440 | tf_op jit(solution)/shard_map/all_to_all | solution.py:291
  19.7 6.3 %collective-permute-start.4 = (bf16[256,256]{1,0:T(8,128)(2,1)S(1)}, bf16[256,256]{1,0:T(8,128)(2,1)S(1)}, u32[]{:S(2)}, u32[]{:S(2)}) collective-permute-start(bf16[256,256]{1,0:T(8,128)(2,1)S(1)} %get-tuple-element.53.l0), channel_id=1, source_target_pairs={{0,16},{1,17},{2,18},{3,19},{4,20},{5,21},{6,22},{7,23},{8,24},{9,... | collective-permute-start | bytes 393224 | tf_op jit(solution)/shard_map/ppermute | solution.py:299
  27.7 3.5 %collective-permute-start.3 = (bf16[384,256]{1,0:T(8,128)(2,1)S(1)}, bf16[384,256]{1,0:T(8,128)(2,1)S(1)}, u32[]{:S(2)}, u32[]{:S(2)}) collective-permute-start(bf16[384,256]{1,0:T(8,128)(2,1)S(1)} %get-tuple-element.52), channel_id=1, source_target_pairs={{0,4},{1,5},{2,6},{3,7},{4,8},{5,9},{6,10},{7,11},{8,12},{9,13},{1... | collective-permute-start | bytes 589832 | tf_op jit(solution)/shard_map/ppermute | solution.py:304
  31.2 1.6 %collective-permute-start.8 = (bf16[256,256]{1,0:T(8,128)(2,1)S(1)}, bf16[256,256]{1,0:T(8,128)(2,1)S(1)}, u32[]{:S(2)}, u32[]{:S(2)}) collective-permute-start(bf16[256,256]{1,0:T(8,128)(2,1)S(1)} %get-tuple-element.53.l0), channel_id=1, source_target_pairs={{0,4},{1,5},{2,6},{3,7},{4,8},{5,9},{6,10},{7,11},{8,12},{9,13},{1... | collective-permute-start | bytes 393224 | tf_op jit(solution)/shard_map/ppermute | solution.py:295
  33.7 2.4 %collective-permute-start.6 = (bf16[256,256]{1,0:T(8,128)(2,1)S(1)}, bf16[256,256]{1,0:T(8,128)(2,1)S(1)}, u32[]{:S(2)}, u32[]{:S(2)}) collective-permute-start(bf16[256,256]{1,0:T(8,128)(2,1)S(1)} %collective-permute-done.4.h0), channel_id=1, source_target_pairs={{0,8},{1,9},{2,10},{3,11},{4,12},{5,13},{6,14},{7,15},{8,0},{9,1},... | collective-permute-start | bytes 393224 | tf_op jit(solution)/shard_map/ppermute | solution.py:295
  37.1 4.3 %collective-permute-done.8.l1 = bf16[256,256]{1,0:T(8,128)(2,1)S(1)} collective-permute-done((bf16[256,256]{1,0:T(8,128)(2,1)S(1)}, bf16[256,256]{1,0:T(8,128)(2,1)S(1)}, u32[]{:S(2)}, u32[]{:S(2)}) %collective-permute-start.8) | collective-permute-done | bytes 131104 | tf_op jit(solution)/shard_map/ppermute | solution.py:295
  41.5 3.0 %collective-permute-done.5.h1 = bf16[256,256]{1,0:T(8,128)(2,1)S(1)} collective-permute-done((bf16[256,256]{1,0:T(8,128)(2,1)S(1)}, bf16[256,256]{1,0:T(8,128)(2,1)S(1)}, u32[]{:S(2)}, u32[]{:S(2)}) %collective-permute-start.5) | collective-permute-done | bytes 131104 | tf_op jit(solution)/shard_map/ppermute | solution.py:295
  46.2 32.0 %attention.1 = (bf16[4,128,1280]{2,1,0:T(8,128)(2,1)}, f32[256,256]{1,0:T(8,128)}, f32[256,256]{1,0:T(8,128)}, f32[256,256]{1,0:T(8,128)}, f32[256,256]{1,0:T(8,...) custom-call(s32[16]{0:T(128)} %len_ref.1, ...), custom_call_target="tpu_custom_call" | custom-call | flops 10066329600 | bytes 8000000 | tf_op jit(solution)/shard_map/attention/pallas_call | solution.py:177
  78.2 4.7 %all-to-all-start.1 = ((bf16[4,128,1280]{2,1,0:T(8,128)(2,1)}), bf16[4,128,1280]{2,1,0:T(8,128)(2,1)S(1)}, u32[]{:S(2)}, u32[]{:S(2)}) async-start(bf16[4,128,1280]{2,1,0:T(8,128)(2,1)} %get-tuple-element.55), calls=%async_computation.1 | async-start | bytes 2621440 | tf_op jit(solution)/shard_map/all_to_all | solution.py:291
  84.2 6.5 %collective-permute-done.16 = f32[256,256]{1,0:T(8,128)S(1)} collective-permute-done((f32[256,256]{1,0:T(8,128)S(1)}, f32[256,256]{1,0:T(8,128)S(1)}, u32[]{:S(2)}, u32[]{:S(2)}) %collective-permute-start.16) | collective-permute-done | bytes 262176 | tf_op jit(solution)/shard_map/ppermute | solution.py:295
  90.8 2.0 %collective-permute-start.17 = (f32[256,256]{1,0:T(8,128)S(1)}, f32[256,256]{1,0:T(8,128)S(1)}, u32[]{:S(2)}, u32[]{:S(2)}) collective-permute-start(f32[256,256]{1,0:T(8,128)S(1)} %add.9), channel_id=1, source_target_pairs={{0,4},{1,5},{2,6},{3,7},{4,8},{5,9},{6,10},{7,11},{8,12},{9,13},{1... | collective-permute-start | bytes 786440 | tf_op jit(solution)/shard_map/ppermute | solution.py:295
  94.2 3.3 %collective-permute-done.17.c = f32[256,256]{1,0:T(8,128)S(1)} collective-permute-done((f32[256,256]{1,0:T(8,128)S(1)}, f32[256,256]{1,0:T(8,128)S(1)}, u32[]{:S(2)}, u32[]{:S(2)}) %collective-permute-start.17) | collective-permute-done | bytes 262176 | tf_op jit(solution)/shard_map/ppermute | solution.py:295
  97.5 3.9 %collective-permute-start.19 = (f32[384,256]{1,0:T(8,128)}, f32[384,256]{1,0:T(8,128)S(1)}, u32[]{:S(2)}, u32[]{:S(2)}) collective-permute-start(f32[384,256]{1,0:T(8,128)} %get-tuple-element.73), channel_id=1, source_target_pairs={{4,0},{5,1},{6,2},{7,3},{8,4},{9,5},{10,6},{11,7},{12,8},{13,9},{1... | collective-permute-start | bytes 1179656 | tf_op jit(solution)/shard_map/ppermute | solution.py:334
  101.6 2.4 %collective-permute-start.13 = (f32[256,256]{1,0:T(8,128)}, f32[256,256]{1,0:T(8,128)}, u32[]{:S(2)}, u32[]{:S(2)}) collective-permute-start(f32[256,256]{1,0:T(8,128)} %get-tuple-element.64), channel_id=1, source_target_pairs={{0,8},{1,9},{2,10},{3,11},{4,12},{5,13},{6,14},{7,15},{8,0},{9,1},... | collective-permute-start | bytes 786440 | tf_op jit(solution)/shard_map/ppermute | solution.py:295
  103.9 2.9 %collective-permute-done.15.b = f32[256,256]{1,0:T(8,128)S(1)} collective-permute-done((f32[256,256]{1,0:T(8,128)S(1)}, f32[256,256]{1,0:T(8,128)S(1)}, u32[]{:S(2)}, u32[]{:S(2)}) %collective-permute-start.15) | collective-permute-done | bytes 262176 | tf_op jit(solution)/shard_map/ppermute | solution.py:295
  106.9 14.2 %collective-permute-done.11.crossing_ref = f32[384,256]{1,0:T(8,128)S(1)} collective-permute-done((f32[384,256]{1,0:T(8,128)}, f32[384,256]{1,0:T(8,128)S(1)}, u32[]{:S(2)}, u32[]{:S(2)}) %collective-permute-start.11) | collective-permute-done | bytes 393248 | tf_op jit(solution)/shard_map/ppermute | solution.py:332
  122.3 9.1 %collective-permute-done.18.got_ref = f32[256,256]{1,0:T(8,128)S(1)} collective-permute-done((f32[256,256]{1,0:T(8,128)S(1)}, f32[256,256]{1,0:T(8,128)S(1)}, u32[]{:S(2)}, u32[]{:S(2)}) %collective-permute-start.18) | collective-permute-done | bytes 262176 | tf_op jit(solution)/shard_map/ppermute | solution.py:299
  132.7 3.3 %collective-permute-start.20 = (bf16[192,256]{1,0:T(8,128)(2,1)S(1)}, bf16[192,256]{1,0:T(8,128)(2,1)S(1)}, u32[]{:S(2)}, u32[]{:S(2)}) collective-permute-start(bf16[192,256]{1,0:T(8,128)(2,1)S(1)} %get-tuple-element.75), channel_id=1, source_target_pairs={{0,3},{1,0},{2,1},{3,2},{4,7},{5,4},{6,5},{7,6},{8,11},{9,8},{10,9... | collective-permute-start | bytes 294920 | tf_op jit(solution)/shard_map/ppermute | solution.py:287
  137.0 2.2 %collective-permute-done.20.f1 = bf16[192,256]{1,0:T(8,128)(2,1)S(1)} collective-permute-done((bf16[192,256]{1,0:T(8,128)(2,1)S(1)}, bf16[192,256]{1,0:T(8,128)(2,1)S(1)}, u32[]{:S(2)}, u32[]{:S(2)}) %collective-permute-start.20) | collective-permute-done | bytes 98336 | tf_op jit(solution)/shard_map/ppermute | solution.py:287
  139.2 3.0 %collective-permute-done.21.f2 = bf16[192,256]{1,0:T(8,128)(2,1)S(1)} collective-permute-done((bf16[192,256]{1,0:T(8,128)(2,1)S(1)}, bf16[192,256]{1,0:T(8,128)(2,1)S(1)}, u32[]{:S(2)}, u32[]{:S(2)}) %collective-permute-start.21) | collective-permute-done | bytes 98336 | tf_op jit(solution)/shard_map/ppermute | solution.py:287
  (79 shorter events, 18.1 us)
Async XLA Ops:
  5.1 6.4 %collective-permute-start = (bf16[192,256]{1,0:T(8,128)(2,1)}, bf16[192,256]{1,0:T(8,128)(2,1)S(1)}, u32[]{:S(2)}, u32[]{:S(2)}) collective-permute-start(bf16[192,256]{1,0:T(8,128)(2,1)} %get-tuple-element.45), channel_id=1, source_target_pairs={{0,1},{1,2},{2,3},{3,0},{4,5},{5,6},{6,7},{7,4},{8,9},{9,10},{10,1... | collective-permute-start | bytes 294920 | tf_op jit(solution)/shard_map/ppermute | solution.py:287
  6.6 7.6 %collective-permute-start.1 = (bf16[192,256]{1,0:T(8,128)(2,1)}, bf16[192,256]{1,0:T(8,128)(2,1)S(1)}, u32[]{:S(2)}, u32[]{:S(2)}) collective-permute-start(bf16[192,256]{1,0:T(8,128)(2,1)} %get-tuple-element.46), channel_id=1, source_target_pairs={{0,2},{1,3},{2,0},{3,1},{4,6},{5,7},{6,4},{7,5},{8,10},{9,11},{10,... | collective-permute-start | bytes 294920 | tf_op jit(solution)/shard_map/ppermute | solution.py:287
  15.8 28.7 %all-to-all-start = ((bf16[4,128,1280]{2,1,0:T(8,128)(2,1)}), bf16[4,128,1280]{2,1,0:T(8,128)(2,1)S(1)}, u32[]{:S(2)}, u32[]{:S(2)}) async-start(bf16[4,128,1280]{2,1,0:T(8,128)(2,1)} %get-tuple-element.51), calls=%async_computation | async-start | bytes 2621440 | tf_op jit(solution)/shard_map/all_to_all | solution.py:291
  19.7 13.1 %collective-permute-start.4 = (bf16[256,256]{1,0:T(8,128)(2,1)S(1)}, bf16[256,256]{1,0:T(8,128)(2,1)S(1)}, u32[]{:S(2)}, u32[]{:S(2)}) collective-permute-start(bf16[256,256]{1,0:T(8,128)(2,1)S(1)} %get-tuple-element.53.l0), channel_id=1, source_target_pairs={{0,16},{1,17},{2,18},{3,19},{4,20},{5,21},{6,22},{7,23},{8,24},{9,... | collective-permute-start | bytes 393224 | tf_op jit(solution)/shard_map/ppermute | solution.py:299
  26.0 7.8 %collective-permute-start.10 = (bf16[256,256]{1,0:T(8,128)(2,1)S(1)}, bf16[256,256]{1,0:T(8,128)(2,1)S(1)}, u32[]{:S(2)}, u32[]{:S(2)}) collective-permute-start(bf16[256,256]{1,0:T(8,128)(2,1)S(1)} %get-tuple-element.53.l0), channel_id=1, source_target_pairs={{0,12},{1,13},{2,14},{3,15},{4,0},{5,1},{6,2},{7,3},{8,4},{9,5},{1... | collective-permute-start | bytes 393224 | tf_op jit(solution)/shard_map/ppermute | solution.py:295
  26.7 9.5 %collective-permute-start.9 = (bf16[256,256]{1,0:T(8,128)(2,1)S(1)}, bf16[256,256]{1,0:T(8,128)(2,1)S(1)}, u32[]{:S(2)}, u32[]{:S(2)}) collective-permute-start(bf16[256,256]{1,0:T(8,128)(2,1)S(1)} %get-tuple-element.53.l0), channel_id=1, source_target_pairs={{0,8},{1,9},{2,10},{3,11},{4,12},{5,13},{6,14},{7,15},{8,0},{9,1},... | collective-permute-start | bytes 393224 | tf_op jit(solution)/shard_map/ppermute | solution.py:295
  27.7 13.8 %collective-permute-start.3 = (bf16[384,256]{1,0:T(8,128)(2,1)S(1)}, bf16[384,256]{1,0:T(8,128)(2,1)S(1)}, u32[]{:S(2)}, u32[]{:S(2)}) collective-permute-start(bf16[384,256]{1,0:T(8,128)(2,1)S(1)} %get-tuple-element.52), channel_id=1, source_target_pairs={{0,4},{1,5},{2,6},{3,7},{4,8},{5,9},{6,10},{7,11},{8,12},{9,13},{1... | collective-permute-start | bytes 589832 | tf_op jit(solution)/shard_map/ppermute | solution.py:304
  31.2 10.3 %collective-permute-start.8 = (bf16[256,256]{1,0:T(8,128)(2,1)S(1)}, bf16[256,256]{1,0:T(8,128)(2,1)S(1)}, u32[]{:S(2)}, u32[]{:S(2)}) collective-permute-start(bf16[256,256]{1,0:T(8,128)(2,1)S(1)} %get-tuple-element.53.l0), channel_id=1, source_target_pairs={{0,4},{1,5},{2,6},{3,7},{4,8},{5,9},{6,10},{7,11},{8,12},{9,13},{1... | collective-permute-start | bytes 393224 | tf_op jit(solution)/shard_map/ppermute | solution.py:295
  32.8 8.6 %collective-permute-start.7 = (bf16[256,256]{1,0:T(8,128)(2,1)S(1)}, bf16[256,256]{1,0:T(8,128)(2,1)S(1)}, u32[]{:S(2)}, u32[]{:S(2)}) collective-permute-start(bf16[256,256]{1,0:T(8,128)(2,1)S(1)} %collective-permute-done.4.h0), channel_id=1, source_target_pairs={{0,12},{1,13},{2,14},{3,15},{4,0},{5,1},{6,2},{7,3},{8,4},{9,5},{1... | collective-permute-start | bytes 393224 | tf_op jit(solution)/shard_map/ppermute | solution.py:295
  33.7 7.7 %collective-permute-start.6 = (bf16[256,256]{1,0:T(8,128)(2,1)S(1)}, bf16[256,256]{1,0:T(8,128)(2,1)S(1)}, u32[]{:S(2)}, u32[]{:S(2)}) collective-permute-start(bf16[256,256]{1,0:T(8,128)(2,1)S(1)} %collective-permute-done.4.h0), channel_id=1, source_target_pairs={{0,8},{1,9},{2,10},{3,11},{4,12},{5,13},{6,14},{7,15},{8,0},{9,1},... | collective-permute-start | bytes 393224 | tf_op jit(solution)/shard_map/ppermute | solution.py:295
  36.2 8.3 %collective-permute-start.5 = (bf16[256,256]{1,0:T(8,128)(2,1)S(1)}, bf16[256,256]{1,0:T(8,128)(2,1)S(1)}, u32[]{:S(2)}, u32[]{:S(2)}) collective-permute-start(bf16[256,256]{1,0:T(8,128)(2,1)S(1)} %collective-permute-done.4.h0), channel_id=1, source_target_pairs={{0,4},{1,5},{2,6},{3,7},{4,8},{5,9},{6,10},{7,11},{8,12},{9,13},{1... | collective-permute-start | bytes 393224 | tf_op jit(solution)/shard_map/ppermute | solution.py:295
  78.2 42.9 %all-to-all-start.1 = ((bf16[4,128,1280]{2,1,0:T(8,128)(2,1)}), bf16[4,128,1280]{2,1,0:T(8,128)(2,1)S(1)}, u32[]{:S(2)}, u32[]{:S(2)}) async-start(bf16[4,128,1280]{2,1,0:T(8,128)(2,1)} %get-tuple-element.55), calls=%async_computation.1 | async-start | bytes 2621440 | tf_op jit(solution)/shard_map/all_to_all | solution.py:291
  82.9 7.8 %collective-permute-start.16 = (f32[256,256]{1,0:T(8,128)S(1)}, f32[256,256]{1,0:T(8,128)S(1)}, u32[]{:S(2)}, u32[]{:S(2)}) collective-permute-start(f32[256,256]{1,0:T(8,128)S(1)} %copy-done.13), channel_id=1, source_target_pairs={{0,4},{1,5},{2,6},{3,7},{4,8},{5,9},{6,10},{7,11},{8,12},{9,13},{1... | collective-permute-start | bytes 786440 | tf_op jit(solution)/shard_map/ppermute | solution.py:295
  90.8 6.7 %collective-permute-start.17 = (f32[256,256]{1,0:T(8,128)S(1)}, f32[256,256]{1,0:T(8,128)S(1)}, u32[]{:S(2)}, u32[]{:S(2)}) collective-permute-start(f32[256,256]{1,0:T(8,128)S(1)} %add.9), channel_id=1, source_target_pairs={{0,4},{1,5},{2,6},{3,7},{4,8},{5,9},{6,10},{7,11},{8,12},{9,13},{1... | collective-permute-start | bytes 786440 | tf_op jit(solution)/shard_map/ppermute | solution.py:295
  92.8 28.3 %collective-permute-start.11 = (f32[384,256]{1,0:T(8,128)}, f32[384,256]{1,0:T(8,128)S(1)}, u32[]{:S(2)}, u32[]{:S(2)}) collective-permute-start(f32[384,256]{1,0:T(8,128)} %get-tuple-element.73), channel_id=1, source_target_pairs={{16,12},{17,13},{18,14},{19,15},{48,44},{49,45},{50,46},{51,47},{8... | collective-permute-start | bytes 1179656 | tf_op jit(solution)/shard_map/ppermute | solution.py:332
  94.1 12.7 %collective-permute-start.15 = (f32[256,256]{1,0:T(8,128)S(1)}, f32[256,256]{1,0:T(8,128)S(1)}, u32[]{:S(2)}, u32[]{:S(2)}) collective-permute-start(f32[256,256]{1,0:T(8,128)S(1)} %copy-done.12), channel_id=1, source_target_pairs={{0,12},{1,13},{2,14},{3,15},{4,0},{5,1},{6,2},{7,3},{8,4},{9,5},{1... | collective-permute-start | bytes 786440 | tf_op jit(solution)/shard_map/ppermute | solution.py:295
  97.5 33.8 %collective-permute-start.19 = (f32[384,256]{1,0:T(8,128)}, f32[384,256]{1,0:T(8,128)S(1)}, u32[]{:S(2)}, u32[]{:S(2)}) collective-permute-start(f32[384,256]{1,0:T(8,128)} %get-tuple-element.73), channel_id=1, source_target_pairs={{4,0},{5,1},{6,2},{7,3},{8,4},{9,5},{10,6},{11,7},{12,8},{13,9},{1... | collective-permute-start | bytes 1179656 | tf_op jit(solution)/shard_map/ppermute | solution.py:334
  101.5 20.8 %collective-permute-start.12 = (f32[256,256]{1,0:T(8,128)}, f32[256,256]{1,0:T(8,128)}, u32[]{:S(2)}, u32[]{:S(2)}) collective-permute-start(f32[256,256]{1,0:T(8,128)} %get-tuple-element.63), channel_id=1, source_target_pairs={{0,12},{1,13},{2,14},{3,15},{4,0},{5,1},{6,2},{7,3},{8,4},{9,5},{1... | collective-permute-start | bytes 786440 | tf_op jit(solution)/shard_map/ppermute | solution.py:295
  101.6 20.7 %collective-permute-start.13 = (f32[256,256]{1,0:T(8,128)}, f32[256,256]{1,0:T(8,128)}, u32[]{:S(2)}, u32[]{:S(2)}) collective-permute-start(f32[256,256]{1,0:T(8,128)} %get-tuple-element.64), channel_id=1, source_target_pairs={{0,8},{1,9},{2,10},{3,11},{4,12},{5,13},{6,14},{7,15},{8,0},{9,1},... | collective-permute-start | bytes 786440 | tf_op jit(solution)/shard_map/ppermute | solution.py:295
  106.8 15.4 %collective-permute-start.14 = (f32[256,256]{1,0:T(8,128)}, f32[256,256]{1,0:T(8,128)}, u32[]{:S(2)}, u32[]{:S(2)}) collective-permute-start(f32[256,256]{1,0:T(8,128)} %get-tuple-element.65), channel_id=1, source_target_pairs={{0,4},{1,5},{2,6},{3,7},{4,8},{5,9},{6,10},{7,11},{8,12},{9,13},{1... | collective-permute-start | bytes 786440 | tf_op jit(solution)/shard_map/ppermute | solution.py:295
  121.1 10.3 %collective-permute-start.18 = (f32[256,256]{1,0:T(8,128)S(1)}, f32[256,256]{1,0:T(8,128)S(1)}, u32[]{:S(2)}, u32[]{:S(2)}) collective-permute-start(f32[256,256]{1,0:T(8,128)S(1)} %far_sum.1), channel_id=1, source_target_pairs={{0,16},{1,17},{2,18},{3,19},{4,20},{5,21},{6,22},{7,23},{8,24},{9,... | collective-permute-start | bytes 786440 | tf_op jit(solution)/shard_map/ppermute | solution.py:299
  132.7 6.5 %collective-permute-start.20 = (bf16[192,256]{1,0:T(8,128)(2,1)S(1)}, bf16[192,256]{1,0:T(8,128)(2,1)S(1)}, u32[]{:S(2)}, u32[]{:S(2)}) collective-permute-start(bf16[192,256]{1,0:T(8,128)(2,1)S(1)} %get-tuple-element.75), channel_id=1, source_target_pairs={{0,3},{1,0},{2,1},{3,2},{4,7},{5,4},{6,5},{7,6},{8,11},{9,8},{10,9... | collective-permute-start | bytes 294920 | tf_op jit(solution)/shard_map/ppermute | solution.py:287
  136.0 6.2 %collective-permute-start.21 = (bf16[192,256]{1,0:T(8,128)(2,1)S(1)}, bf16[192,256]{1,0:T(8,128)(2,1)S(1)}, u32[]{:S(2)}, u32[]{:S(2)}) collective-permute-start(bf16[192,256]{1,0:T(8,128)(2,1)S(1)} %get-tuple-element.76), channel_id=1, source_target_pairs={{0,2},{1,3},{2,0},{3,1},{4,6},{5,7},{6,4},{7,5},{8,10},{9,11},{10,... | collective-permute-start | bytes 294920 | tf_op jit(solution)/shard_map/ppermute | solution.py:287
  136.2 6.9 %collective-permute-start.22 = (bf16[192,256]{1,0:T(8,128)(2,1)S(1)}, bf16[192,256]{1,0:T(8,128)(2,1)S(1)}, u32[]{:S(2)}, u32[]{:S(2)}) collective-permute-start(bf16[192,256]{1,0:T(8,128)(2,1)S(1)} %get-tuple-element.77), channel_id=1, source_target_pairs={{0,1},{1,2},{2,3},{3,0},{4,5},{5,6},{6,7},{7,4},{8,9},{9,10},{10,1... | collective-permute-start | bytes 294920 | tf_op jit(solution)/shard_map/ppermute | solution.py:287
  (23 other events, 269.9 us)
